TPU v7x, 256 devices: a whole 4x4x8 slice. The times are simulated.
256 devices in a mesh: query: 8 (over y, core), passage: 32 (over x, z).
Axes of the slice: x: 4, y: 4, z: 8, core: 2. Of those that a mesh axis runs over, the one named last changes fastest.
Arguments:
- tokens: bfloat16 [4096, 32, 768], P(('query', 'passage')), may hold values from -6 to 6
- weight_in: bfloat16 [768, 3072], replicated, may hold values from -0.21875 to 0.21875
- bias_in: float32 [3072], replicated, may hold values from -3 to 3
- weight_out: bfloat16 [3072, 768], replicated, may hold values from -0.109375 to 0.109375
- bias_out: float32 [768], replicated, may hold values from -3 to 3
- norm_gain: float32 [768], replicated, may hold values from 0.5 to 1.5
- norm_shift: float32 [768], replicated, may hold values from -2 to 2
- projection: bfloat16 [768, 128], replicated, may hold values from -0.21875 to 0.21875
- tiles: bfloat16 [384, 128, 128], P('passage'), may hold values from -0.5 to 0.5
- lengths: int32 [384], P('passage'), may hold values from 16 to 128
- slots: int32 [4096, 32, 4], P('query', 'passage'), may hold values from 0 to 11
- counts: int32 [4096, 32], P('query', 'passage'), may hold values from 0 to 4
Outputs:
- scores: float32 [4096, 32, 4], P(('query', 'passage'))
Inputs may be any that keep to these rules, and one draw needn't show every extreme that they name: `slots`: slot of a candidate tile among the 12 tiles of its shard. slots c with c >= counts[q, s] are unused. Positions j >= lengths[t] of a tile are padding.
All inputs are finite; a program needn't handle non-finite values.
Results may differ from a plain program's by a relative error of at most 0.0004.
Values may be sent and summed in bfloat16 or wider, within the bound.
No kernel may reach another device: no remote copies, remote signals or barrier semaphores. Data moves between devices by JAX's collectives and lax.ppermute only.
A program may use at most 64 MiB of HBM per device.

v0:
```python
import math

import jax
import jax.numpy as jnp
from jax import lax
from jax.sharding import PartitionSpec as P


def score_queries(query_emb, slot_block, count_block, flat_tiles, tile_mask, tile_count):
    group = query_emb.shape[0]
    query_len = query_emb.shape[1]
    rows = query_emb.reshape(group * query_len, query_emb.shape[2])
    similar = lax.dot_general(
        rows, flat_tiles, (((1,), (1,)), ((), ())), preferred_element_type=jnp.float32
    )
    similar = similar.reshape(group, query_len, tile_count, similar.shape[1] // tile_count)
    best = jnp.max(jnp.where(tile_mask[None, None, :, :], similar, jnp.float32(-1e30)), axis=-1)
    tile_score = jnp.sum(best, axis=1)
    tile_ids = jnp.arange(tile_count, dtype=jnp.int32)
    picks = slot_block[:, :, None] == tile_ids[None, None, :]
    summed = jnp.sum(jnp.where(picks, tile_score[:, None, :], jnp.float32(0.0)), axis=-1)
    valid = jnp.arange(slot_block.shape[1], dtype=jnp.int32)[None, :] < count_block[:, None]
    return jnp.where(valid, summed, jnp.float32(0.0))


def shards(
    tokens,
    weight_in,
    bias_in,
    weight_out,
    bias_out,
    norm_gain,
    norm_shift,
    projection,
    tiles,
    lengths,
    slots,
    counts,
):
    queries_here = tokens.shape[0]
    query_len = tokens.shape[1]
    width = tokens.shape[2]
    flat_tokens = tokens.reshape(queries_here * query_len, width)
    pre = jnp.dot(flat_tokens, weight_in, preferred_element_type=jnp.float32) + bias_in
    hidden = jax.nn.gelu(pre, approximate=False).astype(jnp.bfloat16)
    total = jnp.dot(hidden, weight_out, preferred_element_type=jnp.float32)
    total = total + bias_out + flat_tokens.astype(jnp.float32)
    center = jnp.mean(total, axis=-1, keepdims=True)
    spread = jnp.mean((total - center) ** 2, axis=-1, keepdims=True)
    normed = ((total - center) / jnp.sqrt(spread + 1e-05) * norm_gain + norm_shift).astype(
        jnp.bfloat16
    )
    projected = jnp.dot(normed, projection, preferred_element_type=jnp.float32)
    scale = 1.0 / jnp.sqrt(jnp.sum(projected * projected, axis=-1, keepdims=True) + 1e-06)
    embeds = (
        (projected * scale)
        .astype(jnp.bfloat16)
        .reshape(queries_here, query_len, projection.shape[1])
    )
    tile_count = tiles.shape[0]
    tile_len = tiles.shape[1]
    flat_tiles = tiles.reshape(tile_count * tile_len, tiles.shape[2])
    position = jnp.arange(tile_len, dtype=jnp.int32)
    tile_mask = position[None, :] < lengths[:, None]
    slot_count = slots.shape[2]
    slot_table = slots[:, 0, :]
    count_table = counts[:, 0]
    piece = lax.all_gather(embeds, "passage", axis=0, tiled=True)
    amount = piece.shape[0]
    block_size = math.gcd(amount, queries_here)
    blocks = amount // block_size

    def one_block(inputs):
        return score_queries(inputs[0], inputs[1], inputs[2], flat_tiles, tile_mask, tile_count)

    result = lax.map(
        one_block,
        (
            piece.reshape(blocks, block_size, piece.shape[1], piece.shape[2]),
            slot_table.reshape(blocks, block_size, slot_count),
            count_table.reshape(blocks, block_size),
        ),
    )
    local_scores = result.reshape(amount, slot_count)
    return lax.all_to_all(
        local_scores[:, None, :], "passage", split_axis=0, concat_axis=1, tiled=True
    )


def solution(mesh):
    placed = (
        P(("query", "passage"), None, None),
        P(),
        P(),
        P(),
        P(),
        P(),
        P(),
        P(),
        P("passage", None, None),
        P("passage"),
        P("query", "passage", None),
        P("query", "passage"),
    )
    return jax.shard_map(
        shards,
        mesh=mesh,
        in_specs=placed,
        out_specs=P(("query", "passage"), None, None),
        check_vma=False,
    )
```

profile of v0, /device:TPU:16, one launch (start us, length us, event | category | flops | bytes accessed | tf_op | source)
XLA Modules:
  0.0 213.6 jit_solution(11252586063001302154)
XLA Ops:
  6.5 21.3 %fusion.49 = (f32[512]{0:T(512)S(1)}, f32[512,768]{1,0:T(8,128)S(1)}) fusion(bf16[512,768]{1,0:T(8,128)(2,1)} %bitcast.53, f32[768]{0:T(1024)} %param.18, bf16[3072,768]{1,0:T(8,128)(2,1)} %param.17, bf16[768,3072]{1,0:T(8,128)(2,1)} %param.15, f32[3072]{0:T(1024)} %param.16), kind=kOutput, calls=%fused_computation.73 | convolution fusion | flops 4937219584 | bytes 11813888 | tf_op jit(solution)/shard_map/dot_general | solution.py:46
  27.9 0.3 multiply_reduce_fusion
  28.3 0.6 multiply_reduce_fusion.1
  28.8 0.8 multiply_convert_fusion
  29.7 0.5 broadcast.78
  30.2 0.6 reduce.3
  31.0 83.3 %all-gather.2.cloned.1.call-done = bf16[512,32,128]{2,1,0:T(8,128)(2,1)} async-done(((bf16[16,32,128]{2,1,0:T(8,128)(2,1)}), bf16[512,32,128]{2,1,0:T(8,128)(2,1)}) %all-gather.2.cloned.1.call-update) | async-done | bytes 4194320 | tf_op jit(solution)/shard_map/all_gather | solution.py:68
  114.4 74.6 %while.11 = (s32[]{:T(128)}, f32[32,16,4]{1,2,0:T(4,128)S(1)}, s32[32,16]{1,0:T(8,128)S(1)}, s32[32,16,4]{1,0,2:T(8,128)S(1)}, bf16[32,16,32,128]{3,2,1,0:T(8,12...) while((s32[]{:T(128)}, f32[32,16,4]{1,2,0:T(4,128)S(1)}, ...), condition=%wide.region_7.8_spmd.clone, body=%wide.region_3.7_spmd.clone.sunk | while | flops 202903168 | bytes 586013 | solution.py:76
  114.4 2.0 select_reduce_fusion.4
  116.4 0.1 reduce_sum.60
  116.8 2.0 select_reduce_fusion.4
  118.7 0.1 reduce_sum.60
  119.1 2.0 select_reduce_fusion.4
  121.1 0.1 reduce_sum.60
  121.4 2.0 select_reduce_fusion.4
  123.4 0.1 reduce_sum.60
  123.8 2.0 select_reduce_fusion.4
  125.7 0.1 reduce_sum.60
  126.1 2.0 select_reduce_fusion.4
  128.1 0.1 reduce_sum.60
  128.4 2.0 select_reduce_fusion.4
  130.4 0.1 reduce_sum.60
  130.8 2.0 select_reduce_fusion.4
  132.7 0.1 reduce_sum.60
  133.1 2.0 select_reduce_fusion.4
  135.1 0.1 reduce_sum.60
  135.4 2.0 select_reduce_fusion.4
  137.4 0.1 reduce_sum.60
  137.8 2.0 select_reduce_fusion.4
  139.7 0.1 reduce_sum.60
  140.1 2.0 select_reduce_fusion.4
  142.1 0.1 reduce_sum.60
  142.4 2.0 select_reduce_fusion.4
  144.8 2.0 select_reduce_fusion.4
  146.7 0.1 reduce_sum.60
  147.1 2.0 select_reduce_fusion.4
  149.4 2.0 select_reduce_fusion.4
  151.4 0.1 reduce_sum.60
  151.8 2.0 select_reduce_fusion.4
  153.7 0.1 reduce_sum.60
  154.1 2.0 select_reduce_fusion.4
  156.4 2.0 select_reduce_fusion.4
  158.4 0.1 reduce_sum.60
  158.8 2.0 select_reduce_fusion.4
  161.1 2.0 select_reduce_fusion.4
  163.1 0.1 reduce_sum.60
  163.4 2.0 select_reduce_fusion.4
  165.7 2.0 select_reduce_fusion.4
  168.1 2.0 select_reduce_fusion.4
  170.1 0.1 reduce_sum.60
  170.4 2.0 select_reduce_fusion.4
  172.7 2.0 select_reduce_fusion.4
  174.7 0.1 reduce_sum.60
  175.1 2.0 select_reduce_fusion.4
  177.4 2.0 select_reduce_fusion.4
  179.4 0.1 reduce_sum.60
  179.7 2.0 select_reduce_fusion.4
  182.1 2.0 select_reduce_fusion.4
  184.4 2.0 select_reduce_fusion.4
  186.4 0.1 reduce_sum.60
  186.7 2.0 select_reduce_fusion.4
  189.0 0.3 copy.36
  189.3 16.6 %all_to_all.18 = f32[512,1,4]{2,1,0:T(1,128)S(1)} all-to-all(f32[512,1,4]{2,1,0:T(1,128)S(1)} %bitcast.48), channel_id=1, replica_groups=mesh['query'=8,'passage'=32] {'passage'}, dimensions={0} | all-to-all | bytes 16384 | tf_op jit(solution)/shard_map/all_to_all | solution.py:85
  205.9 0.8 copy.34
  (225 shorter events, 8.2 us)
Async XLA Ops:
  6.5 21.7 %copy-start = (bf16[768,128]{1,0:T(8,128)(2,1)S(1)}, bf16[768,128]{1,0:T(8,128)(2,1)}, u32[]{:S(2)}) copy-start(bf16[768,128]{1,0:T(8,128)(2,1)} %param.21) | copy-start | bytes 589828
  6.5 107.8 %all-gather.2.cloned.1.call-start = ((), (), s32[]{:S(2)}) async-start(), calls=%async_computation.1 | async-start | bytes 4325376 | tf_op jit(solution)/shard_map/all_gather | solution.py:68
  6.5 21.7 %copy-start.5 = (f32[768]{0:T(1024)S(1)}, f32[768]{0:T(1024)}, u32[]{:S(2)}) copy-start(f32[768]{0:T(1024)} %param.20) | copy-start | bytes 9220
  6.5 21.7 %copy-start.6 = (f32[768]{0:T(1024)S(1)}, f32[768]{0:T(1024)}, u32[]{:S(2)}) copy-start(f32[768]{0:T(1024)} %param.19) | copy-start | bytes 9220
  27.9 2.4 %copy-start.3 = (s32[512,1]{0,1:T(1,128)S(1)}, s32[512,1]{0,1:T(1,128)}, u32[]{:S(2)}) copy-start(s32[512,1]{0,1:T(1,128)} %param.25) | copy-start | bytes 6148
  27.9 3.1 %copy-start.2 = (s32[512,1,4]{0,2,1:T(4,128)S(1)}, s32[512,1,4]{0,2,1:T(4,128)}, u32[]{:S(2)}) copy-start(s32[512,1,4]{0,2,1:T(4,128)} %param.24) | copy-start | bytes 24580
  27.9 86.5 %copy-start.1 = (s32[12]{0:T(128)S(1)}, s32[12]{0:T(128)}, u32[]{:S(2)}) copy-start(s32[12]{0:T(128)} %param.23) | copy-start | bytes 148
  27.9 86.5 %copy-start.4 = (bf16[12,128,128]{2,1,0:T(8,128)(2,1)S(1)}, bf16[12,128,128]{2,1,0:T(8,128)(2,1)}, u32[]{:S(2)}) copy-start(bf16[12,128,128]{2,1,0:T(8,128)(2,1)} %param.22) | copy-start | bytes 1179652
Sparse Core Ops, SparseCore 0:
  29.8 84.5 all-gather.1
where the time goes:
time: 214 us
  matrix products  85 us (40%)
  waiting for transfers between devices  83.3 us (39%)
  blocking collectives  16.6 us (8%)
  between operations  13.5 us (6%)
  other arithmetic  8.73 us (4%)
  local copies, waits for them, and re-layouts  5.04 us (2%)
    all_gather x1, waiting for transfers between devices, shards(): piece = lax.all_gather(embeds, 'passage', axis=0, tiled=True)  83.3 us
    dot_general x32, matrix products, score_queries(): lax.dot_general(rows, flat_tiles, (((1,), (1,)), ((), ())), preferred_ele...  63.1 us
    dot_general x1, matrix products, shards(): total = jnp.dot(hidden, weight_out, preferred_element_type=jnp.float32)  21.3 us
    all_to_all x1, blocking collectives, shards(): lax.all_to_all(local_scores[:, None, :], 'passage', split_axis=0, concat_...  16.6 us
  transfers between devices with their start and end apart: 1, of which 1 were waited for; matrix products, arithmetic and copies ran while one was open for 1% of the time, Pallas kernels for 0%

commit v1 on v0

v1 whole, which is shorter than its diff:
```python
import functools

import jax
import jax.numpy as jnp
from jax import lax
from jax.experimental import pallas as pl
from jax.experimental.pallas import tpu as pltpu
from jax.sharding import Mesh
from jax.sharding import PartitionSpec as P

Y, CORES, X, Z = 4, 2, 4, 8
HALF_ROOT = 0.7071067811865476


def turn(size, step):
    return [(i, (i + step) % size) for i in range(size)]


def gelu(pre):
    return 0.5 * pre * (1.0 + lax.erf(pre * jnp.float32(HALF_ROOT)))


def ffn_part(tok, w_in, b_in, w_out):
    pre = jnp.dot(tok[...], w_in[...], preferred_element_type=jnp.float32) + b_in[...]
    hidden = gelu(pre).astype(jnp.bfloat16)
    return jnp.dot(hidden, w_out[...], preferred_element_type=jnp.float32)


def ffn_first(tok, w_in, b_in, w_out, acc):
    part = ffn_part(tok, w_in, b_in, w_out)

    @pl.when(pl.program_id(0) == 0)
    def _():
        acc[...] = part

    @pl.when(pl.program_id(0) > 0)
    def _():
        acc[...] += part


def ffn_second(tok, w_in, b_in, w_out, begun, b_out, gain, shift, proj, out, acc, turned, *, queries, tokens):
    part = ffn_part(tok, w_in, b_in, w_out)

    @pl.when(pl.program_id(0) == 0)
    def _():
        acc[...] = begun[...] + part

    @pl.when(pl.program_id(0) > 0)
    def _():
        acc[...] += part

    @pl.when(pl.program_id(0) == pl.num_programs(0) - 1)
    def _():
        total = acc[...] + b_out[...] + tok[...].astype(jnp.float32)
        diff = total - jnp.mean(total, axis=-1, keepdims=True)
        spread = jnp.mean(diff * diff, axis=-1, keepdims=True)
        normed = (diff * lax.rsqrt(spread + 1e-5) * gain[...] + shift[...]).astype(jnp.bfloat16)
        projected = jnp.dot(normed, proj[...], preferred_element_type=jnp.float32)
        scale = lax.rsqrt(jnp.sum(projected * projected, axis=-1, keepdims=True) + 1e-6)
        embeds = projected * scale
        for q in range(queries):
            turned[pl.ds(q, tokens, stride=queries), :] = embeds[q * tokens : (q + 1) * tokens, :]
        out[...] = turned[...].astype(jnp.bfloat16)


def encode(tok, w_in, b_in, w_out, b_out, gain, shift, proj, queries, tokens, chunk=768):
    rows, width = tok.shape
    steps = w_in.shape[1] // chunk
    first = steps // 2
    params = pltpu.CompilerParams(vmem_limit_bytes=40 << 20)

    def whole(a):
        return pl.BlockSpec(a.shape, lambda j: (0,) * a.ndim)

    def pieces(skip):
        return [
            whole(tok),
            pl.BlockSpec((width, chunk), lambda j: (0, j + skip)),
            pl.BlockSpec((1, chunk), lambda j: (0, j + skip)),
            pl.BlockSpec((chunk, width), lambda j: (j + skip, 0)),
        ]

    def cost(n):
        return pl.CostEstimate(flops=4 * rows * width * chunk * n, bytes_accessed=4 * width * chunk * n, transcendentals=0)

    begun = pl.pallas_call(
        ffn_first,
        grid=(first,),
        in_specs=pieces(0),
        out_specs=pl.BlockSpec((rows, width), lambda j: (0, 0)),
        out_shape=jax.ShapeDtypeStruct((rows, width), jnp.float32),
        compiler_params=params,
        cost_estimate=cost(first),
        name="ffn_first",
    )(tok, w_in, b_in, w_out)
    return begun, lambda begun: pl.pallas_call(
        functools.partial(ffn_second, queries=queries, tokens=tokens),
        grid=(steps - first,),
        in_specs=pieces(first) + [whole(begun), whole(b_out), whole(gain), whole(shift), whole(proj)],
        out_specs=pl.BlockSpec((rows, proj.shape[1]), lambda j: (0, 0)),
        out_shape=jax.ShapeDtypeStruct((rows, proj.shape[1]), jnp.bfloat16),
        scratch_shapes=[pltpu.VMEM((rows, width), jnp.float32), pltpu.VMEM((rows, proj.shape[1]), jnp.float32)],
        compiler_params=params,
        cost_estimate=cost(steps - first),
        name="ffn_second",
    )(tok, w_in, b_in, w_out, begun, b_out, gain, shift, proj)


def score_kernel(place, mine, other, *refs, tiles, length, group):
    parcels, out, acc = refs[:-2], refs[-2], refs[-1]
    rows = tiles * length
    lane_group = lax.broadcasted_iota(jnp.int32, (8, 128), 1) // group
    for side, queries in enumerate((mine, other)):

        def one(step, _, queries=queries, side=side):
            start = pl.multiple_of(step * 512, 512)
            block = queries[pl.ds(start, 512), :]
            here = lane_group == place[side * 4 + step]
            for n, parcel in enumerate(parcels):
                similar = lax.dot_general(
                    parcel[0:rows, :], block, (((1,), (1,)), ((), ())), preferred_element_type=jnp.float32
                )
                sums = []
                for t in range(tiles):
                    best = jnp.max(similar[t * length : (t + 1) * length], axis=0, keepdims=True)
                    sums.append(best[:, 0:128] + best[:, 128:256] + best[:, 256:384] + best[:, 384:512])
                sums = jnp.concatenate(sums + [jnp.zeros((8 - tiles, 128), jnp.float32)], axis=0)
                sums = sums + pltpu.roll(sums, 64, 1)
                sums = sums + pltpu.roll(sums, 32, 1)
                sums = sums + pltpu.roll(sums, 16, 1)
                acc[n] = jnp.where(here, sums, acc[n])
            return 0

        lax.fori_loop(0, 4, one, 0)
    own_z, first_tile = place[8], place[9]
    row = lax.broadcasted_iota(jnp.int32, (8, 128), 0)
    for n, parcel in enumerate(parcels):
        codes = parcel[rows : rows + 32, :].astype(jnp.float32)
        lines = []
        for c in range(4):
            code = jnp.sum(jnp.where(row == own_z, codes[c * 8 : c * 8 + 8], 0.0), axis=0, keepdims=True)
            picked = code.astype(jnp.int32) - first_tile == row
            lines.append(jnp.sum(jnp.where(picked & (row < tiles), acc[n], 0.0), axis=0, keepdims=True))
        out[n] = jnp.concatenate(lines, axis=0)


def score(place, mine, other, parcels, tiles, length, group):
    n = len(parcels)
    vm = pl.BlockSpec(memory_space=pltpu.VMEM)
    flops = 2 * n * tiles * length * 128 * 4096
    return pl.pallas_call(
        functools.partial(score_kernel, tiles=tiles, length=length, group=group),
        in_specs=[pl.BlockSpec(memory_space=pltpu.SMEM)] + [vm] * (2 + n),
        out_specs=vm,
        out_shape=jax.ShapeDtypeStruct((n, 4, 128), jnp.float32),
        scratch_shapes=[pltpu.VMEM((n, 8, 128), jnp.float32)],
        compiler_params=pltpu.CompilerParams(vmem_limit_bytes=32 << 20),
        cost_estimate=pl.CostEstimate(flops=2 * flops, bytes_accessed=0, transcendentals=0),
        name=f"score_{n}",
    )(place, mine, other, *parcels)


def shards(tokens, w_in, b_in, w_out, b_out, gain, shift, proj, tiles, lengths, slots, counts):
    queries, query_len, width = tokens.shape
    count, length, dims = tiles.shape
    half = count // CORES
    core, x, z = lax.axis_index("core"), lax.axis_index("x"), lax.axis_index("z")

    valid = jnp.arange(4, dtype=jnp.int32)[None, :] < counts
    codes = jnp.where(valid, slots[:, 0, :], count).astype(jnp.bfloat16)
    codes = codes.reshape(X, Z, queries, 4).transpose(3, 1, 0, 2).reshape(4 * Z, X * queries)
    codes_far = lax.ppermute(codes, "core", turn(CORES, 1))
    low, high = jnp.where(core == 0, codes, codes_far), jnp.where(core == 0, codes_far, codes)
    both = jnp.concatenate([low, high], axis=1)

    part = lax.dynamic_slice(tiles, (core * half, 0, 0), (half, length, dims))
    sizes = lax.dynamic_slice(lengths, (core * half,), (half,))
    real = jnp.arange(length, dtype=jnp.int32)[None, :] < sizes[:, None]
    part = jnp.where(real[:, :, None], part, part[:, 0:1, :])
    own = jnp.concatenate([part.reshape(half * length, dims), both], axis=0)

    up, down = [own], [own]
    for _ in range(3):
        up.append(lax.ppermute(up[-1], "z", turn(Z, 1)))
        down.append(lax.ppermute(down[-1], "z", turn(Z, -1)))
    up.append(lax.ppermute(up[-1], "z", turn(Z, 1)))

    flat = tokens.reshape(queries * query_len, width)
    begun, finish = encode(
        flat, w_in, b_in[None], w_out, b_out[None], gain[None], shift[None], proj, queries, query_len
    )
    embeds = finish(begun)
    near = [embeds] + [lax.ppermute(embeds, "x", turn(X, k)) for k in (1, -1, 2)]
    mine = jnp.concatenate(near, axis=0)
    other = lax.ppermute(mine, "core", turn(CORES, 1))

    xs = jnp.stack([x, (x - 1) % X, (x + 1) % X, (x + 2) % X])
    place = jnp.concatenate([core * X + xs, (1 - core) * X + xs, jnp.stack([z, core * half])]).astype(jnp.int32)
    args = (half, length, queries)
    part_a = score(place, mine, other, [own, up[1], down[1], up[2], down[2]], *args)
    part_b = score(place, mine, other, [up[3], down[3]], *args)
    part_c = score(place, mine, other, [up[4]], *args)
    ring = [part_a[0], part_a[2], part_a[4], part_b[1], part_c[0], part_b[0], part_a[3], part_a[1]]
    ring = jnp.stack(ring + ring)
    found = lax.dynamic_slice(ring, (Z - z, 0, 0), (Z, 4, 128))
    found = found.reshape(Z, 4, CORES, X * queries)
    give = jnp.where(core == 0, found[:, :, 1], found[:, :, 0])
    keep = jnp.where(core == 0, found[:, :, 0], found[:, :, 1])
    summed = keep + lax.ppermute(give, "core", turn(CORES, 1))
    summed = summed.reshape(Z, 4, X, queries).transpose(2, 0, 1, 3)
    summed = lax.all_to_all(summed, "x", split_axis=0, concat_axis=0, tiled=True)
    return summed.transpose(3, 0, 1, 2).reshape(queries, X * Z, 4)


def solution(mesh):
    fine = Mesh(mesh.devices.reshape(Y, CORES, X, Z), ("y", "core", "x", "z"))
    group, shard = ("y", "core"), ("x", "z")
    placed = (P(group + shard),) + (P(),) * 7 + (P(shard), P(shard), P(group, shard), P(group, shard))
    return jax.shard_map(shards, mesh=fine, in_specs=placed, out_specs=P(group + shard), check_vma=False)
```

time: 214 us -> 86.7 us (0.41)
  matrix products: 85 us -> 0 us
  waiting for transfers between devices: 83.3 us -> 8.24 us
  Pallas kernels: 0 us -> 32.1 us
  starting transfers between devices: 0.01 us -> 18.7 us
  between operations: 13.5 us -> 0.44 us
  local copies, waits for them, and re-layouts: 5.04 us -> 15.4 us
  blocking collectives: 16.6 us -> 8.74 us
  other arithmetic: 8.73 us -> 2.59 us
    dot_general x34 -> x0, matrix products: 85 us -> none  [the longest x32 63.1 us: score_queries(): lax.dot_general(rows, flat_tiles, (((1,), (1,)), ((), ())), preferred_ele...]
    all_gather x1 -> x0, waiting for transfers between devices: 83.3 us -> none  [shards(): piece = lax.all_gather(embeds, 'passage', axis=0, tiled=True)]
    pallas_call x0 -> x5, Pallas kernels: none -> 32.1 us  [the longest x3 24 us: score(): pl.pallas_call(functools.partial(score_kernel, tiles=tiles, length=length...]
    ppermute x0 -> x13, starting transfers between devices: none -> 18.7 us  [the longest x3 11.4 us: shards(): down.append(lax.ppermute(down[-1], 'z', turn(Z, -1)))]
    unnamed x15 -> x45, local copies, waits for them, and re-layouts: 0.58 us -> 12.2 us
    ppermute x0 -> x13, waiting for transfers between devices: none -> 8.24 us  [the longest x3 5.55 us: shards(): down.append(lax.ppermute(down[-1], 'z', turn(Z, -1)))]
    all_to_all x1, blocking collectives: 16.6 us -> 8.74 us  [shards(): lax.all_to_all(summed, 'x', split_axis=0, concat_axis=0, tiled=True)]
    reduce_sum x65 -> x0, other arithmetic: 4.43 us -> none  [the longest x32 3.39 us: score_queries(): tile_score = jnp.sum(best, axis=1)]
  transfers between devices with their start and end apart: 1 -> 13, of which waited for: 1 -> 5; matrix products, arithmetic and copies ran while one was open for 1% -> 2% of each run, Pallas kernels for 0% -> 31%
where the time goes in v1:
time: 86.7 us; the launch traced here: 86.1 us
  Pallas kernels  32.1 us (37%)
  starting transfers between devices  18.7 us (22%)
  local copies, waits for them, and re-layouts  15.4 us (18%)
  blocking collectives  8.74 us (10%)
  waiting for transfers between devices  8.24 us (10%)
  other arithmetic  2.59 us (3%)
    pallas_call x3, Pallas kernels, score(): pl.pallas_call(functools.partial(score_kernel, tiles=tiles, length=length...  24 us
    unnamed x45, local copies, waits for them, and re-layouts  12.2 us
    ppermute x3, starting transfers between devices, shards(): down.append(lax.ppermute(down[-1], 'z', turn(Z, -1)))  11.4 us
    all_to_all x1, blocking collectives, shards(): lax.all_to_all(summed, 'x', split_axis=0, concat_axis=0, tiled=True)  8.74 us
    ppermute x3, waiting for transfers between devices, shards(): down.append(lax.ppermute(down[-1], 'z', turn(Z, -1)))  5.55 us
    ppermute x3, starting transfers between devices, shards(): lax.ppermute(embeds, 'x', turn(X, k))  5.14 us
    pallas_call x1, Pallas kernels, encode(): pl.pallas_call(functools.partial(ffn_second, queries=queries, tokens=toke...  4.49 us
    pallas_call x1, Pallas kernels, encode(): pl.pallas_call(ffn_first, grid=(first,), in_specs=pieces(0), out_specs=pl...  3.52 us
  transfers between devices with their start and end apart: 13, of which 5 were waited for; matrix products, arithmetic and copies ran while one was open for 2% of the time, Pallas kernels for 31%

profile of v1, /device:TPU:16, one launch (start us, length us, event | category | flops | bytes accessed | tf_op | source)
XLA Modules:
  0.0 86.1 jit_solution(7934893707633663060)
XLA Ops:
  0.0 0.0 copy-start
  0.0 0.8 squeeze.2
  0.8 0.5 broadcast.29
  1.4 1.3 %reduce.3 = s32[512]{0:T(512)S(1)} reduce(s32[512,1]{0,1:T(1,128)} %param.23, s32[]{:T(128)} %broadcast.29), dimensions={1}, to_apply=%param.23.reduce_sub_computation.3 | reduce | bytes 4100 | tf_op args[11]
  2.7 0.1 lt.62
  2.8 0.1 reshape.55
  2.9 0.0 collective-permute-start.4
  3.0 0.7 dynamic_slice.9
  3.7 0.0 copy-done
  3.8 0.1 copy.41
  3.9 0.2 broadcast_select_fusion
  4.1 0.0 copy-start.1
  4.1 2.3 %copy-done.1 = bf16[768,3072]{1,0:T(8,128)(2,1)S(1)} copy-done((bf16[768,3072]{1,0:T(8,128)(2,1)S(1)}, bf16[768,3072]{1,0:T(8,128)(2,1)}, u32[]{:S(2)}) %copy-start.1) | copy-done | bytes 4718616
  6.5 2.3 %copy-done.3 = bf16[3072,768]{1,0:T(8,128)(2,1)S(1)} copy-done((bf16[3072,768]{1,0:T(8,128)(2,1)S(1)}, bf16[3072,768]{1,0:T(8,128)(2,1)}, u32[]{:S(2)}) %copy-start.3) | copy-done | bytes 4718616
  8.8 1.1 %copy-done.5 = bf16[16,32,768]{2,1,0:T(8,128)(2,1)S(1)} copy-done((bf16[16,32,768]{2,1,0:T(8,128)(2,1)S(1)}, bf16[16,32,768]{2,1,0:T(8,128)(2,1)}, u32[]{:S(2)}) %copy-start.5) | copy-done | bytes 786456
  9.9 0.7 copy-done.8
  10.7 0.0 copy-start.7
  10.7 0.0 copy-start.9
  10.7 3.5 %ffn_first.1.begun = f32[512,768]{1,0:T(8,128)S(1)} custom-call(bf16[512,768]{1,0:T(8,128)(2,1)S(1)} %bitcast.39, bf16[768,3072]{1,0:T(8,128)(2,1)S(1)} %copy-done.1, f32[1,3072]{1,0:T(1,128)S(1)} %bitcast.41, bf16[3072,768]{1,0:T(8,128)(2,1)S(1)} %copy-done.3), custom_call_target="tpu_custom_call" | custom-call | flops 2415919104 | bytes 4718592 | tf_op jit(solution)/shard_map/ffn_first/pallas_call | solution.py:86
  14.2 0.0 copy-done.10
  14.2 0.0 copy-done.11
  14.3 0.0 copy-done.12
  14.3 0.0 collective-permute-done.4
  14.3 0.1 maximum_maximum_fusion.refs_0_
  14.4 1.9 %collective-permute-start.5 = (bf16[800,128]{1,0:T(8,128)(2,1)S(1)}, bf16[800,128]{1,0:T(8,128)(2,1)S(1)}, u32[]{:S(2)}, u32[]{:S(2)}) collective-permute-start(bf16[800,128]{1,0:T(8,128)(2,1)S(1)} %maximum_maximum_fusion.refs_0_), channel_id=1, source_target_pairs={{0,1},{1,2},{2,3},{3,4},{4,5},{5,6},{6,7},{7,0},{8,9},{9,10},{10,1... | collective-permute-start | bytes 614408 | tf_op jit(solution)/shard_map/ppermute | solution.py:184
  16.4 2.3 %copy-done.2 = bf16[768,3072]{1,0:T(8,128)(2,1)S(1)} copy-done((bf16[768,3072]{1,0:T(8,128)(2,1)S(1)}, bf16[768,3072]{1,0:T(8,128)(2,1)}, u32[]{:S(2)}) %copy-start.2) | copy-done | bytes 4718616
  18.7 2.3 %copy-done.4 = bf16[3072,768]{1,0:T(8,128)(2,1)S(1)} copy-done((bf16[3072,768]{1,0:T(8,128)(2,1)S(1)}, bf16[3072,768]{1,0:T(8,128)(2,1)}, u32[]{:S(2)}) %copy-start.4) | copy-done | bytes 4718616
  21.0 4.5 %ffn_second.1 = bf16[512,128]{1,0:T(8,128)(2,1)S(1)} custom-call(bf16[512,768]{1,0:T(8,128)(2,1)S(1)} %bitcast.40, bf16[768,3072]{1,0:T(8,128)(2,1)S(1)} %copy-done.2, f32[1,3072]{1,0:T(1,128)S(1)} %bitcast.42, bf16[3072,768]{1,0:T(8,128)(2,1)S(1)} %copy-done.4, f32[512,768]{1,0:T(8,128)S(1)} %ffn_first.1.begun, f32[1,768]{1,0:T(1,128)S(1)} %broadcast_in_dim.39.b_out, ...), custom_call_target="tpu_custom_call" | custom-call | flops 2415919104 | bytes 4718592 | tf_op jit(solution)/shard_map/ffn_second/pallas_call | solution.py:96
  25.5 3.1 %collective-permute-start.2 = (bf16[512,128]{1,0:T(8,128)(2,1)S(1)}, bf16[512,128]{1,0:T(8,128)(2,1)S(1)}, u32[]{:S(2)}, u32[]{:S(2)}) collective-permute-start(bf16[512,128]{1,0:T(8,128)(2,1)S(1)} %ffn_second.1), channel_id=1, source_target_pairs={{0,16},{8,24},{16,0},{24,8},{1,17},{9,25},{17,1},{25,9},{2,18},{10... | collective-permute-start | bytes 393224 | tf_op jit(solution)/shard_map/ppermute | solution.py:193
  28.7 1.1 %collective-permute-start.1 = (bf16[512,128]{1,0:T(8,128)(2,1)S(1)}, bf16[512,128]{1,0:T(8,128)(2,1)S(1)}, u32[]{:S(2)}, u32[]{:S(2)}) collective-permute-start(bf16[512,128]{1,0:T(8,128)(2,1)S(1)} %ffn_second.1), channel_id=1, source_target_pairs={{0,24},{8,0},{16,8},{24,16},{1,25},{9,1},{17,9},{25,17},{2,26},{10... | collective-permute-start | bytes 393224 | tf_op jit(solution)/shard_map/ppermute | solution.py:193
  29.8 0.9 %collective-permute-start = (bf16[512,128]{1,0:T(8,128)(2,1)S(1)}, bf16[512,128]{1,0:T(8,128)(2,1)S(1)}, u32[]{:S(2)}, u32[]{:S(2)}) collective-permute-start(bf16[512,128]{1,0:T(8,128)(2,1)S(1)} %ffn_second.1), channel_id=1, source_target_pairs={{0,8},{8,16},{16,24},{24,0},{1,9},{9,17},{17,25},{25,1},{2,10},{10... | collective-permute-start | bytes 393224 | tf_op jit(solution)/shard_map/ppermute | solution.py:193
  30.7 4.0 %collective-permute-start.6 = (bf16[800,128]{1,0:T(8,128)(2,1)S(1)}, bf16[800,128]{1,0:T(8,128)(2,1)S(1)}, u32[]{:S(2)}, u32[]{:S(2)}) collective-permute-start(bf16[800,128]{1,0:T(8,128)(2,1)S(1)} %maximum_maximum_fusion.refs_0_), channel_id=1, source_target_pairs={{0,7},{1,0},{2,1},{3,2},{4,3},{5,4},{6,5},{7,6},{8,15},{9,8},{10,9... | collective-permute-start | bytes 614408 | tf_op jit(solution)/shard_map/ppermute | solution.py:185
  34.7 0.0 collective-permute-done.5.refs_1_
  34.7 0.0 collective-permute-start.7
  34.7 0.0 collective-permute-done.2
  34.7 1.0 %collective-permute-done.1 = bf16[512,128]{1,0:T(8,128)(2,1)S(1)} collective-permute-done((bf16[512,128]{1,0:T(8,128)(2,1)S(1)}, bf16[512,128]{1,0:T(8,128)(2,1)S(1)}, u32[]{:S(2)}, u32[]{:S(2)}) %collective-permute-start.1) | collective-permute-done | bytes 131104 | tf_op jit(solution)/shard_map/ppermute | solution.py:193
  35.6 0.5 collective-permute-done
  36.2 0.1 collective-permute-start.3
  36.4 0.1 broadcast_add_fusion.1
  36.4 2.4 %collective-permute-done.6.refs_2_ = bf16[800,128]{1,0:T(8,128)(2,1)S(1)} collective-permute-done((bf16[800,128]{1,0:T(8,128)(2,1)S(1)}, bf16[800,128]{1,0:T(8,128)(2,1)S(1)}, u32[]{:S(2)}, u32[]{:S(2)}) %collective-permute-start.6) | collective-permute-done | bytes 204832 | tf_op jit(solution)/shard_map/ppermute | solution.py:185
  38.8 3.7 %collective-permute-start.8 = (bf16[800,128]{1,0:T(8,128)(2,1)S(1)}, bf16[800,128]{1,0:T(8,128)(2,1)S(1)}, u32[]{:S(2)}, u32[]{:S(2)}) collective-permute-start(bf16[800,128]{1,0:T(8,128)(2,1)S(1)} %collective-permute-done.6.refs_2_), channel_id=1, source_target_pairs={{0,7},{1,0},{2,1},{3,2},{4,3},{5,4},{6,5},{7,6},{8,15},{9,8},{10,9... | collective-permute-start | bytes 614408 | tf_op jit(solution)/shard_map/ppermute | solution.py:185
  42.5 0.0 collective-permute-done.7.refs_3_
  42.5 0.0 collective-permute-start.9
  42.5 0.1 pad_add_fusion.1.place
  42.6 3.2 %collective-permute-done.8.refs_4_ = bf16[800,128]{1,0:T(8,128)(2,1)S(1)} collective-permute-done((bf16[800,128]{1,0:T(8,128)(2,1)S(1)}, bf16[800,128]{1,0:T(8,128)(2,1)S(1)}, u32[]{:S(2)}, u32[]{:S(2)}) %collective-permute-start.8) | collective-permute-done | bytes 204832 | tf_op jit(solution)/shard_map/ppermute | solution.py:185
  45.8 3.7 %collective-permute-start.10 = (bf16[800,128]{1,0:T(8,128)(2,1)S(1)}, bf16[800,128]{1,0:T(8,128)(2,1)S(1)}, u32[]{:S(2)}, u32[]{:S(2)}) collective-permute-start(bf16[800,128]{1,0:T(8,128)(2,1)S(1)} %collective-permute-done.8.refs_4_), channel_id=1, source_target_pairs={{0,7},{1,0},{2,1},{3,2},{4,3},{5,4},{6,5},{7,6},{8,15},{9,8},{10,9... | collective-permute-start | bytes 614408 | tf_op jit(solution)/shard_map/ppermute | solution.py:185
  49.5 0.0 collective-permute-done.9.refs_0_
  49.5 0.0 collective-permute-start.11
  49.5 0.0 collective-permute-done.3.other
  49.5 11.9 %score_5.1 = f32[5,4,128]{2,1,0:T(4,128)S(1)} custom-call(s32[10]{0:T(128)S(1)} %pad_add_fusion.1.place, bf16[2048,128]{1,0:T(8,128)(2,1)S(1)} %pad_maximum_fusion.mine, bf16[2048,128]{1,0:T(8,128)(2,1)S(1)} %collective-permute-done.3.other, bf16[800,128]{1,0:T(8,128)(2,1)S(1)} %maximum_maximum_fusion.refs_0_, ...), custom_call_target="tpu_custom_call" | custom-call | flops 8053063680 | tf_op jit(solution)/shard_map/score_5/pallas_call | solution.py:151
  61.4 0.0 collective-permute-done.10.refs_1_
  61.4 6.9 %score_2.1 = f32[2,4,128]{2,1,0:T(4,128)S(1)} custom-call(s32[10]{0:T(128)S(1)} %pad_add_fusion.1.place, bf16[2048,128]{1,0:T(8,128)(2,1)S(1)} %pad_maximum_fusion.mine, bf16[2048,128]{1,0:T(8,128)(2,1)S(1)} %collective-permute-done.3.other, bf16[800,128]{1,0:T(8,128)(2,1)S(1)} %collective-permute-done.9.refs_0_, ...), custom_call_target="tpu_custom_call" | custom-call | flops 3221225472 | tf_op jit(solution)/shard_map/score_2/pallas_call | solution.py:151
  68.3 0.0 collective-permute-done.11.refs_0_
  68.3 5.3 %score_1.1 = f32[1,4,128]{2,1,0:T(4,128)S(1)} custom-call(s32[10]{0:T(128)S(1)} %pad_add_fusion.1.place, bf16[2048,128]{1,0:T(8,128)(2,1)S(1)} %pad_maximum_fusion.mine, bf16[2048,128]{1,0:T(8,128)(2,1)S(1)} %collective-permute-done.3.other, bf16[800,128]{1,0:T(8,128)(2,1)S(1)} %collective-permute-done.11.refs_0_), custom_call_target="tpu_custom_call" | custom-call | flops 1610612736 | tf_op jit(solution)/shard_map/score_1/pallas_call | solution.py:151
  73.8 0.1 reshape.56
  73.9 0.1 collective-permute-start.12
  74.0 1.2 %collective-permute-done.12 = f32[8,4,64]{2,0,1:T(8,128)S(1)} collective-permute-done((f32[8,4,64]{2,0,1:T(8,128)S(1)}, f32[8,4,64]{2,0,1:T(8,128)S(1)}, u32[]{:S(2)}, u32[]{:S(2)}) %collective-permute-start.12) | collective-permute-done | bytes 8224 | tf_op jit(solution)/shard_map/ppermute | solution.py:209
  75.2 0.1 reshape.57
  75.3 0.1 reshape.68
  75.4 8.7 %all_to_all.5 = f32[4,1,512]{2,1,0:T(1,128)S(1)} all-to-all(f32[4,1,512]{2,1,0:T(1,128)S(1)} %reshape.68), channel_id=1, replica_groups=mesh['y'=4,'core'=2,'x'=4,'z'=8] {'x'}, dimensions={0} | all-to-all | bytes 16384 | tf_op jit(solution)/shard_map/all_to_all | solution.py:211
  84.1 0.5 broadcast.30
  84.6 0.7 reduce.4
  85.3 0.1 reshape.69
  85.4 0.7 copy.40
  (46 shorter events, 0.4 us)
Async XLA Ops:
  0.0 3.7 %copy-start = (bf16[12,128,128]{2,1,0:T(8,128)(2,1)S(1)}, bf16[12,128,128]{2,1,0:T(8,128)(2,1)}, u32[]{:S(2)}) copy-start(bf16[12,128,128]{2,1,0:T(8,128)(2,1)} %param.20) | copy-start | bytes 1179652
  2.9 11.4 %collective-permute-start.4 = (bf16[32,64]{1,0:T(8,128)(2,1)S(1)}, bf16[32,64]{1,0:T(8,128)(2,1)S(1)}, u32[]{:S(2)}, u32[]{:S(2)}) collective-permute-start(bf16[32,64]{1,0:T(8,128)(2,1)S(1)} %reshape.55), channel_id=1, source_target_pairs={{0,32},{32,0},{1,33},{33,1},{2,34},{34,2},{3,35},{35,3},{4,36},{36... | collective-permute-start | bytes 12296 | tf_op jit(solution)/shard_map/ppermute | solution.py:172
  4.1 2.3 %copy-start.1 = (bf16[768,3072]{1,0:T(8,128)(2,1)S(1)}, bf16[768,3072]{1,0:T(8,128)(2,1)}, u32[]{:S(2)}) copy-start(bf16[768,3072]{1,0:T(8,128)(2,1)} %w_in.3) | copy-start | bytes 14155780
  6.5 2.3 %copy-start.3 = (bf16[3072,768]{1,0:T(8,128)(2,1)S(1)}, bf16[3072,768]{1,0:T(8,128)(2,1)}, u32[]{:S(2)}) copy-start(bf16[3072,768]{1,0:T(8,128)(2,1)} %w_out.3) | copy-start | bytes 14155780
  8.8 1.1 %copy-start.5 = (bf16[16,32,768]{2,1,0:T(8,128)(2,1)S(1)}, bf16[16,32,768]{2,1,0:T(8,128)(2,1)}, u32[]{:S(2)}) copy-start(bf16[16,32,768]{2,1,0:T(8,128)(2,1)} %param.12) | copy-start | bytes 2359300
  9.9 0.7 copy-start.8
  10.6 3.6 %copy-start.10 = (f32[768]{0:T(1024)S(1)}, f32[768]{0:T(1024)}, u32[]{:S(2)}) copy-start(f32[768]{0:T(1024)} %param.16) | copy-start | bytes 9220
  10.6 3.6 %copy-start.11 = (f32[768]{0:T(1024)S(1)}, f32[768]{0:T(1024)}, u32[]{:S(2)}) copy-start(f32[768]{0:T(1024)} %param.17) | copy-start | bytes 9220
  10.7 3.6 %copy-start.12 = (f32[768]{0:T(1024)S(1)}, f32[768]{0:T(1024)}, u32[]{:S(2)}) copy-start(f32[768]{0:T(1024)} %param.18) | copy-start | bytes 9220
  10.7 5.7 %copy-start.6 = (bf16[16,32,768]{2,1,0:T(8,128)(2,1)S(1)}, bf16[16,32,768]{2,1,0:T(8,128)(2,1)}, u32[]{:S(2)}) copy-start(bf16[16,32,768]{2,1,0:T(8,128)(2,1)} %param.12) | copy-start | bytes 2359300
  10.7 5.7 %copy-start.7 = (bf16[768,128]{1,0:T(8,128)(2,1)S(1)}, bf16[768,128]{1,0:T(8,128)(2,1)}, u32[]{:S(2)}) copy-start(bf16[768,128]{1,0:T(8,128)(2,1)} %proj.1) | copy-start | bytes 589828
  10.7 5.7 %copy-start.9 = (f32[3072]{0:T(1024)S(1)}, f32[3072]{0:T(1024)}, u32[]{:S(2)}) copy-start(f32[3072]{0:T(1024)} %param.14) | copy-start | bytes 36868
  14.4 20.2 %collective-permute-start.5 = (bf16[800,128]{1,0:T(8,128)(2,1)S(1)}, bf16[800,128]{1,0:T(8,128)(2,1)S(1)}, u32[]{:S(2)}, u32[]{:S(2)}) collective-permute-start(bf16[800,128]{1,0:T(8,128)(2,1)S(1)} %maximum_maximum_fusion.refs_0_), channel_id=1, source_target_pairs={{0,1},{1,2},{2,3},{3,4},{4,5},{5,6},{6,7},{7,0},{8,9},{9,10},{10,1... | collective-permute-start | bytes 614408 | tf_op jit(solution)/shard_map/ppermute | solution.py:184
  16.4 2.3 %copy-start.2 = (bf16[768,3072]{1,0:T(8,128)(2,1)S(1)}, bf16[768,3072]{1,0:T(8,128)(2,1)}, u32[]{:S(2)}) copy-start(bf16[768,3072]{1,0:T(8,128)(2,1)} %w_in.3) | copy-start | bytes 14155780
  18.7 2.3 %copy-start.4 = (bf16[3072,768]{1,0:T(8,128)(2,1)S(1)}, bf16[3072,768]{1,0:T(8,128)(2,1)}, u32[]{:S(2)}) copy-start(bf16[3072,768]{1,0:T(8,128)(2,1)} %w_out.3) | copy-start | bytes 14155780
  25.5 9.1 %collective-permute-start.2 = (bf16[512,128]{1,0:T(8,128)(2,1)S(1)}, bf16[512,128]{1,0:T(8,128)(2,1)S(1)}, u32[]{:S(2)}, u32[]{:S(2)}) collective-permute-start(bf16[512,128]{1,0:T(8,128)(2,1)S(1)} %ffn_second.1), channel_id=1, source_target_pairs={{0,16},{8,24},{16,0},{24,8},{1,17},{9,25},{17,1},{25,9},{2,18},{10... | collective-permute-start | bytes 393224 | tf_op jit(solution)/shard_map/ppermute | solution.py:193
  28.7 7.0 %collective-permute-start.1 = (bf16[512,128]{1,0:T(8,128)(2,1)S(1)}, bf16[512,128]{1,0:T(8,128)(2,1)S(1)}, u32[]{:S(2)}, u32[]{:S(2)}) collective-permute-start(bf16[512,128]{1,0:T(8,128)(2,1)S(1)} %ffn_second.1), channel_id=1, source_target_pairs={{0,24},{8,0},{16,8},{24,16},{1,25},{9,1},{17,9},{25,17},{2,26},{10... | collective-permute-start | bytes 393224 | tf_op jit(solution)/shard_map/ppermute | solution.py:193
  29.8 6.4 %collective-permute-start = (bf16[512,128]{1,0:T(8,128)(2,1)S(1)}, bf16[512,128]{1,0:T(8,128)(2,1)S(1)}, u32[]{:S(2)}, u32[]{:S(2)}) collective-permute-start(bf16[512,128]{1,0:T(8,128)(2,1)S(1)} %ffn_second.1), channel_id=1, source_target_pairs={{0,8},{8,16},{16,24},{24,0},{1,9},{9,17},{17,25},{25,1},{2,10},{10... | collective-permute-start | bytes 393224 | tf_op jit(solution)/shard_map/ppermute | solution.py:193
  30.7 8.1 %collective-permute-start.6 = (bf16[800,128]{1,0:T(8,128)(2,1)S(1)}, bf16[800,128]{1,0:T(8,128)(2,1)S(1)}, u32[]{:S(2)}, u32[]{:S(2)}) collective-permute-start(bf16[800,128]{1,0:T(8,128)(2,1)S(1)} %maximum_maximum_fusion.refs_0_), channel_id=1, source_target_pairs={{0,7},{1,0},{2,1},{3,2},{4,3},{5,4},{6,5},{7,6},{8,15},{9,8},{10,9... | collective-permute-start | bytes 614408 | tf_op jit(solution)/shard_map/ppermute | solution.py:185
  34.7 7.8 %collective-permute-start.7 = (bf16[800,128]{1,0:T(8,128)(2,1)S(1)}, bf16[800,128]{1,0:T(8,128)(2,1)S(1)}, u32[]{:S(2)}, u32[]{:S(2)}) collective-permute-start(bf16[800,128]{1,0:T(8,128)(2,1)S(1)} %collective-permute-done.5.refs_1_), channel_id=1, source_target_pairs={{0,1},{1,2},{2,3},{3,4},{4,5},{5,6},{6,7},{7,0},{8,9},{9,10},{10,1... | collective-permute-start | bytes 614408 | tf_op jit(solution)/shard_map/ppermute | solution.py:184
  36.2 13.3 %collective-permute-start.3 = (bf16[2048,128]{1,0:T(8,128)(2,1)S(1)}, bf16[2048,128]{1,0:T(8,128)(2,1)S(1)}, u32[]{:S(2)}, u32[]{:S(2)}) collective-permute-start(bf16[2048,128]{1,0:T(8,128)(2,1)S(1)} %pad_maximum_fusion.mine), channel_id=1, source_target_pairs={{0,32},{32,0},{1,33},{33,1},{2,34},{34,2},{3,35},{35,3},{4,36},{36... | collective-permute-start | bytes 1572872 | tf_op jit(solution)/shard_map/ppermute | solution.py:195
  38.8 7.0 %collective-permute-start.8 = (bf16[800,128]{1,0:T(8,128)(2,1)S(1)}, bf16[800,128]{1,0:T(8,128)(2,1)S(1)}, u32[]{:S(2)}, u32[]{:S(2)}) collective-permute-start(bf16[800,128]{1,0:T(8,128)(2,1)S(1)} %collective-permute-done.6.refs_2_), channel_id=1, source_target_pairs={{0,7},{1,0},{2,1},{3,2},{4,3},{5,4},{6,5},{7,6},{8,15},{9,8},{10,9... | collective-permute-start | bytes 614408 | tf_op jit(solution)/shard_map/ppermute | solution.py:185
  42.5 7.0 %collective-permute-start.9 = (bf16[800,128]{1,0:T(8,128)(2,1)S(1)}, bf16[800,128]{1,0:T(8,128)(2,1)S(1)}, u32[]{:S(2)}, u32[]{:S(2)}) collective-permute-start(bf16[800,128]{1,0:T(8,128)(2,1)S(1)} %collective-permute-done.7.refs_3_), channel_id=1, source_target_pairs={{0,1},{1,2},{2,3},{3,4},{4,5},{5,6},{6,7},{7,0},{8,9},{9,10},{10,1... | collective-permute-start | bytes 614408 | tf_op jit(solution)/shard_map/ppermute | solution.py:184
  45.8 15.6 %collective-permute-start.10 = (bf16[800,128]{1,0:T(8,128)(2,1)S(1)}, bf16[800,128]{1,0:T(8,128)(2,1)S(1)}, u32[]{:S(2)}, u32[]{:S(2)}) collective-permute-start(bf16[800,128]{1,0:T(8,128)(2,1)S(1)} %collective-permute-done.8.refs_4_), channel_id=1, source_target_pairs={{0,7},{1,0},{2,1},{3,2},{4,3},{5,4},{6,5},{7,6},{8,15},{9,8},{10,9... | collective-permute-start | bytes 614408 | tf_op jit(solution)/shard_map/ppermute | solution.py:185
  49.5 18.9 %collective-permute-start.11 = (bf16[800,128]{1,0:T(8,128)(2,1)S(1)}, bf16[800,128]{1,0:T(8,128)(2,1)S(1)}, u32[]{:S(2)}, u32[]{:S(2)}) collective-permute-start(bf16[800,128]{1,0:T(8,128)(2,1)S(1)} %collective-permute-done.9.refs_0_), channel_id=1, source_target_pairs={{0,1},{1,2},{2,3},{3,4},{4,5},{5,6},{6,7},{7,0},{8,9},{9,10},{10,1... | collective-permute-start | bytes 614408 | tf_op jit(solution)/shard_map/ppermute | solution.py:186
  73.9 1.3 %collective-permute-start.12 = (f32[8,4,64]{2,0,1:T(8,128)S(1)}, f32[8,4,64]{2,0,1:T(8,128)S(1)}, u32[]{:S(2)}, u32[]{:S(2)}) collective-permute-start(f32[8,4,64]{2,0,1:T(8,128)S(1)} %bitcast.48), channel_id=1, source_target_pairs={{0,32},{32,0},{1,33},{33,1},{2,34},{34,2},{3,35},{35,3},{4,36},{36... | collective-permute-start | bytes 24584 | tf_op jit(solution)/shard_map/ppermute | solution.py:209

commit v2 on v1

v2 whole, which is shorter than its diff:
```python
import functools

import jax
import jax.numpy as jnp
from jax import lax
from jax.experimental import pallas as pl
from jax.experimental.pallas import tpu as pltpu
from jax.sharding import Mesh
from jax.sharding import PartitionSpec as P

Y, CORES, X, Z = 4, 2, 4, 8
HALF_ROOT = 0.7071067811865476


def turn(size, step):
    return [(i, (i + step) % size) for i in range(size)]


def gelu(pre):
    return 0.5 * pre * (1.0 + lax.erf(pre * jnp.float32(HALF_ROOT)))


def ffn_kernel(tok, w_in, b_in, w_out, b_out, gain, shift, proj, out, acc, turned, *, queries, tokens):
    step = pl.program_id(0)
    pre = jnp.dot(tok[...], w_in[...], preferred_element_type=jnp.float32) + b_in[...]
    hidden = gelu(pre).astype(jnp.bfloat16)
    part = jnp.dot(hidden, w_out[...], preferred_element_type=jnp.float32)

    @pl.when(step == 0)
    def _():
        acc[...] = part

    @pl.when(step > 0)
    def _():
        acc[...] += part

    @pl.when(step == pl.num_programs(0) - 1)
    def _():
        total = acc[...] + b_out[...] + tok[...].astype(jnp.float32)
        diff = total - jnp.mean(total, axis=-1, keepdims=True)
        spread = jnp.mean(diff * diff, axis=-1, keepdims=True)
        normed = (diff * lax.rsqrt(spread + 1e-5) * gain[...] + shift[...]).astype(jnp.bfloat16)
        projected = jnp.dot(normed, proj[...], preferred_element_type=jnp.float32)
        scale = lax.rsqrt(jnp.sum(projected * projected, axis=-1, keepdims=True) + 1e-6)
        embeds = projected * scale
        for q in range(queries):
            turned[pl.ds(q, tokens, stride=queries), :] = embeds[q * tokens : (q + 1) * tokens, :]
        out[...] = turned[...].astype(jnp.bfloat16)


def encode(tok, w_in, b_in, w_out, b_out, gain, shift, proj, queries, tokens, chunk=1024):
    rows, width = tok.shape

    def whole(a):
        return pl.BlockSpec(a.shape, lambda j: (0,) * a.ndim)

    return pl.pallas_call(
        functools.partial(ffn_kernel, queries=queries, tokens=tokens),
        grid=(w_in.shape[1] // chunk,),
        in_specs=[
            whole(tok),
            pl.BlockSpec((width, chunk), lambda j: (0, j)),
            pl.BlockSpec((1, chunk), lambda j: (0, j)),
            pl.BlockSpec((chunk, width), lambda j: (j, 0)),
            whole(b_out),
            whole(gain),
            whole(shift),
            whole(proj),
        ],
        out_specs=pl.BlockSpec((rows, proj.shape[1]), lambda j: (0, 0)),
        out_shape=jax.ShapeDtypeStruct((rows, proj.shape[1]), jnp.bfloat16),
        scratch_shapes=[pltpu.VMEM((rows, width), jnp.float32), pltpu.VMEM((rows, proj.shape[1]), jnp.float32)],
        compiler_params=pltpu.CompilerParams(vmem_limit_bytes=60 << 20),
        cost_estimate=pl.CostEstimate(flops=8 * rows * w_in.size, bytes_accessed=4 * w_in.size, transcendentals=0),
        name="encode",
    )(tok, w_in, b_in, w_out, b_out, gain, shift, proj)


def parcel_kernel(place, sizes, near, far, tiles, out):
    half, length, _ = tiles.shape
    column = lax.broadcasted_iota(jnp.int32, tiles.shape[1:], 0)
    for t in range(half):
        tile = tiles[t].astype(jnp.float32)
        size = sizes[place[0] * half + t]
        out[t * length : (t + 1) * length, :] = jnp.where(column < size, tile, tile[0:1, :]).astype(jnp.bfloat16)
    for source, core in ((near, place[0]), (far, 1 - place[0])):
        codes = source[...]
        blank = jnp.zeros((4, 128), jnp.float32)
        lines = []
        for x in range(X):
            lines += [codes[:, x * 128 : (x + 1) * 128], blank]
        start = pl.multiple_of(half * length + core * (8 * X), 8 * X)
        out[pl.ds(start, 8 * X), :] = jnp.concatenate(lines, axis=0).astype(jnp.bfloat16)


def make_parcel(place, sizes, near, far, tiles):
    count, length, dims = tiles.shape
    half = count // CORES
    rows = half * length + 8 * X * CORES
    return pl.pallas_call(
        parcel_kernel,
        grid_spec=pltpu.PrefetchScalarGridSpec(
            num_scalar_prefetch=2,
            grid=(1,),
            in_specs=[
                pl.BlockSpec(near.shape, lambda i, *_: (0, 0)),
                pl.BlockSpec(far.shape, lambda i, *_: (0, 0)),
                pl.BlockSpec((half, length, dims), lambda i, place, sizes: (place[0], 0, 0)),
            ],
            out_specs=pl.BlockSpec((rows, dims), lambda i, *_: (0, 0)),
        ),
        out_shape=jax.ShapeDtypeStruct((rows, dims), jnp.bfloat16),
        name="parcel",
    )(place, sizes, near, far, tiles)


def score_kernel(place, mine, other, *refs, tiles, length, group, steps, shards, chained):
    parcels, out, acc = refs[: len(shards)], refs[-2], refs[-1]
    rows = tiles * length
    lane_group = lax.broadcasted_iota(jnp.int32, (8, 128), 1) // group
    row = lax.broadcasted_iota(jnp.int32, (8, 128), 0)
    core, x, z = place[0], place[1], place[2]

    def one(step, _):
        for side, queries in enumerate((mine, other)):
            start = pl.multiple_of(step * 512, 512)
            block = queries[pl.ds(start, 512), :]
            source = lax.rem(x + place[4 + step], X)
            here = lane_group == source + X * (core if side == 0 else 1 - core)
            for n, parcel in enumerate(parcels):
                similar = lax.dot_general(
                    parcel[0:rows, :], block, (((1,), (1,)), ((), ())), preferred_element_type=jnp.float32
                )
                sums = []
                for t in range(tiles):
                    best = jnp.max(similar[t * length : (t + 1) * length], axis=0, keepdims=True)
                    sums.append(best[:, 0:128] + best[:, 128:256] + best[:, 256:384] + best[:, 384:512])
                sums = jnp.concatenate(sums + [jnp.zeros((8 - tiles, 128), jnp.float32)], axis=0)
                sums = sums + pltpu.roll(sums, 64, 1)
                sums = sums + pltpu.roll(sums, 32, 1)
                sums = sums + pltpu.roll(sums, 16, 1)
                acc[n] = jnp.where(here, sums, acc[n])
        return 0

    lax.fori_loop(0, 4, one, 0, unroll=steps)
    first_tile = core * tiles
    if chained:
        out[...] = refs[len(shards)][...]
    for n, parcel in enumerate(parcels):
        codes = parcel[rows : rows + 8 * X * CORES, :].astype(jnp.float32)
        code = jnp.zeros((8, 128), jnp.float32)
        for d in range(X * CORES):
            turned = pltpu.roll(codes[d * 8 : d * 8 + 8], lax.rem((d - z) * group + 128, 128), 1)
            code = jnp.where(lane_group == d, turned, code)
        code = code.astype(jnp.int32) - first_tile
        shard = lax.rem(z + shards[n], Z)
        for c in range(4):
            picked = (code[c : c + 1] == row) & (row < tiles)
            line = jnp.sum(jnp.where(picked, acc[n], 0.0), axis=0, keepdims=True)
            out[pl.ds(c * Z + shard, 1), :] = line


def score(place, mine, other, parcels, shards, tiles, length, group, begun=None, steps=1):
    n = len(parcels)
    vm = pl.BlockSpec(memory_space=pltpu.VMEM)
    more = [] if begun is None else [begun]
    return pl.pallas_call(
        functools.partial(
            score_kernel,
            tiles=tiles,
            length=length,
            group=group,
            steps=steps,
            shards=shards,
            chained=begun is not None,
        ),
        in_specs=[pl.BlockSpec(memory_space=pltpu.SMEM)] + [vm] * (2 + n + len(more)),
        out_specs=vm,
        out_shape=jax.ShapeDtypeStruct((4 * Z, 128), jnp.float32),
        scratch_shapes=[pltpu.VMEM((n, 8, 128), jnp.float32)],
        compiler_params=pltpu.CompilerParams(vmem_limit_bytes=32 << 20),
        cost_estimate=pl.CostEstimate(flops=2 * n * tiles * length * 128 * 4096, bytes_accessed=0, transcendentals=0),
        name=f"score_{n}",
    )(place, mine, other, *parcels, *more)


def finish_kernel(place, *refs, group):
    sources, out, table = refs[:4], refs[4], refs[5]
    core, x = place[0], place[1]
    for k, source in enumerate(sources):
        lines = pltpu.roll(source[...], lax.rem(128 - (core * X + x) * group, 128), 1)
        shard = lax.rem(x + place[4 + k], X) * Z
        for c in range(4):
            table[pl.ds(pl.multiple_of(c * X * Z + shard, Z), Z), :] = lines[c * Z : (c + 1) * Z]
    turned = table[...].T
    for c in range(4):
        out[:, c, :] = turned[0:group, c * X * Z : (c + 1) * X * Z]


def finish(place, sources, group):
    vm = pl.BlockSpec(memory_space=pltpu.VMEM)
    return pl.pallas_call(
        functools.partial(finish_kernel, group=group),
        in_specs=[pl.BlockSpec(memory_space=pltpu.SMEM)] + [vm] * 4,
        out_specs=vm,
        out_shape=jax.ShapeDtypeStruct((group, 4, X * Z), jnp.float32),
        scratch_shapes=[pltpu.VMEM((128, 128), jnp.float32)],
        name="finish",
    )(place, *sources)


def shards(tokens, w_in, b_in, w_out, b_out, gain, shift, proj, tiles, lengths, slots, counts):
    queries, query_len, width = tokens.shape
    count, length, dims = tiles.shape
    half = count // CORES
    core, x, z = lax.axis_index("core"), lax.axis_index("x"), lax.axis_index("z")
    place = jnp.stack([core, x, z, 0, 0, X - 1, 1, 2]).astype(jnp.int32)

    wanted = slots.transpose(1, 2, 0)[0]
    valid = jnp.arange(4, dtype=jnp.int32)[:, None] < counts.transpose(1, 0)
    codes = jnp.where(valid, wanted, count).astype(jnp.float32)
    codes_far = lax.ppermute(codes, "core", turn(CORES, 1))
    own = make_parcel(place, lengths, codes, codes_far, tiles)

    def along(a, k):
        return lax.ppermute(a, "z", turn(Z, k))

    up1, down1, up2, down2 = along(own, 1), along(own, -1), along(own, 2), along(own, -2)
    flat, _ = lax.optimization_barrier((tokens.reshape(queries * query_len, width), own))
    embeds = encode(flat, w_in, b_in[None], w_out, b_out[None], gain[None], shift[None], proj, queries, query_len)
    embeds, up1, down1, up2, down2 = lax.optimization_barrier((embeds, up1, down1, up2, down2))
    up3, down3, up4 = along(up2, 1), along(down2, -1), along(up2, 2)

    near = [embeds] + [lax.ppermute(embeds, "x", turn(X, k)) for k in (1, -1, 2)]
    mine = jnp.concatenate(near, axis=0)
    other = lax.ppermute(mine, "core", turn(CORES, 1))

    args = (half, length, queries)
    found = score(place, mine, other, [own, up1, down1, up2, down2], [0, 7, 1, 6, 2], *args)
    found = score(place, mine, other, [up3, down3, up4], [5, 3, 4], *args, begun=found)
    found = found + lax.ppermute(found, "core", turn(CORES, 1))
    sources = [found] + [lax.ppermute(found, "x", turn(X, k)) for k in (1, -1, 2)]
    return finish(place, sources, queries).transpose(0, 2, 1)


def solution(mesh):
    fine = Mesh(mesh.devices.reshape(Y, CORES, X, Z), ("y", "core", "x", "z"))
    group, shard = ("y", "core"), ("x", "z")
    placed = (P(group + shard),) + (P(),) * 7 + (P(shard), P(shard), P(group, shard), P(group, shard))
    return jax.shard_map(shards, mesh=fine, in_specs=placed, out_specs=P(group + shard), check_vma=False)
```

time: 86.7 us -> 79 us (0.911)
  blocking collectives: 8.74 us -> 0 us
  local copies, waits for them, and re-layouts: 15.4 us -> 6.69 us
  starting transfers between devices: 18.7 us -> 27.4 us
  waiting for transfers between devices: 8.24 us -> 12 us
  other arithmetic: 2.59 us -> 0.71 us
    unnamed x45 -> x19, local copies, waits for them, and re-layouts: 12.2 us -> 2.19 us
    all_to_all x1 -> x0, blocking collectives: 8.74 us -> none  [shards(): lax.all_to_all(summed, 'x', split_axis=0, concat_axis=0, tiled=True)]
    ppermute x8 -> x11, starting transfers between devices: 13.4 us -> 22.1 us  [the longest x7 18.1 us: along(): return lax.ppermute(a, 'z', turn(Z, k))]
    pallas_call x3 -> x2, Pallas kernels: 24 us -> 17.5 us  [score(): pl.pallas_call(functools.partial(score_kernel, tiles=tiles, length=length...]
    pallas_call x2 -> x3, Pallas kernels: 8.01 us -> 14.1 us  [the longest x1 10 us: encode(): pl.pallas_call(functools.partial(ffn_kernel, queries=queries, tokens=toke...]
    ppermute x3, waiting for transfers between devices: 1.5 us -> 4.83 us  [shards(): lax.ppermute(embeds, 'x', turn(X, k))]
    unnamed x1 -> x0, other arithmetic: 1.34 us -> none
    broadcast_in_dim x1, local copies, waits for them, and re-layouts: 0.01 us -> 1.28 us  [shards(): shift[None]]
  transfers between devices with their start and end apart: 13 -> 16, of which waited for: 5 -> 8; matrix products, arithmetic and copies ran while one was open for 2% -> 7% of each run, Pallas kernels for 31% -> 26%
where the time goes in v2:
time: 79 us; the launch traced here: 78.5 us
  Pallas kernels  31.6 us (40%)
  starting transfers between devices  27.4 us (35%)
  waiting for transfers between devices  12 us (15%)
  local copies, waits for them, and re-layouts  6.69 us (8%)
    ppermute x7, starting transfers between devices, along(): return lax.ppermute(a, 'z', turn(Z, k))  18.1 us
    pallas_call x2, Pallas kernels, score(): pl.pallas_call(functools.partial(score_kernel, tiles=tiles, length=length...  17.5 us
    pallas_call x1, Pallas kernels, encode(): pl.pallas_call(functools.partial(ffn_kernel, queries=queries, tokens=toke...  10 us
    ppermute x3, starting transfers between devices, shards(): lax.ppermute(embeds, 'x', turn(X, k))  5.14 us
    ppermute x3, waiting for transfers between devices, shards(): lax.ppermute(embeds, 'x', turn(X, k))  4.83 us
    ppermute x3, waiting for transfers between devices, shards(): lax.ppermute(found, 'x', turn(X, k))  4.64 us
    ppermute x3, starting transfers between devices, shards(): lax.ppermute(found, 'x', turn(X, k))  3.84 us
    pallas_call x1, Pallas kernels, make_parcel(): pl.pallas_call(parcel_kernel, grid_spec=pltpu.PrefetchScalarGridSpec(num_...  2.37 us
  transfers between devices with their start and end apart: 16, of which 8 were waited for; matrix products, arithmetic and copies ran while one was open for 7% of the time, Pallas kernels for 26%

profile of v2, /device:TPU:16, one launch (start us, length us, event | category | flops | bytes accessed | tf_op | source)
XLA Modules:
  0.0 78.5 jit_solution(5646144948122019250)
XLA Ops:
  0.0 0.7 fusion.near
  0.7 0.0 copy-start.3
  0.7 0.1 collective-permute-start
  0.8 1.3 %broadcast_in_dim.19.b_out = f32[1,768]{1,0:T(1,128)} reshape(f32[768]{0:T(1024)} %param.16) | data formatting | bytes 6144 | tf_op jit(solution)/shard_map/broadcast_in_dim | solution.py:230
  2.1 1.3 %broadcast_in_dim.20.gain = f32[1,768]{1,0:T(1,128)} reshape(f32[768]{0:T(1024)} %param.17) | data formatting | bytes 6144 | tf_op jit(solution)/shard_map/broadcast_in_dim | solution.py:230
  3.3 1.3 %broadcast_in_dim.21.shift = f32[1,768]{1,0:T(1,128)} reshape(f32[768]{0:T(1024)} %param.18) | data formatting | bytes 6144 | tf_op jit(solution)/shard_map/broadcast_in_dim | solution.py:230
  4.6 0.7 stack.15.place
  5.3 0.0 collective-permute-done.far
  5.3 0.0 copy-done.3
  5.3 0.0 copy-start.7
  5.3 0.6 copy-done.7
  5.9 2.4 %parcel.1.refs_0_ = bf16[832,128]{1,0:T(8,128)(2,1)} custom-call(s32[8]{0:T(128)} %stack.15.place, s32[12]{0:T(128)} %sizes.1, f32[4,512]{1,0:T(4,128)} %copy-done.3, f32[4,512]{1,0:T(4,128)} %copy-done.7, bf16[12,128,128]{2,1,0:T(8,128)(2,1)} %tiles.1), custom_call_target="tpu_custom_call" | custom-call | tf_op jit(solution)/shard_map/parcel/pallas_call | solution.py:100
  8.3 1.9 %collective-permute-start.1 = (bf16[832,128]{1,0:T(8,128)(2,1)}, bf16[832,128]{1,0:T(8,128)(2,1)S(1)}, u32[]{:S(2)}, u32[]{:S(2)}) collective-permute-start(bf16[832,128]{1,0:T(8,128)(2,1)} %parcel.1.refs_0_), channel_id=1, source_target_pairs={{0,1},{1,2},{2,3},{3,4},{4,5},{5,6},{6,7},{7,0},{8,9},{9,10},{10,1... | collective-permute-start | bytes 638984 | tf_op jit(solution)/shard_map/ppermute | solution.py:226
  10.2 3.9 %collective-permute-start.2 = (bf16[832,128]{1,0:T(8,128)(2,1)}, bf16[832,128]{1,0:T(8,128)(2,1)S(1)}, u32[]{:S(2)}, u32[]{:S(2)}) collective-permute-start(bf16[832,128]{1,0:T(8,128)(2,1)} %parcel.1.refs_0_), channel_id=1, source_target_pairs={{0,7},{1,0},{2,1},{3,2},{4,3},{5,4},{6,5},{7,6},{8,15},{9,8},{10,9... | collective-permute-start | bytes 638984 | tf_op jit(solution)/shard_map/ppermute | solution.py:226
  14.1 0.0 collective-permute-start.3
  14.1 4.1 %collective-permute-start.4 = (bf16[832,128]{1,0:T(8,128)(2,1)}, bf16[832,128]{1,0:T(8,128)(2,1)S(1)}, u32[]{:S(2)}, u32[]{:S(2)}) collective-permute-start(bf16[832,128]{1,0:T(8,128)(2,1)} %parcel.1.refs_0_), channel_id=1, source_target_pairs={{0,6},{1,7},{2,0},{3,1},{4,2},{5,3},{6,4},{7,5},{8,14},{9,15},{10,... | collective-permute-start | bytes 638984 | tf_op jit(solution)/shard_map/ppermute | solution.py:226
  18.3 0.0 copy-start
  18.3 0.0 copy-start.1
  18.3 10.0 %encode.1 = bf16[512,128]{1,0:T(8,128)(2,1)} custom-call(bf16[512,768]{1,0:T(8,128)(2,1)} %bitcast.14, bf16[768,3072]{1,0:T(8,128)(2,1)} %w_in.1, f32[1,3072]{1,0:T(1,128)} %bitcast.15, bf16[3072,768]{1,0:T(8,128)(2,1)} %w_out.1, f32[1,768]{1,0:T(1,128)} %broadcast_in_dim.19.b_out, f32[1,768]{1,0:T(1,128)} %broadcast_in_dim.20.gain, ...), custom_call_target="tpu_custom_call" | custom-call | flops 9663676416 | bytes 9437184 | tf_op jit(solution)/shard_map/encode/pallas_call | solution.py:57
  28.3 0.0 collective-permute-done.1.refs_1_
  28.3 0.0 collective-permute-done.2.refs_2_
  28.3 0.0 collective-permute-done.3.refs_3_
  28.3 0.9 %collective-permute-done.4.refs_4_ = bf16[832,128]{1,0:T(8,128)(2,1)S(1)} collective-permute-done((bf16[832,128]{1,0:T(8,128)(2,1)}, bf16[832,128]{1,0:T(8,128)(2,1)S(1)}, u32[]{:S(2)}, u32[]{:S(2)}) %collective-permute-start.4) | collective-permute-done | bytes 213024 | tf_op jit(solution)/shard_map/ppermute | solution.py:226
  29.2 1.5 %collective-permute-start.5 = (bf16[512,128]{1,0:T(8,128)(2,1)}, bf16[512,128]{1,0:T(8,128)(2,1)S(1)}, u32[]{:S(2)}, u32[]{:S(2)}) collective-permute-start(bf16[512,128]{1,0:T(8,128)(2,1)} %encode.1), channel_id=1, source_target_pairs={{0,8},{8,16},{16,24},{24,0},{1,9},{9,17},{17,25},{25,1},{2,10},{10... | collective-permute-start | bytes 393224 | tf_op jit(solution)/shard_map/ppermute | solution.py:234
  30.7 1.7 %collective-permute-start.6 = (bf16[512,128]{1,0:T(8,128)(2,1)}, bf16[512,128]{1,0:T(8,128)(2,1)S(1)}, u32[]{:S(2)}, u32[]{:S(2)}) collective-permute-start(bf16[512,128]{1,0:T(8,128)(2,1)} %encode.1), channel_id=1, source_target_pairs={{0,24},{8,0},{16,8},{24,16},{1,25},{9,1},{17,9},{25,17},{2,26},{10... | collective-permute-start | bytes 393224 | tf_op jit(solution)/shard_map/ppermute | solution.py:234
  32.4 0.9 %constant_dynamic-update-slice_fusion.3 = bf16[2048,128]{1,0:T(8,128)(2,1)S(1)} fusion(bf16[512,128]{1,0:T(8,128)(2,1)} %encode.1), kind=kLoop, calls=%fused_computation.3 | loop fusion | bytes 262144
  33.4 1.9 %collective-permute-start.7 = (bf16[512,128]{1,0:T(8,128)(2,1)}, bf16[512,128]{1,0:T(8,128)(2,1)S(1)}, u32[]{:S(2)}, u32[]{:S(2)}) collective-permute-start(bf16[512,128]{1,0:T(8,128)(2,1)} %encode.1), channel_id=1, source_target_pairs={{0,16},{8,24},{16,0},{24,8},{1,17},{9,25},{17,1},{25,9},{2,18},{10... | collective-permute-start | bytes 393224 | tf_op jit(solution)/shard_map/ppermute | solution.py:234
  35.3 0.3 collective-permute-done.5
  35.6 1.1 %collective-permute-done.6 = bf16[512,128]{1,0:T(8,128)(2,1)S(1)} collective-permute-done((bf16[512,128]{1,0:T(8,128)(2,1)}, bf16[512,128]{1,0:T(8,128)(2,1)S(1)}, u32[]{:S(2)}, u32[]{:S(2)}) %collective-permute-start.6) | collective-permute-done | bytes 131104 | tf_op jit(solution)/shard_map/ppermute | solution.py:234
  36.7 3.5 %collective-permute-done.7 = bf16[512,128]{1,0:T(8,128)(2,1)S(1)} collective-permute-done((bf16[512,128]{1,0:T(8,128)(2,1)}, bf16[512,128]{1,0:T(8,128)(2,1)S(1)}, u32[]{:S(2)}, u32[]{:S(2)}) %collective-permute-start.7) | collective-permute-done | bytes 131104 | tf_op jit(solution)/shard_map/ppermute | solution.py:234
  40.1 0.1 collective-permute-start.8
  40.2 4.8 %collective-permute-start.11 = (bf16[832,128]{1,0:T(8,128)(2,1)S(1)}, bf16[832,128]{1,0:T(8,128)(2,1)S(1)}, u32[]{:S(2)}, u32[]{:S(2)}) collective-permute-start(bf16[832,128]{1,0:T(8,128)(2,1)S(1)} %collective-permute-done.3.refs_3_), channel_id=1, source_target_pairs={{0,2},{1,3},{2,4},{3,5},{4,6},{5,7},{6,0},{7,1},{8,10},{9,11},{10,... | collective-permute-start | bytes 638984 | tf_op jit(solution)/shard_map/ppermute | solution.py:226
  45.1 0.0 collective-permute-start.9
  45.1 3.2 %collective-permute-start.10 = (bf16[832,128]{1,0:T(8,128)(2,1)S(1)}, bf16[832,128]{1,0:T(8,128)(2,1)S(1)}, u32[]{:S(2)}, u32[]{:S(2)}) collective-permute-start(bf16[832,128]{1,0:T(8,128)(2,1)S(1)} %collective-permute-done.4.refs_4_), channel_id=1, source_target_pairs={{0,7},{1,0},{2,1},{3,2},{4,3},{5,4},{6,5},{7,6},{8,15},{9,8},{10,9... | collective-permute-start | bytes 638984 | tf_op jit(solution)/shard_map/ppermute | solution.py:226
  48.3 0.0 collective-permute-done.8.other
  48.3 0.0 copy-done
  48.3 0.0 copy-done.1
  48.3 10.4 %score_5.1.refs_3_ = f32[32,128]{1,0:T(8,128)S(1)} custom-call(s32[8]{0:T(128)S(1)} %copy-done.1, bf16[2048,128]{1,0:T(8,128)(2,1)S(1)} %constant_dynamic-update-slice_fusion.mine, bf16[2048,128]{1,0:T(8,128)(2,1)S(1)} %collective-permute-done.8.other, bf16[832,128]{1,0:T(8,128)(2,1)S(1)} %copy-done, bf16[832,128]{1,0:T(8,128)(2,1)S(1)} %collective-permute-done.1.refs_1_, ...), custom_call_target="tpu_custom_call" | custom-call | flops 4026531840 | tf_op jit(solution)/shard_map/score_5/pallas_call | solution.py:167
  58.7 0.0 collective-permute-done.11.refs_2_
  58.7 0.6 collective-permute-done.9.refs_0_
  59.3 0.0 collective-permute-done.10.refs_1_
  59.3 7.1 %score_3.1 = f32[32,128]{1,0:T(8,128)S(1)} custom-call(s32[8]{0:T(128)S(1)} %copy-done.1, bf16[2048,128]{1,0:T(8,128)(2,1)S(1)} %constant_dynamic-update-slice_fusion.mine, bf16[2048,128]{1,0:T(8,128)(2,1)S(1)} %collective-permute-done.8.other, bf16[832,128]{1,0:T(8,128)(2,1)S(1)} %collective-permute-done.9.refs_0_, ...), custom_call_target="tpu_custom_call" | custom-call | flops 2415919104 | tf_op jit(solution)/shard_map/score_3/pallas_call | solution.py:167
  66.4 0.2 collective-permute-start.12
  66.6 1.1 %collective-permute-done.12 = f32[32,128]{1,0:T(8,128)S(1)} collective-permute-done((f32[32,128]{1,0:T(8,128)S(1)}, f32[32,128]{1,0:T(8,128)S(1)}, u32[]{:S(2)}, u32[]{:S(2)}) %collective-permute-start.12) | collective-permute-done | bytes 16416 | tf_op jit(solution)/shard_map/ppermute | solution.py:241
  67.7 0.0 copy-start.2
  67.7 0.6 collective-permute-start.13
  68.4 2.6 %collective-permute-start.14 = (f32[32,128]{1,0:T(8,128)S(1)}, f32[32,128]{1,0:T(8,128)S(1)}, u32[]{:S(2)}, u32[]{:S(2)}) collective-permute-start(f32[32,128]{1,0:T(8,128)S(1)} %add.3.refs_0_), channel_id=1, source_target_pairs={{0,24},{8,0},{16,8},{24,16},{1,25},{9,1},{17,9},{25,17},{2,26},{10... | collective-permute-start | bytes 49160 | tf_op jit(solution)/shard_map/ppermute | solution.py:242
  71.0 0.6 collective-permute-start.15
  71.6 1.1 %collective-permute-done.13.refs_1_ = f32[32,128]{1,0:T(8,128)S(1)} collective-permute-done((f32[32,128]{1,0:T(8,128)S(1)}, f32[32,128]{1,0:T(8,128)S(1)}, u32[]{:S(2)}, u32[]{:S(2)}) %collective-permute-start.13) | collective-permute-done | bytes 16416 | tf_op jit(solution)/shard_map/ppermute | solution.py:242
  72.7 0.0 copy-start.4
  72.7 0.0 collective-permute-done.14.refs_2_
  72.7 0.0 copy-start.5
  72.7 3.5 %collective-permute-done.15.refs_3_ = f32[32,128]{1,0:T(8,128)S(1)} collective-permute-done((f32[32,128]{1,0:T(8,128)S(1)}, f32[32,128]{1,0:T(8,128)S(1)}, u32[]{:S(2)}, u32[]{:S(2)}) %collective-permute-start.15) | collective-permute-done | bytes 16416 | tf_op jit(solution)/shard_map/ppermute | solution.py:242
  76.2 0.0 copy-done.2
  76.2 0.0 copy-done.4
  76.2 0.0 copy-done.5
  76.2 0.0 copy-start.6
  76.2 0.6 copy-done.6
  76.8 1.7 %finish.1 = f32[16,4,32]{2,1,0:T(4,128)} custom-call(s32[8]{0:T(128)} %stack.15.place, f32[32,128]{1,0:T(8,128)} %copy-done.2, f32[32,128]{1,0:T(8,128)} %copy-done.4, f32[32,128]{1,0:T(8,128)} %copy-done.5, f32[32,128]{1,0:T(8,128)} %copy-done.6), custom_call_target="tpu_custom_call" | custom-call | tf_op jit(solution)/shard_map/finish/pallas_call | solution.py:202
  (5 shorter events, 0.1 us)
Async XLA Ops:
  0.7 4.6 %copy-start.3 = (f32[4,512]{1,0:T(4,128)}, f32[4,512]{1,0:T(4,128)S(1)}, u32[]{:S(2)}) copy-start(f32[4,512]{1,0:T(4,128)S(1)} %fusion.near) | copy-start | bytes 24580
  0.7 4.6 %collective-permute-start = (f32[4,512]{1,0:T(4,128)S(1)}, f32[4,512]{1,0:T(4,128)S(1)}, u32[]{:S(2)}, u32[]{:S(2)}) collective-permute-start(f32[4,512]{1,0:T(4,128)S(1)} %fusion.near), channel_id=1, source_target_pairs={{0,32},{32,0},{1,33},{33,1},{2,34},{34,2},{3,35},{35,3},{4,36},{36... | collective-permute-start | bytes 24584 | tf_op jit(solution)/shard_map/ppermute | solution.py:222
  5.3 0.6 copy-start.7
  8.3 20.0 %collective-permute-start.1 = (bf16[832,128]{1,0:T(8,128)(2,1)}, bf16[832,128]{1,0:T(8,128)(2,1)S(1)}, u32[]{:S(2)}, u32[]{:S(2)}) collective-permute-start(bf16[832,128]{1,0:T(8,128)(2,1)} %parcel.1.refs_0_), channel_id=1, source_target_pairs={{0,1},{1,2},{2,3},{3,4},{4,5},{5,6},{6,7},{7,0},{8,9},{9,10},{10,1... | collective-permute-start | bytes 638984 | tf_op jit(solution)/shard_map/ppermute | solution.py:226
  10.2 18.1 %collective-permute-start.2 = (bf16[832,128]{1,0:T(8,128)(2,1)}, bf16[832,128]{1,0:T(8,128)(2,1)S(1)}, u32[]{:S(2)}, u32[]{:S(2)}) collective-permute-start(bf16[832,128]{1,0:T(8,128)(2,1)} %parcel.1.refs_0_), channel_id=1, source_target_pairs={{0,7},{1,0},{2,1},{3,2},{4,3},{5,4},{6,5},{7,6},{8,15},{9,8},{10,9... | collective-permute-start | bytes 638984 | tf_op jit(solution)/shard_map/ppermute | solution.py:226
  14.1 14.2 %collective-permute-start.3 = (bf16[832,128]{1,0:T(8,128)(2,1)}, bf16[832,128]{1,0:T(8,128)(2,1)S(1)}, u32[]{:S(2)}, u32[]{:S(2)}) collective-permute-start(bf16[832,128]{1,0:T(8,128)(2,1)} %parcel.1.refs_0_), channel_id=1, source_target_pairs={{0,2},{1,3},{2,4},{3,5},{4,6},{5,7},{6,0},{7,1},{8,10},{9,11},{10,... | collective-permute-start | bytes 638984 | tf_op jit(solution)/shard_map/ppermute | solution.py:226
  14.1 15.0 %collective-permute-start.4 = (bf16[832,128]{1,0:T(8,128)(2,1)}, bf16[832,128]{1,0:T(8,128)(2,1)S(1)}, u32[]{:S(2)}, u32[]{:S(2)}) collective-permute-start(bf16[832,128]{1,0:T(8,128)(2,1)} %parcel.1.refs_0_), channel_id=1, source_target_pairs={{0,6},{1,7},{2,0},{3,1},{4,2},{5,3},{6,4},{7,5},{8,14},{9,15},{10,... | collective-permute-start | bytes 638984 | tf_op jit(solution)/shard_map/ppermute | solution.py:226
  18.3 30.1 %copy-start = (bf16[832,128]{1,0:T(8,128)(2,1)S(1)}, bf16[832,128]{1,0:T(8,128)(2,1)}, u32[]{:S(2)}) copy-start(bf16[832,128]{1,0:T(8,128)(2,1)} %parcel.1.refs_0_) | copy-start | bytes 638980
  18.3 30.1 %copy-start.1 = (s32[8]{0:T(128)S(1)}, s32[8]{0:T(128)}, u32[]{:S(2)}) copy-start(s32[8]{0:T(128)} %stack.15.place) | copy-start | bytes 100
  29.2 6.4 %collective-permute-start.5 = (bf16[512,128]{1,0:T(8,128)(2,1)}, bf16[512,128]{1,0:T(8,128)(2,1)S(1)}, u32[]{:S(2)}, u32[]{:S(2)}) collective-permute-start(bf16[512,128]{1,0:T(8,128)(2,1)} %encode.1), channel_id=1, source_target_pairs={{0,8},{8,16},{16,24},{24,0},{1,9},{9,17},{17,25},{25,1},{2,10},{10... | collective-permute-start | bytes 393224 | tf_op jit(solution)/shard_map/ppermute | solution.py:234
  30.7 6.0 %collective-permute-start.6 = (bf16[512,128]{1,0:T(8,128)(2,1)}, bf16[512,128]{1,0:T(8,128)(2,1)S(1)}, u32[]{:S(2)}, u32[]{:S(2)}) collective-permute-start(bf16[512,128]{1,0:T(8,128)(2,1)} %encode.1), channel_id=1, source_target_pairs={{0,24},{8,0},{16,8},{24,16},{1,25},{9,1},{17,9},{25,17},{2,26},{10... | collective-permute-start | bytes 393224 | tf_op jit(solution)/shard_map/ppermute | solution.py:234
  33.4 6.8 %collective-permute-start.7 = (bf16[512,128]{1,0:T(8,128)(2,1)}, bf16[512,128]{1,0:T(8,128)(2,1)S(1)}, u32[]{:S(2)}, u32[]{:S(2)}) collective-permute-start(bf16[512,128]{1,0:T(8,128)(2,1)} %encode.1), channel_id=1, source_target_pairs={{0,16},{8,24},{16,0},{24,8},{1,17},{9,25},{17,1},{25,9},{2,18},{10... | collective-permute-start | bytes 393224 | tf_op jit(solution)/shard_map/ppermute | solution.py:234
  40.1 8.2 %collective-permute-start.8 = (bf16[2048,128]{1,0:T(8,128)(2,1)S(1)}, bf16[2048,128]{1,0:T(8,128)(2,1)S(1)}, u32[]{:S(2)}, u32[]{:S(2)}) collective-permute-start(bf16[2048,128]{1,0:T(8,128)(2,1)S(1)} %constant_dynamic-update-slice_fusion.mine), channel_id=1, source_target_pairs={{0,32},{32,0},{1,33},{33,1},{2,34},{34,2},{3,35},{35,3},{4,36},{36... | collective-permute-start | bytes 1572872 | tf_op jit(solution)/shard_map/ppermute | solution.py:236
  40.2 18.5 %collective-permute-start.11 = (bf16[832,128]{1,0:T(8,128)(2,1)S(1)}, bf16[832,128]{1,0:T(8,128)(2,1)S(1)}, u32[]{:S(2)}, u32[]{:S(2)}) collective-permute-start(bf16[832,128]{1,0:T(8,128)(2,1)S(1)} %collective-permute-done.3.refs_3_), channel_id=1, source_target_pairs={{0,2},{1,3},{2,4},{3,5},{4,6},{5,7},{6,0},{7,1},{8,10},{9,11},{10,... | collective-permute-start | bytes 638984 | tf_op jit(solution)/shard_map/ppermute | solution.py:226
  45.1 14.2 %collective-permute-start.9 = (bf16[832,128]{1,0:T(8,128)(2,1)S(1)}, bf16[832,128]{1,0:T(8,128)(2,1)S(1)}, u32[]{:S(2)}, u32[]{:S(2)}) collective-permute-start(bf16[832,128]{1,0:T(8,128)(2,1)S(1)} %collective-permute-done.3.refs_3_), channel_id=1, source_target_pairs={{0,1},{1,2},{2,3},{3,4},{4,5},{5,6},{6,7},{7,0},{8,9},{9,10},{10,1... | collective-permute-start | bytes 638984 | tf_op jit(solution)/shard_map/ppermute | solution.py:226
  45.1 14.2 %collective-permute-start.10 = (bf16[832,128]{1,0:T(8,128)(2,1)S(1)}, bf16[832,128]{1,0:T(8,128)(2,1)S(1)}, u32[]{:S(2)}, u32[]{:S(2)}) collective-permute-start(bf16[832,128]{1,0:T(8,128)(2,1)S(1)} %collective-permute-done.4.refs_4_), channel_id=1, source_target_pairs={{0,7},{1,0},{2,1},{3,2},{4,3},{5,4},{6,5},{7,6},{8,15},{9,8},{10,9... | collective-permute-start | bytes 638984 | tf_op jit(solution)/shard_map/ppermute | solution.py:226
  66.4 1.3 %collective-permute-start.12 = (f32[32,128]{1,0:T(8,128)S(1)}, f32[32,128]{1,0:T(8,128)S(1)}, u32[]{:S(2)}, u32[]{:S(2)}) collective-permute-start(f32[32,128]{1,0:T(8,128)S(1)} %score_3.1), channel_id=1, source_target_pairs={{0,32},{32,0},{1,33},{33,1},{2,34},{34,2},{3,35},{35,3},{4,36},{36... | collective-permute-start | bytes 49160 | tf_op jit(solution)/shard_map/ppermute | solution.py:241
  67.7 8.5 %copy-start.2 = (f32[32,128]{1,0:T(8,128)}, f32[32,128]{1,0:T(8,128)S(1)}, u32[]{:S(2)}) copy-start(f32[32,128]{1,0:T(8,128)S(1)} %add.3.refs_0_) | copy-start | bytes 49156
  67.7 4.9 %collective-permute-start.13 = (f32[32,128]{1,0:T(8,128)S(1)}, f32[32,128]{1,0:T(8,128)S(1)}, u32[]{:S(2)}, u32[]{:S(2)}) collective-permute-start(f32[32,128]{1,0:T(8,128)S(1)} %add.3.refs_0_), channel_id=1, source_target_pairs={{0,8},{8,16},{16,24},{24,0},{1,9},{9,17},{17,25},{25,1},{2,10},{10... | collective-permute-start | bytes 49160 | tf_op jit(solution)/shard_map/ppermute | solution.py:242
  68.4 4.3 %collective-permute-start.14 = (f32[32,128]{1,0:T(8,128)S(1)}, f32[32,128]{1,0:T(8,128)S(1)}, u32[]{:S(2)}, u32[]{:S(2)}) collective-permute-start(f32[32,128]{1,0:T(8,128)S(1)} %add.3.refs_0_), channel_id=1, source_target_pairs={{0,24},{8,0},{16,8},{24,16},{1,25},{9,1},{17,9},{25,17},{2,26},{10... | collective-permute-start | bytes 49160 | tf_op jit(solution)/shard_map/ppermute | solution.py:242
  71.0 5.2 %collective-permute-start.15 = (f32[32,128]{1,0:T(8,128)S(1)}, f32[32,128]{1,0:T(8,128)S(1)}, u32[]{:S(2)}, u32[]{:S(2)}) collective-permute-start(f32[32,128]{1,0:T(8,128)S(1)} %add.3.refs_0_), channel_id=1, source_target_pairs={{0,16},{8,24},{16,0},{24,8},{1,17},{9,25},{17,1},{25,9},{2,18},{10... | collective-permute-start | bytes 49160 | tf_op jit(solution)/shard_map/ppermute | solution.py:242
  72.7 3.5 %copy-start.4 = (f32[32,128]{1,0:T(8,128)}, f32[32,128]{1,0:T(8,128)S(1)}, u32[]{:S(2)}) copy-start(f32[32,128]{1,0:T(8,128)S(1)} %collective-permute-done.13.refs_1_) | copy-start | bytes 49156
  72.7 3.5 %copy-start.5 = (f32[32,128]{1,0:T(8,128)}, f32[32,128]{1,0:T(8,128)S(1)}, u32[]{:S(2)}) copy-start(f32[32,128]{1,0:T(8,128)S(1)} %collective-permute-done.14.refs_2_) | copy-start | bytes 49156
  76.2 0.6 copy-start.6

commit v3 on v2

v3 whole, which is shorter than its diff:
```python
import functools

import jax
import jax.numpy as jnp
from jax import lax
from jax.experimental import pallas as pl
from jax.experimental.pallas import tpu as pltpu
from jax.sharding import Mesh
from jax.sharding import PartitionSpec as P

Y, CORES, X, Z = 4, 2, 4, 8
HALF_ROOT = 0.7071067811865476


def turn(size, step):
    return [(i, (i + step) % size) for i in range(size)]


def gelu(pre):
    return 0.5 * pre * (1.0 + lax.erf(pre * jnp.float32(HALF_ROOT)))


def ffn_part(tok, w_in, b_in, w_out, skip):
    chunk = w_in.shape[1]
    start = pl.multiple_of((pl.program_id(0) + skip) * chunk, chunk)
    pre = jnp.dot(tok[...], w_in[...], preferred_element_type=jnp.float32) + b_in[pl.ds(start, chunk)][None, :]
    hidden = gelu(pre).astype(jnp.bfloat16)
    return jnp.dot(hidden, w_out[...], preferred_element_type=jnp.float32)


def encode_first(tok, w_in, b_in, w_out, acc):
    part = ffn_part(tok, w_in, b_in, w_out, 0)

    @pl.when(pl.program_id(0) == 0)
    def _():
        acc[...] = part

    @pl.when(pl.program_id(0) > 0)
    def _():
        acc[...] += part


def encode_second(tok, w_in, b_in, w_out, begun, b_out, gain, shift, proj, out, acc, turned, *, queries, tokens, skip):
    step = pl.program_id(0)
    part = ffn_part(tok, w_in, b_in, w_out, skip)

    @pl.when(step == 0)
    def _():
        acc[...] = begun[...] + part

    @pl.when(step > 0)
    def _():
        acc[...] += part

    @pl.when(step == pl.num_programs(0) - 1)
    def _():
        total = acc[...] + b_out[...][None, :] + tok[...].astype(jnp.float32)
        diff = total - jnp.mean(total, axis=-1, keepdims=True)
        spread = jnp.mean(diff * diff, axis=-1, keepdims=True)
        normed = diff * lax.rsqrt(spread + 1e-5) * gain[...][None, :] + shift[...][None, :]
        projected = jnp.dot(normed.astype(jnp.bfloat16), proj[...], preferred_element_type=jnp.float32)
        scale = lax.rsqrt(jnp.sum(projected * projected, axis=-1, keepdims=True) + 1e-6)
        embeds = projected * scale
        for q in range(queries):
            turned[pl.ds(q, tokens, stride=queries), :] = embeds[q * tokens : (q + 1) * tokens, :]
        out[...] = turned[...].astype(jnp.bfloat16)


def whole(a):
    return pl.BlockSpec(a.shape, lambda j: (0,) * a.ndim)


def ffn_specs(tok, w_in, b_in, chunk, skip):
    width = tok.shape[1]
    return [
        whole(tok),
        pl.BlockSpec((width, chunk), lambda j: (0, j + skip)),
        whole(b_in),
        pl.BlockSpec((chunk, width), lambda j: (j + skip, 0)),
    ]


FREE = pl.CostEstimate(flops=1000, bytes_accessed=1000, transcendentals=0)


def encode(tok, w_in, b_in, w_out, chunk=768):
    steps = w_in.shape[1] // chunk // 2
    return pl.pallas_call(
        encode_first,
        grid=(steps,),
        in_specs=ffn_specs(tok, w_in, b_in, chunk, 0),
        out_specs=whole(tok),
        out_shape=jax.ShapeDtypeStruct(tok.shape, jnp.float32),
        compiler_params=pltpu.CompilerParams(vmem_limit_bytes=60 << 20),
        cost_estimate=FREE,
        name="encode_first",
    )(tok, w_in, b_in, w_out)


def encode_rest(tok, w_in, b_in, w_out, begun, b_out, gain, shift, proj, queries, tokens, chunk=768):
    rows, width = tok.shape
    steps = w_in.shape[1] // chunk // 2
    return pl.pallas_call(
        functools.partial(encode_second, queries=queries, tokens=tokens, skip=steps),
        grid=(steps,),
        in_specs=ffn_specs(tok, w_in, b_in, chunk, steps) + [whole(a) for a in (begun, b_out, gain, shift, proj)],
        out_specs=pl.BlockSpec((rows, proj.shape[1]), lambda j: (0, 0)),
        out_shape=jax.ShapeDtypeStruct((rows, proj.shape[1]), jnp.bfloat16),
        scratch_shapes=[pltpu.VMEM((rows, width), jnp.float32), pltpu.VMEM((rows, proj.shape[1]), jnp.float32)],
        compiler_params=pltpu.CompilerParams(vmem_limit_bytes=60 << 20),
        cost_estimate=FREE,
        name="encode_second",
    )(tok, w_in, b_in, w_out, begun, b_out, gain, shift, proj)


def parcel_kernel(sizes, near, far, tiles, out, *, half):
    length = tiles.shape[1]
    core = lax.axis_index("core")
    column = lax.broadcasted_iota(jnp.int32, tiles.shape[1:], 0)
    for t in range(half):
        tile = tiles[core * half + t].astype(jnp.float32)
        size = sizes[core * half + t]
        out[t * length : (t + 1) * length, :] = jnp.where(column < size, tile, tile[0:1, :]).astype(jnp.bfloat16)
    for source, side in ((near, core), (far, 1 - core)):
        codes = source[...]
        blank = jnp.zeros((4, 128), jnp.float32)
        lines = []
        for x in range(X):
            lines += [codes[:, x * 128 : (x + 1) * 128], blank]
        start = pl.multiple_of(half * length + side * (8 * X), 8 * X)
        out[pl.ds(start, 8 * X), :] = jnp.concatenate(lines, axis=0).astype(jnp.bfloat16)


VM = pl.BlockSpec(memory_space=pltpu.VMEM)


def make_parcel(sizes, near, far, tiles):
    count, length, dims = tiles.shape
    half = count // CORES
    return pl.pallas_call(
        functools.partial(parcel_kernel, half=half),
        in_specs=[pl.BlockSpec(memory_space=pltpu.SMEM), VM, VM, VM],
        out_specs=VM,
        out_shape=jax.ShapeDtypeStruct((half * length + 8 * X * CORES, dims), jnp.bfloat16),
        name="parcel",
    )(sizes, near, far, tiles)


SENDER = (0, X - 1, 1, 2)


def score_kernel(*refs, sides, tiles, length, group, shards, chained):
    n, s = len(shards), len(sides)
    blocks, parcels, out, acc = refs[:s], refs[s : s + n], refs[-2], refs[-1]
    rows = tiles * length
    lane_group = lax.broadcasted_iota(jnp.int32, (8, 128), 1) // group
    row = lax.broadcasted_iota(jnp.int32, (8, 128), 0)
    core, x, z = lax.axis_index("core"), lax.axis_index("x"), lax.axis_index("z")
    acc[...] = jnp.zeros_like(acc)

    for step in range(X):
        for side, queries in zip(sides, blocks):
            block = queries[step * 512 : (step + 1) * 512, :]
            source = lax.rem(x + SENDER[step], X)
            here = lane_group == source + X * (core if side == 0 else 1 - core)
            for n, parcel in enumerate(parcels):
                similar = lax.dot_general(
                    parcel[0:rows, :], block, (((1,), (1,)), ((), ())), preferred_element_type=jnp.float32
                )
                sums = []
                for t in range(tiles):
                    best = jnp.max(similar[t * length : (t + 1) * length], axis=0, keepdims=True)
                    sums.append(best[:, 0:128] + best[:, 128:256] + best[:, 256:384] + best[:, 384:512])
                sums = jnp.concatenate(sums + [jnp.zeros((8 - tiles, 128), jnp.float32)], axis=0)
                sums = sums + pltpu.roll(sums, 64, 1)
                sums = sums + pltpu.roll(sums, 32, 1)
                sums = sums + pltpu.roll(sums, 16, 1)
                acc[n] = jnp.where(here, sums, acc[n])

    first_tile = core * tiles
    out[...] = refs[s + len(shards)][...] if chained else jnp.zeros_like(out)
    for n, parcel in enumerate(parcels):
        codes = parcel[rows : rows + 8 * X * CORES, :].astype(jnp.float32)
        code = jnp.zeros((8, 128), jnp.float32)
        for d in range(X * CORES):
            turned = pltpu.roll(codes[d * 8 : d * 8 + 8], lax.rem((d - z) * group + 128, 128), 1)
            code = jnp.where(lane_group == d, turned, code)
        code = code.astype(jnp.int32) - first_tile
        shard = lax.rem(z + shards[n] * (2 * core - 1) + Z, Z)
        for c in range(4):
            picked = (code[c : c + 1] == row) & (row < tiles)
            line = jnp.sum(jnp.where(picked, acc[n], 0.0), axis=0, keepdims=True)
            out[pl.ds(c * Z + shard, 1), :] += line


def score(blocks, parcels, shards, tiles, length, group, begun=None):
    n = len(parcels)
    more = [] if begun is None else [begun]
    return pl.pallas_call(
        functools.partial(
            score_kernel,
            sides=tuple(blocks),
            tiles=tiles,
            length=length,
            group=group,
            shards=shards,
            chained=begun is not None,
        ),
        in_specs=[VM] * (len(blocks) + n + len(more)),
        out_specs=VM,
        out_shape=jax.ShapeDtypeStruct((4 * Z, 128), jnp.float32),
        scratch_shapes=[pltpu.VMEM((n, 8, 128), jnp.float32)],
        compiler_params=pltpu.CompilerParams(vmem_limit_bytes=32 << 20),
        cost_estimate=FREE,
        name=f"score_{len(blocks)}_{n}",
    )(*blocks.values(), *parcels, *more)


def finish_kernel(*refs, group):
    sources, out, table = refs[:4], refs[4], refs[5]
    core, x = lax.axis_index("core"), lax.axis_index("x")
    for sender, source in zip(SENDER, sources):
        lines = pltpu.roll(source[...], lax.rem(128 - (core * X + x) * group, 128), 1)
        shard = lax.rem(x + sender, X) * Z
        for c in range(4):
            table[pl.ds(pl.multiple_of(c * X * Z + shard, Z), Z), :] = lines[c * Z : (c + 1) * Z]
    turned = table[...].T
    for c in range(4):
        out[:, c, :] = turned[0:group, c * X * Z : (c + 1) * X * Z]


def finish(sources, group):
    return pl.pallas_call(
        functools.partial(finish_kernel, group=group),
        in_specs=[VM] * 4,
        out_specs=VM,
        out_shape=jax.ShapeDtypeStruct((group, 4, X * Z), jnp.float32),
        scratch_shapes=[pltpu.VMEM((128, 128), jnp.float32)],
        name="finish",
    )(*sources)


def tied(*arrays):
    return lax.optimization_barrier(arrays)


def shards(tokens, w_in, b_in, w_out, b_out, gain, shift, proj, tiles, lengths, slots, counts):
    queries, query_len, width = tokens.shape
    count, length, dims = tiles.shape
    half = count // CORES

    wanted = slots.transpose(1, 2, 0)[0]
    valid = jnp.arange(4, dtype=jnp.int32)[:, None] < counts.transpose(1, 0)
    codes = jnp.where(valid, wanted, count).astype(jnp.float32)
    codes_far = lax.ppermute(codes, "core", turn(CORES, 1))
    own = make_parcel(lengths, codes, codes_far, tiles)

    ways = [(z, (z + 1) % Z) for z in range(Z)] + [(Z + z, Z + (z - 1) % Z) for z in range(Z)]

    def along(a):
        return lax.ppermute(a, ("core", "z"), ways)

    def across(a, k):
        return lax.ppermute(a, "x", turn(X, k))

    first = along(own)
    flat, _ = tied(tokens.reshape(queries * query_len, width), own)
    begun = encode(flat, w_in, b_in, w_out)
    first, begun = tied(first, begun)
    second = along(first)
    embeds = encode_rest(flat, w_in, b_in, w_out, begun, b_out, gain, shift, proj, queries, query_len)
    second, embeds = tied(second, embeds)
    third = along(second)
    mine = jnp.concatenate([embeds] + [across(embeds, k) for k in (1, -1, 2)], axis=0)
    third, mine = tied(third, mine)
    other = lax.ppermute(mine, "core", turn(CORES, 1))
    fourth = along(third)
    args = (half, length, queries)
    found = score({0: mine}, [own, first, second], (0, 1, 2), *args)
    fourth, found = tied(fourth, found)
    fifth = along(fourth)
    found = score({1: other}, [own, first, second], (0, 1, 2), *args, begun=found)
    fifth, found = tied(fifth, found)
    sixth = along(fifth)
    both = {0: mine, 1: other}
    found = score(both, [third, fourth], (3, 4), *args, begun=found)
    sixth, found = tied(sixth, found)
    seventh = along(sixth)
    found = score(both, [fifth, sixth], (5, 6), *args, begun=found)
    found = score(both, [seventh], (7,), *args, begun=found)
    found = found + lax.ppermute(found, "core", turn(CORES, 1))
    sources = [found] + [across(found, k) for k in (1, -1, 2)]
    return finish(sources, queries).transpose(0, 2, 1)


def solution(mesh):
    fine = Mesh(mesh.devices.reshape(Y, CORES, X, Z), ("y", "core", "x", "z"))
    group, shard = ("y", "core"), ("x", "z")
    placed = (P(group + shard),) + (P(),) * 7 + (P(shard), P(shard), P(group, shard), P(group, shard))
    return jax.shard_map(shards, mesh=fine, in_specs=placed, out_specs=P(group + shard), check_vma=False)
```

time: 79 us -> 77.2 us (0.977)
  waiting for transfers between devices: 12 us -> 25.7 us
  starting transfers between devices: 27.4 us -> 16.1 us
  local copies, waits for them, and re-layouts: 6.69 us -> 1.21 us
  other arithmetic: 0.71 us -> 1.65 us
    ppermute x13, waiting for transfers between devices: 10.9 us -> 23.3 us  [the longest x7 14.2 us: along(): return lax.ppermute(a, ('core', 'z'), ways)]
    ppermute x13, starting transfers between devices: 27 us -> 15.5 us  [the longest x6 8.67 us: across(): return lax.ppermute(a, 'x', turn(X, k))]
    broadcast_in_dim x3 -> x0, local copies, waits for them, and re-layouts: 3.81 us -> none  [the longest x1 1.28 us: shards(): shift[None]]
    ppermute x1, waiting for transfers between devices: 0.01 us -> 1.16 us  [shards(): codes_far = lax.ppermute(codes, 'core', turn(CORES, 1))]
    unnamed x19 -> x14, local copies, waits for them, and re-layouts: 2.19 us -> 1.21 us
    concatenate x0 -> x1, other arithmetic: none -> 0.94 us  [shards(): jnp.concatenate([embeds] + [across(embeds, k) for k in (1, -1, 2)], axis=0)]
    pallas_call x5 -> x9, Pallas kernels: 31.6 us -> 32.3 us  [the longest x5 15 us: score(): pl.pallas_call(functools.partial(score_kernel, sides=tuple(blocks), tiles...]
  transfers between devices with their start and end apart: 16 -> 16, of which waited for: 8 -> 10; matrix products, arithmetic and copies ran while one was open for 7% -> 1% of each run, Pallas kernels for 26% -> 35%
where the time goes in v3:
time: 77.2 us; the launch traced here: 77 us
  Pallas kernels  32.3 us (42%)
  waiting for transfers between devices  25.7 us (33%)
  starting transfers between devices  16.1 us (21%)
  other arithmetic  1.65 us (2%)
  local copies, waits for them, and re-layouts  1.21 us (2%)
    pallas_call x5, Pallas kernels, score(): pl.pallas_call(functools.partial(score_kernel, sides=tuple(blocks), tiles...  15 us
    ppermute x7, waiting for transfers between devices, along(): return lax.ppermute(a, ('core', 'z'), ways)  14.2 us
    ppermute x6, waiting for transfers between devices, across(): return lax.ppermute(a, 'x', turn(X, k))  9.15 us
    ppermute x6, starting transfers between devices, across(): return lax.ppermute(a, 'x', turn(X, k))  8.67 us
    pallas_call x1, Pallas kernels, encode_rest(): pl.pallas_call(functools.partial(encode_second, queries=queries, tokens=t...  7.4 us
    ppermute x7, starting transfers between devices, along(): return lax.ppermute(a, ('core', 'z'), ways)  6.84 us
    pallas_call x1, Pallas kernels, encode(): pl.pallas_call(encode_first, grid=(steps,), in_specs=ffn_specs(tok, w_in,...  6.37 us
    pallas_call x1, Pallas kernels, make_parcel(): pl.pallas_call(functools.partial(parcel_kernel, half=half), in_specs=[pl....  1.77 us
  transfers between devices with their start and end apart: 16, of which 10 were waited for; matrix products, arithmetic and copies ran while one was open for 1% of the time, Pallas kernels for 35%

profile of v3, /device:TPU:16, one launch (start us, length us, event | category | flops | bytes accessed | tf_op | source)
XLA Modules:
  0.0 77.0 jit_solution(13267451199719953765)
XLA Ops:
  0.0 0.7 fusion.near
  0.7 0.0 copy-start.2
  0.7 0.1 collective-permute-start
  0.8 1.2 %collective-permute-done.far = f32[4,512]{1,0:T(4,128)S(1)} collective-permute-done((f32[4,512]{1,0:T(4,128)S(1)}, f32[4,512]{1,0:T(4,128)S(1)}, u32[]{:S(2)}, u32[]{:S(2)}) %collective-permute-start) | collective-permute-done | bytes 8224 | tf_op jit(solution)/shard_map/ppermute | solution.py:255
  2.0 0.0 copy-done.2
  2.0 0.0 copy-start.6
  2.0 0.6 copy-done.6
  2.6 1.8 %parcel.1.refs_1_ = bf16[832,128]{1,0:T(8,128)(2,1)} custom-call(s32[12]{0:T(128)} %sizes.1, f32[4,512]{1,0:T(4,128)} %copy-done.2, f32[4,512]{1,0:T(4,128)} %copy-done.6, bf16[12,128,128]{2,1,0:T(8,128)(2,1)} %tiles.1), custom_call_target="tpu_custom_call" | custom-call | tf_op jit(solution)/shard_map/parcel/pallas_call | solution.py:140
  4.3 1.9 %collective-permute-start.1 = (bf16[832,128]{1,0:T(8,128)(2,1)}, bf16[832,128]{1,0:T(8,128)(2,1)S(1)}, u32[]{:S(2)}, u32[]{:S(2)}) collective-permute-start(bf16[832,128]{1,0:T(8,128)(2,1)} %parcel.1.refs_1_), channel_id=1, source_target_pairs={{0,1},{1,2},{2,3},{3,4},{4,5},{5,6},{6,7},{7,0},{32,39},{33,32},{3... | collective-permute-start | bytes 638984 | tf_op jit(solution)/shard_map/ppermute | solution.py:261
  6.2 6.4 %encode_first.1.begun = f32[512,768]{1,0:T(8,128)} custom-call(bf16[512,768]{1,0:T(8,128)(2,1)} %bitcast.9, bf16[768,3072]{1,0:T(8,128)(2,1)} %w_in.3, f32[3072]{0:T(1024)} %b_in.3, bf16[3072,768]{1,0:T(8,128)(2,1)} %w_out.3), custom_call_target="tpu_custom_call" | custom-call | flops 1000 | bytes 1000 | tf_op jit(solution)/shard_map/encode_first/pallas_call | solution.py:88
  12.6 0.0 copy-start
  12.6 1.6 %collective-permute-done.1.refs_2_ = bf16[832,128]{1,0:T(8,128)(2,1)S(1)} collective-permute-done((bf16[832,128]{1,0:T(8,128)(2,1)}, bf16[832,128]{1,0:T(8,128)(2,1)S(1)}, u32[]{:S(2)}, u32[]{:S(2)}) %collective-permute-start.1) | collective-permute-done | bytes 213024 | tf_op jit(solution)/shard_map/ppermute | solution.py:261
  14.2 0.4 collective-permute-start.2
  14.6 7.4 %encode_second.1 = bf16[512,128]{1,0:T(8,128)(2,1)} custom-call(bf16[512,768]{1,0:T(8,128)(2,1)} %bitcast.10, bf16[768,3072]{1,0:T(8,128)(2,1)} %w_in.3, f32[3072]{0:T(1024)} %b_in.3, bf16[3072,768]{1,0:T(8,128)(2,1)} %w_out.3, f32[512,768]{1,0:T(8,128)} %encode_first.1.begun, f32[768]{0:T(1024)} %b_out.1, f32[768]{0:T(1024)} %gain.1, f32[768]{0:T(1024)} %shift.1, ...), custom_call_target="tpu_custom_call" | custom-call | flops 1000 | bytes 1000 | tf_op jit(solution)/shard_map/encode_second/pallas_call | solution.py:103
  22.0 0.0 collective-permute-done.2.refs_3_
  22.0 1.5 %collective-permute-start.4 = (bf16[512,128]{1,0:T(8,128)(2,1)}, bf16[512,128]{1,0:T(8,128)(2,1)S(1)}, u32[]{:S(2)}, u32[]{:S(2)}) collective-permute-start(bf16[512,128]{1,0:T(8,128)(2,1)} %encode_second.1), channel_id=1, source_target_pairs={{0,8},{8,16},{16,24},{24,0},{1,9},{9,17},{17,25},{25,1},{2,10},{10... | collective-permute-start | bytes 393224 | tf_op jit(solution)/shard_map/ppermute | solution.py:264
  23.5 1.7 %collective-permute-start.5 = (bf16[512,128]{1,0:T(8,128)(2,1)}, bf16[512,128]{1,0:T(8,128)(2,1)S(1)}, u32[]{:S(2)}, u32[]{:S(2)}) collective-permute-start(bf16[512,128]{1,0:T(8,128)(2,1)} %encode_second.1), channel_id=1, source_target_pairs={{0,24},{8,0},{16,8},{24,16},{1,25},{9,1},{17,9},{25,17},{2,26},{10... | collective-permute-start | bytes 393224 | tf_op jit(solution)/shard_map/ppermute | solution.py:264
  25.3 1.8 %collective-permute-start.6 = (bf16[512,128]{1,0:T(8,128)(2,1)}, bf16[512,128]{1,0:T(8,128)(2,1)S(1)}, u32[]{:S(2)}, u32[]{:S(2)}) collective-permute-start(bf16[512,128]{1,0:T(8,128)(2,1)} %encode_second.1), channel_id=1, source_target_pairs={{0,16},{8,24},{16,0},{24,8},{1,17},{9,25},{17,1},{25,9},{2,18},{10... | collective-permute-start | bytes 393224 | tf_op jit(solution)/shard_map/ppermute | solution.py:264
  27.1 1.9 %collective-permute-start.3 = (bf16[832,128]{1,0:T(8,128)(2,1)S(1)}, bf16[832,128]{1,0:T(8,128)(2,1)S(1)}, u32[]{:S(2)}, u32[]{:S(2)}) collective-permute-start(bf16[832,128]{1,0:T(8,128)(2,1)S(1)} %collective-permute-done.2.refs_3_), channel_id=1, source_target_pairs={{0,1},{1,2},{2,3},{3,4},{4,5},{5,6},{6,7},{7,0},{32,39},{33,32},{3... | collective-permute-start | bytes 638984 | tf_op jit(solution)/shard_map/ppermute | solution.py:261
  29.0 0.0 collective-permute-done.4
  29.0 0.0 collective-permute-done.5
  29.0 4.3 %collective-permute-done.6 = bf16[512,128]{1,0:T(8,128)(2,1)S(1)} collective-permute-done((bf16[512,128]{1,0:T(8,128)(2,1)}, bf16[512,128]{1,0:T(8,128)(2,1)S(1)}, u32[]{:S(2)}, u32[]{:S(2)}) %collective-permute-start.6) | collective-permute-done | bytes 131104 | tf_op jit(solution)/shard_map/ppermute | solution.py:264
  33.3 0.9 %pad_maximum_fusion.refs_0_ = bf16[2048,128]{1,0:T(8,128)(2,1)S(1)} fusion(bf16[512,128]{1,0:T(8,128)(2,1)S(1)} %collective-permute-done.6, bf16[512,128]{1,0:T(8,128)(2,1)S(1)} %collective-permute-done.5, bf16[512,128]{1,0:T(8,128)(2,1)S(1)} %collective-permute-done.4, bf16[512,128]{1,0:T(8,128)(2,1)} %encode_second.1), kind=kLoop, calls=%fused_computation | loop fusion | flops 2097152 | bytes 1048576 | tf_op jit(solution)/shard_map/concatenate | solution.py:274
  34.2 0.0 collective-permute-done.3.refs_2_
  34.2 0.5 collective-permute-start.7
  34.7 1.9 %collective-permute-start.8 = (bf16[832,128]{1,0:T(8,128)(2,1)S(1)}, bf16[832,128]{1,0:T(8,128)(2,1)S(1)}, u32[]{:S(2)}, u32[]{:S(2)}) collective-permute-start(bf16[832,128]{1,0:T(8,128)(2,1)S(1)} %collective-permute-done.3.refs_2_), channel_id=1, source_target_pairs={{0,1},{1,2},{2,3},{3,4},{4,5},{5,6},{6,7},{7,0},{32,39},{33,32},{3... | collective-permute-start | bytes 638984 | tf_op jit(solution)/shard_map/ppermute | solution.py:261
  36.6 0.0 copy-done
  36.6 2.8 %score_1_3.2.refs_4_ = f32[32,128]{1,0:T(8,128)S(1)} custom-call(bf16[2048,128]{1,0:T(8,128)(2,1)S(1)} %pad_maximum_fusion.refs_0_, bf16[832,128]{1,0:T(8,128)(2,1)S(1)} %copy-done, bf16[832,128]{1,0:T(8,128)(2,1)S(1)} %collective-permute-done.1.refs_2_, bf16[832,128]{1,0:T(8,128)(2,1)S(1)} %collective-permute-done.2.refs_3_), custom_call_target="tpu_custom_call" | custom-call | flops 1000 | bytes 1000 | tf_op jit(solution)/shard_map/score_1_3/pallas_call | solution.py:199
  39.5 2.3 %collective-permute-done.8.refs_3_ = bf16[832,128]{1,0:T(8,128)(2,1)S(1)} collective-permute-done((bf16[832,128]{1,0:T(8,128)(2,1)S(1)}, bf16[832,128]{1,0:T(8,128)(2,1)S(1)}, u32[]{:S(2)}, u32[]{:S(2)}) %collective-permute-start.8) | collective-permute-done | bytes 213024 | tf_op jit(solution)/shard_map/ppermute | solution.py:261
  41.8 0.7 collective-permute-start.9
  42.5 0.0 collective-permute-done.7.refs_0_.refs_1_
  42.5 2.8 %score_1_3.3.refs_4_ = f32[32,128]{1,0:T(8,128)S(1)} custom-call(bf16[2048,128]{1,0:T(8,128)(2,1)S(1)} %collective-permute-done.7.refs_0_.refs_1_, bf16[832,128]{1,0:T(8,128)(2,1)S(1)} %copy-done, bf16[832,128]{1,0:T(8,128)(2,1)S(1)} %collective-permute-done.1.refs_2_, bf16[832,128]{1,0:T(8,128)(2,1)S(1)} %collective-permute-done.2.refs_3_, ...), custom_call_target="tpu_custom_call" | custom-call | flops 1000 | bytes 1000 | tf_op jit(solution)/shard_map/score_1_3/pallas_call | solution.py:199
  45.3 3.5 %collective-permute-done.9.refs_2_ = bf16[832,128]{1,0:T(8,128)(2,1)S(1)} collective-permute-done((bf16[832,128]{1,0:T(8,128)(2,1)S(1)}, bf16[832,128]{1,0:T(8,128)(2,1)S(1)}, u32[]{:S(2)}, u32[]{:S(2)}) %collective-permute-start.9) | collective-permute-done | bytes 213024 | tf_op jit(solution)/shard_map/ppermute | solution.py:261
  48.9 0.0 collective-permute-start.10
  48.9 3.7 %score_2_2.2.refs_4_ = f32[32,128]{1,0:T(8,128)S(1)} custom-call(bf16[2048,128]{1,0:T(8,128)(2,1)S(1)} %pad_maximum_fusion.refs_0_, bf16[2048,128]{1,0:T(8,128)(2,1)S(1)} %collective-permute-done.7.refs_0_.refs_1_, bf16[832,128]{1,0:T(8,128)(2,1)S(1)} %collective-permute-done.3.refs_2_, bf16[832,128]{1,0:T(8,128)(2,1)S(1)} %collective-permute-done.8.refs_3_, ...), custom_call_target="tpu_custom_call" | custom-call | flops 1000 | bytes 1000 | tf_op jit(solution)/shard_map/score_2_2/pallas_call | solution.py:199
  52.5 3.4 %collective-permute-done.10.refs_3_ = bf16[832,128]{1,0:T(8,128)(2,1)S(1)} collective-permute-done((bf16[832,128]{1,0:T(8,128)(2,1)S(1)}, bf16[832,128]{1,0:T(8,128)(2,1)S(1)}, u32[]{:S(2)}, u32[]{:S(2)}) %collective-permute-start.10) | collective-permute-done | bytes 213024 | tf_op jit(solution)/shard_map/ppermute | solution.py:261
  55.9 0.0 collective-permute-start.11
  55.9 3.7 %score_2_2.3.refs_3_ = f32[32,128]{1,0:T(8,128)S(1)} custom-call(bf16[2048,128]{1,0:T(8,128)(2,1)S(1)} %pad_maximum_fusion.refs_0_, bf16[2048,128]{1,0:T(8,128)(2,1)S(1)} %collective-permute-done.7.refs_0_.refs_1_, bf16[832,128]{1,0:T(8,128)(2,1)S(1)} %collective-permute-done.9.refs_2_, bf16[832,128]{1,0:T(8,128)(2,1)S(1)} %collective-permute-done.10.refs_3_, ...), custom_call_target="tpu_custom_call" | custom-call | flops 1000 | bytes 1000 | tf_op jit(solution)/shard_map/score_2_2/pallas_call | solution.py:199
  59.6 3.4 %collective-permute-done.11.refs_2_ = bf16[832,128]{1,0:T(8,128)(2,1)S(1)} collective-permute-done((bf16[832,128]{1,0:T(8,128)(2,1)S(1)}, bf16[832,128]{1,0:T(8,128)(2,1)S(1)}, u32[]{:S(2)}, u32[]{:S(2)}) %collective-permute-start.11) | collective-permute-done | bytes 213024 | tf_op jit(solution)/shard_map/ppermute | solution.py:261
  63.0 2.0 %score_2_1.1 = f32[32,128]{1,0:T(8,128)S(1)} custom-call(bf16[2048,128]{1,0:T(8,128)(2,1)S(1)} %pad_maximum_fusion.refs_0_, bf16[2048,128]{1,0:T(8,128)(2,1)S(1)} %collective-permute-done.7.refs_0_.refs_1_, bf16[832,128]{1,0:T(8,128)(2,1)S(1)} %collective-permute-done.11.refs_2_, f32[32,128]{1,0:T(8,128)S(1)} %score_2_2.3.refs_3_), custom_call_target="tpu_custom_call" | custom-call | flops 1000 | bytes 1000 | tf_op jit(solution)/shard_map/score_2_1/pallas_call | solution.py:199
  65.0 0.0 collective-permute-start.12
  65.0 1.2 %collective-permute-done.12 = f32[32,128]{1,0:T(8,128)S(1)} collective-permute-done((f32[32,128]{1,0:T(8,128)S(1)}, f32[32,128]{1,0:T(8,128)S(1)}, u32[]{:S(2)}, u32[]{:S(2)}) %collective-permute-start.12) | collective-permute-done | bytes 16416 | tf_op jit(solution)/shard_map/ppermute | solution.py:291
  66.2 0.0 copy-start.1
  66.2 1.2 %collective-permute-start.13 = (f32[32,128]{1,0:T(8,128)S(1)}, f32[32,128]{1,0:T(8,128)S(1)}, u32[]{:S(2)}, u32[]{:S(2)}) collective-permute-start(f32[32,128]{1,0:T(8,128)S(1)} %add.3.refs_0_), channel_id=1, source_target_pairs={{0,8},{8,16},{16,24},{24,0},{1,9},{9,17},{17,25},{25,1},{2,10},{10... | collective-permute-start | bytes 49160 | tf_op jit(solution)/shard_map/ppermute | solution.py:264
  67.4 2.1 %collective-permute-start.14 = (f32[32,128]{1,0:T(8,128)S(1)}, f32[32,128]{1,0:T(8,128)S(1)}, u32[]{:S(2)}, u32[]{:S(2)}) collective-permute-start(f32[32,128]{1,0:T(8,128)S(1)} %add.3.refs_0_), channel_id=1, source_target_pairs={{0,24},{8,0},{16,8},{24,16},{1,25},{9,1},{17,9},{25,17},{2,26},{10... | collective-permute-start | bytes 49160 | tf_op jit(solution)/shard_map/ppermute | solution.py:264
  69.5 0.4 collective-permute-start.15
  69.8 1.3 %collective-permute-done.13.refs_1_ = f32[32,128]{1,0:T(8,128)S(1)} collective-permute-done((f32[32,128]{1,0:T(8,128)S(1)}, f32[32,128]{1,0:T(8,128)S(1)}, u32[]{:S(2)}, u32[]{:S(2)}) %collective-permute-start.13) | collective-permute-done | bytes 16416 | tf_op jit(solution)/shard_map/ppermute | solution.py:264
  71.2 0.0 copy-start.3
  71.2 0.0 collective-permute-done.14.refs_2_
  71.2 0.0 copy-start.4
  71.2 3.5 %collective-permute-done.15.refs_3_ = f32[32,128]{1,0:T(8,128)S(1)} collective-permute-done((f32[32,128]{1,0:T(8,128)S(1)}, f32[32,128]{1,0:T(8,128)S(1)}, u32[]{:S(2)}, u32[]{:S(2)}) %collective-permute-start.15) | collective-permute-done | bytes 16416 | tf_op jit(solution)/shard_map/ppermute | solution.py:264
  74.7 0.0 copy-done.1
  74.7 0.0 copy-done.3
  74.7 0.0 copy-done.4
  74.7 0.0 copy-start.5
  74.7 0.6 copy-done.5
  75.3 1.7 %finish.1 = f32[16,4,32]{2,1,0:T(4,128)} custom-call(f32[32,128]{1,0:T(8,128)} %copy-done.1, f32[32,128]{1,0:T(8,128)} %copy-done.3, f32[32,128]{1,0:T(8,128)} %copy-done.4, f32[32,128]{1,0:T(8,128)} %copy-done.5), custom_call_target="tpu_custom_call" | custom-call | tf_op jit(solution)/shard_map/finish/pallas_call | solution.py:233
  (1 shorter events, 0.0 us)
Async XLA Ops:
  0.7 1.3 %copy-start.2 = (f32[4,512]{1,0:T(4,128)}, f32[4,512]{1,0:T(4,128)S(1)}, u32[]{:S(2)}) copy-start(f32[4,512]{1,0:T(4,128)S(1)} %fusion.near) | copy-start | bytes 24580
  0.7 1.3 %collective-permute-start = (f32[4,512]{1,0:T(4,128)S(1)}, f32[4,512]{1,0:T(4,128)S(1)}, u32[]{:S(2)}, u32[]{:S(2)}) collective-permute-start(f32[4,512]{1,0:T(4,128)S(1)} %fusion.near), channel_id=1, source_target_pairs={{0,32},{32,0},{1,33},{33,1},{2,34},{34,2},{3,35},{35,3},{4,36},{36... | collective-permute-start | bytes 24584 | tf_op jit(solution)/shard_map/ppermute | solution.py:255
  2.0 0.6 copy-start.6
  4.3 9.9 %collective-permute-start.1 = (bf16[832,128]{1,0:T(8,128)(2,1)}, bf16[832,128]{1,0:T(8,128)(2,1)S(1)}, u32[]{:S(2)}, u32[]{:S(2)}) collective-permute-start(bf16[832,128]{1,0:T(8,128)(2,1)} %parcel.1.refs_1_), channel_id=1, source_target_pairs={{0,1},{1,2},{2,3},{3,4},{4,5},{5,6},{6,7},{7,0},{32,39},{33,32},{3... | collective-permute-start | bytes 638984 | tf_op jit(solution)/shard_map/ppermute | solution.py:261
  12.6 24.0 %copy-start = (bf16[832,128]{1,0:T(8,128)(2,1)S(1)}, bf16[832,128]{1,0:T(8,128)(2,1)}, u32[]{:S(2)}) copy-start(bf16[832,128]{1,0:T(8,128)(2,1)} %parcel.1.refs_1_) | copy-start | bytes 638980
  14.2 7.8 %collective-permute-start.2 = (bf16[832,128]{1,0:T(8,128)(2,1)S(1)}, bf16[832,128]{1,0:T(8,128)(2,1)S(1)}, u32[]{:S(2)}, u32[]{:S(2)}) collective-permute-start(bf16[832,128]{1,0:T(8,128)(2,1)S(1)} %collective-permute-done.1.refs_2_), channel_id=1, source_target_pairs={{0,1},{1,2},{2,3},{3,4},{4,5},{5,6},{6,7},{7,0},{32,39},{33,32},{3... | collective-permute-start | bytes 638984 | tf_op jit(solution)/shard_map/ppermute | solution.py:261
  22.0 7.0 %collective-permute-start.4 = (bf16[512,128]{1,0:T(8,128)(2,1)}, bf16[512,128]{1,0:T(8,128)(2,1)S(1)}, u32[]{:S(2)}, u32[]{:S(2)}) collective-permute-start(bf16[512,128]{1,0:T(8,128)(2,1)} %encode_second.1), channel_id=1, source_target_pairs={{0,8},{8,16},{16,24},{24,0},{1,9},{9,17},{17,25},{25,1},{2,10},{10... | collective-permute-start | bytes 393224 | tf_op jit(solution)/shard_map/ppermute | solution.py:264
  23.5 5.5 %collective-permute-start.5 = (bf16[512,128]{1,0:T(8,128)(2,1)}, bf16[512,128]{1,0:T(8,128)(2,1)S(1)}, u32[]{:S(2)}, u32[]{:S(2)}) collective-permute-start(bf16[512,128]{1,0:T(8,128)(2,1)} %encode_second.1), channel_id=1, source_target_pairs={{0,24},{8,0},{16,8},{24,16},{1,25},{9,1},{17,9},{25,17},{2,26},{10... | collective-permute-start | bytes 393224 | tf_op jit(solution)/shard_map/ppermute | solution.py:264
  25.3 8.0 %collective-permute-start.6 = (bf16[512,128]{1,0:T(8,128)(2,1)}, bf16[512,128]{1,0:T(8,128)(2,1)S(1)}, u32[]{:S(2)}, u32[]{:S(2)}) collective-permute-start(bf16[512,128]{1,0:T(8,128)(2,1)} %encode_second.1), channel_id=1, source_target_pairs={{0,16},{8,24},{16,0},{24,8},{1,17},{9,25},{17,1},{25,9},{2,18},{10... | collective-permute-start | bytes 393224 | tf_op jit(solution)/shard_map/ppermute | solution.py:264
  27.1 7.1 %collective-permute-start.3 = (bf16[832,128]{1,0:T(8,128)(2,1)S(1)}, bf16[832,128]{1,0:T(8,128)(2,1)S(1)}, u32[]{:S(2)}, u32[]{:S(2)}) collective-permute-start(bf16[832,128]{1,0:T(8,128)(2,1)S(1)} %collective-permute-done.2.refs_3_), channel_id=1, source_target_pairs={{0,1},{1,2},{2,3},{3,4},{4,5},{5,6},{6,7},{7,0},{32,39},{33,32},{3... | collective-permute-start | bytes 638984 | tf_op jit(solution)/shard_map/ppermute | solution.py:261
  34.2 8.3 %collective-permute-start.7 = (bf16[2048,128]{1,0:T(8,128)(2,1)S(1)}, bf16[2048,128]{1,0:T(8,128)(2,1)S(1)}, u32[]{:S(2)}, u32[]{:S(2)}) collective-permute-start(bf16[2048,128]{1,0:T(8,128)(2,1)S(1)} %pad_maximum_fusion.refs_0_), channel_id=1, source_target_pairs={{0,32},{32,0},{1,33},{33,1},{2,34},{34,2},{3,35},{35,3},{4,36},{36... | collective-permute-start | bytes 1572872 | tf_op jit(solution)/shard_map/ppermute | solution.py:276
  34.7 7.1 %collective-permute-start.8 = (bf16[832,128]{1,0:T(8,128)(2,1)S(1)}, bf16[832,128]{1,0:T(8,128)(2,1)S(1)}, u32[]{:S(2)}, u32[]{:S(2)}) collective-permute-start(bf16[832,128]{1,0:T(8,128)(2,1)S(1)} %collective-permute-done.3.refs_2_), channel_id=1, source_target_pairs={{0,1},{1,2},{2,3},{3,4},{4,5},{5,6},{6,7},{7,0},{32,39},{33,32},{3... | collective-permute-start | bytes 638984 | tf_op jit(solution)/shard_map/ppermute | solution.py:261
  41.8 7.1 %collective-permute-start.9 = (bf16[832,128]{1,0:T(8,128)(2,1)S(1)}, bf16[832,128]{1,0:T(8,128)(2,1)S(1)}, u32[]{:S(2)}, u32[]{:S(2)}) collective-permute-start(bf16[832,128]{1,0:T(8,128)(2,1)S(1)} %collective-permute-done.8.refs_3_), channel_id=1, source_target_pairs={{0,1},{1,2},{2,3},{3,4},{4,5},{5,6},{6,7},{7,0},{32,39},{33,32},{3... | collective-permute-start | bytes 638984 | tf_op jit(solution)/shard_map/ppermute | solution.py:261
  48.9 7.1 %collective-permute-start.10 = (bf16[832,128]{1,0:T(8,128)(2,1)S(1)}, bf16[832,128]{1,0:T(8,128)(2,1)S(1)}, u32[]{:S(2)}, u32[]{:S(2)}) collective-permute-start(bf16[832,128]{1,0:T(8,128)(2,1)S(1)} %collective-permute-done.9.refs_2_), channel_id=1, source_target_pairs={{0,1},{1,2},{2,3},{3,4},{4,5},{5,6},{6,7},{7,0},{32,39},{33,32},{3... | collective-permute-start | bytes 638984 | tf_op jit(solution)/shard_map/ppermute | solution.py:261
  55.9 7.1 %collective-permute-start.11 = (bf16[832,128]{1,0:T(8,128)(2,1)S(1)}, bf16[832,128]{1,0:T(8,128)(2,1)S(1)}, u32[]{:S(2)}, u32[]{:S(2)}) collective-permute-start(bf16[832,128]{1,0:T(8,128)(2,1)S(1)} %collective-permute-done.10.refs_3_), channel_id=1, source_target_pairs={{0,1},{1,2},{2,3},{3,4},{4,5},{5,6},{6,7},{7,0},{32,39},{33,32},{3... | collective-permute-start | bytes 638984 | tf_op jit(solution)/shard_map/ppermute | solution.py:261
  65.0 1.2 %collective-permute-start.12 = (f32[32,128]{1,0:T(8,128)S(1)}, f32[32,128]{1,0:T(8,128)S(1)}, u32[]{:S(2)}, u32[]{:S(2)}) collective-permute-start(f32[32,128]{1,0:T(8,128)S(1)} %score_2_1.1), channel_id=1, source_target_pairs={{0,32},{32,0},{1,33},{33,1},{2,34},{34,2},{3,35},{35,3},{4,36},{36... | collective-permute-start | bytes 49160 | tf_op jit(solution)/shard_map/ppermute | solution.py:291
  66.2 8.5 %copy-start.1 = (f32[32,128]{1,0:T(8,128)}, f32[32,128]{1,0:T(8,128)S(1)}, u32[]{:S(2)}) copy-start(f32[32,128]{1,0:T(8,128)S(1)} %add.3.refs_0_) | copy-start | bytes 49156
  66.2 4.9 %collective-permute-start.13 = (f32[32,128]{1,0:T(8,128)S(1)}, f32[32,128]{1,0:T(8,128)S(1)}, u32[]{:S(2)}, u32[]{:S(2)}) collective-permute-start(f32[32,128]{1,0:T(8,128)S(1)} %add.3.refs_0_), channel_id=1, source_target_pairs={{0,8},{8,16},{16,24},{24,0},{1,9},{9,17},{17,25},{25,1},{2,10},{10... | collective-permute-start | bytes 49160 | tf_op jit(solution)/shard_map/ppermute | solution.py:264
  67.4 3.8 %collective-permute-start.14 = (f32[32,128]{1,0:T(8,128)S(1)}, f32[32,128]{1,0:T(8,128)S(1)}, u32[]{:S(2)}, u32[]{:S(2)}) collective-permute-start(f32[32,128]{1,0:T(8,128)S(1)} %add.3.refs_0_), channel_id=1, source_target_pairs={{0,24},{8,0},{16,8},{24,16},{1,25},{9,1},{17,9},{25,17},{2,26},{10... | collective-permute-start | bytes 49160 | tf_op jit(solution)/shard_map/ppermute | solution.py:264
  69.5 5.2 %collective-permute-start.15 = (f32[32,128]{1,0:T(8,128)S(1)}, f32[32,128]{1,0:T(8,128)S(1)}, u32[]{:S(2)}, u32[]{:S(2)}) collective-permute-start(f32[32,128]{1,0:T(8,128)S(1)} %add.3.refs_0_), channel_id=1, source_target_pairs={{0,16},{8,24},{16,0},{24,8},{1,17},{9,25},{17,1},{25,9},{2,18},{10... | collective-permute-start | bytes 49160 | tf_op jit(solution)/shard_map/ppermute | solution.py:264
  71.2 3.5 %copy-start.3 = (f32[32,128]{1,0:T(8,128)}, f32[32,128]{1,0:T(8,128)S(1)}, u32[]{:S(2)}) copy-start(f32[32,128]{1,0:T(8,128)S(1)} %collective-permute-done.13.refs_1_) | copy-start | bytes 49156
  71.2 3.5 %copy-start.4 = (f32[32,128]{1,0:T(8,128)}, f32[32,128]{1,0:T(8,128)S(1)}, u32[]{:S(2)}) copy-start(f32[32,128]{1,0:T(8,128)S(1)} %collective-permute-done.14.refs_2_) | copy-start | bytes 49156
  74.7 0.6 copy-start.5

commit v4 on v3

--- a/solution.py
+++ b/solution.py
@@ -20,33 +20,20 @@
     return 0.5 * pre * (1.0 + lax.erf(pre * jnp.float32(HALF_ROOT)))
 
 
-def ffn_part(tok, w_in, b_in, w_out, skip):
+FREE = pl.CostEstimate(flops=1000, bytes_accessed=1000, transcendentals=0)
+
+
+def ffn_kernel(tok, w_in, b_in, w_out, b_out, gain, shift, proj, out, acc, turned, *, queries, tokens):
+    step = pl.program_id(0)
     chunk = w_in.shape[1]
-    start = pl.multiple_of((pl.program_id(0) + skip) * chunk, chunk)
+    start = pl.multiple_of(step * chunk, chunk)
     pre = jnp.dot(tok[...], w_in[...], preferred_element_type=jnp.float32) + b_in[pl.ds(start, chunk)][None, :]
     hidden = gelu(pre).astype(jnp.bfloat16)
-    return jnp.dot(hidden, w_out[...], preferred_element_type=jnp.float32)
-
-
-def encode_first(tok, w_in, b_in, w_out, acc):
-    part = ffn_part(tok, w_in, b_in, w_out, 0)
-
-    @pl.when(pl.program_id(0) == 0)
+    part = jnp.dot(hidden, w_out[...], preferred_element_type=jnp.float32)
+
+    @pl.when(step == 0)
     def _():
         acc[...] = part
-
-    @pl.when(pl.program_id(0) > 0)
-    def _():
-        acc[...] += part
-
-
-def encode_second(tok, w_in, b_in, w_out, begun, b_out, gain, shift, proj, out, acc, turned, *, queries, tokens, skip):
-    step = pl.program_id(0)
-    part = ffn_part(tok, w_in, b_in, w_out, skip)
-
-    @pl.when(step == 0)
-    def _():
-        acc[...] = begun[...] + part
 
     @pl.when(step > 0)
     def _():
@@ -57,8 +44,8 @@
         total = acc[...] + b_out[...][None, :] + tok[...].astype(jnp.float32)
         diff = total - jnp.mean(total, axis=-1, keepdims=True)
         spread = jnp.mean(diff * diff, axis=-1, keepdims=True)
-        normed = diff * lax.rsqrt(spread + 1e-5) * gain[...][None, :] + shift[...][None, :]
-        projected = jnp.dot(normed.astype(jnp.bfloat16), proj[...], preferred_element_type=jnp.float32)
+        normed = (diff * lax.rsqrt(spread + 1e-5) * gain[...][None, :] + shift[...][None, :]).astype(jnp.bfloat16)
+        projected = jnp.dot(normed, proj[...], preferred_element_type=jnp.float32)
         scale = lax.rsqrt(jnp.sum(projected * projected, axis=-1, keepdims=True) + 1e-6)
         embeds = projected * scale
         for q in range(queries):
@@ -66,51 +53,32 @@
         out[...] = turned[...].astype(jnp.bfloat16)
 
 
-def whole(a):
-    return pl.BlockSpec(a.shape, lambda j: (0,) * a.ndim)
-
-
-def ffn_specs(tok, w_in, b_in, chunk, skip):
-    width = tok.shape[1]
-    return [
-        whole(tok),
-        pl.BlockSpec((width, chunk), lambda j: (0, j + skip)),
-        whole(b_in),
-        pl.BlockSpec((chunk, width), lambda j: (j + skip, 0)),
-    ]
-
-
-FREE = pl.CostEstimate(flops=1000, bytes_accessed=1000, transcendentals=0)
-
-
-def encode(tok, w_in, b_in, w_out, chunk=768):
-    steps = w_in.shape[1] // chunk // 2
-    return pl.pallas_call(
-        encode_first,
-        grid=(steps,),
-        in_specs=ffn_specs(tok, w_in, b_in, chunk, 0),
-        out_specs=whole(tok),
-        out_shape=jax.ShapeDtypeStruct(tok.shape, jnp.float32),
-        compiler_params=pltpu.CompilerParams(vmem_limit_bytes=60 << 20),
-        cost_estimate=FREE,
-        name="encode_first",
-    )(tok, w_in, b_in, w_out)
-
-
-def encode_rest(tok, w_in, b_in, w_out, begun, b_out, gain, shift, proj, queries, tokens, chunk=768):
+def encode(tok, w_in, b_in, w_out, b_out, gain, shift, proj, queries, tokens, chunk=1024):
     rows, width = tok.shape
-    steps = w_in.shape[1] // chunk // 2
-    return pl.pallas_call(
-        functools.partial(encode_second, queries=queries, tokens=tokens, skip=steps),
-        grid=(steps,),
-        in_specs=ffn_specs(tok, w_in, b_in, chunk, steps) + [whole(a) for a in (begun, b_out, gain, shift, proj)],
+
+    def whole(a):
+        return pl.BlockSpec(a.shape, lambda j: (0,) * a.ndim)
+
+    return pl.pallas_call(
+        functools.partial(ffn_kernel, queries=queries, tokens=tokens),
+        grid=(w_in.shape[1] // chunk,),
+        in_specs=[
+            whole(tok),
+            pl.BlockSpec((width, chunk), lambda j: (0, j)),
+            whole(b_in),
+            pl.BlockSpec((chunk, width), lambda j: (j, 0)),
+            whole(b_out),
+            whole(gain),
+            whole(shift),
+            whole(proj),
+        ],
         out_specs=pl.BlockSpec((rows, proj.shape[1]), lambda j: (0, 0)),
         out_shape=jax.ShapeDtypeStruct((rows, proj.shape[1]), jnp.bfloat16),
         scratch_shapes=[pltpu.VMEM((rows, width), jnp.float32), pltpu.VMEM((rows, proj.shape[1]), jnp.float32)],
         compiler_params=pltpu.CompilerParams(vmem_limit_bytes=60 << 20),
         cost_estimate=FREE,
-        name="encode_second",
-    )(tok, w_in, b_in, w_out, begun, b_out, gain, shift, proj)
+        name="encode",
+    )(tok, w_in, b_in, w_out, b_out, gain, shift, proj)
 
 
 def parcel_kernel(sizes, near, far, tiles, out, *, half):
@@ -158,24 +126,23 @@
     core, x, z = lax.axis_index("core"), lax.axis_index("x"), lax.axis_index("z")
     acc[...] = jnp.zeros_like(acc)
 
-    for step in range(X):
-        for side, queries in zip(sides, blocks):
-            block = queries[step * 512 : (step + 1) * 512, :]
-            source = lax.rem(x + SENDER[step], X)
-            here = lane_group == source + X * (core if side == 0 else 1 - core)
-            for n, parcel in enumerate(parcels):
-                similar = lax.dot_general(
-                    parcel[0:rows, :], block, (((1,), (1,)), ((), ())), preferred_element_type=jnp.float32
-                )
-                sums = []
-                for t in range(tiles):
-                    best = jnp.max(similar[t * length : (t + 1) * length], axis=0, keepdims=True)
-                    sums.append(best[:, 0:128] + best[:, 128:256] + best[:, 256:384] + best[:, 384:512])
-                sums = jnp.concatenate(sums + [jnp.zeros((8 - tiles, 128), jnp.float32)], axis=0)
-                sums = sums + pltpu.roll(sums, 64, 1)
-                sums = sums + pltpu.roll(sums, 32, 1)
-                sums = sums + pltpu.roll(sums, 16, 1)
-                acc[n] = jnp.where(here, sums, acc[n])
+    for (side, step), queries in zip(sides, blocks):
+        block = queries[...]
+        source = lax.rem(x + SENDER[step], X)
+        here = lane_group == source + X * (core if side == 0 else 1 - core)
+        for n, parcel in enumerate(parcels):
+            similar = lax.dot_general(
+                parcel[0:rows, :], block, (((1,), (1,)), ((), ())), preferred_element_type=jnp.float32
+            )
+            sums = []
+            for t in range(tiles):
+                best = jnp.max(similar[t * length : (t + 1) * length], axis=0, keepdims=True)
+                sums.append(best[:, 0:128] + best[:, 128:256] + best[:, 256:384] + best[:, 384:512])
+            sums = jnp.concatenate(sums + [jnp.zeros((8 - tiles, 128), jnp.float32)], axis=0)
+            sums = sums + pltpu.roll(sums, 64, 1)
+            sums = sums + pltpu.roll(sums, 32, 1)
+            sums = sums + pltpu.roll(sums, 16, 1)
+            acc[n] = jnp.where(here, sums, acc[n])
 
     first_tile = core * tiles
     out[...] = refs[s + len(shards)][...] if chained else jnp.zeros_like(out)
@@ -255,40 +222,34 @@
     codes_far = lax.ppermute(codes, "core", turn(CORES, 1))
     own = make_parcel(lengths, codes, codes_far, tiles)
 
-    ways = [(z, (z + 1) % Z) for z in range(Z)] + [(Z + z, Z + (z - 1) % Z) for z in range(Z)]
-
-    def along(a):
+    def along(a, k):
+        ways = [(z, (z + k) % Z) for z in range(Z)] + [(Z + z, Z + (z - k) % Z) for z in range(Z)]
         return lax.ppermute(a, ("core", "z"), ways)
 
     def across(a, k):
         return lax.ppermute(a, "x", turn(X, k))
 
-    first = along(own)
+    def swap(a):
+        return lax.ppermute(a, "core", turn(CORES, 1))
+
+    near = {k: along(own, k) for k in (1, -1, 2, -2)}
     flat, _ = tied(tokens.reshape(queries * query_len, width), own)
-    begun = encode(flat, w_in, b_in, w_out)
-    first, begun = tied(first, begun)
-    second = along(first)
-    embeds = encode_rest(flat, w_in, b_in, w_out, begun, b_out, gain, shift, proj, queries, query_len)
-    second, embeds = tied(second, embeds)
-    third = along(second)
-    mine = jnp.concatenate([embeds] + [across(embeds, k) for k in (1, -1, 2)], axis=0)
-    third, mine = tied(third, mine)
-    other = lax.ppermute(mine, "core", turn(CORES, 1))
-    fourth = along(third)
+    embeds = encode(flat, w_in, b_in, w_out, b_out, gain, shift, proj, queries, query_len)
+    near[1], near[-1], near[2], near[-2], embeds = tied(near[1], near[-1], near[2], near[-2], embeds)
+    near[3], near[-3], near[4] = along(near[2], 1), along(near[-2], -1), along(near[2], 2)
+    mine = [embeds] + [across(embeds, k) for k in (1, -1, 2)]
+    other = [swap(embeds)]
     args = (half, length, queries)
-    found = score({0: mine}, [own, first, second], (0, 1, 2), *args)
-    fourth, found = tied(fourth, found)
-    fifth = along(fourth)
-    found = score({1: other}, [own, first, second], (0, 1, 2), *args, begun=found)
-    fifth, found = tied(fifth, found)
-    sixth = along(fifth)
-    both = {0: mine, 1: other}
-    found = score(both, [third, fourth], (3, 4), *args, begun=found)
-    sixth, found = tied(sixth, found)
-    seventh = along(sixth)
-    found = score(both, [fifth, sixth], (5, 6), *args, begun=found)
-    found = score(both, [seventh], (7,), *args, begun=found)
-    found = found + lax.ppermute(found, "core", turn(CORES, 1))
+    early = ([own, near[1], near[-1], near[2], near[-2]], (0, 1, -1, 2, -2))
+    found = score({(0, 0): embeds, (1, 0): other[0]}, *early, *args)
+    found, mine[1], mine[2], mine[3] = tied(found, mine[1], mine[2], mine[3])
+    other += [swap(a) for a in mine[1:]]
+    found = score({(0, k): mine[k] for k in (1, 2, 3)}, *early, *args, begun=found)
+    found, near[3], near[-3], near[4] = tied(found, near[3], near[-3], near[4])
+    found = score({(1, k): other[k] for k in (1, 2, 3)}, *early, *args, begun=found)
+    every = {(0, k): mine[k] for k in range(4)} | {(1, k): other[k] for k in range(4)}
+    found = score(every, [near[3], near[-3], near[4]], (3, -3, 4), *args, begun=found)
+    found = found + swap(found)
     sources = [found] + [across(found, k) for k in (1, -1, 2)]
     return finish(sources, queries).transpose(0, 2, 1)
 

time: 77.2 us -> 65.4 us (0.85)
  waiting for transfers between devices: 25.7 us -> 7.35 us
  starting transfers between devices: 16.1 us -> 25.6 us
  Pallas kernels: 32.3 us -> 28.4 us
  local copies, waits for them, and re-layouts: 1.21 us -> 3.01 us
  other arithmetic: 1.65 us -> 0.71 us
    ppermute x7, waiting for transfers between devices: 14.2 us -> 0.1 us  [along(): return lax.ppermute(a, ('core', 'z'), ways)]
    ppermute x7, starting transfers between devices: 6.84 us -> 14.7 us  [along(): return lax.ppermute(a, ('core', 'z'), ways)]
    ppermute x6, waiting for transfers between devices: 9.15 us -> 5 us  [across(): return lax.ppermute(a, 'x', turn(X, k))]
    pallas_call x2 -> x1, Pallas kernels: 13.8 us -> 10 us  [encode(): pl.pallas_call(functools.partial(ffn_kernel, queries=queries, tokens=toke...]
    unnamed x14 -> x18, local copies, waits for them, and re-layouts: 1.21 us -> 3.01 us
    ppermute x2 -> x5, starting transfers between devices: 0.55 us -> 1.85 us  [swap(): return lax.ppermute(a, 'core', turn(CORES, 1))]
    concatenate x1 -> x0, other arithmetic: 0.94 us -> none  [shards(): jnp.concatenate([embeds] + [across(embeds, k) for k in (1, -1, 2)], axis=0)]
    pallas_call x5 -> x4, Pallas kernels: 15 us -> 14.8 us  [score(): pl.pallas_call(functools.partial(score_kernel, sides=tuple(blocks), tiles...]
  transfers between devices with their start and end apart: 16 -> 19, of which waited for: 10 -> 6; matrix products, arithmetic and copies ran while one was open for 1% -> 0% of each run, Pallas kernels for 35% -> 24%
where the time goes in v4:
time: 65.4 us; the launch traced here: 65.1 us
  Pallas kernels  28.4 us (43%)
  starting transfers between devices  25.6 us (39%)
  waiting for transfers between devices  7.35 us (11%)
  local copies, waits for them, and re-layouts  3.01 us (5%)
  other arithmetic  0.71 us (1%)
    pallas_call x4, Pallas kernels, score(): pl.pallas_call(functools.partial(score_kernel, sides=tuple(blocks), tiles...  14.8 us
    ppermute x7, starting transfers between devices, along(): return lax.ppermute(a, ('core', 'z'), ways)  14.7 us
    pallas_call x1, Pallas kernels, encode(): pl.pallas_call(functools.partial(ffn_kernel, queries=queries, tokens=toke...  10 us
    ppermute x6, starting transfers between devices, across(): return lax.ppermute(a, 'x', turn(X, k))  8.97 us
    ppermute x6, waiting for transfers between devices, across(): return lax.ppermute(a, 'x', turn(X, k))  5 us
    unnamed x18, local copies, waits for them, and re-layouts  3.01 us
    ppermute x5, starting transfers between devices, swap(): return lax.ppermute(a, 'core', turn(CORES, 1))  1.85 us
    pallas_call x1, Pallas kernels, make_parcel(): pl.pallas_call(functools.partial(parcel_kernel, half=half), in_specs=[pl....  1.79 us
  transfers between devices with their start and end apart: 19, of which 6 were waited for; matrix products, arithmetic and copies ran while one was open for 0% of the time, Pallas kernels for 24%

profile of v4, /device:TPU:16, one launch (start us, length us, event | category | flops | bytes accessed | tf_op | source)
XLA Modules:
  0.0 65.1 jit_solution(14154511638226997126)
XLA Ops:
  0.0 0.7 %fusion.near = f32[4,512]{1,0:T(4,128)S(1)} fusion(s32[512,1,4]{0,2,1:T(4,128)} %param.22, s32[512]{0:T(512)} %bitcast.10), kind=kLoop, calls=%fused_computation.1 | loop fusion | flops 6144 | bytes 18432 | tf_op jit(solution)/shard_map/convert_element_type | solution.py:221
  0.7 0.0 copy-start.4
  0.7 0.1 collective-permute-start
  0.8 1.2 %collective-permute-done.far = f32[4,512]{1,0:T(4,128)S(1)} collective-permute-done((f32[4,512]{1,0:T(4,128)S(1)}, f32[4,512]{1,0:T(4,128)S(1)}, u32[]{:S(2)}, u32[]{:S(2)}) %collective-permute-start) | collective-permute-done | bytes 8224 | tf_op jit(solution)/shard_map/ppermute | solution.py:222
  2.0 0.0 copy-done.4
  2.0 0.0 copy-start.8
  2.0 0.6 copy-done.8
  2.6 1.8 %parcel.1.refs_2_.refs_3_ = bf16[832,128]{1,0:T(8,128)(2,1)} custom-call(s32[12]{0:T(128)} %sizes.1, f32[4,512]{1,0:T(4,128)} %copy-done.4, f32[4,512]{1,0:T(4,128)} %copy-done.8, bf16[12,128,128]{2,1,0:T(8,128)(2,1)} %tiles.1), custom_call_target="tpu_custom_call" | custom-call | tf_op jit(solution)/shard_map/parcel/pallas_call | solution.py:108
  4.3 1.9 %collective-permute-start.1 = (bf16[832,128]{1,0:T(8,128)(2,1)}, bf16[832,128]{1,0:T(8,128)(2,1)S(1)}, u32[]{:S(2)}, u32[]{:S(2)}) collective-permute-start(bf16[832,128]{1,0:T(8,128)(2,1)} %parcel.1.refs_2_.refs_3_), channel_id=1, source_target_pairs={{0,1},{1,2},{2,3},{3,4},{4,5},{5,6},{6,7},{7,0},{32,39},{33,32},{3... | collective-permute-start | bytes 638984 | tf_op jit(solution)/shard_map/ppermute | solution.py:227
  6.3 3.9 %collective-permute-start.2 = (bf16[832,128]{1,0:T(8,128)(2,1)}, bf16[832,128]{1,0:T(8,128)(2,1)S(1)}, u32[]{:S(2)}, u32[]{:S(2)}) collective-permute-start(bf16[832,128]{1,0:T(8,128)(2,1)} %parcel.1.refs_2_.refs_3_), channel_id=1, source_target_pairs={{0,7},{1,0},{2,1},{3,2},{4,3},{5,4},{6,5},{7,6},{32,33},{33,34},{3... | collective-permute-start | bytes 638984 | tf_op jit(solution)/shard_map/ppermute | solution.py:227
  10.2 0.0 collective-permute-start.3
  10.2 4.1 %collective-permute-start.4 = (bf16[832,128]{1,0:T(8,128)(2,1)}, bf16[832,128]{1,0:T(8,128)(2,1)S(1)}, u32[]{:S(2)}, u32[]{:S(2)}) collective-permute-start(bf16[832,128]{1,0:T(8,128)(2,1)} %parcel.1.refs_2_.refs_3_), channel_id=1, source_target_pairs={{0,6},{1,7},{2,0},{3,1},{4,2},{5,3},{6,4},{7,5},{32,34},{33,35},{3... | collective-permute-start | bytes 638984 | tf_op jit(solution)/shard_map/ppermute | solution.py:227
  14.3 0.0 copy-start
  14.3 10.0 %encode.1.refs_0_ = bf16[512,128]{1,0:T(8,128)(2,1)} custom-call(bf16[512,768]{1,0:T(8,128)(2,1)} %bitcast.9, bf16[768,3072]{1,0:T(8,128)(2,1)} %w_in.1, f32[3072]{0:T(1024)} %b_in.1, bf16[3072,768]{1,0:T(8,128)(2,1)} %w_out.1, f32[768]{0:T(1024)} %b_out.1, f32[768]{0:T(1024)} %gain.1, f32[768]{0:T(1024)} %shift.1, bf16[768,128]{1,0:T(8,128)(2,1)} %proj.1), custom_call_target="tpu_custom_call" | custom-call | flops 1000 | bytes 1000 | tf_op jit(solution)/shard_map/encode/pallas_call | solution.py:62
  24.4 0.0 collective-permute-done.1.refs_3_.refs_4_
  24.4 0.0 collective-permute-done.2.refs_4_.refs_5_
  24.4 0.0 collective-permute-done.3.refs_5_.refs_6_
  24.4 0.1 collective-permute-done.4.refs_6_.refs_7_
  24.5 0.0 collective-permute-start.5
  24.5 1.6 %collective-permute-start.6 = (bf16[512,128]{1,0:T(8,128)(2,1)}, bf16[512,128]{1,0:T(8,128)(2,1)S(1)}, u32[]{:S(2)}, u32[]{:S(2)}) collective-permute-start(bf16[512,128]{1,0:T(8,128)(2,1)} %encode.1.refs_0_), channel_id=1, source_target_pairs={{0,8},{8,16},{16,24},{24,0},{1,9},{9,17},{17,25},{25,1},{2,10},{10... | collective-permute-start | bytes 393224 | tf_op jit(solution)/shard_map/ppermute | solution.py:230
  26.1 2.3 %collective-permute-start.12 = (bf16[832,128]{1,0:T(8,128)(2,1)S(1)}, bf16[832,128]{1,0:T(8,128)(2,1)S(1)}, u32[]{:S(2)}, u32[]{:S(2)}) collective-permute-start(bf16[832,128]{1,0:T(8,128)(2,1)S(1)} %collective-permute-done.3.refs_5_.refs_6_), channel_id=1, source_target_pairs={{0,1},{1,2},{2,3},{3,4},{4,5},{5,6},{6,7},{7,0},{32,39},{33,32},{3... | collective-permute-start | bytes 638984 | tf_op jit(solution)/shard_map/ppermute | solution.py:227
  28.4 1.7 %collective-permute-start.7 = (bf16[512,128]{1,0:T(8,128)(2,1)}, bf16[512,128]{1,0:T(8,128)(2,1)S(1)}, u32[]{:S(2)}, u32[]{:S(2)}) collective-permute-start(bf16[512,128]{1,0:T(8,128)(2,1)} %encode.1.refs_0_), channel_id=1, source_target_pairs={{0,24},{8,0},{16,8},{24,16},{1,25},{9,1},{17,9},{25,17},{2,26},{10... | collective-permute-start | bytes 393224 | tf_op jit(solution)/shard_map/ppermute | solution.py:230
  30.2 1.8 %collective-permute-start.8 = (bf16[512,128]{1,0:T(8,128)(2,1)}, bf16[512,128]{1,0:T(8,128)(2,1)S(1)}, u32[]{:S(2)}, u32[]{:S(2)}) collective-permute-start(bf16[512,128]{1,0:T(8,128)(2,1)} %encode.1.refs_0_), channel_id=1, source_target_pairs={{0,16},{8,24},{16,0},{24,8},{1,17},{9,25},{17,1},{25,9},{2,18},{10... | collective-permute-start | bytes 393224 | tf_op jit(solution)/shard_map/ppermute | solution.py:230
  32.0 0.0 collective-permute-done.5.refs_1_.refs_4_
  32.0 1.2 %collective-permute-start.13 = (bf16[832,128]{1,0:T(8,128)(2,1)S(1)}, bf16[832,128]{1,0:T(8,128)(2,1)S(1)}, u32[]{:S(2)}, u32[]{:S(2)}) collective-permute-start(bf16[832,128]{1,0:T(8,128)(2,1)S(1)} %collective-permute-done.4.refs_6_.refs_7_), channel_id=1, source_target_pairs={{0,7},{1,0},{2,1},{3,2},{4,3},{5,4},{6,5},{7,6},{32,33},{33,34},{3... | collective-permute-start | bytes 638984 | tf_op jit(solution)/shard_map/ppermute | solution.py:227
  33.1 0.0 collective-permute-done.6.refs_0_.refs_1_
  33.1 1.2 %collective-permute-start.14 = (bf16[832,128]{1,0:T(8,128)(2,1)S(1)}, bf16[832,128]{1,0:T(8,128)(2,1)S(1)}, u32[]{:S(2)}, u32[]{:S(2)}) collective-permute-start(bf16[832,128]{1,0:T(8,128)(2,1)S(1)} %collective-permute-done.3.refs_5_.refs_6_), channel_id=1, source_target_pairs={{0,2},{1,3},{2,4},{3,5},{4,6},{5,7},{6,0},{7,1},{32,38},{33,39},{3... | collective-permute-start | bytes 638984 | tf_op jit(solution)/shard_map/ppermute | solution.py:227
  34.4 0.0 copy-done
  34.4 0.0 copy-start.1
  34.4 0.9 %copy-done.1 = bf16[512,128]{1,0:T(8,128)(2,1)S(1)} copy-done((bf16[512,128]{1,0:T(8,128)(2,1)S(1)}, bf16[512,128]{1,0:T(8,128)(2,1)}, u32[]{:S(2)}) %copy-start.1) | copy-done | bytes 131096
  35.3 2.4 %score_2_5.1.refs_8_ = f32[32,128]{1,0:T(8,128)S(1)} custom-call(bf16[512,128]{1,0:T(8,128)(2,1)S(1)} %copy-done.1, bf16[512,128]{1,0:T(8,128)(2,1)S(1)} %collective-permute-done.5.refs_1_.refs_4_, bf16[832,128]{1,0:T(8,128)(2,1)S(1)} %copy-done, bf16[832,128]{1,0:T(8,128)(2,1)S(1)} %collective-permute-done.1.refs_3_.refs_4_, ...), custom_call_target="tpu_custom_call" | custom-call | flops 1000 | bytes 1000 | tf_op jit(solution)/shard_map/score_2_5/pallas_call | solution.py:166
  37.7 0.0 collective-permute-done.7.refs_1_.refs_2_
  37.7 0.4 collective-permute-done.8.refs_2_.refs_3_
  38.1 1.1 %collective-permute-start.9 = (bf16[512,128]{1,0:T(8,128)(2,1)S(1)}, bf16[512,128]{1,0:T(8,128)(2,1)S(1)}, u32[]{:S(2)}, u32[]{:S(2)}) collective-permute-start(bf16[512,128]{1,0:T(8,128)(2,1)S(1)} %collective-permute-done.6.refs_0_.refs_1_), channel_id=1, source_target_pairs={{0,32},{32,0},{1,33},{33,1},{2,34},{34,2},{3,35},{35,3},{4,36},{36... | collective-permute-start | bytes 393224 | tf_op jit(solution)/shard_map/ppermute | solution.py:233
  39.2 0.1 collective-permute-start.10
  39.3 0.0 collective-permute-done.12.refs_8_
  39.3 0.4 collective-permute-start.11
  39.7 3.5 %score_3_5.2.refs_8_ = f32[32,128]{1,0:T(8,128)S(1)} custom-call(bf16[512,128]{1,0:T(8,128)(2,1)S(1)} %collective-permute-done.6.refs_0_.refs_1_, bf16[512,128]{1,0:T(8,128)(2,1)S(1)} %collective-permute-done.7.refs_1_.refs_2_, bf16[512,128]{1,0:T(8,128)(2,1)S(1)} %collective-permute-done.8.refs_2_.refs_3_, bf16[832,128]{1,0:T(8,128)(2,1)S(1)} %copy-done, ...), custom_call_target="tpu_custom_call" | custom-call | flops 1000 | bytes 1000 | tf_op jit(solution)/shard_map/score_3_5/pallas_call | solution.py:166
  43.2 0.0 collective-permute-done.13.refs_9_
  43.2 0.0 collective-permute-done.14.refs_10_
  43.2 0.0 collective-permute-done.9.refs_0_.refs_5_
  43.2 0.0 collective-permute-done.10.refs_1_.refs_6_
  43.2 0.0 collective-permute-done.11.refs_2_.refs_7_
  43.2 3.5 %score_3_5.3.refs_11_ = f32[32,128]{1,0:T(8,128)S(1)} custom-call(bf16[512,128]{1,0:T(8,128)(2,1)S(1)} %collective-permute-done.9.refs_0_.refs_5_, bf16[512,128]{1,0:T(8,128)(2,1)S(1)} %collective-permute-done.10.refs_1_.refs_6_, bf16[512,128]{1,0:T(8,128)(2,1)S(1)} %collective-permute-done.11.refs_2_.refs_7_, bf16[832,128]{1,0:T(8,128)(2,1)S(1)} %copy-done, ...), custom_call_target="tpu_custom_call" | custom-call | flops 1000 | bytes 1000 | tf_op jit(solution)/shard_map/score_3_5/pallas_call | solution.py:166
  46.7 0.0 copy-start.2
  46.7 0.9 %copy-done.2 = bf16[512,128]{1,0:T(8,128)(2,1)S(1)} copy-done((bf16[512,128]{1,0:T(8,128)(2,1)S(1)}, bf16[512,128]{1,0:T(8,128)(2,1)}, u32[]{:S(2)}) %copy-start.2) | copy-done | bytes 131096
  47.6 5.5 %score_8_3.1 = f32[32,128]{1,0:T(8,128)S(1)} custom-call(bf16[512,128]{1,0:T(8,128)(2,1)S(1)} %copy-done.2, bf16[512,128]{1,0:T(8,128)(2,1)S(1)} %collective-permute-done.6.refs_0_.refs_1_, bf16[512,128]{1,0:T(8,128)(2,1)S(1)} %collective-permute-done.7.refs_1_.refs_2_, bf16[512,128]{1,0:T(8,128)(2,1)S(1)} %collective-permute-done.8.refs_2_.refs_3_, ...), custom_call_target="tpu_custom_call" | custom-call | flops 1000 | bytes 1000 | tf_op jit(solution)/shard_map/score_8_3/pallas_call | solution.py:166
  53.1 0.2 collective-permute-start.15
  53.3 1.1 %collective-permute-done.15 = f32[32,128]{1,0:T(8,128)S(1)} collective-permute-done((f32[32,128]{1,0:T(8,128)S(1)}, f32[32,128]{1,0:T(8,128)S(1)}, u32[]{:S(2)}, u32[]{:S(2)}) %collective-permute-start.15) | collective-permute-done | bytes 16416 | tf_op jit(solution)/shard_map/ppermute | solution.py:233
  54.4 0.0 copy-start.3
  54.4 0.9 %collective-permute-start.16 = (f32[32,128]{1,0:T(8,128)S(1)}, f32[32,128]{1,0:T(8,128)S(1)}, u32[]{:S(2)}, u32[]{:S(2)}) collective-permute-start(f32[32,128]{1,0:T(8,128)S(1)} %add.3.refs_0_), channel_id=1, source_target_pairs={{0,8},{8,16},{16,24},{24,0},{1,9},{9,17},{17,25},{25,1},{2,10},{10... | collective-permute-start | bytes 49160 | tf_op jit(solution)/shard_map/ppermute | solution.py:230
  55.2 2.4 %collective-permute-start.17 = (f32[32,128]{1,0:T(8,128)S(1)}, f32[32,128]{1,0:T(8,128)S(1)}, u32[]{:S(2)}, u32[]{:S(2)}) collective-permute-start(f32[32,128]{1,0:T(8,128)S(1)} %add.3.refs_0_), channel_id=1, source_target_pairs={{0,24},{8,0},{16,8},{24,16},{1,25},{9,1},{17,9},{25,17},{2,26},{10... | collective-permute-start | bytes 49160 | tf_op jit(solution)/shard_map/ppermute | solution.py:230
  57.6 0.6 collective-permute-start.18
  58.2 1.1 %collective-permute-done.16.refs_1_ = f32[32,128]{1,0:T(8,128)S(1)} collective-permute-done((f32[32,128]{1,0:T(8,128)S(1)}, f32[32,128]{1,0:T(8,128)S(1)}, u32[]{:S(2)}, u32[]{:S(2)}) %collective-permute-start.16) | collective-permute-done | bytes 16416 | tf_op jit(solution)/shard_map/ppermute | solution.py:230
  59.3 0.0 copy-start.5
  59.3 0.0 collective-permute-done.17.refs_2_
  59.3 0.0 copy-start.6
  59.3 3.5 %collective-permute-done.18.refs_3_ = f32[32,128]{1,0:T(8,128)S(1)} collective-permute-done((f32[32,128]{1,0:T(8,128)S(1)}, f32[32,128]{1,0:T(8,128)S(1)}, u32[]{:S(2)}, u32[]{:S(2)}) %collective-permute-start.18) | collective-permute-done | bytes 16416 | tf_op jit(solution)/shard_map/ppermute | solution.py:230
  62.8 0.0 copy-done.3
  62.8 0.0 copy-done.5
  62.9 0.0 copy-done.6
  62.9 0.0 copy-start.7
  62.9 0.6 copy-done.7
  63.5 1.7 %finish.1 = f32[16,4,32]{2,1,0:T(4,128)} custom-call(f32[32,128]{1,0:T(8,128)} %copy-done.3, f32[32,128]{1,0:T(8,128)} %copy-done.5, f32[32,128]{1,0:T(8,128)} %copy-done.6, f32[32,128]{1,0:T(8,128)} %copy-done.7), custom_call_target="tpu_custom_call" | custom-call | tf_op jit(solution)/shard_map/finish/pallas_call | solution.py:200
  (1 shorter events, 0.0 us)
Async XLA Ops:
  0.7 1.3 %copy-start.4 = (f32[4,512]{1,0:T(4,128)}, f32[4,512]{1,0:T(4,128)S(1)}, u32[]{:S(2)}) copy-start(f32[4,512]{1,0:T(4,128)S(1)} %fusion.near) | copy-start | bytes 24580
  0.7 1.3 %collective-permute-start = (f32[4,512]{1,0:T(4,128)S(1)}, f32[4,512]{1,0:T(4,128)S(1)}, u32[]{:S(2)}, u32[]{:S(2)}) collective-permute-start(f32[4,512]{1,0:T(4,128)S(1)} %fusion.near), channel_id=1, source_target_pairs={{0,32},{32,0},{1,33},{33,1},{2,34},{34,2},{3,35},{35,3},{4,36},{36... | collective-permute-start | bytes 24584 | tf_op jit(solution)/shard_map/ppermute | solution.py:222
  2.0 0.6 copy-start.8
  4.3 20.0 %collective-permute-start.1 = (bf16[832,128]{1,0:T(8,128)(2,1)}, bf16[832,128]{1,0:T(8,128)(2,1)S(1)}, u32[]{:S(2)}, u32[]{:S(2)}) collective-permute-start(bf16[832,128]{1,0:T(8,128)(2,1)} %parcel.1.refs_2_.refs_3_), channel_id=1, source_target_pairs={{0,1},{1,2},{2,3},{3,4},{4,5},{5,6},{6,7},{7,0},{32,39},{33,32},{3... | collective-permute-start | bytes 638984 | tf_op jit(solution)/shard_map/ppermute | solution.py:227
  6.3 18.1 %collective-permute-start.2 = (bf16[832,128]{1,0:T(8,128)(2,1)}, bf16[832,128]{1,0:T(8,128)(2,1)S(1)}, u32[]{:S(2)}, u32[]{:S(2)}) collective-permute-start(bf16[832,128]{1,0:T(8,128)(2,1)} %parcel.1.refs_2_.refs_3_), channel_id=1, source_target_pairs={{0,7},{1,0},{2,1},{3,2},{4,3},{5,4},{6,5},{7,6},{32,33},{33,34},{3... | collective-permute-start | bytes 638984 | tf_op jit(solution)/shard_map/ppermute | solution.py:227
  10.2 14.2 %collective-permute-start.3 = (bf16[832,128]{1,0:T(8,128)(2,1)}, bf16[832,128]{1,0:T(8,128)(2,1)S(1)}, u32[]{:S(2)}, u32[]{:S(2)}) collective-permute-start(bf16[832,128]{1,0:T(8,128)(2,1)} %parcel.1.refs_2_.refs_3_), channel_id=1, source_target_pairs={{0,2},{1,3},{2,4},{3,5},{4,6},{5,7},{6,0},{7,1},{32,38},{33,39},{3... | collective-permute-start | bytes 638984 | tf_op jit(solution)/shard_map/ppermute | solution.py:227
  10.2 14.3 %collective-permute-start.4 = (bf16[832,128]{1,0:T(8,128)(2,1)}, bf16[832,128]{1,0:T(8,128)(2,1)S(1)}, u32[]{:S(2)}, u32[]{:S(2)}) collective-permute-start(bf16[832,128]{1,0:T(8,128)(2,1)} %parcel.1.refs_2_.refs_3_), channel_id=1, source_target_pairs={{0,6},{1,7},{2,0},{3,1},{4,2},{5,3},{6,4},{7,5},{32,34},{33,35},{3... | collective-permute-start | bytes 638984 | tf_op jit(solution)/shard_map/ppermute | solution.py:227
  14.3 20.0 %copy-start = (bf16[832,128]{1,0:T(8,128)(2,1)S(1)}, bf16[832,128]{1,0:T(8,128)(2,1)}, u32[]{:S(2)}) copy-start(bf16[832,128]{1,0:T(8,128)(2,1)} %parcel.1.refs_2_.refs_3_) | copy-start | bytes 638980
  24.5 7.5 %collective-permute-start.5 = (bf16[512,128]{1,0:T(8,128)(2,1)}, bf16[512,128]{1,0:T(8,128)(2,1)S(1)}, u32[]{:S(2)}, u32[]{:S(2)}) collective-permute-start(bf16[512,128]{1,0:T(8,128)(2,1)} %encode.1.refs_0_), channel_id=1, source_target_pairs={{0,32},{32,0},{1,33},{33,1},{2,34},{34,2},{3,35},{35,3},{4,36},{36... | collective-permute-start | bytes 393224 | tf_op jit(solution)/shard_map/ppermute | solution.py:233
  24.5 8.6 %collective-permute-start.6 = (bf16[512,128]{1,0:T(8,128)(2,1)}, bf16[512,128]{1,0:T(8,128)(2,1)S(1)}, u32[]{:S(2)}, u32[]{:S(2)}) collective-permute-start(bf16[512,128]{1,0:T(8,128)(2,1)} %encode.1.refs_0_), channel_id=1, source_target_pairs={{0,8},{8,16},{16,24},{24,0},{1,9},{9,17},{17,25},{25,1},{2,10},{10... | collective-permute-start | bytes 393224 | tf_op jit(solution)/shard_map/ppermute | solution.py:230
  26.1 13.2 %collective-permute-start.12 = (bf16[832,128]{1,0:T(8,128)(2,1)S(1)}, bf16[832,128]{1,0:T(8,128)(2,1)S(1)}, u32[]{:S(2)}, u32[]{:S(2)}) collective-permute-start(bf16[832,128]{1,0:T(8,128)(2,1)S(1)} %collective-permute-done.3.refs_5_.refs_6_), channel_id=1, source_target_pairs={{0,1},{1,2},{2,3},{3,4},{4,5},{5,6},{6,7},{7,0},{32,39},{33,32},{3... | collective-permute-start | bytes 638984 | tf_op jit(solution)/shard_map/ppermute | solution.py:227
  28.4 9.3 %collective-permute-start.7 = (bf16[512,128]{1,0:T(8,128)(2,1)}, bf16[512,128]{1,0:T(8,128)(2,1)S(1)}, u32[]{:S(2)}, u32[]{:S(2)}) collective-permute-start(bf16[512,128]{1,0:T(8,128)(2,1)} %encode.1.refs_0_), channel_id=1, source_target_pairs={{0,24},{8,0},{16,8},{24,16},{1,25},{9,1},{17,9},{25,17},{2,26},{10... | collective-permute-start | bytes 393224 | tf_op jit(solution)/shard_map/ppermute | solution.py:230
  30.2 7.9 %collective-permute-start.8 = (bf16[512,128]{1,0:T(8,128)(2,1)}, bf16[512,128]{1,0:T(8,128)(2,1)S(1)}, u32[]{:S(2)}, u32[]{:S(2)}) collective-permute-start(bf16[512,128]{1,0:T(8,128)(2,1)} %encode.1.refs_0_), channel_id=1, source_target_pairs={{0,16},{8,24},{16,0},{24,8},{1,17},{9,25},{17,1},{25,9},{2,18},{10... | collective-permute-start | bytes 393224 | tf_op jit(solution)/shard_map/ppermute | solution.py:230
  32.0 11.2 %collective-permute-start.13 = (bf16[832,128]{1,0:T(8,128)(2,1)S(1)}, bf16[832,128]{1,0:T(8,128)(2,1)S(1)}, u32[]{:S(2)}, u32[]{:S(2)}) collective-permute-start(bf16[832,128]{1,0:T(8,128)(2,1)S(1)} %collective-permute-done.4.refs_6_.refs_7_), channel_id=1, source_target_pairs={{0,7},{1,0},{2,1},{3,2},{4,3},{5,4},{6,5},{7,6},{32,33},{33,34},{3... | collective-permute-start | bytes 638984 | tf_op jit(solution)/shard_map/ppermute | solution.py:227
  33.1 10.0 %collective-permute-start.14 = (bf16[832,128]{1,0:T(8,128)(2,1)S(1)}, bf16[832,128]{1,0:T(8,128)(2,1)S(1)}, u32[]{:S(2)}, u32[]{:S(2)}) collective-permute-start(bf16[832,128]{1,0:T(8,128)(2,1)S(1)} %collective-permute-done.3.refs_5_.refs_6_), channel_id=1, source_target_pairs={{0,2},{1,3},{2,4},{3,5},{4,6},{5,7},{6,0},{7,1},{32,38},{33,39},{3... | collective-permute-start | bytes 638984 | tf_op jit(solution)/shard_map/ppermute | solution.py:227
  34.4 0.9 %copy-start.1 = (bf16[512,128]{1,0:T(8,128)(2,1)S(1)}, bf16[512,128]{1,0:T(8,128)(2,1)}, u32[]{:S(2)}) copy-start(bf16[512,128]{1,0:T(8,128)(2,1)} %encode.1.refs_0_) | copy-start | bytes 393220
  38.1 5.1 %collective-permute-start.9 = (bf16[512,128]{1,0:T(8,128)(2,1)S(1)}, bf16[512,128]{1,0:T(8,128)(2,1)S(1)}, u32[]{:S(2)}, u32[]{:S(2)}) collective-permute-start(bf16[512,128]{1,0:T(8,128)(2,1)S(1)} %collective-permute-done.6.refs_0_.refs_1_), channel_id=1, source_target_pairs={{0,32},{32,0},{1,33},{33,1},{2,34},{34,2},{3,35},{35,3},{4,36},{36... | collective-permute-start | bytes 393224 | tf_op jit(solution)/shard_map/ppermute | solution.py:233
  39.2 4.0 %collective-permute-start.10 = (bf16[512,128]{1,0:T(8,128)(2,1)S(1)}, bf16[512,128]{1,0:T(8,128)(2,1)S(1)}, u32[]{:S(2)}, u32[]{:S(2)}) collective-permute-start(bf16[512,128]{1,0:T(8,128)(2,1)S(1)} %collective-permute-done.7.refs_1_.refs_2_), channel_id=1, source_target_pairs={{0,32},{32,0},{1,33},{33,1},{2,34},{34,2},{3,35},{35,3},{4,36},{36... | collective-permute-start | bytes 393224 | tf_op jit(solution)/shard_map/ppermute | solution.py:233
  39.3 3.9 %collective-permute-start.11 = (bf16[512,128]{1,0:T(8,128)(2,1)S(1)}, bf16[512,128]{1,0:T(8,128)(2,1)S(1)}, u32[]{:S(2)}, u32[]{:S(2)}) collective-permute-start(bf16[512,128]{1,0:T(8,128)(2,1)S(1)} %collective-permute-done.8.refs_2_.refs_3_), channel_id=1, source_target_pairs={{0,32},{32,0},{1,33},{33,1},{2,34},{34,2},{3,35},{35,3},{4,36},{36... | collective-permute-start | bytes 393224 | tf_op jit(solution)/shard_map/ppermute | solution.py:233
  46.7 0.9 %copy-start.2 = (bf16[512,128]{1,0:T(8,128)(2,1)S(1)}, bf16[512,128]{1,0:T(8,128)(2,1)}, u32[]{:S(2)}) copy-start(bf16[512,128]{1,0:T(8,128)(2,1)} %encode.1.refs_0_) | copy-start | bytes 393220
  53.1 1.3 %collective-permute-start.15 = (f32[32,128]{1,0:T(8,128)S(1)}, f32[32,128]{1,0:T(8,128)S(1)}, u32[]{:S(2)}, u32[]{:S(2)}) collective-permute-start(f32[32,128]{1,0:T(8,128)S(1)} %score_8_3.1), channel_id=1, source_target_pairs={{0,32},{32,0},{1,33},{33,1},{2,34},{34,2},{3,35},{35,3},{4,36},{36... | collective-permute-start | bytes 49160 | tf_op jit(solution)/shard_map/ppermute | solution.py:233
  54.4 8.5 %copy-start.3 = (f32[32,128]{1,0:T(8,128)}, f32[32,128]{1,0:T(8,128)S(1)}, u32[]{:S(2)}) copy-start(f32[32,128]{1,0:T(8,128)S(1)} %add.3.refs_0_) | copy-start | bytes 49156
  54.4 4.9 %collective-permute-start.16 = (f32[32,128]{1,0:T(8,128)S(1)}, f32[32,128]{1,0:T(8,128)S(1)}, u32[]{:S(2)}, u32[]{:S(2)}) collective-permute-start(f32[32,128]{1,0:T(8,128)S(1)} %add.3.refs_0_), channel_id=1, source_target_pairs={{0,8},{8,16},{16,24},{24,0},{1,9},{9,17},{17,25},{25,1},{2,10},{10... | collective-permute-start | bytes 49160 | tf_op jit(solution)/shard_map/ppermute | solution.py:230
  55.2 4.1 %collective-permute-start.17 = (f32[32,128]{1,0:T(8,128)S(1)}, f32[32,128]{1,0:T(8,128)S(1)}, u32[]{:S(2)}, u32[]{:S(2)}) collective-permute-start(f32[32,128]{1,0:T(8,128)S(1)} %add.3.refs_0_), channel_id=1, source_target_pairs={{0,24},{8,0},{16,8},{24,16},{1,25},{9,1},{17,9},{25,17},{2,26},{10... | collective-permute-start | bytes 49160 | tf_op jit(solution)/shard_map/ppermute | solution.py:230
  57.6 5.2 %collective-permute-start.18 = (f32[32,128]{1,0:T(8,128)S(1)}, f32[32,128]{1,0:T(8,128)S(1)}, u32[]{:S(2)}, u32[]{:S(2)}) collective-permute-start(f32[32,128]{1,0:T(8,128)S(1)} %add.3.refs_0_), channel_id=1, source_target_pairs={{0,16},{8,24},{16,0},{24,8},{1,17},{9,25},{17,1},{25,9},{2,18},{10... | collective-permute-start | bytes 49160 | tf_op jit(solution)/shard_map/ppermute | solution.py:230
  59.3 3.5 %copy-start.5 = (f32[32,128]{1,0:T(8,128)}, f32[32,128]{1,0:T(8,128)S(1)}, u32[]{:S(2)}) copy-start(f32[32,128]{1,0:T(8,128)S(1)} %collective-permute-done.16.refs_1_) | copy-start | bytes 49156
  59.3 3.5 %copy-start.6 = (f32[32,128]{1,0:T(8,128)}, f32[32,128]{1,0:T(8,128)S(1)}, u32[]{:S(2)}) copy-start(f32[32,128]{1,0:T(8,128)S(1)} %collective-permute-done.17.refs_2_) | copy-start | bytes 49156
  62.9 0.6 copy-start.7

commit v5 on v4

v5 whole, which is shorter than its diff:
```python
import functools

import jax
import jax.numpy as jnp
from jax import lax
from jax.experimental import pallas as pl
from jax.experimental.pallas import tpu as pltpu
from jax.sharding import Mesh
from jax.sharding import PartitionSpec as P

Y, CORES, X, Z = 4, 2, 4, 8
HALF_ROOT = 0.7071067811865476


def turn(size, step):
    return [(i, (i + step) % size) for i in range(size)]


def gelu(pre):
    return 0.5 * pre * (1.0 + lax.erf(pre * jnp.float32(HALF_ROOT)))


FREE = pl.CostEstimate(flops=1000, bytes_accessed=1000, transcendentals=0)


def ffn_kernel(tok, w_in, b_in, w_out, b_out, gain, shift, proj, out, again, acc, turned, *, queries, tokens):
    step = pl.program_id(0)
    chunk = w_in.shape[1]
    start = pl.multiple_of(step * chunk, chunk)
    pre = jnp.dot(tok[...], w_in[...], preferred_element_type=jnp.float32) + b_in[pl.ds(start, chunk)][None, :]
    hidden = gelu(pre).astype(jnp.bfloat16)
    part = jnp.dot(hidden, w_out[...], preferred_element_type=jnp.float32)

    @pl.when(step == 0)
    def _():
        acc[...] = part

    @pl.when(step > 0)
    def _():
        acc[...] += part

    @pl.when(step == pl.num_programs(0) - 1)
    def _():
        total = acc[...] + b_out[...][None, :] + tok[...].astype(jnp.float32)
        diff = total - jnp.mean(total, axis=-1, keepdims=True)
        spread = jnp.mean(diff * diff, axis=-1, keepdims=True)
        normed = (diff * lax.rsqrt(spread + 1e-5) * gain[...][None, :] + shift[...][None, :]).astype(jnp.bfloat16)
        projected = jnp.dot(normed, proj[...], preferred_element_type=jnp.float32)
        scale = lax.rsqrt(jnp.sum(projected * projected, axis=-1, keepdims=True) + 1e-6)
        embeds = projected * scale
        for q in range(queries):
            turned[pl.ds(q, tokens, stride=queries), :] = embeds[q * tokens : (q + 1) * tokens, :]
        out[...] = turned[...].astype(jnp.bfloat16)
        again[...] = turned[...].astype(jnp.bfloat16)


def encode(tok, w_in, b_in, w_out, b_out, gain, shift, proj, queries, tokens, chunk=1024):
    rows, width = tok.shape

    def whole(a):
        return pl.BlockSpec(a.shape, lambda j: (0,) * a.ndim)

    return pl.pallas_call(
        functools.partial(ffn_kernel, queries=queries, tokens=tokens),
        grid=(w_in.shape[1] // chunk,),
        in_specs=[
            whole(tok),
            pl.BlockSpec((width, chunk), lambda j: (0, j)),
            whole(b_in),
            pl.BlockSpec((chunk, width), lambda j: (j, 0)),
            whole(b_out),
            whole(gain),
            whole(shift),
            whole(proj),
        ],
        out_specs=[pl.BlockSpec((rows, proj.shape[1]), lambda j: (0, 0))] * 2,
        out_shape=[jax.ShapeDtypeStruct((rows, proj.shape[1]), jnp.bfloat16)] * 2,
        scratch_shapes=[pltpu.VMEM((rows, width), jnp.float32), pltpu.VMEM((rows, proj.shape[1]), jnp.float32)],
        compiler_params=pltpu.CompilerParams(vmem_limit_bytes=60 << 20),
        cost_estimate=FREE,
        name="encode",
    )(tok, w_in, b_in, w_out, b_out, gain, shift, proj)


def parcel_kernel(sizes, slots, counts, tiles, out, *, half):
    count, length = tiles.shape[:2]
    core = lax.axis_index("core")
    column = lax.broadcasted_iota(jnp.int32, tiles.shape[1:], 0)
    for t in range(half):
        tile = tiles[core * half + t].astype(jnp.float32)
        size = sizes[core * half + t]
        out[t * length : (t + 1) * length, :] = jnp.where(column < size, tile, tile[0:1, :]).astype(jnp.bfloat16)
    order = lax.broadcasted_iota(jnp.int32, slots.shape, 0)
    codes = jnp.where(order < counts[...], slots[...], count).astype(jnp.float32)
    lines = []
    for x in range(X):
        lines += [codes[:, x * 128 : (x + 1) * 128], jnp.zeros((4, 128), jnp.float32)]
    out[half * length : half * length + 8 * X, :] = jnp.concatenate(lines, axis=0).astype(jnp.bfloat16)


VM = pl.BlockSpec(memory_space=pltpu.VMEM)


def make_parcel(sizes, slots, counts, tiles):
    count, length, dims = tiles.shape
    half = count // CORES
    return pl.pallas_call(
        functools.partial(parcel_kernel, half=half),
        in_specs=[pl.BlockSpec(memory_space=pltpu.SMEM), VM, VM, VM],
        out_specs=VM,
        out_shape=jax.ShapeDtypeStruct((half * length + 8 * X, dims), jnp.bfloat16),
        name="parcel",
    )(sizes, slots, counts, tiles)


SENDER = (0, X - 1, 1, 2)


def score_kernel(*refs, senders, items, arrays, tiles, length, group, chained):
    s, n = len(senders), len(items)
    blocks, held, out, acc = refs[:s], refs[s : s + arrays], refs[-2], refs[-1]
    rows = tiles * length
    lane_group = lax.broadcasted_iota(jnp.int32, (8, 128), 1) // group
    row = lax.broadcasted_iota(jnp.int32, (8, 128), 0)
    core, x, z = lax.axis_index("core"), lax.axis_index("x"), lax.axis_index("z")
    acc[...] = jnp.zeros_like(acc)

    for sender, queries in zip(senders, blocks):
        block = queries[...]
        here = lane_group == lax.rem(x + SENDER[sender], X)
        for n, (parcel, *_) in enumerate(items):
            similar = lax.dot_general(
                held[parcel][0:rows, :], block, (((1,), (1,)), ((), ())), preferred_element_type=jnp.float32
            )
            sums = []
            for t in range(tiles):
                best = jnp.max(similar[t * length : (t + 1) * length], axis=0, keepdims=True)
                sums.append(best[:, 0:128] + best[:, 128:256] + best[:, 256:384] + best[:, 384:512])
            sums = jnp.concatenate(sums + [jnp.zeros((8 - tiles, 128), jnp.float32)], axis=0)
            sums = sums + pltpu.roll(sums, 64, 1)
            sums = sums + pltpu.roll(sums, 32, 1)
            sums = sums + pltpu.roll(sums, 16, 1)
            acc[n] = jnp.where(here, sums, acc[n])

    out[...] = refs[s + arrays][...] if chained else jnp.zeros_like(out)
    way = 2 * core - 1
    for n, (_, label, steps, far) in enumerate(items):
        codes = held[label][rows : rows + 8 * X, :].astype(jnp.float32)
        code = jnp.full((8, 128), -1.0, jnp.float32)
        for d in range(X):
            turned = pltpu.roll(codes[d * 8 : d * 8 + 8], lax.rem((d - z) * group + 128, 128), 1)
            code = jnp.where(lane_group == d, turned, code)
        code = code.astype(jnp.int32) - tiles * (1 - core if far else core)
        shard = lax.rem(z + steps * way + Z, Z)
        for c in range(4):
            picked = (code[c : c + 1] == row) & (row < tiles)
            line = jnp.sum(jnp.where(picked, acc[n], 0.0), axis=0, keepdims=True)
            out[pl.ds(c * Z + shard, 1), :] += line


def score(blocks, items, tiles, length, group, begun=None):
    held = []

    def at(array):
        for i, one in enumerate(held):
            if one is array:
                return i
        held.append(array)
        return len(held) - 1

    plan = tuple((at(parcel), at(label), steps, far) for parcel, label, steps, far in items)
    more = [] if begun is None else [begun]
    return pl.pallas_call(
        functools.partial(
            score_kernel,
            senders=tuple(blocks),
            items=plan,
            arrays=len(held),
            tiles=tiles,
            length=length,
            group=group,
            chained=begun is not None,
        ),
        in_specs=[VM] * (len(blocks) + len(held) + len(more)),
        out_specs=VM,
        out_shape=jax.ShapeDtypeStruct((4 * Z, 128), jnp.float32),
        scratch_shapes=[pltpu.VMEM((len(plan), 8, 128), jnp.float32)],
        compiler_params=pltpu.CompilerParams(vmem_limit_bytes=32 << 20),
        cost_estimate=FREE,
        name=f"score_{len(blocks)}_{len(plan)}",
    )(*blocks.values(), *held, *more)


def finish_kernel(*refs, group):
    sources, out, table = refs[:4], refs[4], refs[5]
    x = lax.axis_index("x")
    for sender, source in zip(SENDER, sources):
        lines = pltpu.roll(source[...], lax.rem(128 - x * group, 128), 1)
        shard = lax.rem(x + sender, X) * Z
        for c in range(4):
            table[pl.ds(pl.multiple_of(c * X * Z + shard, Z), Z), :] = lines[c * Z : (c + 1) * Z]
    turned = table[...].T
    for c in range(4):
        out[:, c, :] = turned[0:group, c * X * Z : (c + 1) * X * Z]


def finish(sources, group):
    return pl.pallas_call(
        functools.partial(finish_kernel, group=group),
        in_specs=[VM] * 4,
        out_specs=VM,
        out_shape=jax.ShapeDtypeStruct((group, 4, X * Z), jnp.float32),
        scratch_shapes=[pltpu.VMEM((128, 128), jnp.float32)],
        name="finish",
    )(*sources)


def tied(*arrays):
    return lax.optimization_barrier(arrays)


def shards(tokens, w_in, b_in, w_out, b_out, gain, shift, proj, tiles, lengths, slots, counts):
    queries, query_len, width = tokens.shape
    count, length, dims = tiles.shape
    half = count // CORES
    own = make_parcel(lengths, slots.transpose(1, 2, 0)[0], counts.transpose(1, 0), tiles)

    def along(a, k):
        ways = [(z, (z + k) % Z) for z in range(Z)] + [(Z + z, Z + (z - k) % Z) for z in range(Z)]
        return lax.ppermute(a, ("core", "z"), ways)

    def across(a, k):
        return lax.ppermute(a, "x", turn(X, k))

    def swap(a):
        return lax.ppermute(a, "core", turn(CORES, 1))

    near = {0: own} | {k: along(own, k) for k in (1, -1, 2, -2)}
    far = {0: swap(own)}
    flat, _ = tied(tokens.reshape(queries * query_len, width), own)
    embeds, embeds_here = encode(flat, w_in, b_in, w_out, b_out, gain, shift, proj, queries, query_len)
    near[1], near[-1], near[2], near[-2], far[0], embeds = tied(near[1], near[-1], near[2], near[-2], far[0], embeds)
    near[3], near[-3], near[4] = along(near[2], 1), along(near[-2], -1), along(near[2], 2)
    blocks = {0: embeds_here} | {i: across(embeds, k) for i, k in ((1, 1), (2, -1), (3, 2))}
    far |= {k: swap(near[k]) for k in (1, -1, 2, -2)}
    args = (half, length, queries)

    def mine(*ks):
        return [(near[k], near[k], k, False) for k in ks]

    def others(*ks):
        return [(far[k], near[k if k == 4 else -k], -k, True) for k in ks]

    found = score({0: blocks[0]}, mine(0, 1, -1, 2, -2) + others(0), *args)
    found, blocks[1], blocks[2], blocks[3] = tied(found, blocks[1], blocks[2], blocks[3])
    three = {i: blocks[i] for i in (1, 2, 3)}
    found = score(three, mine(0, 1, -1, 2, -2) + others(0), *args, begun=found)
    found, near[3], near[-3], near[4] = tied(found, near[3], near[-3], near[4])
    far |= {k: swap(near[k]) for k in (3, -3, 4)}
    found = score(blocks, others(1, -1, 2, -2), *args, begun=found)
    found = score(blocks, mine(3, -3, 4) + others(3, -3, 4), *args, begun=found)
    sources = [found] + [across(found, k) for k in (1, -1, 2)]
    return finish(sources, queries).transpose(0, 2, 1)


def solution(mesh):
    fine = Mesh(mesh.devices.reshape(Y, CORES, X, Z), ("y", "core", "x", "z"))
    group, shard = ("y", "core"), ("x", "z")
    placed = (P(group + shard),) + (P(),) * 7 + (P(shard), P(shard), P(group, shard), P(group, shard))
    return jax.shard_map(shards, mesh=fine, in_specs=placed, out_specs=P(group + shard), check_vma=False)
```

time: 65.4 us -> 62.8 us (0.960)
  starting transfers between devices: 25.6 us -> 24.1 us
  other arithmetic: 0.71 us -> 0 us
    ppermute x6, waiting for transfers between devices: 5 us -> 6.48 us  [across(): return lax.ppermute(a, 'x', turn(X, k))]
    ppermute x1 -> x0, waiting for transfers between devices: 1.16 us -> none  [shards(): codes_far = lax.ppermute(codes, 'core', turn(CORES, 1))]
    ppermute x7, starting transfers between devices: 14.7 us -> 13.6 us  [along(): return lax.ppermute(a, ('core', 'z'), ways)]
    ppermute x7, waiting for transfers between devices: 0.1 us -> 0.84 us  [along(): return lax.ppermute(a, ('core', 'z'), ways)]
    convert_element_type x1 -> x0, other arithmetic: 0.7 us -> none  [shards(): codes = jnp.where(valid, wanted, count).astype(jnp.float32)]
    unnamed x18 -> x16, local copies, waits for them, and re-layouts: 3.01 us -> 2.42 us
    ppermute x5 -> x8, starting transfers between devices: 1.85 us -> 1.63 us  [swap(): return lax.ppermute(a, 'core', turn(CORES, 1))]
  transfers between devices with their start and end apart: 19 -> 21, of which waited for: 6 -> 9; matrix products, arithmetic and copies ran while one was open for 0% -> 0% of each run, Pallas kernels for 24% -> 31%
where the time goes in v5:
time: 62.8 us; the launch traced here: 62.6 us
  Pallas kernels  28.3 us (45%)
  starting transfers between devices  24.1 us (38%)
  waiting for transfers between devices  7.76 us (12%)
  local copies, waits for them, and re-layouts  2.42 us (4%)
    pallas_call x4, Pallas kernels, score(): pl.pallas_call(functools.partial(score_kernel, senders=tuple(blocks), ite...  14.7 us
    ppermute x7, starting transfers between devices, along(): return lax.ppermute(a, ('core', 'z'), ways)  13.6 us
    pallas_call x1, Pallas kernels, encode(): pl.pallas_call(functools.partial(ffn_kernel, queries=queries, tokens=toke...  10.1 us
    ppermute x6, starting transfers between devices, across(): return lax.ppermute(a, 'x', turn(X, k))  8.9 us
    ppermute x6, waiting for transfers between devices, across(): return lax.ppermute(a, 'x', turn(X, k))  6.48 us
    unnamed x16, local copies, waits for them, and re-layouts  2.42 us
    pallas_call x1, Pallas kernels, make_parcel(): pl.pallas_call(functools.partial(parcel_kernel, half=half), in_specs=[pl....  1.78 us
    pallas_call x1, Pallas kernels, finish(): pl.pallas_call(functools.partial(finish_kernel, group=group), in_specs=[V...  1.69 us
  transfers between devices with their start and end apart: 21, of which 9 were waited for; matrix products, arithmetic and copies ran while one was open for 0% of the time, Pallas kernels for 31%

profile of v5, /device:TPU:16, one launch (start us, length us, event | category | flops | bytes accessed | tf_op | source)
XLA Modules:
  0.0 62.6 jit_solution(9815160121188044901)
XLA Ops:
  0.0 1.8 %parcel.1.refs_1_.refs_3_ = bf16[800,128]{1,0:T(8,128)(2,1)} custom-call(s32[12]{0:T(128)} %sizes.1, s32[4,512]{1,0:T(4,128)} %bitcast.7, s32[1,512]{1,0:T(1,128)} %bitcast.8, bf16[12,128,128]{2,1,0:T(8,128)(2,1)} %tiles.1), custom_call_target="tpu_custom_call" | custom-call | tf_op jit(solution)/shard_map/parcel/pallas_call | solution.py:107
  1.8 0.0 collective-permute-start.4
  1.8 6.3 %collective-permute-start.3 = (bf16[800,128]{1,0:T(8,128)(2,1)}, bf16[800,128]{1,0:T(8,128)(2,1)S(1)}, u32[]{:S(2)}, u32[]{:S(2)}) collective-permute-start(bf16[800,128]{1,0:T(8,128)(2,1)} %parcel.1.refs_1_.refs_3_), channel_id=1, source_target_pairs={{0,6},{1,7},{2,0},{3,1},{4,2},{5,3},{6,4},{7,5},{32,34},{33,35},{3... | collective-permute-start | bytes 614408 | tf_op jit(solution)/shard_map/ppermute | solution.py:230
  8.1 0.0 collective-permute-start.2
  8.1 3.7 %collective-permute-start.1 = (bf16[800,128]{1,0:T(8,128)(2,1)}, bf16[800,128]{1,0:T(8,128)(2,1)S(1)}, u32[]{:S(2)}, u32[]{:S(2)}) collective-permute-start(bf16[800,128]{1,0:T(8,128)(2,1)} %parcel.1.refs_1_.refs_3_), channel_id=1, source_target_pairs={{0,7},{1,0},{2,1},{3,2},{4,3},{5,4},{6,5},{7,6},{32,33},{33,34},{3... | collective-permute-start | bytes 614408 | tf_op jit(solution)/shard_map/ppermute | solution.py:230
  11.8 0.0 collective-permute-start
  11.8 0.0 copy-start
  11.8 10.1 %encode.1 = (bf16[512,128]{1,0:T(8,128)(2,1)}, bf16[512,128]{1,0:T(8,128)(2,1)}) custom-call(bf16[512,768]{1,0:T(8,128)(2,1)} %bitcast.6, bf16[768,3072]{1,0:T(8,128)(2,1)} %w_in.1, f32[3072]{0:T(1024)} %b_in.1, bf16[3072,768]{1,0:T(8,128)(2,1)} %w_out.1, f32[768]{0:T(1024)} %b_out.1, f32[768]{0:T(1024)} %gain.1, f32[768]{0:T(1024)} %shift.1, ...), custom_call_target="tpu_custom_call" | custom-call | flops 1000 | bytes 1000 | tf_op jit(solution)/shard_map/encode/pallas_call | solution.py:63
  21.9 0.0 collective-permute-done.4.refs_6_.refs_8_
  21.9 0.0 collective-permute-done.3.refs_5_.refs_7_.refs_9_
  21.9 0.0 collective-permute-done.2.refs_4_.refs_6_.refs_11_
  21.9 0.3 collective-permute-done.1.refs_3_.refs_5_
  22.2 0.2 collective-permute-done.refs_2_.refs_4_.refs_7_
  22.4 3.0 %collective-permute-start.7 = (bf16[512,128]{1,0:T(8,128)(2,1)}, bf16[512,128]{1,0:T(8,128)(2,1)S(1)}, u32[]{:S(2)}, u32[]{:S(2)}) collective-permute-start(bf16[512,128]{1,0:T(8,128)(2,1)} %get-tuple-element.30), channel_id=1, source_target_pairs={{0,16},{8,24},{16,0},{24,8},{1,17},{9,25},{17,1},{25,9},{2,18},{10... | collective-permute-start | bytes 393224 | tf_op jit(solution)/shard_map/ppermute | solution.py:233
  25.4 1.1 %collective-permute-start.6 = (bf16[512,128]{1,0:T(8,128)(2,1)}, bf16[512,128]{1,0:T(8,128)(2,1)S(1)}, u32[]{:S(2)}, u32[]{:S(2)}) collective-permute-start(bf16[512,128]{1,0:T(8,128)(2,1)} %get-tuple-element.30), channel_id=1, source_target_pairs={{0,24},{8,0},{16,8},{24,16},{1,25},{9,1},{17,9},{25,17},{2,26},{10... | collective-permute-start | bytes 393224 | tf_op jit(solution)/shard_map/ppermute | solution.py:233
  26.5 0.9 %collective-permute-start.5 = (bf16[512,128]{1,0:T(8,128)(2,1)}, bf16[512,128]{1,0:T(8,128)(2,1)S(1)}, u32[]{:S(2)}, u32[]{:S(2)}) collective-permute-start(bf16[512,128]{1,0:T(8,128)(2,1)} %get-tuple-element.30), channel_id=1, source_target_pairs={{0,8},{8,16},{16,24},{24,0},{1,9},{9,17},{17,25},{25,1},{2,10},{10... | collective-permute-start | bytes 393224 | tf_op jit(solution)/shard_map/ppermute | solution.py:233
  27.4 3.4 %collective-permute-start.9 = (bf16[800,128]{1,0:T(8,128)(2,1)S(1)}, bf16[800,128]{1,0:T(8,128)(2,1)S(1)}, u32[]{:S(2)}, u32[]{:S(2)}) collective-permute-start(bf16[800,128]{1,0:T(8,128)(2,1)S(1)} %collective-permute-done.3.refs_5_.refs_7_.refs_9_), channel_id=1, source_target_pairs={{0,7},{1,0},{2,1},{3,2},{4,3},{5,4},{6,5},{7,6},{32,33},{33,34},{3... | collective-permute-start | bytes 614408 | tf_op jit(solution)/shard_map/ppermute | solution.py:230
  30.8 0.0 collective-permute-start.10
  30.8 0.0 collective-permute-done.7.refs_2_.refs_3_
  30.8 0.1 collective-permute-start.8
  31.0 1.1 %collective-permute-done.6.refs_1_.refs_2_ = bf16[512,128]{1,0:T(8,128)(2,1)S(1)} collective-permute-done((bf16[512,128]{1,0:T(8,128)(2,1)}, bf16[512,128]{1,0:T(8,128)(2,1)S(1)}, u32[]{:S(2)}, u32[]{:S(2)}) %collective-permute-start.6) | collective-permute-done | bytes 131104 | tf_op jit(solution)/shard_map/ppermute | solution.py:233
  32.1 0.0 collective-permute-start.14
  32.1 0.8 %collective-permute-done.5.refs_0_.refs_1_ = bf16[512,128]{1,0:T(8,128)(2,1)S(1)} collective-permute-done((bf16[512,128]{1,0:T(8,128)(2,1)}, bf16[512,128]{1,0:T(8,128)(2,1)S(1)}, u32[]{:S(2)}, u32[]{:S(2)}) %collective-permute-start.5) | collective-permute-done | bytes 131104 | tf_op jit(solution)/shard_map/ppermute | solution.py:233
  32.9 0.0 collective-permute-start.15
  32.9 0.0 copy-done
  32.9 0.0 copy-start.1
  32.9 0.9 %copy-done.1 = bf16[512,128]{1,0:T(8,128)(2,1)S(1)} copy-done((bf16[512,128]{1,0:T(8,128)(2,1)S(1)}, bf16[512,128]{1,0:T(8,128)(2,1)}, u32[]{:S(2)}) %copy-start.1) | copy-done | bytes 131096
  33.8 0.0 copy-start.3
  33.8 1.6 %score_1_6.1.refs_9_ = f32[32,128]{1,0:T(8,128)S(1)} custom-call(bf16[512,128]{1,0:T(8,128)(2,1)S(1)} %copy-done.1, bf16[800,128]{1,0:T(8,128)(2,1)S(1)} %copy-done, bf16[800,128]{1,0:T(8,128)(2,1)S(1)} %collective-permute-done.refs_2_.refs_4_.refs_7_, bf16[800,128]{1,0:T(8,128)(2,1)S(1)} %collective-permute-done.1.refs_3_.refs_5_, ...), custom_call_target="tpu_custom_call" | custom-call | flops 1000 | bytes 1000 | tf_op jit(solution)/shard_map/score_1_6/pallas_call | solution.py:173
  35.5 4.1 %score_3_6.1.refs_12_ = f32[32,128]{1,0:T(8,128)S(1)} custom-call(bf16[512,128]{1,0:T(8,128)(2,1)S(1)} %collective-permute-done.5.refs_0_.refs_1_, bf16[512,128]{1,0:T(8,128)(2,1)S(1)} %collective-permute-done.6.refs_1_.refs_2_, bf16[512,128]{1,0:T(8,128)(2,1)S(1)} %collective-permute-done.7.refs_2_.refs_3_, bf16[800,128]{1,0:T(8,128)(2,1)S(1)} %copy-done, ...), custom_call_target="tpu_custom_call" | custom-call | flops 1000 | bytes 1000 | tf_op jit(solution)/shard_map/score_3_6/pallas_call | solution.py:173
  39.5 0.0 collective-permute-done.9.refs_5_
  39.5 0.6 collective-permute-start.17
  40.1 0.4 collective-permute-done.10.refs_6_
  40.5 0.0 collective-permute-start.16
  40.5 0.0 collective-permute-done.8.refs_4_
  40.5 0.5 collective-permute-start.11
  41.0 0.0 collective-permute-done.14.refs_4_
  41.0 0.1 collective-permute-start.12
  41.1 0.0 collective-permute-done.15.refs_6_
  41.1 0.4 collective-permute-start.13
  41.5 0.0 collective-permute-done.17.refs_10_
  41.5 0.4 collective-permute-done.16.refs_8_
  42.0 0.0 copy-start.2
  42.0 0.9 %copy-done.2 = bf16[512,128]{1,0:T(8,128)(2,1)S(1)} copy-done((bf16[512,128]{1,0:T(8,128)(2,1)S(1)}, bf16[512,128]{1,0:T(8,128)(2,1)}, u32[]{:S(2)}) %copy-start.2) | copy-done | bytes 131096
  42.9 3.7 %score_4_4.1.refs_10_ = f32[32,128]{1,0:T(8,128)S(1)} custom-call(bf16[512,128]{1,0:T(8,128)(2,1)S(1)} %copy-done.2, bf16[512,128]{1,0:T(8,128)(2,1)S(1)} %collective-permute-done.5.refs_0_.refs_1_, bf16[512,128]{1,0:T(8,128)(2,1)S(1)} %collective-permute-done.6.refs_1_.refs_2_, bf16[512,128]{1,0:T(8,128)(2,1)S(1)} %collective-permute-done.7.refs_2_.refs_3_, ...), custom_call_target="tpu_custom_call" | custom-call | flops 1000 | bytes 1000 | tf_op jit(solution)/shard_map/score_4_4/pallas_call | solution.py:173
  46.5 0.0 collective-permute-done.11.refs_7_
  46.5 0.0 collective-permute-done.12.refs_8_
  46.6 0.0 collective-permute-done.13.refs_9_
  46.6 0.0 copy-done.3
  46.6 5.3 %score_4_6.1.refs_0_ = f32[32,128]{1,0:T(8,128)S(1)} custom-call(bf16[512,128]{1,0:T(8,128)(2,1)S(1)} %copy-done.3, bf16[512,128]{1,0:T(8,128)(2,1)S(1)} %collective-permute-done.5.refs_0_.refs_1_, bf16[512,128]{1,0:T(8,128)(2,1)S(1)} %collective-permute-done.6.refs_1_.refs_2_, bf16[512,128]{1,0:T(8,128)(2,1)S(1)} %collective-permute-done.7.refs_2_.refs_3_, ...), custom_call_target="tpu_custom_call" | custom-call | flops 1000 | bytes 1000 | tf_op jit(solution)/shard_map/score_4_6/pallas_call | solution.py:173
  51.9 0.0 copy-start.4
  51.9 1.8 %collective-permute-start.20 = (f32[32,128]{1,0:T(8,128)S(1)}, f32[32,128]{1,0:T(8,128)S(1)}, u32[]{:S(2)}, u32[]{:S(2)}) collective-permute-start(f32[32,128]{1,0:T(8,128)S(1)} %score_4_6.1.refs_0_), channel_id=1, source_target_pairs={{0,16},{8,24},{16,0},{24,8},{1,17},{9,25},{17,1},{25,9},{2,18},{10... | collective-permute-start | bytes 49160 | tf_op jit(solution)/shard_map/ppermute | solution.py:233
  53.7 1.6 %collective-permute-start.19 = (f32[32,128]{1,0:T(8,128)S(1)}, f32[32,128]{1,0:T(8,128)S(1)}, u32[]{:S(2)}, u32[]{:S(2)}) collective-permute-start(f32[32,128]{1,0:T(8,128)S(1)} %score_4_6.1.refs_0_), channel_id=1, source_target_pairs={{0,24},{8,0},{16,8},{24,16},{1,25},{9,1},{17,9},{25,17},{2,26},{10... | collective-permute-start | bytes 49160 | tf_op jit(solution)/shard_map/ppermute | solution.py:233
  55.3 0.4 collective-permute-start.18
  55.7 1.5 %collective-permute-done.20.refs_3_ = f32[32,128]{1,0:T(8,128)S(1)} collective-permute-done((f32[32,128]{1,0:T(8,128)S(1)}, f32[32,128]{1,0:T(8,128)S(1)}, u32[]{:S(2)}, u32[]{:S(2)}) %collective-permute-start.20) | collective-permute-done | bytes 16416 | tf_op jit(solution)/shard_map/ppermute | solution.py:233
  57.2 0.0 copy-start.5
  57.2 0.2 collective-permute-done.19.refs_2_
  57.5 2.8 %collective-permute-done.18.refs_1_ = f32[32,128]{1,0:T(8,128)S(1)} collective-permute-done((f32[32,128]{1,0:T(8,128)S(1)}, f32[32,128]{1,0:T(8,128)S(1)}, u32[]{:S(2)}, u32[]{:S(2)}) %collective-permute-start.18) | collective-permute-done | bytes 16416 | tf_op jit(solution)/shard_map/ppermute | solution.py:233
  60.3 0.0 copy-done.4
  60.3 0.0 copy-done.5
  60.3 0.0 copy-done.6
  60.3 0.0 copy-start.7
  60.3 0.6 copy-done.7
  60.9 1.7 %finish.1 = f32[16,4,32]{2,1,0:T(4,128)} custom-call(f32[32,128]{1,0:T(8,128)} %copy-done.4, f32[32,128]{1,0:T(8,128)} %copy-done.7, f32[32,128]{1,0:T(8,128)} %copy-done.6, f32[32,128]{1,0:T(8,128)} %copy-done.5), custom_call_target="tpu_custom_call" | custom-call | tf_op jit(solution)/shard_map/finish/pallas_call | solution.py:208
  (1 shorter events, 0.0 us)
Async XLA Ops:
  1.8 20.1 %collective-permute-start.4 = (bf16[800,128]{1,0:T(8,128)(2,1)}, bf16[800,128]{1,0:T(8,128)(2,1)S(1)}, u32[]{:S(2)}, u32[]{:S(2)}) collective-permute-start(bf16[800,128]{1,0:T(8,128)(2,1)} %parcel.1.refs_1_.refs_3_), channel_id=1, source_target_pairs={{0,32},{32,0},{1,33},{33,1},{2,34},{34,2},{3,35},{35,3},{4,36},{36... | collective-permute-start | bytes 614408 | tf_op jit(solution)/shard_map/ppermute | solution.py:236
  1.8 20.1 %collective-permute-start.3 = (bf16[800,128]{1,0:T(8,128)(2,1)}, bf16[800,128]{1,0:T(8,128)(2,1)S(1)}, u32[]{:S(2)}, u32[]{:S(2)}) collective-permute-start(bf16[800,128]{1,0:T(8,128)(2,1)} %parcel.1.refs_1_.refs_3_), channel_id=1, source_target_pairs={{0,6},{1,7},{2,0},{3,1},{4,2},{5,3},{6,4},{7,5},{32,34},{33,35},{3... | collective-permute-start | bytes 614408 | tf_op jit(solution)/shard_map/ppermute | solution.py:230
  8.1 13.8 %collective-permute-start.2 = (bf16[800,128]{1,0:T(8,128)(2,1)}, bf16[800,128]{1,0:T(8,128)(2,1)S(1)}, u32[]{:S(2)}, u32[]{:S(2)}) collective-permute-start(bf16[800,128]{1,0:T(8,128)(2,1)} %parcel.1.refs_1_.refs_3_), channel_id=1, source_target_pairs={{0,2},{1,3},{2,4},{3,5},{4,6},{5,7},{6,0},{7,1},{32,38},{33,39},{3... | collective-permute-start | bytes 614408 | tf_op jit(solution)/shard_map/ppermute | solution.py:230
  8.1 14.1 %collective-permute-start.1 = (bf16[800,128]{1,0:T(8,128)(2,1)}, bf16[800,128]{1,0:T(8,128)(2,1)S(1)}, u32[]{:S(2)}, u32[]{:S(2)}) collective-permute-start(bf16[800,128]{1,0:T(8,128)(2,1)} %parcel.1.refs_1_.refs_3_), channel_id=1, source_target_pairs={{0,7},{1,0},{2,1},{3,2},{4,3},{5,4},{6,5},{7,6},{32,33},{33,34},{3... | collective-permute-start | bytes 614408 | tf_op jit(solution)/shard_map/ppermute | solution.py:230
  11.8 10.6 %collective-permute-start = (bf16[800,128]{1,0:T(8,128)(2,1)}, bf16[800,128]{1,0:T(8,128)(2,1)S(1)}, u32[]{:S(2)}, u32[]{:S(2)}) collective-permute-start(bf16[800,128]{1,0:T(8,128)(2,1)} %parcel.1.refs_1_.refs_3_), channel_id=1, source_target_pairs={{0,1},{1,2},{2,3},{3,4},{4,5},{5,6},{6,7},{7,0},{32,39},{33,32},{3... | collective-permute-start | bytes 614408 | tf_op jit(solution)/shard_map/ppermute | solution.py:230
  11.8 21.2 %copy-start = (bf16[800,128]{1,0:T(8,128)(2,1)S(1)}, bf16[800,128]{1,0:T(8,128)(2,1)}, u32[]{:S(2)}) copy-start(bf16[800,128]{1,0:T(8,128)(2,1)} %parcel.1.refs_1_.refs_3_) | copy-start | bytes 614404
  22.4 8.5 %collective-permute-start.7 = (bf16[512,128]{1,0:T(8,128)(2,1)}, bf16[512,128]{1,0:T(8,128)(2,1)S(1)}, u32[]{:S(2)}, u32[]{:S(2)}) collective-permute-start(bf16[512,128]{1,0:T(8,128)(2,1)} %get-tuple-element.30), channel_id=1, source_target_pairs={{0,16},{8,24},{16,0},{24,8},{1,17},{9,25},{17,1},{25,9},{2,18},{10... | collective-permute-start | bytes 393224 | tf_op jit(solution)/shard_map/ppermute | solution.py:233
  25.4 6.7 %collective-permute-start.6 = (bf16[512,128]{1,0:T(8,128)(2,1)}, bf16[512,128]{1,0:T(8,128)(2,1)S(1)}, u32[]{:S(2)}, u32[]{:S(2)}) collective-permute-start(bf16[512,128]{1,0:T(8,128)(2,1)} %get-tuple-element.30), channel_id=1, source_target_pairs={{0,24},{8,0},{16,8},{24,16},{1,25},{9,1},{17,9},{25,17},{2,26},{10... | collective-permute-start | bytes 393224 | tf_op jit(solution)/shard_map/ppermute | solution.py:233
  26.5 6.4 %collective-permute-start.5 = (bf16[512,128]{1,0:T(8,128)(2,1)}, bf16[512,128]{1,0:T(8,128)(2,1)S(1)}, u32[]{:S(2)}, u32[]{:S(2)}) collective-permute-start(bf16[512,128]{1,0:T(8,128)(2,1)} %get-tuple-element.30), channel_id=1, source_target_pairs={{0,8},{8,16},{16,24},{24,0},{1,9},{9,17},{17,25},{25,1},{2,10},{10... | collective-permute-start | bytes 393224 | tf_op jit(solution)/shard_map/ppermute | solution.py:233
  27.4 12.1 %collective-permute-start.9 = (bf16[800,128]{1,0:T(8,128)(2,1)S(1)}, bf16[800,128]{1,0:T(8,128)(2,1)S(1)}, u32[]{:S(2)}, u32[]{:S(2)}) collective-permute-start(bf16[800,128]{1,0:T(8,128)(2,1)S(1)} %collective-permute-done.3.refs_5_.refs_7_.refs_9_), channel_id=1, source_target_pairs={{0,7},{1,0},{2,1},{3,2},{4,3},{5,4},{6,5},{7,6},{32,33},{33,34},{3... | collective-permute-start | bytes 614408 | tf_op jit(solution)/shard_map/ppermute | solution.py:230
  30.8 9.7 %collective-permute-start.10 = (bf16[800,128]{1,0:T(8,128)(2,1)S(1)}, bf16[800,128]{1,0:T(8,128)(2,1)S(1)}, u32[]{:S(2)}, u32[]{:S(2)}) collective-permute-start(bf16[800,128]{1,0:T(8,128)(2,1)S(1)} %collective-permute-done.2.refs_4_.refs_6_.refs_11_), channel_id=1, source_target_pairs={{0,2},{1,3},{2,4},{3,5},{4,6},{5,7},{6,0},{7,1},{32,38},{33,39},{3... | collective-permute-start | bytes 614408 | tf_op jit(solution)/shard_map/ppermute | solution.py:230
  30.8 9.7 %collective-permute-start.8 = (bf16[800,128]{1,0:T(8,128)(2,1)S(1)}, bf16[800,128]{1,0:T(8,128)(2,1)S(1)}, u32[]{:S(2)}, u32[]{:S(2)}) collective-permute-start(bf16[800,128]{1,0:T(8,128)(2,1)S(1)} %collective-permute-done.2.refs_4_.refs_6_.refs_11_), channel_id=1, source_target_pairs={{0,1},{1,2},{2,3},{3,4},{4,5},{5,6},{6,7},{7,0},{32,39},{33,32},{3... | collective-permute-start | bytes 614408 | tf_op jit(solution)/shard_map/ppermute | solution.py:230
  32.1 8.9 %collective-permute-start.14 = (bf16[800,128]{1,0:T(8,128)(2,1)S(1)}, bf16[800,128]{1,0:T(8,128)(2,1)S(1)}, u32[]{:S(2)}, u32[]{:S(2)}) collective-permute-start(bf16[800,128]{1,0:T(8,128)(2,1)S(1)} %collective-permute-done.refs_2_.refs_4_.refs_7_), channel_id=1, source_target_pairs={{0,32},{32,0},{1,33},{33,1},{2,34},{34,2},{3,35},{35,3},{4,36},{36... | collective-permute-start | bytes 614408 | tf_op jit(solution)/shard_map/ppermute | solution.py:236
  32.9 8.2 %collective-permute-start.15 = (bf16[800,128]{1,0:T(8,128)(2,1)S(1)}, bf16[800,128]{1,0:T(8,128)(2,1)S(1)}, u32[]{:S(2)}, u32[]{:S(2)}) collective-permute-start(bf16[800,128]{1,0:T(8,128)(2,1)S(1)} %collective-permute-done.1.refs_3_.refs_5_), channel_id=1, source_target_pairs={{0,32},{32,0},{1,33},{33,1},{2,34},{34,2},{3,35},{35,3},{4,36},{36... | collective-permute-start | bytes 614408 | tf_op jit(solution)/shard_map/ppermute | solution.py:236
  32.9 0.9 %copy-start.1 = (bf16[512,128]{1,0:T(8,128)(2,1)S(1)}, bf16[512,128]{1,0:T(8,128)(2,1)}, u32[]{:S(2)}) copy-start(bf16[512,128]{1,0:T(8,128)(2,1)} %get-tuple-element.23.refs_0_) | copy-start | bytes 393220
  33.8 12.7 %copy-start.3 = (bf16[512,128]{1,0:T(8,128)(2,1)S(1)}, bf16[512,128]{1,0:T(8,128)(2,1)}, u32[]{:S(2)}) copy-start(bf16[512,128]{1,0:T(8,128)(2,1)} %get-tuple-element.23.refs_0_) | copy-start | bytes 393220
  39.5 2.0 %collective-permute-start.17 = (bf16[800,128]{1,0:T(8,128)(2,1)S(1)}, bf16[800,128]{1,0:T(8,128)(2,1)S(1)}, u32[]{:S(2)}, u32[]{:S(2)}) collective-permute-start(bf16[800,128]{1,0:T(8,128)(2,1)S(1)} %collective-permute-done.3.refs_5_.refs_7_.refs_9_), channel_id=1, source_target_pairs={{0,32},{32,0},{1,33},{33,1},{2,34},{34,2},{3,35},{35,3},{4,36},{36... | collective-permute-start | bytes 614408 | tf_op jit(solution)/shard_map/ppermute | solution.py:236
  40.5 1.5 %collective-permute-start.16 = (bf16[800,128]{1,0:T(8,128)(2,1)S(1)}, bf16[800,128]{1,0:T(8,128)(2,1)S(1)}, u32[]{:S(2)}, u32[]{:S(2)}) collective-permute-start(bf16[800,128]{1,0:T(8,128)(2,1)S(1)} %collective-permute-done.2.refs_4_.refs_6_.refs_11_), channel_id=1, source_target_pairs={{0,32},{32,0},{1,33},{33,1},{2,34},{34,2},{3,35},{35,3},{4,36},{36... | collective-permute-start | bytes 614408 | tf_op jit(solution)/shard_map/ppermute | solution.py:236
  40.5 6.0 %collective-permute-start.11 = (bf16[800,128]{1,0:T(8,128)(2,1)S(1)}, bf16[800,128]{1,0:T(8,128)(2,1)S(1)}, u32[]{:S(2)}, u32[]{:S(2)}) collective-permute-start(bf16[800,128]{1,0:T(8,128)(2,1)S(1)} %collective-permute-done.8.refs_4_), channel_id=1, source_target_pairs={{0,32},{32,0},{1,33},{33,1},{2,34},{34,2},{3,35},{35,3},{4,36},{36... | collective-permute-start | bytes 614408 | tf_op jit(solution)/shard_map/ppermute | solution.py:236
  41.0 5.5 %collective-permute-start.12 = (bf16[800,128]{1,0:T(8,128)(2,1)S(1)}, bf16[800,128]{1,0:T(8,128)(2,1)S(1)}, u32[]{:S(2)}, u32[]{:S(2)}) collective-permute-start(bf16[800,128]{1,0:T(8,128)(2,1)S(1)} %collective-permute-done.9.refs_5_), channel_id=1, source_target_pairs={{0,32},{32,0},{1,33},{33,1},{2,34},{34,2},{3,35},{35,3},{4,36},{36... | collective-permute-start | bytes 614408 | tf_op jit(solution)/shard_map/ppermute | solution.py:236
  41.1 5.4 %collective-permute-start.13 = (bf16[800,128]{1,0:T(8,128)(2,1)S(1)}, bf16[800,128]{1,0:T(8,128)(2,1)S(1)}, u32[]{:S(2)}, u32[]{:S(2)}) collective-permute-start(bf16[800,128]{1,0:T(8,128)(2,1)S(1)} %collective-permute-done.10.refs_6_), channel_id=1, source_target_pairs={{0,32},{32,0},{1,33},{33,1},{2,34},{34,2},{3,35},{35,3},{4,36},{36... | collective-permute-start | bytes 614408 | tf_op jit(solution)/shard_map/ppermute | solution.py:236
  42.0 0.9 %copy-start.2 = (bf16[512,128]{1,0:T(8,128)(2,1)S(1)}, bf16[512,128]{1,0:T(8,128)(2,1)}, u32[]{:S(2)}) copy-start(bf16[512,128]{1,0:T(8,128)(2,1)} %get-tuple-element.23.refs_0_) | copy-start | bytes 393220
  51.9 8.4 %copy-start.4 = (f32[32,128]{1,0:T(8,128)}, f32[32,128]{1,0:T(8,128)S(1)}, u32[]{:S(2)}) copy-start(f32[32,128]{1,0:T(8,128)S(1)} %score_4_6.1.refs_0_) | copy-start | bytes 49156
  51.9 5.3 %collective-permute-start.20 = (f32[32,128]{1,0:T(8,128)S(1)}, f32[32,128]{1,0:T(8,128)S(1)}, u32[]{:S(2)}, u32[]{:S(2)}) collective-permute-start(f32[32,128]{1,0:T(8,128)S(1)} %score_4_6.1.refs_0_), channel_id=1, source_target_pairs={{0,16},{8,24},{16,0},{24,8},{1,17},{9,25},{17,1},{25,9},{2,18},{10... | collective-permute-start | bytes 49160 | tf_op jit(solution)/shard_map/ppermute | solution.py:233
  53.7 3.7 %collective-permute-start.19 = (f32[32,128]{1,0:T(8,128)S(1)}, f32[32,128]{1,0:T(8,128)S(1)}, u32[]{:S(2)}, u32[]{:S(2)}) collective-permute-start(f32[32,128]{1,0:T(8,128)S(1)} %score_4_6.1.refs_0_), channel_id=1, source_target_pairs={{0,24},{8,0},{16,8},{24,16},{1,25},{9,1},{17,9},{25,17},{2,26},{10... | collective-permute-start | bytes 49160 | tf_op jit(solution)/shard_map/ppermute | solution.py:233
  55.3 4.9 %collective-permute-start.18 = (f32[32,128]{1,0:T(8,128)S(1)}, f32[32,128]{1,0:T(8,128)S(1)}, u32[]{:S(2)}, u32[]{:S(2)}) collective-permute-start(f32[32,128]{1,0:T(8,128)S(1)} %score_4_6.1.refs_0_), channel_id=1, source_target_pairs={{0,8},{8,16},{16,24},{24,0},{1,9},{9,17},{17,25},{25,1},{2,10},{10... | collective-permute-start | bytes 49160 | tf_op jit(solution)/shard_map/ppermute | solution.py:233
  57.2 3.1 %copy-start.5 = (f32[32,128]{1,0:T(8,128)}, f32[32,128]{1,0:T(8,128)S(1)}, u32[]{:S(2)}) copy-start(f32[32,128]{1,0:T(8,128)S(1)} %collective-permute-done.20.refs_3_) | copy-start | bytes 49156
  57.5 2.8 %copy-start.6 = (f32[32,128]{1,0:T(8,128)}, f32[32,128]{1,0:T(8,128)S(1)}, u32[]{:S(2)}) copy-start(f32[32,128]{1,0:T(8,128)S(1)} %collective-permute-done.19.refs_2_) | copy-start | bytes 49156
  60.3 0.6 copy-start.7

commit v6 on v5

--- a/solution.py
+++ b/solution.py
@@ -20,6 +20,7 @@
     return 0.5 * pre * (1.0 + lax.erf(pre * jnp.float32(HALF_ROOT)))
 
 
+VM = pl.BlockSpec(memory_space=pltpu.VMEM)
 FREE = pl.CostEstimate(flops=1000, bytes_accessed=1000, transcendentals=0)
 
 
@@ -73,7 +74,7 @@
             whole(shift),
             whole(proj),
         ],
-        out_specs=[pl.BlockSpec((rows, proj.shape[1]), lambda j: (0, 0))] * 2,
+        out_specs=[pl.BlockSpec((rows, proj.shape[1]), lambda j: (0, 0)), VM],
         out_shape=[jax.ShapeDtypeStruct((rows, proj.shape[1]), jnp.bfloat16)] * 2,
         scratch_shapes=[pltpu.VMEM((rows, width), jnp.float32), pltpu.VMEM((rows, proj.shape[1]), jnp.float32)],
         compiler_params=pltpu.CompilerParams(vmem_limit_bytes=60 << 20),
@@ -96,9 +97,6 @@
     for x in range(X):
         lines += [codes[:, x * 128 : (x + 1) * 128], jnp.zeros((4, 128), jnp.float32)]
     out[half * length : half * length + 8 * X, :] = jnp.concatenate(lines, axis=0).astype(jnp.bfloat16)
-
-
-VM = pl.BlockSpec(memory_space=pltpu.VMEM)
 
 
 def make_parcel(sizes, slots, counts, tiles):
@@ -211,6 +209,7 @@
         out_specs=VM,
         out_shape=jax.ShapeDtypeStruct((group, 4, X * Z), jnp.float32),
         scratch_shapes=[pltpu.VMEM((128, 128), jnp.float32)],
+        compiler_params=pltpu.CompilerParams(vmem_limit_bytes=8 << 20),
         name="finish",
     )(*sources)
 
@@ -240,7 +239,6 @@
     flat, _ = tied(tokens.reshape(queries * query_len, width), own)
     embeds, embeds_here = encode(flat, w_in, b_in, w_out, b_out, gain, shift, proj, queries, query_len)
     near[1], near[-1], near[2], near[-2], far[0], embeds = tied(near[1], near[-1], near[2], near[-2], far[0], embeds)
-    near[3], near[-3], near[4] = along(near[2], 1), along(near[-2], -1), along(near[2], 2)
     blocks = {0: embeds_here} | {i: across(embeds, k) for i, k in ((1, 1), (2, -1), (3, 2))}
     far |= {k: swap(near[k]) for k in (1, -1, 2, -2)}
     args = (half, length, queries)
@@ -252,13 +250,24 @@
         return [(far[k], near[k if k == 4 else -k], -k, True) for k in ks]
 
     found = score({0: blocks[0]}, mine(0, 1, -1, 2, -2) + others(0), *args)
-    found, blocks[1], blocks[2], blocks[3] = tied(found, blocks[1], blocks[2], blocks[3])
+    found, blocks[1], blocks[2], blocks[3], near[2] = tied(found, blocks[1], blocks[2], blocks[3], near[2])
+    near[3] = along(near[2], 1)
     three = {i: blocks[i] for i in (1, 2, 3)}
-    found = score(three, mine(0, 1, -1, 2, -2) + others(0), *args, begun=found)
-    found, near[3], near[-3], near[4] = tied(found, near[3], near[-3], near[4])
-    far |= {k: swap(near[k]) for k in (3, -3, 4)}
+    found = score(three, mine(0, 1, -1), *args, begun=found)
+    found, near[-2] = tied(found, near[-2])
+    near[-3] = along(near[-2], -1)
+    found = score(three, mine(2, -2) + others(0), *args, begun=found)
+    found, near[2], near[3] = tied(found, near[2], near[3])
+    near[4] = along(near[2], 2)
+    far[3] = swap(near[3])
     found = score(blocks, others(1, -1, 2, -2), *args, begun=found)
-    found = score(blocks, mine(3, -3, 4) + others(3, -3, 4), *args, begun=found)
+    found, near[-3] = tied(found, near[-3])
+    far[-3] = swap(near[-3])
+    found = score(blocks, mine(3, -3), *args, begun=found)
+    found, near[4] = tied(found, near[4])
+    far[4] = swap(near[4])
+    found = score(blocks, mine(4) + others(3, -3), *args, begun=found)
+    found = score(blocks, others(4), *args, begun=found)
     sources = [found] + [across(found, k) for k in (1, -1, 2)]
     return finish(sources, queries).transpose(0, 2, 1)
 

time: 62.8 us -> 66.2 us (1.054)
  the two profiles are of different devices: /device:TPU:16 before, /device:TPU:32 now
where the time goes in v6:
time: 66.2 us; the launch traced here: 66.1 us
  Pallas kernels  28.6 us (43%)
  starting transfers between devices  21.9 us (33%)
  waiting for transfers between devices  13.7 us (21%)
  local copies, waits for them, and re-layouts  1.81 us (3%)
    pallas_call x7, Pallas kernels, score(): pl.pallas_call(functools.partial(score_kernel, senders=tuple(blocks), ite...  15.8 us
    ppermute x7, starting transfers between devices, along(): return lax.ppermute(a, ('core', 'z'), ways)  11.5 us
    pallas_call x1, Pallas kernels, encode(): pl.pallas_call(functools.partial(ffn_kernel, queries=queries, tokens=toke...  10.1 us
    ppermute x6, waiting for transfers between devices, across(): return lax.ppermute(a, 'x', turn(X, k))  8.85 us
    ppermute x6, starting transfers between devices, across(): return lax.ppermute(a, 'x', turn(X, k))  8.51 us
    ppermute x7, waiting for transfers between devices, along(): return lax.ppermute(a, ('core', 'z'), ways)  4.86 us
    ppermute x8, starting transfers between devices, swap(): return lax.ppermute(a, 'core', turn(CORES, 1))  1.82 us
    unnamed x6, local copies, waits for them, and re-layouts  1.81 us
  transfers between devices with their start and end apart: 21, of which 7 were waited for; matrix products, arithmetic and copies ran while one was open for 0% of the time, Pallas kernels for 37%

profile of v6, /device:TPU:32, one launch (start us, length us, event | category | flops | bytes accessed | tf_op | source)
XLA Modules:
  0.0 66.1 jit_solution(2614086328437843969)
XLA Ops:
  0.0 1.8 %parcel.1.refs_1_.refs_3_.refs_6_ = bf16[800,128]{1,0:T(8,128)(2,1)} custom-call(s32[12]{0:T(128)} %sizes.1, s32[4,512]{1,0:T(4,128)} %bitcast.7, s32[1,512]{1,0:T(1,128)} %bitcast.8, bf16[12,128,128]{2,1,0:T(8,128)(2,1)} %tiles.1), custom_call_target="tpu_custom_call" | custom-call | tf_op jit(solution)/shard_map/parcel/pallas_call | solution.py:105
  1.8 1.9 %collective-permute-start = (bf16[800,128]{1,0:T(8,128)(2,1)}, bf16[800,128]{1,0:T(8,128)(2,1)S(1)}, u32[]{:S(2)}, u32[]{:S(2)}) collective-permute-start(bf16[800,128]{1,0:T(8,128)(2,1)} %parcel.1.refs_1_.refs_3_.refs_6_), channel_id=1, source_target_pairs={{0,1},{1,2},{2,3},{3,4},{4,5},{5,6},{6,7},{7,0},{32,39},{33,32},{3... | collective-permute-start | bytes 614408 | tf_op jit(solution)/shard_map/ppermute | solution.py:229
  3.7 0.1 collective-permute-start.1
  3.8 4.4 %collective-permute-start.2 = (bf16[800,128]{1,0:T(8,128)(2,1)}, bf16[800,128]{1,0:T(8,128)(2,1)S(1)}, u32[]{:S(2)}, u32[]{:S(2)}) collective-permute-start(bf16[800,128]{1,0:T(8,128)(2,1)} %parcel.1.refs_1_.refs_3_.refs_6_), channel_id=1, source_target_pairs={{0,2},{1,3},{2,4},{3,5},{4,6},{5,7},{6,0},{7,1},{32,38},{33,39},{3... | collective-permute-start | bytes 614408 | tf_op jit(solution)/shard_map/ppermute | solution.py:229
  8.2 1.0 %collective-permute-start.3 = (bf16[800,128]{1,0:T(8,128)(2,1)}, bf16[800,128]{1,0:T(8,128)(2,1)S(1)}, u32[]{:S(2)}, u32[]{:S(2)}) collective-permute-start(bf16[800,128]{1,0:T(8,128)(2,1)} %parcel.1.refs_1_.refs_3_.refs_6_), channel_id=1, source_target_pairs={{0,6},{1,7},{2,0},{3,1},{4,2},{5,3},{6,4},{7,5},{32,34},{33,35},{3... | collective-permute-start | bytes 614408 | tf_op jit(solution)/shard_map/ppermute | solution.py:229
  9.2 0.2 collective-permute-start.4
  9.4 0.0 copy-start
  9.4 10.1 %encode.1 = (bf16[512,128]{1,0:T(8,128)(2,1)}, bf16[512,128]{1,0:T(8,128)(2,1)}) custom-call(bf16[512,768]{1,0:T(8,128)(2,1)} %bitcast.6, bf16[768,3072]{1,0:T(8,128)(2,1)} %w_in.1, f32[3072]{0:T(1024)} %b_in.1, bf16[3072,768]{1,0:T(8,128)(2,1)} %w_out.1, f32[768]{0:T(1024)} %b_out.1, f32[768]{0:T(1024)} %gain.1, f32[768]{0:T(1024)} %shift.1, ...), custom_call_target="tpu_custom_call" | custom-call | flops 1000 | bytes 1000 | tf_op jit(solution)/shard_map/encode/pallas_call | solution.py:64
  19.5 0.0 collective-permute-done.refs_2_.refs_4_.refs_7_
  19.5 0.0 collective-permute-done.1.refs_3_.refs_5_
  19.5 0.7 %collective-permute-done.2.refs_4_.refs_3_.refs_11_ = bf16[800,128]{1,0:T(8,128)(2,1)S(1)} collective-permute-done((bf16[800,128]{1,0:T(8,128)(2,1)}, bf16[800,128]{1,0:T(8,128)(2,1)S(1)}, u32[]{:S(2)}, u32[]{:S(2)}) %collective-permute-start.2) | collective-permute-done | bytes 204832 | tf_op jit(solution)/shard_map/ppermute | solution.py:229
  20.2 0.0 collective-permute-done.3.refs_5_.refs_4_.refs_9_
  20.2 0.0 collective-permute-done.4.refs_6_.refs_5_
  20.2 1.5 %collective-permute-start.5 = (bf16[512,128]{1,0:T(8,128)(2,1)}, bf16[512,128]{1,0:T(8,128)(2,1)S(1)}, u32[]{:S(2)}, u32[]{:S(2)}) collective-permute-start(bf16[512,128]{1,0:T(8,128)(2,1)} %get-tuple-element.36), channel_id=1, source_target_pairs={{0,8},{8,16},{16,24},{24,0},{1,9},{9,17},{17,25},{25,1},{2,10},{10... | collective-permute-start | bytes 393224 | tf_op jit(solution)/shard_map/ppermute | solution.py:232
  21.7 1.7 %collective-permute-start.6 = (bf16[512,128]{1,0:T(8,128)(2,1)}, bf16[512,128]{1,0:T(8,128)(2,1)S(1)}, u32[]{:S(2)}, u32[]{:S(2)}) collective-permute-start(bf16[512,128]{1,0:T(8,128)(2,1)} %get-tuple-element.36), channel_id=1, source_target_pairs={{0,24},{8,0},{16,8},{24,16},{1,25},{9,1},{17,9},{25,17},{2,26},{10... | collective-permute-start | bytes 393224 | tf_op jit(solution)/shard_map/ppermute | solution.py:232
  23.5 1.8 %collective-permute-start.7 = (bf16[512,128]{1,0:T(8,128)(2,1)}, bf16[512,128]{1,0:T(8,128)(2,1)S(1)}, u32[]{:S(2)}, u32[]{:S(2)}) collective-permute-start(bf16[512,128]{1,0:T(8,128)(2,1)} %get-tuple-element.36), channel_id=1, source_target_pairs={{0,16},{8,24},{16,0},{24,8},{1,17},{9,25},{17,1},{25,9},{2,18},{10... | collective-permute-start | bytes 393224 | tf_op jit(solution)/shard_map/ppermute | solution.py:232
  25.3 0.0 copy-done
  25.3 0.0 copy-start.1
  25.3 0.9 %copy-done.1 = bf16[512,128]{1,0:T(8,128)(2,1)S(1)} copy-done((bf16[512,128]{1,0:T(8,128)(2,1)S(1)}, bf16[512,128]{1,0:T(8,128)(2,1)}, u32[]{:S(2)}) %copy-start.1) | copy-done | bytes 131096
  26.2 1.6 %score_1_6.1.refs_6_ = f32[32,128]{1,0:T(8,128)S(1)} custom-call(bf16[512,128]{1,0:T(8,128)(2,1)S(1)} %copy-done.1, bf16[800,128]{1,0:T(8,128)(2,1)S(1)} %copy-done, bf16[800,128]{1,0:T(8,128)(2,1)S(1)} %collective-permute-done.refs_2_.refs_4_.refs_7_, bf16[800,128]{1,0:T(8,128)(2,1)S(1)} %collective-permute-done.1.refs_3_.refs_5_, ...), custom_call_target="tpu_custom_call" | custom-call | flops 1000 | bytes 1000 | tf_op jit(solution)/shard_map/score_1_6/pallas_call | solution.py:171
  27.8 0.0 collective-permute-done.5.refs_0_.refs_1_
  27.8 0.1 collective-permute-done.6.refs_1_.refs_2_
  27.9 3.7 %collective-permute-done.7.refs_2_.refs_3_ = bf16[512,128]{1,0:T(8,128)(2,1)S(1)} collective-permute-done((bf16[512,128]{1,0:T(8,128)(2,1)}, bf16[512,128]{1,0:T(8,128)(2,1)S(1)}, u32[]{:S(2)}, u32[]{:S(2)}) %collective-permute-start.7) | collective-permute-done | bytes 131104 | tf_op jit(solution)/shard_map/ppermute | solution.py:232
  31.6 1.1 %collective-permute-start.8 = (bf16[800,128]{1,0:T(8,128)(2,1)S(1)}, bf16[800,128]{1,0:T(8,128)(2,1)S(1)}, u32[]{:S(2)}, u32[]{:S(2)}) collective-permute-start(bf16[800,128]{1,0:T(8,128)(2,1)S(1)} %collective-permute-done.2.refs_4_.refs_3_.refs_11_), channel_id=1, source_target_pairs={{0,1},{1,2},{2,3},{3,4},{4,5},{5,6},{6,7},{7,0},{32,39},{33,32},{3... | collective-permute-start | bytes 614408 | tf_op jit(solution)/shard_map/ppermute | solution.py:229
  32.8 0.0 collective-permute-start.9
  32.8 0.5 collective-permute-start.10
  33.3 0.0 collective-permute-start.11
  33.3 0.5 collective-permute-start.12
  33.8 2.2 %score_3_3.2.refs_7_ = f32[32,128]{1,0:T(8,128)S(1)} custom-call(bf16[512,128]{1,0:T(8,128)(2,1)S(1)} %collective-permute-done.5.refs_0_.refs_1_, bf16[512,128]{1,0:T(8,128)(2,1)S(1)} %collective-permute-done.6.refs_1_.refs_2_, bf16[512,128]{1,0:T(8,128)(2,1)S(1)} %collective-permute-done.7.refs_2_.refs_3_, bf16[800,128]{1,0:T(8,128)(2,1)S(1)} %copy-done, ...), custom_call_target="tpu_custom_call" | custom-call | flops 1000 | bytes 1000 | tf_op jit(solution)/shard_map/score_3_3/pallas_call | solution.py:171
  36.0 1.4 %collective-permute-done.8.refs_4_.refs_8_ = bf16[800,128]{1,0:T(8,128)(2,1)S(1)} collective-permute-done((bf16[800,128]{1,0:T(8,128)(2,1)S(1)}, bf16[800,128]{1,0:T(8,128)(2,1)S(1)}, u32[]{:S(2)}, u32[]{:S(2)}) %collective-permute-start.8) | collective-permute-done | bytes 204832 | tf_op jit(solution)/shard_map/ppermute | solution.py:229
  37.4 2.8 %collective-permute-start.13 = (bf16[800,128]{1,0:T(8,128)(2,1)S(1)}, bf16[800,128]{1,0:T(8,128)(2,1)S(1)}, u32[]{:S(2)}, u32[]{:S(2)}) collective-permute-start(bf16[800,128]{1,0:T(8,128)(2,1)S(1)} %collective-permute-done.3.refs_5_.refs_4_.refs_9_), channel_id=1, source_target_pairs={{0,7},{1,0},{2,1},{3,2},{4,3},{5,4},{6,5},{7,6},{32,33},{33,34},{3... | collective-permute-start | bytes 614408 | tf_op jit(solution)/shard_map/ppermute | solution.py:229
  40.2 2.2 %score_3_3.3.refs_12_ = f32[32,128]{1,0:T(8,128)S(1)} custom-call(bf16[512,128]{1,0:T(8,128)(2,1)S(1)} %collective-permute-done.5.refs_0_.refs_1_, bf16[512,128]{1,0:T(8,128)(2,1)S(1)} %collective-permute-done.6.refs_1_.refs_2_, bf16[512,128]{1,0:T(8,128)(2,1)S(1)} %collective-permute-done.7.refs_2_.refs_3_, ...), custom_call_target="tpu_custom_call" | custom-call | flops 1000 | bytes 1000 | tf_op jit(solution)/shard_map/score_3_3/pallas_call | solution.py:171
  42.4 0.0 collective-permute-done.9.refs_4_
  42.4 0.1 collective-permute-start.14
  42.6 0.0 collective-permute-done.10.refs_6_
  42.6 0.0 collective-permute-done.11.refs_8_
  42.6 0.0 collective-permute-done.12.refs_10_
  42.6 0.0 copy-start.2
  42.6 0.9 %copy-done.2 = bf16[512,128]{1,0:T(8,128)(2,1)S(1)} copy-done((bf16[512,128]{1,0:T(8,128)(2,1)S(1)}, bf16[512,128]{1,0:T(8,128)(2,1)}, u32[]{:S(2)}) %copy-start.2) | copy-done | bytes 131096
  43.5 3.7 %score_4_4.1.refs_6_ = f32[32,128]{1,0:T(8,128)S(1)} custom-call(bf16[512,128]{1,0:T(8,128)(2,1)S(1)} %copy-done.2, bf16[512,128]{1,0:T(8,128)(2,1)S(1)} %collective-permute-done.5.refs_0_.refs_1_, bf16[512,128]{1,0:T(8,128)(2,1)S(1)} %collective-permute-done.6.refs_1_.refs_2_, bf16[512,128]{1,0:T(8,128)(2,1)S(1)} %collective-permute-done.7.refs_2_.refs_3_, ...), custom_call_target="tpu_custom_call" | custom-call | flops 1000 | bytes 1000 | tf_op jit(solution)/shard_map/score_4_4/pallas_call | solution.py:171
  47.1 0.0 collective-permute-done.13.refs_5_.refs_6_
  47.2 0.1 collective-permute-start.16
  47.3 0.5 collective-permute-start.17
  47.8 2.0 %score_4_2.1.refs_9_ = f32[32,128]{1,0:T(8,128)S(1)} custom-call(bf16[512,128]{1,0:T(8,128)(2,1)S(1)} %copy-done.2, bf16[512,128]{1,0:T(8,128)(2,1)S(1)} %collective-permute-done.5.refs_0_.refs_1_, bf16[512,128]{1,0:T(8,128)(2,1)S(1)} %collective-permute-done.6.refs_1_.refs_2_, bf16[512,128]{1,0:T(8,128)(2,1)S(1)} %collective-permute-done.7.refs_2_.refs_3_, ...), custom_call_target="tpu_custom_call" | custom-call | flops 1000 | bytes 1000 | tf_op jit(solution)/shard_map/score_4_2/pallas_call | solution.py:171
  49.8 2.8 %collective-permute-done.14.refs_4_.refs_5_ = bf16[800,128]{1,0:T(8,128)(2,1)S(1)} collective-permute-done((bf16[800,128]{1,0:T(8,128)(2,1)S(1)}, bf16[800,128]{1,0:T(8,128)(2,1)S(1)}, u32[]{:S(2)}, u32[]{:S(2)}) %collective-permute-start.14) | collective-permute-done | bytes 204832 | tf_op jit(solution)/shard_map/ppermute | solution.py:229
  52.6 0.0 collective-permute-start.15
  52.6 0.0 collective-permute-done.16.refs_5_
  52.6 0.0 collective-permute-done.17.refs_7_
  52.6 2.9 %score_4_3.1.refs_6_ = f32[32,128]{1,0:T(8,128)S(1)} custom-call(bf16[512,128]{1,0:T(8,128)(2,1)S(1)} %copy-done.2, bf16[512,128]{1,0:T(8,128)(2,1)S(1)} %collective-permute-done.5.refs_0_.refs_1_, bf16[512,128]{1,0:T(8,128)(2,1)S(1)} %collective-permute-done.6.refs_1_.refs_2_, bf16[512,128]{1,0:T(8,128)(2,1)S(1)} %collective-permute-done.7.refs_2_.refs_3_, ...), custom_call_target="tpu_custom_call" | custom-call | flops 1000 | bytes 1000 | tf_op jit(solution)/shard_map/score_4_3/pallas_call | solution.py:171
  55.4 0.0 collective-permute-done.15.refs_4_
  55.4 1.2 %score_4_1.1.refs_0_ = f32[32,128]{1,0:T(8,128)S(1)} custom-call(bf16[512,128]{1,0:T(8,128)(2,1)S(1)} %copy-done.2, bf16[512,128]{1,0:T(8,128)(2,1)S(1)} %collective-permute-done.5.refs_0_.refs_1_, bf16[512,128]{1,0:T(8,128)(2,1)S(1)} %collective-permute-done.6.refs_1_.refs_2_, bf16[512,128]{1,0:T(8,128)(2,1)S(1)} %collective-permute-done.7.refs_2_.refs_3_, ...), custom_call_target="tpu_custom_call" | custom-call | flops 1000 | bytes 1000 | tf_op jit(solution)/shard_map/score_4_1/pallas_call | solution.py:171
  56.7 1.2 %collective-permute-start.18 = (f32[32,128]{1,0:T(8,128)S(1)}, f32[32,128]{1,0:T(8,128)S(1)}, u32[]{:S(2)}, u32[]{:S(2)}) collective-permute-start(f32[32,128]{1,0:T(8,128)S(1)} %score_4_1.1.refs_0_), channel_id=1, source_target_pairs={{0,8},{8,16},{16,24},{24,0},{1,9},{9,17},{17,25},{25,1},{2,10},{10... | collective-permute-start | bytes 49160 | tf_op jit(solution)/shard_map/ppermute | solution.py:232
  57.8 2.1 %collective-permute-start.19 = (f32[32,128]{1,0:T(8,128)S(1)}, f32[32,128]{1,0:T(8,128)S(1)}, u32[]{:S(2)}, u32[]{:S(2)}) collective-permute-start(f32[32,128]{1,0:T(8,128)S(1)} %score_4_1.1.refs_0_), channel_id=1, source_target_pairs={{0,24},{8,0},{16,8},{24,16},{1,25},{9,1},{17,9},{25,17},{2,26},{10... | collective-permute-start | bytes 49160 | tf_op jit(solution)/shard_map/ppermute | solution.py:232
  59.9 0.2 collective-permute-start.20
  60.1 1.5 %collective-permute-done.18.refs_1_ = f32[32,128]{1,0:T(8,128)S(1)} collective-permute-done((f32[32,128]{1,0:T(8,128)S(1)}, f32[32,128]{1,0:T(8,128)S(1)}, u32[]{:S(2)}, u32[]{:S(2)}) %collective-permute-start.18) | collective-permute-done | bytes 16416 | tf_op jit(solution)/shard_map/ppermute | solution.py:232
  61.6 0.0 collective-permute-done.19.refs_2_
  61.6 3.5 %collective-permute-done.20.refs_3_ = f32[32,128]{1,0:T(8,128)S(1)} collective-permute-done((f32[32,128]{1,0:T(8,128)S(1)}, f32[32,128]{1,0:T(8,128)S(1)}, u32[]{:S(2)}, u32[]{:S(2)}) %collective-permute-start.20) | collective-permute-done | bytes 16416 | tf_op jit(solution)/shard_map/ppermute | solution.py:232
  65.2 0.9 %finish.1 = f32[16,4,32]{2,1,0:T(4,128)} custom-call(f32[32,128]{1,0:T(8,128)S(1)} %score_4_1.1.refs_0_, f32[32,128]{1,0:T(8,128)S(1)} %collective-permute-done.18.refs_1_, f32[32,128]{1,0:T(8,128)S(1)} %collective-permute-done.19.refs_2_, f32[32,128]{1,0:T(8,128)S(1)} %collective-permute-done.20.refs_3_), custom_call_target="tpu_custom_call" | custom-call | tf_op jit(solution)/shard_map/finish/pallas_call | solution.py:206
Async XLA Ops:
  1.8 17.7 %collective-permute-start = (bf16[800,128]{1,0:T(8,128)(2,1)}, bf16[800,128]{1,0:T(8,128)(2,1)S(1)}, u32[]{:S(2)}, u32[]{:S(2)}) collective-permute-start(bf16[800,128]{1,0:T(8,128)(2,1)} %parcel.1.refs_1_.refs_3_.refs_6_), channel_id=1, source_target_pairs={{0,1},{1,2},{2,3},{3,4},{4,5},{5,6},{6,7},{7,0},{32,39},{33,32},{3... | collective-permute-start | bytes 614408 | tf_op jit(solution)/shard_map/ppermute | solution.py:229
  3.7 15.8 %collective-permute-start.1 = (bf16[800,128]{1,0:T(8,128)(2,1)}, bf16[800,128]{1,0:T(8,128)(2,1)S(1)}, u32[]{:S(2)}, u32[]{:S(2)}) collective-permute-start(bf16[800,128]{1,0:T(8,128)(2,1)} %parcel.1.refs_1_.refs_3_.refs_6_), channel_id=1, source_target_pairs={{0,7},{1,0},{2,1},{3,2},{4,3},{5,4},{6,5},{7,6},{32,33},{33,34},{3... | collective-permute-start | bytes 614408 | tf_op jit(solution)/shard_map/ppermute | solution.py:229
  3.8 16.4 %collective-permute-start.2 = (bf16[800,128]{1,0:T(8,128)(2,1)}, bf16[800,128]{1,0:T(8,128)(2,1)S(1)}, u32[]{:S(2)}, u32[]{:S(2)}) collective-permute-start(bf16[800,128]{1,0:T(8,128)(2,1)} %parcel.1.refs_1_.refs_3_.refs_6_), channel_id=1, source_target_pairs={{0,2},{1,3},{2,4},{3,5},{4,6},{5,7},{6,0},{7,1},{32,38},{33,39},{3... | collective-permute-start | bytes 614408 | tf_op jit(solution)/shard_map/ppermute | solution.py:229
  8.2 12.0 %collective-permute-start.3 = (bf16[800,128]{1,0:T(8,128)(2,1)}, bf16[800,128]{1,0:T(8,128)(2,1)S(1)}, u32[]{:S(2)}, u32[]{:S(2)}) collective-permute-start(bf16[800,128]{1,0:T(8,128)(2,1)} %parcel.1.refs_1_.refs_3_.refs_6_), channel_id=1, source_target_pairs={{0,6},{1,7},{2,0},{3,1},{4,2},{5,3},{6,4},{7,5},{32,34},{33,35},{3... | collective-permute-start | bytes 614408 | tf_op jit(solution)/shard_map/ppermute | solution.py:229
  9.2 11.0 %collective-permute-start.4 = (bf16[800,128]{1,0:T(8,128)(2,1)}, bf16[800,128]{1,0:T(8,128)(2,1)S(1)}, u32[]{:S(2)}, u32[]{:S(2)}) collective-permute-start(bf16[800,128]{1,0:T(8,128)(2,1)} %parcel.1.refs_1_.refs_3_.refs_6_), channel_id=1, source_target_pairs={{0,32},{32,0},{1,33},{33,1},{2,34},{34,2},{3,35},{35,3},{4,36},{36... | collective-permute-start | bytes 614408 | tf_op jit(solution)/shard_map/ppermute | solution.py:235
  9.4 15.9 %copy-start = (bf16[800,128]{1,0:T(8,128)(2,1)S(1)}, bf16[800,128]{1,0:T(8,128)(2,1)}, u32[]{:S(2)}) copy-start(bf16[800,128]{1,0:T(8,128)(2,1)} %parcel.1.refs_1_.refs_3_.refs_6_) | copy-start | bytes 614404
  20.2 7.6 %collective-permute-start.5 = (bf16[512,128]{1,0:T(8,128)(2,1)}, bf16[512,128]{1,0:T(8,128)(2,1)S(1)}, u32[]{:S(2)}, u32[]{:S(2)}) collective-permute-start(bf16[512,128]{1,0:T(8,128)(2,1)} %get-tuple-element.36), channel_id=1, source_target_pairs={{0,8},{8,16},{16,24},{24,0},{1,9},{9,17},{17,25},{25,1},{2,10},{10... | collective-permute-start | bytes 393224 | tf_op jit(solution)/shard_map/ppermute | solution.py:232
  21.7 6.2 %collective-permute-start.6 = (bf16[512,128]{1,0:T(8,128)(2,1)}, bf16[512,128]{1,0:T(8,128)(2,1)S(1)}, u32[]{:S(2)}, u32[]{:S(2)}) collective-permute-start(bf16[512,128]{1,0:T(8,128)(2,1)} %get-tuple-element.36), channel_id=1, source_target_pairs={{0,24},{8,0},{16,8},{24,16},{1,25},{9,1},{17,9},{25,17},{2,26},{10... | collective-permute-start | bytes 393224 | tf_op jit(solution)/shard_map/ppermute | solution.py:232
  23.5 8.2 %collective-permute-start.7 = (bf16[512,128]{1,0:T(8,128)(2,1)}, bf16[512,128]{1,0:T(8,128)(2,1)S(1)}, u32[]{:S(2)}, u32[]{:S(2)}) collective-permute-start(bf16[512,128]{1,0:T(8,128)(2,1)} %get-tuple-element.36), channel_id=1, source_target_pairs={{0,16},{8,24},{16,0},{24,8},{1,17},{9,25},{17,1},{25,9},{2,18},{10... | collective-permute-start | bytes 393224 | tf_op jit(solution)/shard_map/ppermute | solution.py:232
  25.3 0.9 %copy-start.1 = (bf16[512,128]{1,0:T(8,128)(2,1)S(1)}, bf16[512,128]{1,0:T(8,128)(2,1)}, u32[]{:S(2)}) copy-start(bf16[512,128]{1,0:T(8,128)(2,1)} %get-tuple-element.29.refs_0_) | copy-start | bytes 393220
  31.6 5.8 %collective-permute-start.8 = (bf16[800,128]{1,0:T(8,128)(2,1)S(1)}, bf16[800,128]{1,0:T(8,128)(2,1)S(1)}, u32[]{:S(2)}, u32[]{:S(2)}) collective-permute-start(bf16[800,128]{1,0:T(8,128)(2,1)S(1)} %collective-permute-done.2.refs_4_.refs_3_.refs_11_), channel_id=1, source_target_pairs={{0,1},{1,2},{2,3},{3,4},{4,5},{5,6},{6,7},{7,0},{32,39},{33,32},{3... | collective-permute-start | bytes 614408 | tf_op jit(solution)/shard_map/ppermute | solution.py:229
  32.8 9.7 %collective-permute-start.9 = (bf16[800,128]{1,0:T(8,128)(2,1)S(1)}, bf16[800,128]{1,0:T(8,128)(2,1)S(1)}, u32[]{:S(2)}, u32[]{:S(2)}) collective-permute-start(bf16[800,128]{1,0:T(8,128)(2,1)S(1)} %collective-permute-done.refs_2_.refs_4_.refs_7_), channel_id=1, source_target_pairs={{0,32},{32,0},{1,33},{33,1},{2,34},{34,2},{3,35},{35,3},{4,36},{36... | collective-permute-start | bytes 614408 | tf_op jit(solution)/shard_map/ppermute | solution.py:235
  32.8 9.8 %collective-permute-start.10 = (bf16[800,128]{1,0:T(8,128)(2,1)S(1)}, bf16[800,128]{1,0:T(8,128)(2,1)S(1)}, u32[]{:S(2)}, u32[]{:S(2)}) collective-permute-start(bf16[800,128]{1,0:T(8,128)(2,1)S(1)} %collective-permute-done.1.refs_3_.refs_5_), channel_id=1, source_target_pairs={{0,32},{32,0},{1,33},{33,1},{2,34},{34,2},{3,35},{35,3},{4,36},{36... | collective-permute-start | bytes 614408 | tf_op jit(solution)/shard_map/ppermute | solution.py:235
  33.3 9.3 %collective-permute-start.11 = (bf16[800,128]{1,0:T(8,128)(2,1)S(1)}, bf16[800,128]{1,0:T(8,128)(2,1)S(1)}, u32[]{:S(2)}, u32[]{:S(2)}) collective-permute-start(bf16[800,128]{1,0:T(8,128)(2,1)S(1)} %collective-permute-done.2.refs_4_.refs_3_.refs_11_), channel_id=1, source_target_pairs={{0,32},{32,0},{1,33},{33,1},{2,34},{34,2},{3,35},{35,3},{4,36},{36... | collective-permute-start | bytes 614408 | tf_op jit(solution)/shard_map/ppermute | solution.py:235
  33.3 9.3 %collective-permute-start.12 = (bf16[800,128]{1,0:T(8,128)(2,1)S(1)}, bf16[800,128]{1,0:T(8,128)(2,1)S(1)}, u32[]{:S(2)}, u32[]{:S(2)}) collective-permute-start(bf16[800,128]{1,0:T(8,128)(2,1)S(1)} %collective-permute-done.3.refs_5_.refs_4_.refs_9_), channel_id=1, source_target_pairs={{0,32},{32,0},{1,33},{33,1},{2,34},{34,2},{3,35},{35,3},{4,36},{36... | collective-permute-start | bytes 614408 | tf_op jit(solution)/shard_map/ppermute | solution.py:235
  37.4 9.8 %collective-permute-start.13 = (bf16[800,128]{1,0:T(8,128)(2,1)S(1)}, bf16[800,128]{1,0:T(8,128)(2,1)S(1)}, u32[]{:S(2)}, u32[]{:S(2)}) collective-permute-start(bf16[800,128]{1,0:T(8,128)(2,1)S(1)} %collective-permute-done.3.refs_5_.refs_4_.refs_9_), channel_id=1, source_target_pairs={{0,7},{1,0},{2,1},{3,2},{4,3},{5,4},{6,5},{7,6},{32,33},{33,34},{3... | collective-permute-start | bytes 614408 | tf_op jit(solution)/shard_map/ppermute | solution.py:229
  42.4 10.1 %collective-permute-start.14 = (bf16[800,128]{1,0:T(8,128)(2,1)S(1)}, bf16[800,128]{1,0:T(8,128)(2,1)S(1)}, u32[]{:S(2)}, u32[]{:S(2)}) collective-permute-start(bf16[800,128]{1,0:T(8,128)(2,1)S(1)} %collective-permute-done.2.refs_4_.refs_3_.refs_11_), channel_id=1, source_target_pairs={{0,2},{1,3},{2,4},{3,5},{4,6},{5,7},{6,0},{7,1},{32,38},{33,39},{3... | collective-permute-start | bytes 614408 | tf_op jit(solution)/shard_map/ppermute | solution.py:229
  42.6 0.9 %copy-start.2 = (bf16[512,128]{1,0:T(8,128)(2,1)S(1)}, bf16[512,128]{1,0:T(8,128)(2,1)}, u32[]{:S(2)}) copy-start(bf16[512,128]{1,0:T(8,128)(2,1)} %get-tuple-element.29.refs_0_) | copy-start | bytes 393220
  47.2 5.4 %collective-permute-start.16 = (bf16[800,128]{1,0:T(8,128)(2,1)S(1)}, bf16[800,128]{1,0:T(8,128)(2,1)S(1)}, u32[]{:S(2)}, u32[]{:S(2)}) collective-permute-start(bf16[800,128]{1,0:T(8,128)(2,1)S(1)} %collective-permute-done.8.refs_4_.refs_8_), channel_id=1, source_target_pairs={{0,32},{32,0},{1,33},{33,1},{2,34},{34,2},{3,35},{35,3},{4,36},{36... | collective-permute-start | bytes 614408 | tf_op jit(solution)/shard_map/ppermute | solution.py:235
  47.3 5.3 %collective-permute-start.17 = (bf16[800,128]{1,0:T(8,128)(2,1)S(1)}, bf16[800,128]{1,0:T(8,128)(2,1)S(1)}, u32[]{:S(2)}, u32[]{:S(2)}) collective-permute-start(bf16[800,128]{1,0:T(8,128)(2,1)S(1)} %collective-permute-done.13.refs_5_.refs_6_), channel_id=1, source_target_pairs={{0,32},{32,0},{1,33},{33,1},{2,34},{34,2},{3,35},{35,3},{4,36},{36... | collective-permute-start | bytes 614408 | tf_op jit(solution)/shard_map/ppermute | solution.py:235
  52.6 2.9 %collective-permute-start.15 = (bf16[800,128]{1,0:T(8,128)(2,1)S(1)}, bf16[800,128]{1,0:T(8,128)(2,1)S(1)}, u32[]{:S(2)}, u32[]{:S(2)}) collective-permute-start(bf16[800,128]{1,0:T(8,128)(2,1)S(1)} %collective-permute-done.14.refs_4_.refs_5_), channel_id=1, source_target_pairs={{0,32},{32,0},{1,33},{33,1},{2,34},{34,2},{3,35},{35,3},{4,36},{36... | collective-permute-start | bytes 614408 | tf_op jit(solution)/shard_map/ppermute | solution.py:235
  56.7 5.0 %collective-permute-start.18 = (f32[32,128]{1,0:T(8,128)S(1)}, f32[32,128]{1,0:T(8,128)S(1)}, u32[]{:S(2)}, u32[]{:S(2)}) collective-permute-start(f32[32,128]{1,0:T(8,128)S(1)} %score_4_1.1.refs_0_), channel_id=1, source_target_pairs={{0,8},{8,16},{16,24},{24,0},{1,9},{9,17},{17,25},{25,1},{2,10},{10... | collective-permute-start | bytes 49160 | tf_op jit(solution)/shard_map/ppermute | solution.py:232
  57.8 3.8 %collective-permute-start.19 = (f32[32,128]{1,0:T(8,128)S(1)}, f32[32,128]{1,0:T(8,128)S(1)}, u32[]{:S(2)}, u32[]{:S(2)}) collective-permute-start(f32[32,128]{1,0:T(8,128)S(1)} %score_4_1.1.refs_0_), channel_id=1, source_target_pairs={{0,24},{8,0},{16,8},{24,16},{1,25},{9,1},{17,9},{25,17},{2,26},{10... | collective-permute-start | bytes 49160 | tf_op jit(solution)/shard_map/ppermute | solution.py:232
  59.9 5.2 %collective-permute-start.20 = (f32[32,128]{1,0:T(8,128)S(1)}, f32[32,128]{1,0:T(8,128)S(1)}, u32[]{:S(2)}, u32[]{:S(2)}) collective-permute-start(f32[32,128]{1,0:T(8,128)S(1)} %score_4_1.1.refs_0_), channel_id=1, source_target_pairs={{0,16},{8,24},{16,0},{24,8},{1,17},{9,25},{17,1},{25,9},{2,18},{10... | collective-permute-start | bytes 49160 | tf_op jit(solution)/shard_map/ppermute | solution.py:232

commit v7 on v5

--- a/solution.py
+++ b/solution.py
@@ -23,7 +23,7 @@
 FREE = pl.CostEstimate(flops=1000, bytes_accessed=1000, transcendentals=0)
 
 
-def ffn_kernel(tok, w_in, b_in, w_out, b_out, gain, shift, proj, out, again, acc, turned, *, queries, tokens):
+def ffn_kernel(tok, w_in, b_in, w_out, b_out, gain, shift, proj, out, acc, turned, *, queries, tokens):
     step = pl.program_id(0)
     chunk = w_in.shape[1]
     start = pl.multiple_of(step * chunk, chunk)
@@ -51,7 +51,6 @@
         for q in range(queries):
             turned[pl.ds(q, tokens, stride=queries), :] = embeds[q * tokens : (q + 1) * tokens, :]
         out[...] = turned[...].astype(jnp.bfloat16)
-        again[...] = turned[...].astype(jnp.bfloat16)
 
 
 def encode(tok, w_in, b_in, w_out, b_out, gain, shift, proj, queries, tokens, chunk=1024):
@@ -73,8 +72,8 @@
             whole(shift),
             whole(proj),
         ],
-        out_specs=[pl.BlockSpec((rows, proj.shape[1]), lambda j: (0, 0))] * 2,
-        out_shape=[jax.ShapeDtypeStruct((rows, proj.shape[1]), jnp.bfloat16)] * 2,
+        out_specs=pl.BlockSpec((rows, proj.shape[1]), lambda j: (0, 0)),
+        out_shape=jax.ShapeDtypeStruct((rows, proj.shape[1]), jnp.bfloat16),
         scratch_shapes=[pltpu.VMEM((rows, width), jnp.float32), pltpu.VMEM((rows, proj.shape[1]), jnp.float32)],
         compiler_params=pltpu.CompilerParams(vmem_limit_bytes=60 << 20),
         cost_estimate=FREE,
@@ -118,7 +117,9 @@
 
 def score_kernel(*refs, senders, items, arrays, tiles, length, group, chained):
     s, n = len(senders), len(items)
-    blocks, held, out, acc = refs[:s], refs[s : s + arrays], refs[-2], refs[-1]
+    blocks, held, out, acc, fetched, arrived = refs[:s], refs[s : s + arrays], *refs[-4:]
+    fetch = pltpu.make_async_copy(blocks[-1], fetched, arrived)
+    fetch.start()
     rows = tiles * length
     lane_group = lax.broadcasted_iota(jnp.int32, (8, 128), 1) // group
     row = lax.broadcasted_iota(jnp.int32, (8, 128), 0)
@@ -126,6 +127,9 @@
     acc[...] = jnp.zeros_like(acc)
 
     for sender, queries in zip(senders, blocks):
+        if queries is blocks[-1]:
+            fetch.wait()
+            queries = fetched
         block = queries[...]
         here = lane_group == lax.rem(x + SENDER[sender], X)
         for n, (parcel, *_) in enumerate(items):
@@ -181,10 +185,14 @@
             group=group,
             chained=begun is not None,
         ),
-        in_specs=[VM] * (len(blocks) + len(held) + len(more)),
+        in_specs=[VM] * (len(blocks) - 1) + [pl.BlockSpec(memory_space=pltpu.HBM)] + [VM] * (len(held) + len(more)),
         out_specs=VM,
         out_shape=jax.ShapeDtypeStruct((4 * Z, 128), jnp.float32),
-        scratch_shapes=[pltpu.VMEM((len(plan), 8, 128), jnp.float32)],
+        scratch_shapes=[
+            pltpu.VMEM((len(plan), 8, 128), jnp.float32),
+            pltpu.VMEM((512, 128), jnp.bfloat16),
+            pltpu.SemaphoreType.DMA,
+        ],
         compiler_params=pltpu.CompilerParams(vmem_limit_bytes=32 << 20),
         cost_estimate=FREE,
         name=f"score_{len(blocks)}_{len(plan)}",
@@ -211,6 +219,7 @@
         out_specs=VM,
         out_shape=jax.ShapeDtypeStruct((group, 4, X * Z), jnp.float32),
         scratch_shapes=[pltpu.VMEM((128, 128), jnp.float32)],
+        compiler_params=pltpu.CompilerParams(vmem_limit_bytes=8 << 20),
         name="finish",
     )(*sources)
 
@@ -238,10 +247,10 @@
     near = {0: own} | {k: along(own, k) for k in (1, -1, 2, -2)}
     far = {0: swap(own)}
     flat, _ = tied(tokens.reshape(queries * query_len, width), own)
-    embeds, embeds_here = encode(flat, w_in, b_in, w_out, b_out, gain, shift, proj, queries, query_len)
+    embeds = encode(flat, w_in, b_in, w_out, b_out, gain, shift, proj, queries, query_len)
     near[1], near[-1], near[2], near[-2], far[0], embeds = tied(near[1], near[-1], near[2], near[-2], far[0], embeds)
     near[3], near[-3], near[4] = along(near[2], 1), along(near[-2], -1), along(near[2], 2)
-    blocks = {0: embeds_here} | {i: across(embeds, k) for i, k in ((1, 1), (2, -1), (3, 2))}
+    blocks = {i: across(embeds, k) for i, k in ((1, 1), (2, -1), (3, 2))} | {0: embeds}
     far |= {k: swap(near[k]) for k in (1, -1, 2, -2)}
     args = (half, length, queries)
 
@@ -251,10 +260,7 @@
     def others(*ks):
         return [(far[k], near[k if k == 4 else -k], -k, True) for k in ks]
 
-    found = score({0: blocks[0]}, mine(0, 1, -1, 2, -2) + others(0), *args)
-    found, blocks[1], blocks[2], blocks[3] = tied(found, blocks[1], blocks[2], blocks[3])
-    three = {i: blocks[i] for i in (1, 2, 3)}
-    found = score(three, mine(0, 1, -1, 2, -2) + others(0), *args, begun=found)
+    found = score(blocks, mine(0, 1, -1, 2, -2) + others(0), *args)
     found, near[3], near[-3], near[4] = tied(found, near[3], near[-3], near[4])
     far |= {k: swap(near[k]) for k in (3, -3, 4)}
     found = score(blocks, others(1, -1, 2, -2), *args, begun=found)

time: 62.8 us -> 61.5 us (0.979)
  local copies, waits for them, and re-layouts: 2.42 us -> 0.91 us
    unnamed x16 -> x4, local copies, waits for them, and re-layouts: 2.42 us -> 0.91 us
    pallas_call x4 -> x3, Pallas kernels: 14.7 us -> 15.9 us  [score(): pl.pallas_call(functools.partial(score_kernel, senders=tuple(blocks), ite...]
    pallas_call x1, Pallas kernels: 1.69 us -> 0.92 us  [finish(): pl.pallas_call(functools.partial(finish_kernel, group=group), in_specs=[V...]
  transfers between devices with their start and end apart: 21 -> 21, of which waited for: 9 -> 9; matrix products, arithmetic and copies ran while one was open for 0% -> 0% of each run, Pallas kernels for 31% -> 33%
where the time goes in v7:
time: 61.5 us; the launch traced here: 61.4 us
  Pallas kernels  28.6 us (47%)
  starting transfers between devices  24.2 us (39%)
  waiting for transfers between devices  7.55 us (12%)
  local copies, waits for them, and re-layouts  0.91 us (1%)
    pallas_call x3, Pallas kernels, score(): pl.pallas_call(functools.partial(score_kernel, senders=tuple(blocks), ite...  15.9 us
    ppermute x7, starting transfers between devices, along(): return lax.ppermute(a, ('core', 'z'), ways)  13.6 us
    pallas_call x1, Pallas kernels, encode(): pl.pallas_call(functools.partial(ffn_kernel, queries=queries, tokens=toke...  10 us
    ppermute x6, starting transfers between devices, across(): return lax.ppermute(a, 'x', turn(X, k))  9.05 us
    ppermute x6, waiting for transfers between devices, across(): return lax.ppermute(a, 'x', turn(X, k))  6.35 us
    pallas_call x1, Pallas kernels, make_parcel(): pl.pallas_call(functools.partial(parcel_kernel, half=half), in_specs=[pl....  1.77 us
    ppermute x8, starting transfers between devices, swap(): return lax.ppermute(a, 'core', turn(CORES, 1))  1.63 us
  transfers between devices with their start and end apart: 21, of which 9 were waited for; matrix products, arithmetic and copies ran while one was open for 0% of the time, Pallas kernels for 33%

profile of v7, /device:TPU:16, one launch (start us, length us, event | category | flops | bytes accessed | tf_op | source)
XLA Modules:
  0.0 61.4 jit_solution(9483882948580045333)
XLA Ops:
  0.0 1.8 %parcel.1.refs_4_ = bf16[800,128]{1,0:T(8,128)(2,1)} custom-call(s32[12]{0:T(128)} %sizes.1, s32[4,512]{1,0:T(4,128)} %bitcast.7, s32[1,512]{1,0:T(1,128)} %bitcast.8, bf16[12,128,128]{2,1,0:T(8,128)(2,1)} %tiles.1), custom_call_target="tpu_custom_call" | custom-call | tf_op jit(solution)/shard_map/parcel/pallas_call | solution.py:106
  1.8 0.0 collective-permute-start.4
  1.8 6.3 %collective-permute-start.3 = (bf16[800,128]{1,0:T(8,128)(2,1)}, bf16[800,128]{1,0:T(8,128)(2,1)S(1)}, u32[]{:S(2)}, u32[]{:S(2)}) collective-permute-start(bf16[800,128]{1,0:T(8,128)(2,1)} %parcel.1.refs_4_), channel_id=1, source_target_pairs={{0,6},{1,7},{2,0},{3,1},{4,2},{5,3},{6,4},{7,5},{32,34},{33,35},{3... | collective-permute-start | bytes 614408 | tf_op jit(solution)/shard_map/ppermute | solution.py:239
  8.1 0.0 collective-permute-start.2
  8.1 3.7 %collective-permute-start.1 = (bf16[800,128]{1,0:T(8,128)(2,1)}, bf16[800,128]{1,0:T(8,128)(2,1)S(1)}, u32[]{:S(2)}, u32[]{:S(2)}) collective-permute-start(bf16[800,128]{1,0:T(8,128)(2,1)} %parcel.1.refs_4_), channel_id=1, source_target_pairs={{0,7},{1,0},{2,1},{3,2},{4,3},{5,4},{6,5},{7,6},{32,33},{33,34},{3... | collective-permute-start | bytes 614408 | tf_op jit(solution)/shard_map/ppermute | solution.py:239
  11.8 0.0 collective-permute-start
  11.8 0.0 copy-start.1
  11.8 10.0 %encode.1.refs_3_ = bf16[512,128]{1,0:T(8,128)(2,1)} custom-call(bf16[512,768]{1,0:T(8,128)(2,1)} %bitcast.6, bf16[768,3072]{1,0:T(8,128)(2,1)} %w_in.1, f32[3072]{0:T(1024)} %b_in.1, bf16[3072,768]{1,0:T(8,128)(2,1)} %w_out.1, f32[768]{0:T(1024)} %b_out.1, f32[768]{0:T(1024)} %gain.1, f32[768]{0:T(1024)} %shift.1, bf16[768,128]{1,0:T(8,128)(2,1)} %proj.1), custom_call_target="tpu_custom_call" | custom-call | flops 1000 | bytes 1000 | tf_op jit(solution)/shard_map/encode/pallas_call | solution.py:62
  21.8 0.0 collective-permute-done.4.refs_9_
  21.8 0.0 collective-permute-done.3.refs_8_.refs_9_
  21.8 0.0 collective-permute-done.2.refs_7_.refs_11_
  21.8 0.3 collective-permute-done.1.refs_6_.refs_5_
  22.2 0.2 collective-permute-done.refs_5_.refs_7_
  22.4 3.0 %collective-permute-start.7 = (bf16[512,128]{1,0:T(8,128)(2,1)}, bf16[512,128]{1,0:T(8,128)(2,1)S(1)}, u32[]{:S(2)}, u32[]{:S(2)}) collective-permute-start(bf16[512,128]{1,0:T(8,128)(2,1)} %encode.1.refs_3_), channel_id=1, source_target_pairs={{0,16},{8,24},{16,0},{24,8},{1,17},{9,25},{17,1},{25,9},{2,18},{10... | collective-permute-start | bytes 393224 | tf_op jit(solution)/shard_map/ppermute | solution.py:242
  25.4 1.1 %collective-permute-start.6 = (bf16[512,128]{1,0:T(8,128)(2,1)}, bf16[512,128]{1,0:T(8,128)(2,1)S(1)}, u32[]{:S(2)}, u32[]{:S(2)}) collective-permute-start(bf16[512,128]{1,0:T(8,128)(2,1)} %encode.1.refs_3_), channel_id=1, source_target_pairs={{0,24},{8,0},{16,8},{24,16},{1,25},{9,1},{17,9},{25,17},{2,26},{10... | collective-permute-start | bytes 393224 | tf_op jit(solution)/shard_map/ppermute | solution.py:242
  26.5 0.9 %collective-permute-start.5 = (bf16[512,128]{1,0:T(8,128)(2,1)}, bf16[512,128]{1,0:T(8,128)(2,1)S(1)}, u32[]{:S(2)}, u32[]{:S(2)}) collective-permute-start(bf16[512,128]{1,0:T(8,128)(2,1)} %encode.1.refs_3_), channel_id=1, source_target_pairs={{0,8},{8,16},{16,24},{24,0},{1,9},{9,17},{17,25},{25,1},{2,10},{10... | collective-permute-start | bytes 393224 | tf_op jit(solution)/shard_map/ppermute | solution.py:242
  27.4 3.4 %collective-permute-start.9 = (bf16[800,128]{1,0:T(8,128)(2,1)S(1)}, bf16[800,128]{1,0:T(8,128)(2,1)S(1)}, u32[]{:S(2)}, u32[]{:S(2)}) collective-permute-start(bf16[800,128]{1,0:T(8,128)(2,1)S(1)} %collective-permute-done.3.refs_8_.refs_9_), channel_id=1, source_target_pairs={{0,7},{1,0},{2,1},{3,2},{4,3},{5,4},{6,5},{7,6},{32,33},{33,34},{3... | collective-permute-start | bytes 614408 | tf_op jit(solution)/shard_map/ppermute | solution.py:239
  30.8 0.0 collective-permute-start.10
  30.8 0.0 collective-permute-done.7.refs_2_
  30.8 0.1 collective-permute-start.8
  31.0 1.1 %collective-permute-done.6.refs_1_ = bf16[512,128]{1,0:T(8,128)(2,1)S(1)} collective-permute-done((bf16[512,128]{1,0:T(8,128)(2,1)}, bf16[512,128]{1,0:T(8,128)(2,1)S(1)}, u32[]{:S(2)}, u32[]{:S(2)}) %collective-permute-start.6) | collective-permute-done | bytes 131104 | tf_op jit(solution)/shard_map/ppermute | solution.py:242
  32.1 0.0 collective-permute-start.14
  32.1 0.8 %collective-permute-done.5.refs_0_ = bf16[512,128]{1,0:T(8,128)(2,1)S(1)} collective-permute-done((bf16[512,128]{1,0:T(8,128)(2,1)}, bf16[512,128]{1,0:T(8,128)(2,1)S(1)}, u32[]{:S(2)}, u32[]{:S(2)}) %collective-permute-start.5) | collective-permute-done | bytes 131104 | tf_op jit(solution)/shard_map/ppermute | solution.py:242
  32.9 0.0 collective-permute-start.15
  32.9 0.0 copy-done.1
  32.9 0.0 copy-start
  32.9 0.9 %copy-done = bf16[512,128]{1,0:T(8,128)(2,1)S(1)} copy-done((bf16[512,128]{1,0:T(8,128)(2,1)S(1)}, bf16[512,128]{1,0:T(8,128)(2,1)}, u32[]{:S(2)}) %copy-start) | copy-done | bytes 131096
  33.8 5.8 %score_4_6.2.refs_12_ = f32[32,128]{1,0:T(8,128)S(1)} custom-call(bf16[512,128]{1,0:T(8,128)(2,1)S(1)} %collective-permute-done.5.refs_0_, bf16[512,128]{1,0:T(8,128)(2,1)S(1)} %collective-permute-done.6.refs_1_, bf16[512,128]{1,0:T(8,128)(2,1)S(1)} %collective-permute-done.7.refs_2_, bf16[512,128]{1,0:T(8,128)(2,1)S(1)} %copy-done, ...), custom_call_target="tpu_custom_call" | custom-call | flops 1000 | bytes 1000 | tf_op jit(solution)/shard_map/score_4_6/pallas_call | solution.py:177
  39.7 0.0 collective-permute-done.9.refs_5_
  39.7 0.6 collective-permute-start.17
  40.3 0.2 collective-permute-done.10.refs_6_
  40.5 0.0 collective-permute-start.16
  40.5 0.0 collective-permute-done.8.refs_4_
  40.5 0.5 collective-permute-start.11
  41.0 0.0 collective-permute-done.14.refs_4_
  41.0 0.1 collective-permute-start.12
  41.1 0.0 collective-permute-done.15.refs_6_
  41.1 0.4 collective-permute-start.13
  41.5 0.0 collective-permute-done.17.refs_10_
  41.5 0.4 collective-permute-done.16.refs_8_
  42.0 4.2 %score_4_4.1.refs_10_ = f32[32,128]{1,0:T(8,128)S(1)} custom-call(bf16[512,128]{1,0:T(8,128)(2,1)S(1)} %collective-permute-done.5.refs_0_, bf16[512,128]{1,0:T(8,128)(2,1)S(1)} %collective-permute-done.6.refs_1_, bf16[512,128]{1,0:T(8,128)(2,1)S(1)} %collective-permute-done.7.refs_2_, bf16[512,128]{1,0:T(8,128)(2,1)S(1)} %copy-done, ...), custom_call_target="tpu_custom_call" | custom-call | flops 1000 | bytes 1000 | tf_op jit(solution)/shard_map/score_4_4/pallas_call | solution.py:177
  46.2 0.0 collective-permute-done.11.refs_7_
  46.2 0.0 collective-permute-done.12.refs_8_
  46.2 0.0 collective-permute-done.13.refs_9_
  46.2 5.9 %score_4_6.3.refs_0_ = f32[32,128]{1,0:T(8,128)S(1)} custom-call(bf16[512,128]{1,0:T(8,128)(2,1)S(1)} %collective-permute-done.5.refs_0_, bf16[512,128]{1,0:T(8,128)(2,1)S(1)} %collective-permute-done.6.refs_1_, bf16[512,128]{1,0:T(8,128)(2,1)S(1)} %collective-permute-done.7.refs_2_, bf16[512,128]{1,0:T(8,128)(2,1)S(1)} %copy-done, ...), custom_call_target="tpu_custom_call" | custom-call | flops 1000 | bytes 1000 | tf_op jit(solution)/shard_map/score_4_6/pallas_call | solution.py:177
  52.1 2.0 %collective-permute-start.20 = (f32[32,128]{1,0:T(8,128)S(1)}, f32[32,128]{1,0:T(8,128)S(1)}, u32[]{:S(2)}, u32[]{:S(2)}) collective-permute-start(f32[32,128]{1,0:T(8,128)S(1)} %score_4_6.3.refs_0_), channel_id=1, source_target_pairs={{0,16},{8,24},{16,0},{24,8},{1,17},{9,25},{17,1},{25,9},{2,18},{10... | collective-permute-start | bytes 49160 | tf_op jit(solution)/shard_map/ppermute | solution.py:242
  54.0 1.5 %collective-permute-start.19 = (f32[32,128]{1,0:T(8,128)S(1)}, f32[32,128]{1,0:T(8,128)S(1)}, u32[]{:S(2)}, u32[]{:S(2)}) collective-permute-start(f32[32,128]{1,0:T(8,128)S(1)} %score_4_6.3.refs_0_), channel_id=1, source_target_pairs={{0,24},{8,0},{16,8},{24,16},{1,25},{9,1},{17,9},{25,17},{2,26},{10... | collective-permute-start | bytes 49160 | tf_op jit(solution)/shard_map/ppermute | solution.py:242
  55.5 0.5 collective-permute-start.18
  56.1 1.3 %collective-permute-done.20.refs_3_ = f32[32,128]{1,0:T(8,128)S(1)} collective-permute-done((f32[32,128]{1,0:T(8,128)S(1)}, f32[32,128]{1,0:T(8,128)S(1)}, u32[]{:S(2)}, u32[]{:S(2)}) %collective-permute-start.20) | collective-permute-done | bytes 16416 | tf_op jit(solution)/shard_map/ppermute | solution.py:242
  57.4 0.4 collective-permute-done.19.refs_2_
  57.8 2.7 %collective-permute-done.18.refs_1_ = f32[32,128]{1,0:T(8,128)S(1)} collective-permute-done((f32[32,128]{1,0:T(8,128)S(1)}, f32[32,128]{1,0:T(8,128)S(1)}, u32[]{:S(2)}, u32[]{:S(2)}) %collective-permute-start.18) | collective-permute-done | bytes 16416 | tf_op jit(solution)/shard_map/ppermute | solution.py:242
  60.5 0.9 %finish.1 = f32[16,4,32]{2,1,0:T(4,128)} custom-call(f32[32,128]{1,0:T(8,128)S(1)} %score_4_6.3.refs_0_, f32[32,128]{1,0:T(8,128)S(1)} %collective-permute-done.18.refs_1_, f32[32,128]{1,0:T(8,128)S(1)} %collective-permute-done.19.refs_2_, f32[32,128]{1,0:T(8,128)S(1)} %collective-permute-done.20.refs_3_), custom_call_target="tpu_custom_call" | custom-call | tf_op jit(solution)/shard_map/finish/pallas_call | solution.py:216
Async XLA Ops:
  1.8 20.0 %collective-permute-start.4 = (bf16[800,128]{1,0:T(8,128)(2,1)}, bf16[800,128]{1,0:T(8,128)(2,1)S(1)}, u32[]{:S(2)}, u32[]{:S(2)}) collective-permute-start(bf16[800,128]{1,0:T(8,128)(2,1)} %parcel.1.refs_4_), channel_id=1, source_target_pairs={{0,32},{32,0},{1,33},{33,1},{2,34},{34,2},{3,35},{35,3},{4,36},{36... | collective-permute-start | bytes 614408 | tf_op jit(solution)/shard_map/ppermute | solution.py:245
  1.8 20.0 %collective-permute-start.3 = (bf16[800,128]{1,0:T(8,128)(2,1)}, bf16[800,128]{1,0:T(8,128)(2,1)S(1)}, u32[]{:S(2)}, u32[]{:S(2)}) collective-permute-start(bf16[800,128]{1,0:T(8,128)(2,1)} %parcel.1.refs_4_), channel_id=1, source_target_pairs={{0,6},{1,7},{2,0},{3,1},{4,2},{5,3},{6,4},{7,5},{32,34},{33,35},{3... | collective-permute-start | bytes 614408 | tf_op jit(solution)/shard_map/ppermute | solution.py:239
  8.1 13.7 %collective-permute-start.2 = (bf16[800,128]{1,0:T(8,128)(2,1)}, bf16[800,128]{1,0:T(8,128)(2,1)S(1)}, u32[]{:S(2)}, u32[]{:S(2)}) collective-permute-start(bf16[800,128]{1,0:T(8,128)(2,1)} %parcel.1.refs_4_), channel_id=1, source_target_pairs={{0,2},{1,3},{2,4},{3,5},{4,6},{5,7},{6,0},{7,1},{32,38},{33,39},{3... | collective-permute-start | bytes 614408 | tf_op jit(solution)/shard_map/ppermute | solution.py:239
  8.1 14.1 %collective-permute-start.1 = (bf16[800,128]{1,0:T(8,128)(2,1)}, bf16[800,128]{1,0:T(8,128)(2,1)S(1)}, u32[]{:S(2)}, u32[]{:S(2)}) collective-permute-start(bf16[800,128]{1,0:T(8,128)(2,1)} %parcel.1.refs_4_), channel_id=1, source_target_pairs={{0,7},{1,0},{2,1},{3,2},{4,3},{5,4},{6,5},{7,6},{32,33},{33,34},{3... | collective-permute-start | bytes 614408 | tf_op jit(solution)/shard_map/ppermute | solution.py:239
  11.8 10.6 %collective-permute-start = (bf16[800,128]{1,0:T(8,128)(2,1)}, bf16[800,128]{1,0:T(8,128)(2,1)S(1)}, u32[]{:S(2)}, u32[]{:S(2)}) collective-permute-start(bf16[800,128]{1,0:T(8,128)(2,1)} %parcel.1.refs_4_), channel_id=1, source_target_pairs={{0,1},{1,2},{2,3},{3,4},{4,5},{5,6},{6,7},{7,0},{32,39},{33,32},{3... | collective-permute-start | bytes 614408 | tf_op jit(solution)/shard_map/ppermute | solution.py:239
  11.8 21.2 %copy-start.1 = (bf16[800,128]{1,0:T(8,128)(2,1)S(1)}, bf16[800,128]{1,0:T(8,128)(2,1)}, u32[]{:S(2)}) copy-start(bf16[800,128]{1,0:T(8,128)(2,1)} %parcel.1.refs_4_) | copy-start | bytes 614404
  22.4 8.5 %collective-permute-start.7 = (bf16[512,128]{1,0:T(8,128)(2,1)}, bf16[512,128]{1,0:T(8,128)(2,1)S(1)}, u32[]{:S(2)}, u32[]{:S(2)}) collective-permute-start(bf16[512,128]{1,0:T(8,128)(2,1)} %encode.1.refs_3_), channel_id=1, source_target_pairs={{0,16},{8,24},{16,0},{24,8},{1,17},{9,25},{17,1},{25,9},{2,18},{10... | collective-permute-start | bytes 393224 | tf_op jit(solution)/shard_map/ppermute | solution.py:242
  25.4 6.7 %collective-permute-start.6 = (bf16[512,128]{1,0:T(8,128)(2,1)}, bf16[512,128]{1,0:T(8,128)(2,1)S(1)}, u32[]{:S(2)}, u32[]{:S(2)}) collective-permute-start(bf16[512,128]{1,0:T(8,128)(2,1)} %encode.1.refs_3_), channel_id=1, source_target_pairs={{0,24},{8,0},{16,8},{24,16},{1,25},{9,1},{17,9},{25,17},{2,26},{10... | collective-permute-start | bytes 393224 | tf_op jit(solution)/shard_map/ppermute | solution.py:242
  26.5 6.4 %collective-permute-start.5 = (bf16[512,128]{1,0:T(8,128)(2,1)}, bf16[512,128]{1,0:T(8,128)(2,1)S(1)}, u32[]{:S(2)}, u32[]{:S(2)}) collective-permute-start(bf16[512,128]{1,0:T(8,128)(2,1)} %encode.1.refs_3_), channel_id=1, source_target_pairs={{0,8},{8,16},{16,24},{24,0},{1,9},{9,17},{17,25},{25,1},{2,10},{10... | collective-permute-start | bytes 393224 | tf_op jit(solution)/shard_map/ppermute | solution.py:242
  27.4 12.3 %collective-permute-start.9 = (bf16[800,128]{1,0:T(8,128)(2,1)S(1)}, bf16[800,128]{1,0:T(8,128)(2,1)S(1)}, u32[]{:S(2)}, u32[]{:S(2)}) collective-permute-start(bf16[800,128]{1,0:T(8,128)(2,1)S(1)} %collective-permute-done.3.refs_8_.refs_9_), channel_id=1, source_target_pairs={{0,7},{1,0},{2,1},{3,2},{4,3},{5,4},{6,5},{7,6},{32,33},{33,34},{3... | collective-permute-start | bytes 614408 | tf_op jit(solution)/shard_map/ppermute | solution.py:239
  30.8 9.7 %collective-permute-start.10 = (bf16[800,128]{1,0:T(8,128)(2,1)S(1)}, bf16[800,128]{1,0:T(8,128)(2,1)S(1)}, u32[]{:S(2)}, u32[]{:S(2)}) collective-permute-start(bf16[800,128]{1,0:T(8,128)(2,1)S(1)} %collective-permute-done.2.refs_7_.refs_11_), channel_id=1, source_target_pairs={{0,2},{1,3},{2,4},{3,5},{4,6},{5,7},{6,0},{7,1},{32,38},{33,39},{3... | collective-permute-start | bytes 614408 | tf_op jit(solution)/shard_map/ppermute | solution.py:239
  30.8 9.7 %collective-permute-start.8 = (bf16[800,128]{1,0:T(8,128)(2,1)S(1)}, bf16[800,128]{1,0:T(8,128)(2,1)S(1)}, u32[]{:S(2)}, u32[]{:S(2)}) collective-permute-start(bf16[800,128]{1,0:T(8,128)(2,1)S(1)} %collective-permute-done.2.refs_7_.refs_11_), channel_id=1, source_target_pairs={{0,1},{1,2},{2,3},{3,4},{4,5},{5,6},{6,7},{7,0},{32,39},{33,32},{3... | collective-permute-start | bytes 614408 | tf_op jit(solution)/shard_map/ppermute | solution.py:239
  32.1 8.9 %collective-permute-start.14 = (bf16[800,128]{1,0:T(8,128)(2,1)S(1)}, bf16[800,128]{1,0:T(8,128)(2,1)S(1)}, u32[]{:S(2)}, u32[]{:S(2)}) collective-permute-start(bf16[800,128]{1,0:T(8,128)(2,1)S(1)} %collective-permute-done.refs_5_.refs_7_), channel_id=1, source_target_pairs={{0,32},{32,0},{1,33},{33,1},{2,34},{34,2},{3,35},{35,3},{4,36},{36... | collective-permute-start | bytes 614408 | tf_op jit(solution)/shard_map/ppermute | solution.py:245
  32.9 8.2 %collective-permute-start.15 = (bf16[800,128]{1,0:T(8,128)(2,1)S(1)}, bf16[800,128]{1,0:T(8,128)(2,1)S(1)}, u32[]{:S(2)}, u32[]{:S(2)}) collective-permute-start(bf16[800,128]{1,0:T(8,128)(2,1)S(1)} %collective-permute-done.1.refs_6_.refs_5_), channel_id=1, source_target_pairs={{0,32},{32,0},{1,33},{33,1},{2,34},{34,2},{3,35},{35,3},{4,36},{36... | collective-permute-start | bytes 614408 | tf_op jit(solution)/shard_map/ppermute | solution.py:245
  32.9 0.9 %copy-start = (bf16[512,128]{1,0:T(8,128)(2,1)S(1)}, bf16[512,128]{1,0:T(8,128)(2,1)}, u32[]{:S(2)}) copy-start(bf16[512,128]{1,0:T(8,128)(2,1)} %encode.1.refs_3_) | copy-start | bytes 393220
  39.7 1.9 %collective-permute-start.17 = (bf16[800,128]{1,0:T(8,128)(2,1)S(1)}, bf16[800,128]{1,0:T(8,128)(2,1)S(1)}, u32[]{:S(2)}, u32[]{:S(2)}) collective-permute-start(bf16[800,128]{1,0:T(8,128)(2,1)S(1)} %collective-permute-done.3.refs_8_.refs_9_), channel_id=1, source_target_pairs={{0,32},{32,0},{1,33},{33,1},{2,34},{34,2},{3,35},{35,3},{4,36},{36... | collective-permute-start | bytes 614408 | tf_op jit(solution)/shard_map/ppermute | solution.py:245
  40.5 1.5 %collective-permute-start.16 = (bf16[800,128]{1,0:T(8,128)(2,1)S(1)}, bf16[800,128]{1,0:T(8,128)(2,1)S(1)}, u32[]{:S(2)}, u32[]{:S(2)}) collective-permute-start(bf16[800,128]{1,0:T(8,128)(2,1)S(1)} %collective-permute-done.2.refs_7_.refs_11_), channel_id=1, source_target_pairs={{0,32},{32,0},{1,33},{33,1},{2,34},{34,2},{3,35},{35,3},{4,36},{36... | collective-permute-start | bytes 614408 | tf_op jit(solution)/shard_map/ppermute | solution.py:245
  40.5 5.7 %collective-permute-start.11 = (bf16[800,128]{1,0:T(8,128)(2,1)S(1)}, bf16[800,128]{1,0:T(8,128)(2,1)S(1)}, u32[]{:S(2)}, u32[]{:S(2)}) collective-permute-start(bf16[800,128]{1,0:T(8,128)(2,1)S(1)} %collective-permute-done.8.refs_4_), channel_id=1, source_target_pairs={{0,32},{32,0},{1,33},{33,1},{2,34},{34,2},{3,35},{35,3},{4,36},{36... | collective-permute-start | bytes 614408 | tf_op jit(solution)/shard_map/ppermute | solution.py:245
  41.0 5.2 %collective-permute-start.12 = (bf16[800,128]{1,0:T(8,128)(2,1)S(1)}, bf16[800,128]{1,0:T(8,128)(2,1)S(1)}, u32[]{:S(2)}, u32[]{:S(2)}) collective-permute-start(bf16[800,128]{1,0:T(8,128)(2,1)S(1)} %collective-permute-done.9.refs_5_), channel_id=1, source_target_pairs={{0,32},{32,0},{1,33},{33,1},{2,34},{34,2},{3,35},{35,3},{4,36},{36... | collective-permute-start | bytes 614408 | tf_op jit(solution)/shard_map/ppermute | solution.py:245
  41.1 5.1 %collective-permute-start.13 = (bf16[800,128]{1,0:T(8,128)(2,1)S(1)}, bf16[800,128]{1,0:T(8,128)(2,1)S(1)}, u32[]{:S(2)}, u32[]{:S(2)}) collective-permute-start(bf16[800,128]{1,0:T(8,128)(2,1)S(1)} %collective-permute-done.10.refs_6_), channel_id=1, source_target_pairs={{0,32},{32,0},{1,33},{33,1},{2,34},{34,2},{3,35},{35,3},{4,36},{36... | collective-permute-start | bytes 614408 | tf_op jit(solution)/shard_map/ppermute | solution.py:245
  52.1 5.3 %collective-permute-start.20 = (f32[32,128]{1,0:T(8,128)S(1)}, f32[32,128]{1,0:T(8,128)S(1)}, u32[]{:S(2)}, u32[]{:S(2)}) collective-permute-start(f32[32,128]{1,0:T(8,128)S(1)} %score_4_6.3.refs_0_), channel_id=1, source_target_pairs={{0,16},{8,24},{16,0},{24,8},{1,17},{9,25},{17,1},{25,9},{2,18},{10... | collective-permute-start | bytes 49160 | tf_op jit(solution)/shard_map/ppermute | solution.py:242
  54.0 3.7 %collective-permute-start.19 = (f32[32,128]{1,0:T(8,128)S(1)}, f32[32,128]{1,0:T(8,128)S(1)}, u32[]{:S(2)}, u32[]{:S(2)}) collective-permute-start(f32[32,128]{1,0:T(8,128)S(1)} %score_4_6.3.refs_0_), channel_id=1, source_target_pairs={{0,24},{8,0},{16,8},{24,16},{1,25},{9,1},{17,9},{25,17},{2,26},{10... | collective-permute-start | bytes 49160 | tf_op jit(solution)/shard_map/ppermute | solution.py:242
  55.5 4.9 %collective-permute-start.18 = (f32[32,128]{1,0:T(8,128)S(1)}, f32[32,128]{1,0:T(8,128)S(1)}, u32[]{:S(2)}, u32[]{:S(2)}) collective-permute-start(f32[32,128]{1,0:T(8,128)S(1)} %score_4_6.3.refs_0_), channel_id=1, source_target_pairs={{0,8},{8,16},{16,24},{24,0},{1,9},{9,17},{17,25},{25,1},{2,10},{10... | collective-permute-start | bytes 49160 | tf_op jit(solution)/shard_map/ppermute | solution.py:242

commit v8 on v7

--- a/solution.py
+++ b/solution.py
@@ -53,7 +53,7 @@
         out[...] = turned[...].astype(jnp.bfloat16)
 
 
-def encode(tok, w_in, b_in, w_out, b_out, gain, shift, proj, queries, tokens, chunk=1024):
+def encode(tok, w_in, b_in, w_out, b_out, gain, shift, proj, queries, tokens, chunk=1536):
     rows, width = tok.shape
 
     def whole(a):
@@ -81,14 +81,15 @@
     )(tok, w_in, b_in, w_out, b_out, gain, shift, proj)
 
 
-def parcel_kernel(sizes, slots, counts, tiles, out, *, half):
+def parcel_kernel(sizes, slots, counts, tiles, out, other, *, half):
     count, length = tiles.shape[:2]
     core = lax.axis_index("core")
     column = lax.broadcasted_iota(jnp.int32, tiles.shape[1:], 0)
-    for t in range(half):
-        tile = tiles[core * half + t].astype(jnp.float32)
-        size = sizes[core * half + t]
-        out[t * length : (t + 1) * length, :] = jnp.where(column < size, tile, tile[0:1, :]).astype(jnp.bfloat16)
+    for side, to in ((core, out), (1 - core, other)):
+        for t in range(half):
+            tile = tiles[side * half + t].astype(jnp.float32)
+            size = sizes[side * half + t]
+            to[t * length : (t + 1) * length, :] = jnp.where(column < size, tile, tile[0:1, :]).astype(jnp.bfloat16)
     order = lax.broadcasted_iota(jnp.int32, slots.shape, 0)
     codes = jnp.where(order < counts[...], slots[...], count).astype(jnp.float32)
     lines = []
@@ -106,8 +107,8 @@
     return pl.pallas_call(
         functools.partial(parcel_kernel, half=half),
         in_specs=[pl.BlockSpec(memory_space=pltpu.SMEM), VM, VM, VM],
-        out_specs=VM,
-        out_shape=jax.ShapeDtypeStruct((half * length + 8 * X, dims), jnp.bfloat16),
+        out_specs=[VM, VM],
+        out_shape=[jax.ShapeDtypeStruct((half * length + r, dims), jnp.bfloat16) for r in (8 * X, 0)],
         name="parcel",
     )(sizes, slots, counts, tiles)
 
@@ -115,24 +116,20 @@
 SENDER = (0, X - 1, 1, 2)
 
 
-def score_kernel(*refs, senders, items, arrays, tiles, length, group, chained):
+def score_kernel(*refs, senders, items, arrays, tiles, length, group, chained, keep):
     s, n = len(senders), len(items)
-    blocks, held, out, acc, fetched, arrived = refs[:s], refs[s : s + arrays], *refs[-4:]
-    fetch = pltpu.make_async_copy(blocks[-1], fetched, arrived)
-    fetch.start()
+    blocks, held, out = refs[:s], refs[s : s + arrays], refs[-2 if keep else -1]
+    if keep:
+        refs[-1][...] = blocks[-1][...]
     rows = tiles * length
     lane_group = lax.broadcasted_iota(jnp.int32, (8, 128), 1) // group
     row = lax.broadcasted_iota(jnp.int32, (8, 128), 0)
     core, x, z = lax.axis_index("core"), lax.axis_index("x"), lax.axis_index("z")
-    acc[...] = jnp.zeros_like(acc)
-
+    best_of = [jnp.zeros((8, 128), jnp.float32)] * n
     for sender, queries in zip(senders, blocks):
-        if queries is blocks[-1]:
-            fetch.wait()
-            queries = fetched
         block = queries[...]
         here = lane_group == lax.rem(x + SENDER[sender], X)
-        for n, (parcel, *_) in enumerate(items):
+        for i, (parcel, *_) in enumerate(items):
             similar = lax.dot_general(
                 held[parcel][0:rows, :], block, (((1,), (1,)), ((), ())), preferred_element_type=jnp.float32
             )
@@ -144,11 +141,11 @@
             sums = sums + pltpu.roll(sums, 64, 1)
             sums = sums + pltpu.roll(sums, 32, 1)
             sums = sums + pltpu.roll(sums, 16, 1)
-            acc[n] = jnp.where(here, sums, acc[n])
-
-    out[...] = refs[s + arrays][...] if chained else jnp.zeros_like(out)
+            best_of[i] = jnp.where(here, sums, best_of[i])
+
+    found = [refs[s + arrays][c * Z : (c + 1) * Z] if chained else jnp.zeros((Z, 128), jnp.float32) for c in range(4)]
     way = 2 * core - 1
-    for n, (_, label, steps, far) in enumerate(items):
+    for i, (_, label, steps, far) in enumerate(items):
         codes = held[label][rows : rows + 8 * X, :].astype(jnp.float32)
         code = jnp.full((8, 128), -1.0, jnp.float32)
         for d in range(X):
@@ -158,11 +155,13 @@
         shard = lax.rem(z + steps * way + Z, Z)
         for c in range(4):
             picked = (code[c : c + 1] == row) & (row < tiles)
-            line = jnp.sum(jnp.where(picked, acc[n], 0.0), axis=0, keepdims=True)
-            out[pl.ds(c * Z + shard, 1), :] += line
-
-
-def score(blocks, items, tiles, length, group, begun=None):
+            line = jnp.sum(jnp.where(picked, best_of[i], 0.0), axis=0, keepdims=True)
+            found[c] = found[c] + jnp.where(row == shard, line, 0.0)
+    for c in range(4):
+        out[c * Z : (c + 1) * Z] = found[c]
+
+
+def score(blocks, items, tiles, length, group, begun=None, keep=False):
     held = []
 
     def at(array):
@@ -174,6 +173,7 @@
 
     plan = tuple((at(parcel), at(label), steps, far) for parcel, label, steps, far in items)
     more = [] if begun is None else [begun]
+    shape = jax.ShapeDtypeStruct((4 * Z, 128), jnp.float32)
     return pl.pallas_call(
         functools.partial(
             score_kernel,
@@ -184,15 +184,11 @@
             length=length,
             group=group,
             chained=begun is not None,
+            keep=keep,
         ),
-        in_specs=[VM] * (len(blocks) - 1) + [pl.BlockSpec(memory_space=pltpu.HBM)] + [VM] * (len(held) + len(more)),
-        out_specs=VM,
-        out_shape=jax.ShapeDtypeStruct((4 * Z, 128), jnp.float32),
-        scratch_shapes=[
-            pltpu.VMEM((len(plan), 8, 128), jnp.float32),
-            pltpu.VMEM((512, 128), jnp.bfloat16),
-            pltpu.SemaphoreType.DMA,
-        ],
+        in_specs=[VM] * (len(blocks) + len(held) + len(more)),
+        out_specs=[VM, VM] if keep else VM,
+        out_shape=[shape, jax.ShapeDtypeStruct((512, 128), jnp.bfloat16)] if keep else shape,
         compiler_params=pltpu.CompilerParams(vmem_limit_bytes=32 << 20),
         cost_estimate=FREE,
         name=f"score_{len(blocks)}_{len(plan)}",
@@ -232,7 +228,7 @@
     queries, query_len, width = tokens.shape
     count, length, dims = tiles.shape
     half = count // CORES
-    own = make_parcel(lengths, slots.transpose(1, 2, 0)[0], counts.transpose(1, 0), tiles)
+    own, own_far = make_parcel(lengths, slots.transpose(1, 2, 0)[0], counts.transpose(1, 0), tiles)
 
     def along(a, k):
         ways = [(z, (z + k) % Z) for z in range(Z)] + [(Z + z, Z + (z - k) % Z) for z in range(Z)]
@@ -245,13 +241,12 @@
         return lax.ppermute(a, "core", turn(CORES, 1))
 
     near = {0: own} | {k: along(own, k) for k in (1, -1, 2, -2)}
-    far = {0: swap(own)}
+    far = {0: own_far}
     flat, _ = tied(tokens.reshape(queries * query_len, width), own)
     embeds = encode(flat, w_in, b_in, w_out, b_out, gain, shift, proj, queries, query_len)
-    near[1], near[-1], near[2], near[-2], far[0], embeds = tied(near[1], near[-1], near[2], near[-2], far[0], embeds)
+    near[1], near[-1], near[2], near[-2], embeds = tied(near[1], near[-1], near[2], near[-2], embeds)
     near[3], near[-3], near[4] = along(near[2], 1), along(near[-2], -1), along(near[2], 2)
     blocks = {i: across(embeds, k) for i, k in ((1, 1), (2, -1), (3, 2))} | {0: embeds}
-    far |= {k: swap(near[k]) for k in (1, -1, 2, -2)}
     args = (half, length, queries)
 
     def mine(*ks):
@@ -260,7 +255,11 @@
     def others(*ks):
         return [(far[k], near[k if k == 4 else -k], -k, True) for k in ks]
 
-    found = score(blocks, mine(0, 1, -1, 2, -2) + others(0), *args)
+    early = mine(0, 1, -1, 2, -2) + others(0)
+    found, blocks[0] = score({0: blocks[0]}, early, *args, keep=True)
+    found, *ready = tied(found, *(near[k] for k in (1, -1, 2, -2)))
+    far |= {k: swap(a) for k, a in zip((1, -1, 2, -2), ready)}
+    found = score({i: blocks[i] for i in (1, 2, 3)}, early, *args, begun=found)
     found, near[3], near[-3], near[4] = tied(found, near[3], near[-3], near[4])
     far |= {k: swap(near[k]) for k in (3, -3, 4)}
     found = score(blocks, others(1, -1, 2, -2), *args, begun=found)

time: 61.5 us -> 60 us (0.976)
  Pallas kernels: 28.6 us -> 27.6 us
    ppermute x7, waiting for transfers between devices: 0.77 us -> 2.27 us  [along(): return lax.ppermute(a, ('core', 'z'), ways)]
    ppermute x6, waiting for transfers between devices: 6.35 us -> 4.95 us  [across(): return lax.ppermute(a, 'x', turn(X, k))]
    pallas_call x3 -> x4, Pallas kernels: 15.9 us -> 14.7 us  [score(): pl.pallas_call(functools.partial(score_kernel, senders=tuple(blocks), ite...]
    ppermute x8 -> x7, starting transfers between devices: 1.63 us -> 2.06 us  [swap(): return lax.ppermute(a, 'core', turn(CORES, 1))]
  transfers between devices with their start and end apart: 21 -> 20, of which waited for: 9 -> 4; matrix products, arithmetic and copies ran while one was open for 0% -> 0% of each run, Pallas kernels for 33% -> 32%
where the time goes in v8:
time: 60 us; the launch traced here: 59.9 us
  Pallas kernels  27.6 us (46%)
  starting transfers between devices  24.1 us (40%)
  waiting for transfers between devices  7.25 us (12%)
  local copies, waits for them, and re-layouts  0.9 us (2%)
    pallas_call x4, Pallas kernels, score(): pl.pallas_call(functools.partial(score_kernel, senders=tuple(blocks), ite...  14.7 us
    ppermute x7, starting transfers between devices, along(): return lax.ppermute(a, ('core', 'z'), ways)  13.5 us
    pallas_call x1, Pallas kernels, encode(): pl.pallas_call(functools.partial(ffn_kernel, queries=queries, tokens=toke...  10.1 us
    ppermute x6, starting transfers between devices, across(): return lax.ppermute(a, 'x', turn(X, k))  8.48 us
    ppermute x6, waiting for transfers between devices, across(): return lax.ppermute(a, 'x', turn(X, k))  4.95 us
    ppermute x7, waiting for transfers between devices, along(): return lax.ppermute(a, ('core', 'z'), ways)  2.27 us
    ppermute x7, starting transfers between devices, swap(): return lax.ppermute(a, 'core', turn(CORES, 1))  2.06 us
    pallas_call x1, Pallas kernels, make_parcel(): pl.pallas_call(functools.partial(parcel_kernel, half=half), in_specs=[pl....  1.89 us
  transfers between devices with their start and end apart: 20, of which 4 were waited for; matrix products, arithmetic and copies ran while one was open for 0% of the time, Pallas kernels for 32%

profile of v8, /device:TPU:16, one launch (start us, length us, event | category | flops | bytes accessed | tf_op | source)
XLA Modules:
  0.0 59.9 jit_solution(5390194931959076987)
XLA Ops:
  0.0 1.9 %parcel.1 = (bf16[800,128]{1,0:T(8,128)(2,1)}, bf16[768,128]{1,0:T(8,128)(2,1)}) custom-call(s32[12]{0:T(128)} %sizes.1, s32[4,512]{1,0:T(4,128)} %bitcast.7, s32[1,512]{1,0:T(1,128)} %bitcast.8, bf16[12,128,128]{2,1,0:T(8,128)(2,1)} %tiles.1), custom_call_target="tpu_custom_call" | custom-call | tf_op jit(solution)/shard_map/parcel/pallas_call | solution.py:107
  1.9 6.3 %collective-permute-start.3 = (bf16[800,128]{1,0:T(8,128)(2,1)}, bf16[800,128]{1,0:T(8,128)(2,1)S(1)}, u32[]{:S(2)}, u32[]{:S(2)}) collective-permute-start(bf16[800,128]{1,0:T(8,128)(2,1)} %get-tuple-element.24.refs_1_.refs_3_), channel_id=1, source_target_pairs={{0,6},{1,7},{2,0},{3,1},{4,2},{5,3},{6,4},{7,5},{32,34},{33,35},{3... | collective-permute-start | bytes 614408 | tf_op jit(solution)/shard_map/ppermute | solution.py:235
  8.2 0.0 collective-permute-start.2
  8.2 3.7 %collective-permute-start.1 = (bf16[800,128]{1,0:T(8,128)(2,1)}, bf16[800,128]{1,0:T(8,128)(2,1)S(1)}, u32[]{:S(2)}, u32[]{:S(2)}) collective-permute-start(bf16[800,128]{1,0:T(8,128)(2,1)} %get-tuple-element.24.refs_1_.refs_3_), channel_id=1, source_target_pairs={{0,7},{1,0},{2,1},{3,2},{4,3},{5,4},{6,5},{7,6},{32,33},{33,34},{3... | collective-permute-start | bytes 614408 | tf_op jit(solution)/shard_map/ppermute | solution.py:235
  11.9 0.0 collective-permute-start
  11.9 0.0 copy-start
  11.9 0.0 copy-start.1
  11.9 10.1 %encode.1.refs_0_ = bf16[512,128]{1,0:T(8,128)(2,1)} custom-call(bf16[512,768]{1,0:T(8,128)(2,1)} %bitcast.6, bf16[768,3072]{1,0:T(8,128)(2,1)} %w_in.1, f32[3072]{0:T(1024)} %b_in.1, bf16[3072,768]{1,0:T(8,128)(2,1)} %w_out.1, f32[768]{0:T(1024)} %b_out.1, f32[768]{0:T(1024)} %gain.1, f32[768]{0:T(1024)} %shift.1, bf16[768,128]{1,0:T(8,128)(2,1)} %proj.1), custom_call_target="tpu_custom_call" | custom-call | flops 1000 | bytes 1000 | tf_op jit(solution)/shard_map/encode/pallas_call | solution.py:62
  22.0 0.0 collective-permute-done.3.refs_5_.refs_7_.refs_9_
  22.0 0.0 collective-permute-done.2.refs_4_.refs_6_.refs_11_
  22.0 0.0 collective-permute-done.1.refs_3_.refs_5_
  22.0 0.0 collective-permute-done.refs_2_.refs_4_.refs_7_
  22.0 3.1 %collective-permute-start.6 = (bf16[512,128]{1,0:T(8,128)(2,1)}, bf16[512,128]{1,0:T(8,128)(2,1)S(1)}, u32[]{:S(2)}, u32[]{:S(2)}) collective-permute-start(bf16[512,128]{1,0:T(8,128)(2,1)} %encode.1.refs_0_), channel_id=1, source_target_pairs={{0,16},{8,24},{16,0},{24,8},{1,17},{9,25},{17,1},{25,9},{2,18},{10... | collective-permute-start | bytes 393224 | tf_op jit(solution)/shard_map/ppermute | solution.py:238
  25.1 1.1 %collective-permute-start.5 = (bf16[512,128]{1,0:T(8,128)(2,1)}, bf16[512,128]{1,0:T(8,128)(2,1)S(1)}, u32[]{:S(2)}, u32[]{:S(2)}) collective-permute-start(bf16[512,128]{1,0:T(8,128)(2,1)} %encode.1.refs_0_), channel_id=1, source_target_pairs={{0,24},{8,0},{16,8},{24,16},{1,25},{9,1},{17,9},{25,17},{2,26},{10... | collective-permute-start | bytes 393224 | tf_op jit(solution)/shard_map/ppermute | solution.py:238
  26.2 0.9 %collective-permute-start.4 = (bf16[512,128]{1,0:T(8,128)(2,1)}, bf16[512,128]{1,0:T(8,128)(2,1)S(1)}, u32[]{:S(2)}, u32[]{:S(2)}) collective-permute-start(bf16[512,128]{1,0:T(8,128)(2,1)} %encode.1.refs_0_), channel_id=1, source_target_pairs={{0,8},{8,16},{16,24},{24,0},{1,9},{9,17},{17,25},{25,1},{2,10},{10... | collective-permute-start | bytes 393224 | tf_op jit(solution)/shard_map/ppermute | solution.py:238
  27.1 3.2 %collective-permute-start.8 = (bf16[800,128]{1,0:T(8,128)(2,1)S(1)}, bf16[800,128]{1,0:T(8,128)(2,1)S(1)}, u32[]{:S(2)}, u32[]{:S(2)}) collective-permute-start(bf16[800,128]{1,0:T(8,128)(2,1)S(1)} %collective-permute-done.3.refs_5_.refs_7_.refs_9_), channel_id=1, source_target_pairs={{0,7},{1,0},{2,1},{3,2},{4,3},{5,4},{6,5},{7,6},{32,33},{33,34},{3... | collective-permute-start | bytes 614408 | tf_op jit(solution)/shard_map/ppermute | solution.py:235
  30.4 0.0 collective-permute-start.9
  30.4 0.0 copy-done
  30.4 0.0 copy-done.1
  30.4 0.0 copy-start.2
  30.4 0.9 %copy-done.2 = bf16[512,128]{1,0:T(8,128)(2,1)S(1)} copy-done((bf16[512,128]{1,0:T(8,128)(2,1)S(1)}, bf16[512,128]{1,0:T(8,128)(2,1)}, u32[]{:S(2)}) %copy-start.2) | copy-done | bytes 131096
  31.3 1.6 %score_1_6.1 = (f32[32,128]{1,0:T(8,128)S(1)}, bf16[512,128]{1,0:T(8,128)(2,1)S(1)}) custom-call(bf16[512,128]{1,0:T(8,128)(2,1)S(1)} %copy-done.2, bf16[800,128]{1,0:T(8,128)(2,1)S(1)} %copy-done, bf16[800,128]{1,0:T(8,128)(2,1)S(1)} %collective-permute-done.refs_2_.refs_4_.refs_7_, bf16[800,128]{1,0:T(8,128)(2,1)S(1)} %collective-permute-done.1.refs_3_.refs_5_, ...), custom_call_target="tpu_custom_call" | custom-call | flops 1000 | bytes 1000 | tf_op jit(solution)/shard_map/score_1_6/pallas_call | solution.py:177
  32.9 0.0 collective-permute-done.6.refs_2_
  32.9 0.3 collective-permute-start.7
  33.2 0.0 collective-permute-done.5.refs_1_
  33.2 0.6 %collective-permute-start.13 = (bf16[800,128]{1,0:T(8,128)(2,1)S(1)}, bf16[800,128]{1,0:T(8,128)(2,1)S(1)}, u32[]{:S(2)}, u32[]{:S(2)}) collective-permute-start(bf16[800,128]{1,0:T(8,128)(2,1)S(1)} %collective-permute-done.refs_2_.refs_4_.refs_7_), channel_id=1, source_target_pairs={{0,32},{32,0},{1,33},{33,1},{2,34},{34,2},{3,35},{35,3},{4,36},{36... | collective-permute-start | bytes 614408 | tf_op jit(solution)/shard_map/ppermute | solution.py:241
  33.9 0.0 collective-permute-done.4.refs_0_
  33.9 0.1 collective-permute-start.14
  34.0 4.1 %score_3_6.1.refs_12_ = f32[32,128]{1,0:T(8,128)S(1)} custom-call(bf16[512,128]{1,0:T(8,128)(2,1)S(1)} %collective-permute-done.4.refs_0_, bf16[512,128]{1,0:T(8,128)(2,1)S(1)} %collective-permute-done.5.refs_1_, bf16[512,128]{1,0:T(8,128)(2,1)S(1)} %collective-permute-done.6.refs_2_, bf16[800,128]{1,0:T(8,128)(2,1)S(1)} %copy-done, ...), custom_call_target="tpu_custom_call" | custom-call | flops 1000 | bytes 1000 | tf_op jit(solution)/shard_map/score_3_6/pallas_call | solution.py:177
  38.0 0.0 collective-permute-done.8.refs_5_
  38.0 0.5 collective-permute-start.15
  38.5 1.4 %collective-permute-done.9.refs_6_ = bf16[800,128]{1,0:T(8,128)(2,1)S(1)} collective-permute-done((bf16[800,128]{1,0:T(8,128)(2,1)S(1)}, bf16[800,128]{1,0:T(8,128)(2,1)S(1)}, u32[]{:S(2)}, u32[]{:S(2)}) %collective-permute-start.9) | collective-permute-done | bytes 204832 | tf_op jit(solution)/shard_map/ppermute | solution.py:235
  40.0 0.0 collective-permute-start.16
  40.0 0.9 %collective-permute-done.7.refs_4_ = bf16[800,128]{1,0:T(8,128)(2,1)S(1)} collective-permute-done((bf16[800,128]{1,0:T(8,128)(2,1)S(1)}, bf16[800,128]{1,0:T(8,128)(2,1)S(1)}, u32[]{:S(2)}, u32[]{:S(2)}) %collective-permute-start.7) | collective-permute-done | bytes 204832 | tf_op jit(solution)/shard_map/ppermute | solution.py:235
  40.8 0.0 collective-permute-start.10
  40.8 0.0 collective-permute-done.13.refs_4_
  40.8 0.5 collective-permute-start.11
  41.3 0.0 collective-permute-done.14.refs_6_
  41.3 0.3 collective-permute-start.12
  41.6 0.0 collective-permute-done.15.refs_8_
  41.6 0.0 collective-permute-done.16.refs_10_
  41.6 3.7 %score_4_4.1.refs_10_ = f32[32,128]{1,0:T(8,128)S(1)} custom-call(bf16[512,128]{1,0:T(8,128)(2,1)S(1)} %collective-permute-done.4.refs_0_, bf16[512,128]{1,0:T(8,128)(2,1)S(1)} %collective-permute-done.5.refs_1_, bf16[512,128]{1,0:T(8,128)(2,1)S(1)} %collective-permute-done.6.refs_2_, bf16[512,128]{1,0:T(8,128)(2,1)S(1)} %get-tuple-element.32.refs_3_, ...), custom_call_target="tpu_custom_call" | custom-call | flops 1000 | bytes 1000 | tf_op jit(solution)/shard_map/score_4_4/pallas_call | solution.py:177
  45.3 0.0 collective-permute-done.10.refs_7_
  45.3 0.0 collective-permute-done.11.refs_8_
  45.3 0.0 collective-permute-done.12.refs_9_
  45.3 5.3 %score_4_6.1.refs_0_ = f32[32,128]{1,0:T(8,128)S(1)} custom-call(bf16[512,128]{1,0:T(8,128)(2,1)S(1)} %collective-permute-done.4.refs_0_, bf16[512,128]{1,0:T(8,128)(2,1)S(1)} %collective-permute-done.5.refs_1_, bf16[512,128]{1,0:T(8,128)(2,1)S(1)} %collective-permute-done.6.refs_2_, bf16[512,128]{1,0:T(8,128)(2,1)S(1)} %get-tuple-element.32.refs_3_, ...), custom_call_target="tpu_custom_call" | custom-call | flops 1000 | bytes 1000 | tf_op jit(solution)/shard_map/score_4_6/pallas_call | solution.py:177
  50.7 0.7 %collective-permute-start.19 = (f32[32,128]{1,0:T(8,128)S(1)}, f32[32,128]{1,0:T(8,128)S(1)}, u32[]{:S(2)}, u32[]{:S(2)}) collective-permute-start(f32[32,128]{1,0:T(8,128)S(1)} %score_4_6.1.refs_0_), channel_id=1, source_target_pairs={{0,16},{8,24},{16,0},{24,8},{1,17},{9,25},{17,1},{25,9},{2,18},{10... | collective-permute-start | bytes 49160 | tf_op jit(solution)/shard_map/ppermute | solution.py:238
  51.4 2.6 %collective-permute-start.18 = (f32[32,128]{1,0:T(8,128)S(1)}, f32[32,128]{1,0:T(8,128)S(1)}, u32[]{:S(2)}, u32[]{:S(2)}) collective-permute-start(f32[32,128]{1,0:T(8,128)S(1)} %score_4_6.1.refs_0_), channel_id=1, source_target_pairs={{0,24},{8,0},{16,8},{24,16},{1,25},{9,1},{17,9},{25,17},{2,26},{10... | collective-permute-start | bytes 49160 | tf_op jit(solution)/shard_map/ppermute | solution.py:238
  54.0 0.0 collective-permute-start.17
  54.0 2.0 %collective-permute-done.19.refs_3_ = f32[32,128]{1,0:T(8,128)S(1)} collective-permute-done((f32[32,128]{1,0:T(8,128)S(1)}, f32[32,128]{1,0:T(8,128)S(1)}, u32[]{:S(2)}, u32[]{:S(2)}) %collective-permute-start.19) | collective-permute-done | bytes 16416 | tf_op jit(solution)/shard_map/ppermute | solution.py:238
  56.0 0.0 collective-permute-done.18.refs_2_
  56.0 3.0 %collective-permute-done.17.refs_1_ = f32[32,128]{1,0:T(8,128)S(1)} collective-permute-done((f32[32,128]{1,0:T(8,128)S(1)}, f32[32,128]{1,0:T(8,128)S(1)}, u32[]{:S(2)}, u32[]{:S(2)}) %collective-permute-start.17) | collective-permute-done | bytes 16416 | tf_op jit(solution)/shard_map/ppermute | solution.py:238
  58.9 0.9 %finish.1 = f32[16,4,32]{2,1,0:T(4,128)} custom-call(f32[32,128]{1,0:T(8,128)S(1)} %score_4_6.1.refs_0_, f32[32,128]{1,0:T(8,128)S(1)} %collective-permute-done.17.refs_1_, f32[32,128]{1,0:T(8,128)S(1)} %collective-permute-done.18.refs_2_, f32[32,128]{1,0:T(8,128)S(1)} %collective-permute-done.19.refs_3_), custom_call_target="tpu_custom_call" | custom-call | tf_op jit(solution)/shard_map/finish/pallas_call | solution.py:212
Async XLA Ops:
  1.9 20.1 %collective-permute-start.3 = (bf16[800,128]{1,0:T(8,128)(2,1)}, bf16[800,128]{1,0:T(8,128)(2,1)S(1)}, u32[]{:S(2)}, u32[]{:S(2)}) collective-permute-start(bf16[800,128]{1,0:T(8,128)(2,1)} %get-tuple-element.24.refs_1_.refs_3_), channel_id=1, source_target_pairs={{0,6},{1,7},{2,0},{3,1},{4,2},{5,3},{6,4},{7,5},{32,34},{33,35},{3... | collective-permute-start | bytes 614408 | tf_op jit(solution)/shard_map/ppermute | solution.py:235
  8.2 13.8 %collective-permute-start.2 = (bf16[800,128]{1,0:T(8,128)(2,1)}, bf16[800,128]{1,0:T(8,128)(2,1)S(1)}, u32[]{:S(2)}, u32[]{:S(2)}) collective-permute-start(bf16[800,128]{1,0:T(8,128)(2,1)} %get-tuple-element.24.refs_1_.refs_3_), channel_id=1, source_target_pairs={{0,2},{1,3},{2,4},{3,5},{4,6},{5,7},{6,0},{7,1},{32,38},{33,39},{3... | collective-permute-start | bytes 614408 | tf_op jit(solution)/shard_map/ppermute | solution.py:235
  8.2 13.8 %collective-permute-start.1 = (bf16[800,128]{1,0:T(8,128)(2,1)}, bf16[800,128]{1,0:T(8,128)(2,1)S(1)}, u32[]{:S(2)}, u32[]{:S(2)}) collective-permute-start(bf16[800,128]{1,0:T(8,128)(2,1)} %get-tuple-element.24.refs_1_.refs_3_), channel_id=1, source_target_pairs={{0,7},{1,0},{2,1},{3,2},{4,3},{5,4},{6,5},{7,6},{32,33},{33,34},{3... | collective-permute-start | bytes 614408 | tf_op jit(solution)/shard_map/ppermute | solution.py:235
  11.9 10.1 %collective-permute-start = (bf16[800,128]{1,0:T(8,128)(2,1)}, bf16[800,128]{1,0:T(8,128)(2,1)S(1)}, u32[]{:S(2)}, u32[]{:S(2)}) collective-permute-start(bf16[800,128]{1,0:T(8,128)(2,1)} %get-tuple-element.24.refs_1_.refs_3_), channel_id=1, source_target_pairs={{0,1},{1,2},{2,3},{3,4},{4,5},{5,6},{6,7},{7,0},{32,39},{33,32},{3... | collective-permute-start | bytes 614408 | tf_op jit(solution)/shard_map/ppermute | solution.py:235
  11.9 18.5 %copy-start = (bf16[800,128]{1,0:T(8,128)(2,1)S(1)}, bf16[800,128]{1,0:T(8,128)(2,1)}, u32[]{:S(2)}) copy-start(bf16[800,128]{1,0:T(8,128)(2,1)} %get-tuple-element.24.refs_1_.refs_3_) | copy-start | bytes 614404
  11.9 18.5 %copy-start.1 = (bf16[768,128]{1,0:T(8,128)(2,1)S(1)}, bf16[768,128]{1,0:T(8,128)(2,1)}, u32[]{:S(2)}) copy-start(bf16[768,128]{1,0:T(8,128)(2,1)} %get-tuple-element.31.refs_6_.refs_8_) | copy-start | bytes 589828
  22.0 10.9 %collective-permute-start.6 = (bf16[512,128]{1,0:T(8,128)(2,1)}, bf16[512,128]{1,0:T(8,128)(2,1)S(1)}, u32[]{:S(2)}, u32[]{:S(2)}) collective-permute-start(bf16[512,128]{1,0:T(8,128)(2,1)} %encode.1.refs_0_), channel_id=1, source_target_pairs={{0,16},{8,24},{16,0},{24,8},{1,17},{9,25},{17,1},{25,9},{2,18},{10... | collective-permute-start | bytes 393224 | tf_op jit(solution)/shard_map/ppermute | solution.py:238
  25.1 8.1 %collective-permute-start.5 = (bf16[512,128]{1,0:T(8,128)(2,1)}, bf16[512,128]{1,0:T(8,128)(2,1)S(1)}, u32[]{:S(2)}, u32[]{:S(2)}) collective-permute-start(bf16[512,128]{1,0:T(8,128)(2,1)} %encode.1.refs_0_), channel_id=1, source_target_pairs={{0,24},{8,0},{16,8},{24,16},{1,25},{9,1},{17,9},{25,17},{2,26},{10... | collective-permute-start | bytes 393224 | tf_op jit(solution)/shard_map/ppermute | solution.py:238
  26.2 7.6 %collective-permute-start.4 = (bf16[512,128]{1,0:T(8,128)(2,1)}, bf16[512,128]{1,0:T(8,128)(2,1)S(1)}, u32[]{:S(2)}, u32[]{:S(2)}) collective-permute-start(bf16[512,128]{1,0:T(8,128)(2,1)} %encode.1.refs_0_), channel_id=1, source_target_pairs={{0,8},{8,16},{16,24},{24,0},{1,9},{9,17},{17,25},{25,1},{2,10},{10... | collective-permute-start | bytes 393224 | tf_op jit(solution)/shard_map/ppermute | solution.py:238
  27.1 10.9 %collective-permute-start.8 = (bf16[800,128]{1,0:T(8,128)(2,1)S(1)}, bf16[800,128]{1,0:T(8,128)(2,1)S(1)}, u32[]{:S(2)}, u32[]{:S(2)}) collective-permute-start(bf16[800,128]{1,0:T(8,128)(2,1)S(1)} %collective-permute-done.3.refs_5_.refs_7_.refs_9_), channel_id=1, source_target_pairs={{0,7},{1,0},{2,1},{3,2},{4,3},{5,4},{6,5},{7,6},{32,33},{33,34},{3... | collective-permute-start | bytes 614408 | tf_op jit(solution)/shard_map/ppermute | solution.py:235
  30.4 9.6 %collective-permute-start.9 = (bf16[800,128]{1,0:T(8,128)(2,1)S(1)}, bf16[800,128]{1,0:T(8,128)(2,1)S(1)}, u32[]{:S(2)}, u32[]{:S(2)}) collective-permute-start(bf16[800,128]{1,0:T(8,128)(2,1)S(1)} %collective-permute-done.2.refs_4_.refs_6_.refs_11_), channel_id=1, source_target_pairs={{0,2},{1,3},{2,4},{3,5},{4,6},{5,7},{6,0},{7,1},{32,38},{33,39},{3... | collective-permute-start | bytes 614408 | tf_op jit(solution)/shard_map/ppermute | solution.py:235
  30.4 0.9 %copy-start.2 = (bf16[512,128]{1,0:T(8,128)(2,1)S(1)}, bf16[512,128]{1,0:T(8,128)(2,1)}, u32[]{:S(2)}) copy-start(bf16[512,128]{1,0:T(8,128)(2,1)} %encode.1.refs_0_) | copy-start | bytes 393220
  32.9 7.9 %collective-permute-start.7 = (bf16[800,128]{1,0:T(8,128)(2,1)S(1)}, bf16[800,128]{1,0:T(8,128)(2,1)S(1)}, u32[]{:S(2)}, u32[]{:S(2)}) collective-permute-start(bf16[800,128]{1,0:T(8,128)(2,1)S(1)} %collective-permute-done.2.refs_4_.refs_6_.refs_11_), channel_id=1, source_target_pairs={{0,1},{1,2},{2,3},{3,4},{4,5},{5,6},{6,7},{7,0},{32,39},{33,32},{3... | collective-permute-start | bytes 614408 | tf_op jit(solution)/shard_map/ppermute | solution.py:235
  33.2 7.6 %collective-permute-start.13 = (bf16[800,128]{1,0:T(8,128)(2,1)S(1)}, bf16[800,128]{1,0:T(8,128)(2,1)S(1)}, u32[]{:S(2)}, u32[]{:S(2)}) collective-permute-start(bf16[800,128]{1,0:T(8,128)(2,1)S(1)} %collective-permute-done.refs_2_.refs_4_.refs_7_), channel_id=1, source_target_pairs={{0,32},{32,0},{1,33},{33,1},{2,34},{34,2},{3,35},{35,3},{4,36},{36... | collective-permute-start | bytes 614408 | tf_op jit(solution)/shard_map/ppermute | solution.py:241
  33.9 7.5 %collective-permute-start.14 = (bf16[800,128]{1,0:T(8,128)(2,1)S(1)}, bf16[800,128]{1,0:T(8,128)(2,1)S(1)}, u32[]{:S(2)}, u32[]{:S(2)}) collective-permute-start(bf16[800,128]{1,0:T(8,128)(2,1)S(1)} %collective-permute-done.1.refs_3_.refs_5_), channel_id=1, source_target_pairs={{0,32},{32,0},{1,33},{33,1},{2,34},{34,2},{3,35},{35,3},{4,36},{36... | collective-permute-start | bytes 614408 | tf_op jit(solution)/shard_map/ppermute | solution.py:241
  38.0 3.6 %collective-permute-start.15 = (bf16[800,128]{1,0:T(8,128)(2,1)S(1)}, bf16[800,128]{1,0:T(8,128)(2,1)S(1)}, u32[]{:S(2)}, u32[]{:S(2)}) collective-permute-start(bf16[800,128]{1,0:T(8,128)(2,1)S(1)} %collective-permute-done.2.refs_4_.refs_6_.refs_11_), channel_id=1, source_target_pairs={{0,32},{32,0},{1,33},{33,1},{2,34},{34,2},{3,35},{35,3},{4,36},{36... | collective-permute-start | bytes 614408 | tf_op jit(solution)/shard_map/ppermute | solution.py:241
  40.0 1.7 %collective-permute-start.16 = (bf16[800,128]{1,0:T(8,128)(2,1)S(1)}, bf16[800,128]{1,0:T(8,128)(2,1)S(1)}, u32[]{:S(2)}, u32[]{:S(2)}) collective-permute-start(bf16[800,128]{1,0:T(8,128)(2,1)S(1)} %collective-permute-done.3.refs_5_.refs_7_.refs_9_), channel_id=1, source_target_pairs={{0,32},{32,0},{1,33},{33,1},{2,34},{34,2},{3,35},{35,3},{4,36},{36... | collective-permute-start | bytes 614408 | tf_op jit(solution)/shard_map/ppermute | solution.py:241
  40.8 4.5 %collective-permute-start.10 = (bf16[800,128]{1,0:T(8,128)(2,1)S(1)}, bf16[800,128]{1,0:T(8,128)(2,1)S(1)}, u32[]{:S(2)}, u32[]{:S(2)}) collective-permute-start(bf16[800,128]{1,0:T(8,128)(2,1)S(1)} %collective-permute-done.7.refs_4_), channel_id=1, source_target_pairs={{0,32},{32,0},{1,33},{33,1},{2,34},{34,2},{3,35},{35,3},{4,36},{36... | collective-permute-start | bytes 614408 | tf_op jit(solution)/shard_map/ppermute | solution.py:241
  40.8 4.5 %collective-permute-start.11 = (bf16[800,128]{1,0:T(8,128)(2,1)S(1)}, bf16[800,128]{1,0:T(8,128)(2,1)S(1)}, u32[]{:S(2)}, u32[]{:S(2)}) collective-permute-start(bf16[800,128]{1,0:T(8,128)(2,1)S(1)} %collective-permute-done.8.refs_5_), channel_id=1, source_target_pairs={{0,32},{32,0},{1,33},{33,1},{2,34},{34,2},{3,35},{35,3},{4,36},{36... | collective-permute-start | bytes 614408 | tf_op jit(solution)/shard_map/ppermute | solution.py:241
  41.3 4.0 %collective-permute-start.12 = (bf16[800,128]{1,0:T(8,128)(2,1)S(1)}, bf16[800,128]{1,0:T(8,128)(2,1)S(1)}, u32[]{:S(2)}, u32[]{:S(2)}) collective-permute-start(bf16[800,128]{1,0:T(8,128)(2,1)S(1)} %collective-permute-done.9.refs_6_), channel_id=1, source_target_pairs={{0,32},{32,0},{1,33},{33,1},{2,34},{34,2},{3,35},{35,3},{4,36},{36... | collective-permute-start | bytes 614408 | tf_op jit(solution)/shard_map/ppermute | solution.py:241
  50.7 5.3 %collective-permute-start.19 = (f32[32,128]{1,0:T(8,128)S(1)}, f32[32,128]{1,0:T(8,128)S(1)}, u32[]{:S(2)}, u32[]{:S(2)}) collective-permute-start(f32[32,128]{1,0:T(8,128)S(1)} %score_4_6.1.refs_0_), channel_id=1, source_target_pairs={{0,16},{8,24},{16,0},{24,8},{1,17},{9,25},{17,1},{25,9},{2,18},{10... | collective-permute-start | bytes 49160 | tf_op jit(solution)/shard_map/ppermute | solution.py:238
  51.4 4.6 %collective-permute-start.18 = (f32[32,128]{1,0:T(8,128)S(1)}, f32[32,128]{1,0:T(8,128)S(1)}, u32[]{:S(2)}, u32[]{:S(2)}) collective-permute-start(f32[32,128]{1,0:T(8,128)S(1)} %score_4_6.1.refs_0_), channel_id=1, source_target_pairs={{0,24},{8,0},{16,8},{24,16},{1,25},{9,1},{17,9},{25,17},{2,26},{10... | collective-permute-start | bytes 49160 | tf_op jit(solution)/shard_map/ppermute | solution.py:238
  54.0 4.9 %collective-permute-start.17 = (f32[32,128]{1,0:T(8,128)S(1)}, f32[32,128]{1,0:T(8,128)S(1)}, u32[]{:S(2)}, u32[]{:S(2)}) collective-permute-start(f32[32,128]{1,0:T(8,128)S(1)} %score_4_6.1.refs_0_), channel_id=1, source_target_pairs={{0,8},{8,16},{16,24},{24,0},{1,9},{9,17},{17,25},{25,1},{2,10},{10... | collective-permute-start | bytes 49160 | tf_op jit(solution)/shard_map/ppermute | solution.py:238

commit v9 on v8

--- a/solution.py
+++ b/solution.py
@@ -75,42 +75,46 @@
         out_specs=pl.BlockSpec((rows, proj.shape[1]), lambda j: (0, 0)),
         out_shape=jax.ShapeDtypeStruct((rows, proj.shape[1]), jnp.bfloat16),
         scratch_shapes=[pltpu.VMEM((rows, width), jnp.float32), pltpu.VMEM((rows, proj.shape[1]), jnp.float32)],
-        compiler_params=pltpu.CompilerParams(vmem_limit_bytes=60 << 20),
+        compiler_params=pltpu.CompilerParams(vmem_limit_bytes=36 << 20),
         cost_estimate=FREE,
         name="encode",
     )(tok, w_in, b_in, w_out, b_out, gain, shift, proj)
 
 
-def parcel_kernel(sizes, slots, counts, tiles, out, other, *, half):
-    count, length = tiles.shape[:2]
+VM = pl.BlockSpec(memory_space=pltpu.VMEM)
+
+
+def parcel_kernel(facts, tiles, out, other, *, half):
+    length = tiles.shape[1]
     core = lax.axis_index("core")
-    column = lax.broadcasted_iota(jnp.int32, tiles.shape[1:], 0)
+    column = lax.broadcasted_iota(jnp.int32, tiles.shape[1:], 0).astype(jnp.float32)
+    lane = lax.broadcasted_iota(jnp.int32, (1, 128), 1)
     for side, to in ((core, out), (1 - core, other)):
         for t in range(half):
             tile = tiles[side * half + t].astype(jnp.float32)
-            size = sizes[side * half + t]
+            size = jnp.sum(jnp.where(lane == side * half + t, facts[4:5, 0:128], 0.0), axis=1, keepdims=True)
             to[t * length : (t + 1) * length, :] = jnp.where(column < size, tile, tile[0:1, :]).astype(jnp.bfloat16)
-    order = lax.broadcasted_iota(jnp.int32, slots.shape, 0)
-    codes = jnp.where(order < counts[...], slots[...], count).astype(jnp.float32)
     lines = []
     for x in range(X):
-        lines += [codes[:, x * 128 : (x + 1) * 128], jnp.zeros((4, 128), jnp.float32)]
+        lines += [facts[0:4, x * 128 : (x + 1) * 128], jnp.zeros((4, 128), jnp.float32)]
     out[half * length : half * length + 8 * X, :] = jnp.concatenate(lines, axis=0).astype(jnp.bfloat16)
-
-
-VM = pl.BlockSpec(memory_space=pltpu.VMEM)
 
 
 def make_parcel(sizes, slots, counts, tiles):
     count, length, dims = tiles.shape
     half = count // CORES
+    order = jnp.arange(4, dtype=jnp.int32)[:, None]
+    codes = jnp.where(order < counts, slots, count)
+    facts = jnp.concatenate([codes, jnp.pad(sizes, (0, codes.shape[1] - count))[None, :]], axis=0).astype(jnp.float32)
     return pl.pallas_call(
         functools.partial(parcel_kernel, half=half),
-        in_specs=[pl.BlockSpec(memory_space=pltpu.SMEM), VM, VM, VM],
+        in_specs=[VM, VM],
         out_specs=[VM, VM],
         out_shape=[jax.ShapeDtypeStruct((half * length + r, dims), jnp.bfloat16) for r in (8 * X, 0)],
+        cost_estimate=pl.CostEstimate(flops=20_000_000_000, bytes_accessed=1000, transcendentals=0),
+        compiler_params=pltpu.CompilerParams(vmem_limit_bytes=46 << 20),
         name="parcel",
-    )(sizes, slots, counts, tiles)
+    )(facts, tiles)
 
 
 SENDER = (0, X - 1, 1, 2)

time: 60 us -> 60.4 us (level)
  Pallas kernels: 27.6 us -> 22.9 us
  waiting for transfers between devices: 7.25 us -> 10.8 us
  local copies, waits for them, and re-layouts: 0.9 us -> 1.69 us
  other arithmetic: 0 us -> 0.71 us
    ppermute x7, waiting for transfers between devices: 2.27 us -> 5.72 us  [along(): return lax.ppermute(a, ('core', 'z'), ways)]
    pallas_call x1, Pallas kernels: 10.1 us -> 7.09 us  [encode(): pl.pallas_call(functools.partial(ffn_kernel, queries=queries, tokens=toke...]
    pallas_call x1, Pallas kernels: 1.89 us -> 0.18 us  [make_parcel(): pl.pallas_call(functools.partial(parcel_kernel, half=half), in_specs=[VM,...]
    select_n x0 -> x1, other arithmetic: none -> 0.7 us  [make_parcel(): codes = jnp.where(order < counts, slots, count)]
    pad x0 -> x1, local copies, waits for them, and re-layouts: none -> 0.66 us  [make_parcel(): jnp.pad(sizes, (0, codes.shape[1] - count))[None, :]]
  transfers between devices with their start and end apart: 20 -> 20, of which waited for: 4 -> 9; matrix products, arithmetic and copies ran while one was open for 0% -> 0% of each run, Pallas kernels for 32% -> 27%
where the time goes in v9:
time: 60.4 us; the launch traced here: 60.2 us
  starting transfers between devices  23.9 us (40%)
  Pallas kernels  22.9 us (38%)
  waiting for transfers between devices  10.8 us (18%)
  local copies, waits for them, and re-layouts  1.69 us (3%)
  other arithmetic  0.71 us (1%)
    pallas_call x4, Pallas kernels, score(): pl.pallas_call(functools.partial(score_kernel, senders=tuple(blocks), ite...  14.7 us
    ppermute x7, starting transfers between devices, along(): return lax.ppermute(a, ('core', 'z'), ways)  13.9 us
    ppermute x6, starting transfers between devices, across(): return lax.ppermute(a, 'x', turn(X, k))  8.39 us
    pallas_call x1, Pallas kernels, encode(): pl.pallas_call(functools.partial(ffn_kernel, queries=queries, tokens=toke...  7.09 us
    ppermute x7, waiting for transfers between devices, along(): return lax.ppermute(a, ('core', 'z'), ways)  5.72 us
    ppermute x6, waiting for transfers between devices, across(): return lax.ppermute(a, 'x', turn(X, k))  4.95 us
    ppermute x7, starting transfers between devices, swap(): return lax.ppermute(a, 'core', turn(CORES, 1))  1.67 us
  transfers between devices with their start and end apart: 20, of which 9 were waited for; matrix products, arithmetic and copies ran while one was open for 0% of the time, Pallas kernels for 27%

profile of v9, /device:TPU:16, one launch (start us, length us, event | category | flops | bytes accessed | tf_op | source)
XLA Modules:
  0.0 60.2 jit_solution(3565853625465894176)
XLA Ops:
  0.0 0.7 %pad.4 = s32[512]{0:T(512)S(1)} pad(s32[12]{0:T(128)} %param.21, s32[]{:T(128)} %constant.1.clone.1), padding=0_500 | pad | bytes 2100 | tf_op jit(solution)/shard_map/jit(_pad)/pad | solution.py:108
  0.7 0.7 %bitcast_select_fusion = s32[4,512]{1,0:T(4,128)S(1)} fusion(s32[512,1,4]{0,2,1:T(4,128)} %param.22, s32[512]{0:T(512)} %bitcast.10), kind=kLoop, calls=%fused_computation.1 | loop fusion | flops 4096 | bytes 18432 | tf_op jit(solution)/shard_map/jit(_where)/select_n | solution.py:107
  1.4 0.0 copy-start.8
  1.4 1.0 %copy-done.8 = bf16[12,128,128]{2,1,0:T(8,128)(2,1)S(1)} copy-done((bf16[12,128,128]{2,1,0:T(8,128)(2,1)S(1)}, bf16[12,128,128]{2,1,0:T(8,128)(2,1)}, u32[]{:S(2)}) %copy-start.8) | copy-done | bytes 393240
  2.4 0.0 copy-start
  2.4 0.0 copy-start.4
  2.4 0.0 copy-start.5
  2.4 0.0 copy-start.6
  2.4 0.0 copy-start.7
  2.4 0.2 parcel.1
  2.6 6.4 %collective-permute-start.3 = (bf16[800,128]{1,0:T(8,128)(2,1)S(1)}, bf16[800,128]{1,0:T(8,128)(2,1)S(1)}, u32[]{:S(2)}, u32[]{:S(2)}) collective-permute-start(bf16[800,128]{1,0:T(8,128)(2,1)S(1)} %get-tuple-element.24.refs_1_.refs_3_), channel_id=1, source_target_pairs={{0,6},{1,7},{2,0},{3,1},{4,2},{5,3},{6,4},{7,5},{32,34},{33,35},{3... | collective-permute-start | bytes 614408 | tf_op jit(solution)/shard_map/ppermute | solution.py:239
  9.0 0.0 collective-permute-start.2
  9.0 3.7 %collective-permute-start.1 = (bf16[800,128]{1,0:T(8,128)(2,1)S(1)}, bf16[800,128]{1,0:T(8,128)(2,1)S(1)}, u32[]{:S(2)}, u32[]{:S(2)}) collective-permute-start(bf16[800,128]{1,0:T(8,128)(2,1)S(1)} %get-tuple-element.24.refs_1_.refs_3_), channel_id=1, source_target_pairs={{0,7},{1,0},{2,1},{3,2},{4,3},{5,4},{6,5},{7,6},{32,33},{33,34},{3... | collective-permute-start | bytes 614408 | tf_op jit(solution)/shard_map/ppermute | solution.py:239
  12.7 0.0 collective-permute-start
  12.7 0.0 copy-done
  12.7 0.0 copy-done.1
  12.7 0.0 copy-done.2
  12.7 0.0 copy-done.3
  12.7 0.0 copy-done.4
  12.7 0.0 copy-done.5
  12.7 0.0 copy-done.6
  12.7 0.0 copy-done.7
  12.8 7.1 %encode.1.refs_0_ = bf16[512,128]{1,0:T(8,128)(2,1)S(1)} custom-call(bf16[512,768]{1,0:T(8,128)(2,1)S(1)} %bitcast.8, bf16[768,3072]{1,0:T(8,128)(2,1)S(1)} %copy-done, f32[3072]{0:T(1024)S(1)} %copy-done.4, bf16[3072,768]{1,0:T(8,128)(2,1)S(1)} %copy-done.1, f32[768]{0:T(1024)S(1)} %copy-done.5, f32[768]{0:T(1024)S(1)} %copy-done.6, f32[768]{0:T(1024)S(1)} %copy-done.7, ...), custom_call_target="tpu_custom_call" | custom-call | flops 1000 | bytes 1000 | tf_op jit(solution)/shard_map/encode/pallas_call | solution.py:62
  19.9 0.0 collective-permute-done.3.refs_5_.refs_7_.refs_9_
  19.9 1.2 %collective-permute-done.2.refs_4_.refs_6_.refs_11_ = bf16[800,128]{1,0:T(8,128)(2,1)S(1)} collective-permute-done((bf16[800,128]{1,0:T(8,128)(2,1)S(1)}, bf16[800,128]{1,0:T(8,128)(2,1)S(1)}, u32[]{:S(2)}, u32[]{:S(2)}) %collective-permute-start.2) | collective-permute-done | bytes 204832 | tf_op jit(solution)/shard_map/ppermute | solution.py:239
  21.1 1.2 %collective-permute-done.1.refs_3_.refs_5_ = bf16[800,128]{1,0:T(8,128)(2,1)S(1)} collective-permute-done((bf16[800,128]{1,0:T(8,128)(2,1)S(1)}, bf16[800,128]{1,0:T(8,128)(2,1)S(1)}, u32[]{:S(2)}, u32[]{:S(2)}) %collective-permute-start.1) | collective-permute-done | bytes 204832 | tf_op jit(solution)/shard_map/ppermute | solution.py:239
  22.2 0.2 collective-permute-done.refs_2_.refs_4_.refs_7_
  22.4 3.0 %collective-permute-start.6 = (bf16[512,128]{1,0:T(8,128)(2,1)S(1)}, bf16[512,128]{1,0:T(8,128)(2,1)S(1)}, u32[]{:S(2)}, u32[]{:S(2)}) collective-permute-start(bf16[512,128]{1,0:T(8,128)(2,1)S(1)} %encode.1.refs_0_), channel_id=1, source_target_pairs={{0,16},{8,24},{16,0},{24,8},{1,17},{9,25},{17,1},{25,9},{2,18},{10... | collective-permute-start | bytes 393224 | tf_op jit(solution)/shard_map/ppermute | solution.py:242
  25.4 1.1 %collective-permute-start.5 = (bf16[512,128]{1,0:T(8,128)(2,1)S(1)}, bf16[512,128]{1,0:T(8,128)(2,1)S(1)}, u32[]{:S(2)}, u32[]{:S(2)}) collective-permute-start(bf16[512,128]{1,0:T(8,128)(2,1)S(1)} %encode.1.refs_0_), channel_id=1, source_target_pairs={{0,24},{8,0},{16,8},{24,16},{1,25},{9,1},{17,9},{25,17},{2,26},{10... | collective-permute-start | bytes 393224 | tf_op jit(solution)/shard_map/ppermute | solution.py:242
  26.6 0.9 %collective-permute-start.4 = (bf16[512,128]{1,0:T(8,128)(2,1)S(1)}, bf16[512,128]{1,0:T(8,128)(2,1)S(1)}, u32[]{:S(2)}, u32[]{:S(2)}) collective-permute-start(bf16[512,128]{1,0:T(8,128)(2,1)S(1)} %encode.1.refs_0_), channel_id=1, source_target_pairs={{0,8},{8,16},{16,24},{24,0},{1,9},{9,17},{17,25},{25,1},{2,10},{10... | collective-permute-start | bytes 393224 | tf_op jit(solution)/shard_map/ppermute | solution.py:242
  27.5 3.5 %collective-permute-start.8 = (bf16[800,128]{1,0:T(8,128)(2,1)S(1)}, bf16[800,128]{1,0:T(8,128)(2,1)S(1)}, u32[]{:S(2)}, u32[]{:S(2)}) collective-permute-start(bf16[800,128]{1,0:T(8,128)(2,1)S(1)} %collective-permute-done.3.refs_5_.refs_7_.refs_9_), channel_id=1, source_target_pairs={{0,7},{1,0},{2,1},{3,2},{4,3},{5,4},{6,5},{7,6},{32,33},{33,34},{3... | collective-permute-start | bytes 614408 | tf_op jit(solution)/shard_map/ppermute | solution.py:239
  30.9 0.0 collective-permute-start.9
  30.9 1.6 %score_1_6.1 = (f32[32,128]{1,0:T(8,128)S(1)}, bf16[512,128]{1,0:T(8,128)(2,1)S(1)}) custom-call(bf16[512,128]{1,0:T(8,128)(2,1)S(1)} %encode.1.refs_0_, bf16[800,128]{1,0:T(8,128)(2,1)S(1)} %get-tuple-element.24.refs_1_.refs_3_, bf16[800,128]{1,0:T(8,128)(2,1)S(1)} %collective-permute-done.refs_2_.refs_4_.refs_7_, ...), custom_call_target="tpu_custom_call" | custom-call | flops 1000 | bytes 1000 | tf_op jit(solution)/shard_map/score_1_6/pallas_call | solution.py:181
  32.6 0.0 collective-permute-done.6.refs_2_
  32.6 0.3 collective-permute-start.7
  32.9 0.0 collective-permute-done.5.refs_1_
  32.9 0.6 %collective-permute-start.13 = (bf16[800,128]{1,0:T(8,128)(2,1)S(1)}, bf16[800,128]{1,0:T(8,128)(2,1)S(1)}, u32[]{:S(2)}, u32[]{:S(2)}) collective-permute-start(bf16[800,128]{1,0:T(8,128)(2,1)S(1)} %collective-permute-done.refs_2_.refs_4_.refs_7_), channel_id=1, source_target_pairs={{0,32},{32,0},{1,33},{33,1},{2,34},{34,2},{3,35},{35,3},{4,36},{36... | collective-permute-start | bytes 614408 | tf_op jit(solution)/shard_map/ppermute | solution.py:245
  33.5 0.0 collective-permute-done.4.refs_0_
  33.5 0.1 collective-permute-start.14
  33.6 4.1 %score_3_6.1.refs_12_ = f32[32,128]{1,0:T(8,128)S(1)} custom-call(bf16[512,128]{1,0:T(8,128)(2,1)S(1)} %collective-permute-done.4.refs_0_, bf16[512,128]{1,0:T(8,128)(2,1)S(1)} %collective-permute-done.5.refs_1_, bf16[512,128]{1,0:T(8,128)(2,1)S(1)} %collective-permute-done.6.refs_2_, bf16[800,128]{1,0:T(8,128)(2,1)S(1)} %get-tuple-element.24.refs_1_.refs_3_, ...), custom_call_target="tpu_custom_call" | custom-call | flops 1000 | bytes 1000 | tf_op jit(solution)/shard_map/score_3_6/pallas_call | solution.py:181
  37.7 0.4 collective-permute-done.8.refs_5_
  38.1 0.1 collective-permute-start.15
  38.2 2.3 %collective-permute-done.9.refs_6_ = bf16[800,128]{1,0:T(8,128)(2,1)S(1)} collective-permute-done((bf16[800,128]{1,0:T(8,128)(2,1)S(1)}, bf16[800,128]{1,0:T(8,128)(2,1)S(1)}, u32[]{:S(2)}, u32[]{:S(2)}) %collective-permute-start.9) | collective-permute-done | bytes 204832 | tf_op jit(solution)/shard_map/ppermute | solution.py:239
  40.5 0.0 collective-permute-start.16
  40.5 0.5 collective-permute-done.7.refs_4_
  41.0 0.0 collective-permute-start.10
  41.0 0.0 collective-permute-done.13.refs_4_
  41.0 0.5 collective-permute-start.11
  41.5 0.0 collective-permute-done.14.refs_6_
  41.5 0.3 collective-permute-start.12
  41.8 0.0 collective-permute-done.15.refs_8_
  41.8 0.1 collective-permute-done.16.refs_10_
  42.0 3.7 %score_4_4.1.refs_10_ = f32[32,128]{1,0:T(8,128)S(1)} custom-call(bf16[512,128]{1,0:T(8,128)(2,1)S(1)} %collective-permute-done.4.refs_0_, bf16[512,128]{1,0:T(8,128)(2,1)S(1)} %collective-permute-done.5.refs_1_, bf16[512,128]{1,0:T(8,128)(2,1)S(1)} %collective-permute-done.6.refs_2_, bf16[512,128]{1,0:T(8,128)(2,1)S(1)} %get-tuple-element.32.refs_3_, ...), custom_call_target="tpu_custom_call" | custom-call | flops 1000 | bytes 1000 | tf_op jit(solution)/shard_map/score_4_4/pallas_call | solution.py:181
  45.6 0.0 collective-permute-done.10.refs_7_
  45.6 0.0 collective-permute-done.11.refs_8_
  45.7 0.0 collective-permute-done.12.refs_9_
  45.7 5.3 %score_4_6.1.refs_0_ = f32[32,128]{1,0:T(8,128)S(1)} custom-call(bf16[512,128]{1,0:T(8,128)(2,1)S(1)} %collective-permute-done.4.refs_0_, bf16[512,128]{1,0:T(8,128)(2,1)S(1)} %collective-permute-done.5.refs_1_, bf16[512,128]{1,0:T(8,128)(2,1)S(1)} %collective-permute-done.6.refs_2_, bf16[512,128]{1,0:T(8,128)(2,1)S(1)} %get-tuple-element.32.refs_3_, ...), custom_call_target="tpu_custom_call" | custom-call | flops 1000 | bytes 1000 | tf_op jit(solution)/shard_map/score_4_6/pallas_call | solution.py:181
  51.0 0.7 %collective-permute-start.19 = (f32[32,128]{1,0:T(8,128)S(1)}, f32[32,128]{1,0:T(8,128)S(1)}, u32[]{:S(2)}, u32[]{:S(2)}) collective-permute-start(f32[32,128]{1,0:T(8,128)S(1)} %score_4_6.1.refs_0_), channel_id=1, source_target_pairs={{0,16},{8,24},{16,0},{24,8},{1,17},{9,25},{17,1},{25,9},{2,18},{10... | collective-permute-start | bytes 49160 | tf_op jit(solution)/shard_map/ppermute | solution.py:242
  51.7 2.6 %collective-permute-start.18 = (f32[32,128]{1,0:T(8,128)S(1)}, f32[32,128]{1,0:T(8,128)S(1)}, u32[]{:S(2)}, u32[]{:S(2)}) collective-permute-start(f32[32,128]{1,0:T(8,128)S(1)} %score_4_6.1.refs_0_), channel_id=1, source_target_pairs={{0,24},{8,0},{16,8},{24,16},{1,25},{9,1},{17,9},{25,17},{2,26},{10... | collective-permute-start | bytes 49160 | tf_op jit(solution)/shard_map/ppermute | solution.py:242
  54.3 0.0 collective-permute-start.17
  54.3 2.0 %collective-permute-done.19.refs_3_ = f32[32,128]{1,0:T(8,128)S(1)} collective-permute-done((f32[32,128]{1,0:T(8,128)S(1)}, f32[32,128]{1,0:T(8,128)S(1)}, u32[]{:S(2)}, u32[]{:S(2)}) %collective-permute-start.19) | collective-permute-done | bytes 16416 | tf_op jit(solution)/shard_map/ppermute | solution.py:242
  56.3 0.0 collective-permute-done.18.refs_2_
  56.3 3.0 %collective-permute-done.17.refs_1_ = f32[32,128]{1,0:T(8,128)S(1)} collective-permute-done((f32[32,128]{1,0:T(8,128)S(1)}, f32[32,128]{1,0:T(8,128)S(1)}, u32[]{:S(2)}, u32[]{:S(2)}) %collective-permute-start.17) | collective-permute-done | bytes 16416 | tf_op jit(solution)/shard_map/ppermute | solution.py:242
  59.3 0.9 %finish.1 = f32[16,4,32]{2,1,0:T(4,128)} custom-call(f32[32,128]{1,0:T(8,128)S(1)} %score_4_6.1.refs_0_, f32[32,128]{1,0:T(8,128)S(1)} %collective-permute-done.17.refs_1_, f32[32,128]{1,0:T(8,128)S(1)} %collective-permute-done.18.refs_2_, f32[32,128]{1,0:T(8,128)S(1)} %collective-permute-done.19.refs_3_), custom_call_target="tpu_custom_call" | custom-call | tf_op jit(solution)/shard_map/finish/pallas_call | solution.py:216
  (4 shorter events, 0.0 us)
Async XLA Ops:
  1.4 1.0 %copy-start.8 = (bf16[12,128,128]{2,1,0:T(8,128)(2,1)S(1)}, bf16[12,128,128]{2,1,0:T(8,128)(2,1)}, u32[]{:S(2)}) copy-start(bf16[12,128,128]{2,1,0:T(8,128)(2,1)} %tiles.1) | copy-start | bytes 1179652
  2.4 10.3 %copy-start = (bf16[768,3072]{1,0:T(8,128)(2,1)S(1)}, bf16[768,3072]{1,0:T(8,128)(2,1)}, u32[]{:S(2)}) copy-start(bf16[768,3072]{1,0:T(8,128)(2,1)} %w_in.1) | copy-start | bytes 14155780
  2.4 10.3 %copy-start.1 = (bf16[3072,768]{1,0:T(8,128)(2,1)S(1)}, bf16[3072,768]{1,0:T(8,128)(2,1)}, u32[]{:S(2)}) copy-start(bf16[3072,768]{1,0:T(8,128)(2,1)} %w_out.1) | copy-start | bytes 14155780
  2.4 10.3 %copy-start.2 = (bf16[16,32,768]{2,1,0:T(8,128)(2,1)S(1)}, bf16[16,32,768]{2,1,0:T(8,128)(2,1)}, u32[]{:S(2)}) copy-start(bf16[16,32,768]{2,1,0:T(8,128)(2,1)} %param.12) | copy-start | bytes 2359300
  2.4 10.3 %copy-start.3 = (bf16[768,128]{1,0:T(8,128)(2,1)S(1)}, bf16[768,128]{1,0:T(8,128)(2,1)}, u32[]{:S(2)}) copy-start(bf16[768,128]{1,0:T(8,128)(2,1)} %proj.1) | copy-start | bytes 589828
  2.4 10.3 %copy-start.4 = (f32[3072]{0:T(1024)S(1)}, f32[3072]{0:T(1024)}, u32[]{:S(2)}) copy-start(f32[3072]{0:T(1024)} %b_in.1) | copy-start | bytes 36868
  2.4 10.3 %copy-start.5 = (f32[768]{0:T(1024)S(1)}, f32[768]{0:T(1024)}, u32[]{:S(2)}) copy-start(f32[768]{0:T(1024)} %b_out.1) | copy-start | bytes 9220
  2.4 10.3 %copy-start.6 = (f32[768]{0:T(1024)S(1)}, f32[768]{0:T(1024)}, u32[]{:S(2)}) copy-start(f32[768]{0:T(1024)} %gain.1) | copy-start | bytes 9220
  2.4 10.3 %copy-start.7 = (f32[768]{0:T(1024)S(1)}, f32[768]{0:T(1024)}, u32[]{:S(2)}) copy-start(f32[768]{0:T(1024)} %shift.1) | copy-start | bytes 9220
  2.6 17.2 %collective-permute-start.3 = (bf16[800,128]{1,0:T(8,128)(2,1)S(1)}, bf16[800,128]{1,0:T(8,128)(2,1)S(1)}, u32[]{:S(2)}, u32[]{:S(2)}) collective-permute-start(bf16[800,128]{1,0:T(8,128)(2,1)S(1)} %get-tuple-element.24.refs_1_.refs_3_), channel_id=1, source_target_pairs={{0,6},{1,7},{2,0},{3,1},{4,2},{5,3},{6,4},{7,5},{32,34},{33,35},{3... | collective-permute-start | bytes 614408 | tf_op jit(solution)/shard_map/ppermute | solution.py:239
  9.0 12.1 %collective-permute-start.2 = (bf16[800,128]{1,0:T(8,128)(2,1)S(1)}, bf16[800,128]{1,0:T(8,128)(2,1)S(1)}, u32[]{:S(2)}, u32[]{:S(2)}) collective-permute-start(bf16[800,128]{1,0:T(8,128)(2,1)S(1)} %get-tuple-element.24.refs_1_.refs_3_), channel_id=1, source_target_pairs={{0,2},{1,3},{2,4},{3,5},{4,6},{5,7},{6,0},{7,1},{32,38},{33,39},{3... | collective-permute-start | bytes 614408 | tf_op jit(solution)/shard_map/ppermute | solution.py:239
  9.0 13.2 %collective-permute-start.1 = (bf16[800,128]{1,0:T(8,128)(2,1)S(1)}, bf16[800,128]{1,0:T(8,128)(2,1)S(1)}, u32[]{:S(2)}, u32[]{:S(2)}) collective-permute-start(bf16[800,128]{1,0:T(8,128)(2,1)S(1)} %get-tuple-element.24.refs_1_.refs_3_), channel_id=1, source_target_pairs={{0,7},{1,0},{2,1},{3,2},{4,3},{5,4},{6,5},{7,6},{32,33},{33,34},{3... | collective-permute-start | bytes 614408 | tf_op jit(solution)/shard_map/ppermute | solution.py:239
  12.7 9.7 %collective-permute-start = (bf16[800,128]{1,0:T(8,128)(2,1)S(1)}, bf16[800,128]{1,0:T(8,128)(2,1)S(1)}, u32[]{:S(2)}, u32[]{:S(2)}) collective-permute-start(bf16[800,128]{1,0:T(8,128)(2,1)S(1)} %get-tuple-element.24.refs_1_.refs_3_), channel_id=1, source_target_pairs={{0,1},{1,2},{2,3},{3,4},{4,5},{5,6},{6,7},{7,0},{32,39},{33,32},{3... | collective-permute-start | bytes 614408 | tf_op jit(solution)/shard_map/ppermute | solution.py:239
  22.4 10.2 %collective-permute-start.6 = (bf16[512,128]{1,0:T(8,128)(2,1)S(1)}, bf16[512,128]{1,0:T(8,128)(2,1)S(1)}, u32[]{:S(2)}, u32[]{:S(2)}) collective-permute-start(bf16[512,128]{1,0:T(8,128)(2,1)S(1)} %encode.1.refs_0_), channel_id=1, source_target_pairs={{0,16},{8,24},{16,0},{24,8},{1,17},{9,25},{17,1},{25,9},{2,18},{10... | collective-permute-start | bytes 393224 | tf_op jit(solution)/shard_map/ppermute | solution.py:242
  25.4 7.5 %collective-permute-start.5 = (bf16[512,128]{1,0:T(8,128)(2,1)S(1)}, bf16[512,128]{1,0:T(8,128)(2,1)S(1)}, u32[]{:S(2)}, u32[]{:S(2)}) collective-permute-start(bf16[512,128]{1,0:T(8,128)(2,1)S(1)} %encode.1.refs_0_), channel_id=1, source_target_pairs={{0,24},{8,0},{16,8},{24,16},{1,25},{9,1},{17,9},{25,17},{2,26},{10... | collective-permute-start | bytes 393224 | tf_op jit(solution)/shard_map/ppermute | solution.py:242
  26.6 6.9 %collective-permute-start.4 = (bf16[512,128]{1,0:T(8,128)(2,1)S(1)}, bf16[512,128]{1,0:T(8,128)(2,1)S(1)}, u32[]{:S(2)}, u32[]{:S(2)}) collective-permute-start(bf16[512,128]{1,0:T(8,128)(2,1)S(1)} %encode.1.refs_0_), channel_id=1, source_target_pairs={{0,8},{8,16},{16,24},{24,0},{1,9},{9,17},{17,25},{25,1},{2,10},{10... | collective-permute-start | bytes 393224 | tf_op jit(solution)/shard_map/ppermute | solution.py:242
  27.5 10.6 %collective-permute-start.8 = (bf16[800,128]{1,0:T(8,128)(2,1)S(1)}, bf16[800,128]{1,0:T(8,128)(2,1)S(1)}, u32[]{:S(2)}, u32[]{:S(2)}) collective-permute-start(bf16[800,128]{1,0:T(8,128)(2,1)S(1)} %collective-permute-done.3.refs_5_.refs_7_.refs_9_), channel_id=1, source_target_pairs={{0,7},{1,0},{2,1},{3,2},{4,3},{5,4},{6,5},{7,6},{32,33},{33,34},{3... | collective-permute-start | bytes 614408 | tf_op jit(solution)/shard_map/ppermute | solution.py:239
  30.9 9.6 %collective-permute-start.9 = (bf16[800,128]{1,0:T(8,128)(2,1)S(1)}, bf16[800,128]{1,0:T(8,128)(2,1)S(1)}, u32[]{:S(2)}, u32[]{:S(2)}) collective-permute-start(bf16[800,128]{1,0:T(8,128)(2,1)S(1)} %collective-permute-done.2.refs_4_.refs_6_.refs_11_), channel_id=1, source_target_pairs={{0,2},{1,3},{2,4},{3,5},{4,6},{5,7},{6,0},{7,1},{32,38},{33,39},{3... | collective-permute-start | bytes 614408 | tf_op jit(solution)/shard_map/ppermute | solution.py:239
  32.6 8.4 %collective-permute-start.7 = (bf16[800,128]{1,0:T(8,128)(2,1)S(1)}, bf16[800,128]{1,0:T(8,128)(2,1)S(1)}, u32[]{:S(2)}, u32[]{:S(2)}) collective-permute-start(bf16[800,128]{1,0:T(8,128)(2,1)S(1)} %collective-permute-done.2.refs_4_.refs_6_.refs_11_), channel_id=1, source_target_pairs={{0,1},{1,2},{2,3},{3,4},{4,5},{5,6},{6,7},{7,0},{32,39},{33,32},{3... | collective-permute-start | bytes 614408 | tf_op jit(solution)/shard_map/ppermute | solution.py:239
  32.9 8.1 %collective-permute-start.13 = (bf16[800,128]{1,0:T(8,128)(2,1)S(1)}, bf16[800,128]{1,0:T(8,128)(2,1)S(1)}, u32[]{:S(2)}, u32[]{:S(2)}) collective-permute-start(bf16[800,128]{1,0:T(8,128)(2,1)S(1)} %collective-permute-done.refs_2_.refs_4_.refs_7_), channel_id=1, source_target_pairs={{0,32},{32,0},{1,33},{33,1},{2,34},{34,2},{3,35},{35,3},{4,36},{36... | collective-permute-start | bytes 614408 | tf_op jit(solution)/shard_map/ppermute | solution.py:245
  33.5 8.0 %collective-permute-start.14 = (bf16[800,128]{1,0:T(8,128)(2,1)S(1)}, bf16[800,128]{1,0:T(8,128)(2,1)S(1)}, u32[]{:S(2)}, u32[]{:S(2)}) collective-permute-start(bf16[800,128]{1,0:T(8,128)(2,1)S(1)} %collective-permute-done.1.refs_3_.refs_5_), channel_id=1, source_target_pairs={{0,32},{32,0},{1,33},{33,1},{2,34},{34,2},{3,35},{35,3},{4,36},{36... | collective-permute-start | bytes 614408 | tf_op jit(solution)/shard_map/ppermute | solution.py:245
  38.1 3.8 %collective-permute-start.15 = (bf16[800,128]{1,0:T(8,128)(2,1)S(1)}, bf16[800,128]{1,0:T(8,128)(2,1)S(1)}, u32[]{:S(2)}, u32[]{:S(2)}) collective-permute-start(bf16[800,128]{1,0:T(8,128)(2,1)S(1)} %collective-permute-done.2.refs_4_.refs_6_.refs_11_), channel_id=1, source_target_pairs={{0,32},{32,0},{1,33},{33,1},{2,34},{34,2},{3,35},{35,3},{4,36},{36... | collective-permute-start | bytes 614408 | tf_op jit(solution)/shard_map/ppermute | solution.py:245
  40.5 1.5 %collective-permute-start.16 = (bf16[800,128]{1,0:T(8,128)(2,1)S(1)}, bf16[800,128]{1,0:T(8,128)(2,1)S(1)}, u32[]{:S(2)}, u32[]{:S(2)}) collective-permute-start(bf16[800,128]{1,0:T(8,128)(2,1)S(1)} %collective-permute-done.3.refs_5_.refs_7_.refs_9_), channel_id=1, source_target_pairs={{0,32},{32,0},{1,33},{33,1},{2,34},{34,2},{3,35},{35,3},{4,36},{36... | collective-permute-start | bytes 614408 | tf_op jit(solution)/shard_map/ppermute | solution.py:245
  41.0 4.6 %collective-permute-start.10 = (bf16[800,128]{1,0:T(8,128)(2,1)S(1)}, bf16[800,128]{1,0:T(8,128)(2,1)S(1)}, u32[]{:S(2)}, u32[]{:S(2)}) collective-permute-start(bf16[800,128]{1,0:T(8,128)(2,1)S(1)} %collective-permute-done.7.refs_4_), channel_id=1, source_target_pairs={{0,32},{32,0},{1,33},{33,1},{2,34},{34,2},{3,35},{35,3},{4,36},{36... | collective-permute-start | bytes 614408 | tf_op jit(solution)/shard_map/ppermute | solution.py:245
  41.0 4.6 %collective-permute-start.11 = (bf16[800,128]{1,0:T(8,128)(2,1)S(1)}, bf16[800,128]{1,0:T(8,128)(2,1)S(1)}, u32[]{:S(2)}, u32[]{:S(2)}) collective-permute-start(bf16[800,128]{1,0:T(8,128)(2,1)S(1)} %collective-permute-done.8.refs_5_), channel_id=1, source_target_pairs={{0,32},{32,0},{1,33},{33,1},{2,34},{34,2},{3,35},{35,3},{4,36},{36... | collective-permute-start | bytes 614408 | tf_op jit(solution)/shard_map/ppermute | solution.py:245
  41.5 4.1 %collective-permute-start.12 = (bf16[800,128]{1,0:T(8,128)(2,1)S(1)}, bf16[800,128]{1,0:T(8,128)(2,1)S(1)}, u32[]{:S(2)}, u32[]{:S(2)}) collective-permute-start(bf16[800,128]{1,0:T(8,128)(2,1)S(1)} %collective-permute-done.9.refs_6_), channel_id=1, source_target_pairs={{0,32},{32,0},{1,33},{33,1},{2,34},{34,2},{3,35},{35,3},{4,36},{36... | collective-permute-start | bytes 614408 | tf_op jit(solution)/shard_map/ppermute | solution.py:245
  51.0 5.3 %collective-permute-start.19 = (f32[32,128]{1,0:T(8,128)S(1)}, f32[32,128]{1,0:T(8,128)S(1)}, u32[]{:S(2)}, u32[]{:S(2)}) collective-permute-start(f32[32,128]{1,0:T(8,128)S(1)} %score_4_6.1.refs_0_), channel_id=1, source_target_pairs={{0,16},{8,24},{16,0},{24,8},{1,17},{9,25},{17,1},{25,9},{2,18},{10... | collective-permute-start | bytes 49160 | tf_op jit(solution)/shard_map/ppermute | solution.py:242
  51.7 4.6 %collective-permute-start.18 = (f32[32,128]{1,0:T(8,128)S(1)}, f32[32,128]{1,0:T(8,128)S(1)}, u32[]{:S(2)}, u32[]{:S(2)}) collective-permute-start(f32[32,128]{1,0:T(8,128)S(1)} %score_4_6.1.refs_0_), channel_id=1, source_target_pairs={{0,24},{8,0},{16,8},{24,16},{1,25},{9,1},{17,9},{25,17},{2,26},{10... | collective-permute-start | bytes 49160 | tf_op jit(solution)/shard_map/ppermute | solution.py:242
  54.3 4.9 %collective-permute-start.17 = (f32[32,128]{1,0:T(8,128)S(1)}, f32[32,128]{1,0:T(8,128)S(1)}, u32[]{:S(2)}, u32[]{:S(2)}) collective-permute-start(f32[32,128]{1,0:T(8,128)S(1)} %score_4_6.1.refs_0_), channel_id=1, source_target_pairs={{0,8},{8,16},{16,24},{24,0},{1,9},{9,17},{17,25},{25,1},{2,10},{10... | collective-permute-start | bytes 49160 | tf_op jit(solution)/shard_map/ppermute | solution.py:242

commit v10 on v9

--- a/solution.py
+++ b/solution.py
@@ -248,7 +248,8 @@
     far = {0: own_far}
     flat, _ = tied(tokens.reshape(queries * query_len, width), own)
     embeds = encode(flat, w_in, b_in, w_out, b_out, gain, shift, proj, queries, query_len)
-    near[1], near[-1], near[2], near[-2], embeds = tied(near[1], near[-1], near[2], near[-2], embeds)
+    near[2], near[-2], embeds = tied(near[2], near[-2], embeds)
+    near[1], near[-1], near[2], near[-2] = tied(near[1], near[-1], near[2], near[-2])
     near[3], near[-3], near[4] = along(near[2], 1), along(near[-2], -1), along(near[2], 2)
     blocks = {i: across(embeds, k) for i, k in ((1, 1), (2, -1), (3, 2))} | {0: embeds}
     args = (half, length, queries)

time: 60.4 us -> 58.2 us (0.964)
  starting transfers between devices: 23.9 us -> 22.1 us
    ppermute x7, waiting for transfers between devices: 5.72 us -> 4.55 us  [along(): return lax.ppermute(a, ('core', 'z'), ways)]
    ppermute x7, starting transfers between devices: 13.9 us -> 12.8 us  [along(): return lax.ppermute(a, ('core', 'z'), ways)]
    ppermute x6, waiting for transfers between devices: 4.95 us -> 5.89 us  [across(): return lax.ppermute(a, 'x', turn(X, k))]
    ppermute x7, starting transfers between devices: 1.67 us -> 0.93 us  [swap(): return lax.ppermute(a, 'core', turn(CORES, 1))]
  transfers between devices with their start and end apart: 20 -> 20, of which waited for: 9 -> 7; matrix products, arithmetic and copies ran while one was open for 0% -> 0% of each run, Pallas kernels for 27% -> 28%
where the time goes in v10:
time: 58.2 us; the launch traced here: 58 us
  Pallas kernels  22.9 us (39%)
  starting transfers between devices  22.1 us (38%)
  waiting for transfers between devices  10.5 us (18%)
  local copies, waits for them, and re-layouts  1.69 us (3%)
  other arithmetic  0.71 us (1%)
    pallas_call x4, Pallas kernels, score(): pl.pallas_call(functools.partial(score_kernel, senders=tuple(blocks), ite...  14.7 us
    ppermute x7, starting transfers between devices, along(): return lax.ppermute(a, ('core', 'z'), ways)  12.8 us
    ppermute x6, starting transfers between devices, across(): return lax.ppermute(a, 'x', turn(X, k))  8.4 us
    pallas_call x1, Pallas kernels, encode(): pl.pallas_call(functools.partial(ffn_kernel, queries=queries, tokens=toke...  7.09 us
    ppermute x6, waiting for transfers between devices, across(): return lax.ppermute(a, 'x', turn(X, k))  5.89 us
    ppermute x7, waiting for transfers between devices, along(): return lax.ppermute(a, ('core', 'z'), ways)  4.55 us
  transfers between devices with their start and end apart: 20, of which 7 were waited for; matrix products, arithmetic and copies ran while one was open for 0% of the time, Pallas kernels for 28%

profile of v10, /device:TPU:16, one launch (start us, length us, event | category | flops | bytes accessed | tf_op | source)
XLA Modules:
  0.0 58.0 jit_solution(7073919060745662261)
XLA Ops:
  0.0 0.7 %pad.4 = s32[512]{0:T(512)S(1)} pad(s32[12]{0:T(128)} %param.21, s32[]{:T(128)} %constant.1.clone.1), padding=0_500 | pad | bytes 2100 | tf_op jit(solution)/shard_map/jit(_pad)/pad | solution.py:108
  0.7 0.7 %bitcast_select_fusion = s32[4,512]{1,0:T(4,128)S(1)} fusion(s32[512,1,4]{0,2,1:T(4,128)} %param.22, s32[512]{0:T(512)} %bitcast.10), kind=kLoop, calls=%fused_computation.1 | loop fusion | flops 4096 | bytes 18432 | tf_op jit(solution)/shard_map/jit(_where)/select_n | solution.py:107
  1.4 0.0 copy-start.8
  1.4 1.0 %copy-done.8 = bf16[12,128,128]{2,1,0:T(8,128)(2,1)S(1)} copy-done((bf16[12,128,128]{2,1,0:T(8,128)(2,1)S(1)}, bf16[12,128,128]{2,1,0:T(8,128)(2,1)}, u32[]{:S(2)}) %copy-start.8) | copy-done | bytes 393240
  2.4 0.0 copy-start
  2.4 0.0 copy-start.4
  2.4 0.0 copy-start.5
  2.4 0.0 copy-start.6
  2.4 0.0 copy-start.7
  2.4 0.2 parcel.1
  2.6 6.4 %collective-permute-start.1 = (bf16[800,128]{1,0:T(8,128)(2,1)S(1)}, bf16[800,128]{1,0:T(8,128)(2,1)S(1)}, u32[]{:S(2)}, u32[]{:S(2)}) collective-permute-start(bf16[800,128]{1,0:T(8,128)(2,1)S(1)} %get-tuple-element.26.refs_1_.refs_3_), channel_id=1, source_target_pairs={{0,6},{1,7},{2,0},{3,1},{4,2},{5,3},{6,4},{7,5},{32,34},{33,35},{3... | collective-permute-start | bytes 614408 | tf_op jit(solution)/shard_map/ppermute | solution.py:239
  9.0 0.0 collective-permute-start
  9.0 3.7 %collective-permute-start.6 = (bf16[800,128]{1,0:T(8,128)(2,1)S(1)}, bf16[800,128]{1,0:T(8,128)(2,1)S(1)}, u32[]{:S(2)}, u32[]{:S(2)}) collective-permute-start(bf16[800,128]{1,0:T(8,128)(2,1)S(1)} %get-tuple-element.26.refs_1_.refs_3_), channel_id=1, source_target_pairs={{0,7},{1,0},{2,1},{3,2},{4,3},{5,4},{6,5},{7,6},{32,33},{33,34},{3... | collective-permute-start | bytes 614408 | tf_op jit(solution)/shard_map/ppermute | solution.py:239
  12.7 0.0 collective-permute-start.5
  12.7 0.0 copy-done
  12.7 0.0 copy-done.1
  12.7 0.0 copy-done.2
  12.7 0.0 copy-done.3
  12.7 0.0 copy-done.4
  12.7 0.0 copy-done.5
  12.7 0.0 copy-done.6
  12.7 0.0 copy-done.7
  12.8 7.1 %encode.1.refs_0_ = bf16[512,128]{1,0:T(8,128)(2,1)S(1)} custom-call(bf16[512,768]{1,0:T(8,128)(2,1)S(1)} %bitcast.8, bf16[768,3072]{1,0:T(8,128)(2,1)S(1)} %copy-done, f32[3072]{0:T(1024)S(1)} %copy-done.4, bf16[3072,768]{1,0:T(8,128)(2,1)S(1)} %copy-done.1, f32[768]{0:T(1024)S(1)} %copy-done.5, f32[768]{0:T(1024)S(1)} %copy-done.6, f32[768]{0:T(1024)S(1)} %copy-done.7, ...), custom_call_target="tpu_custom_call" | custom-call | flops 1000 | bytes 1000 | tf_op jit(solution)/shard_map/encode/pallas_call | solution.py:62
  19.9 0.0 collective-permute-done.1.refs_5_.refs_7_.refs_9_
  19.9 1.2 %collective-permute-done.refs_4_.refs_6_.refs_11_ = bf16[800,128]{1,0:T(8,128)(2,1)S(1)} collective-permute-done((bf16[800,128]{1,0:T(8,128)(2,1)S(1)}, bf16[800,128]{1,0:T(8,128)(2,1)S(1)}, u32[]{:S(2)}, u32[]{:S(2)}) %collective-permute-start) | collective-permute-done | bytes 204832 | tf_op jit(solution)/shard_map/ppermute | solution.py:239
  21.1 3.0 %collective-permute-start.4 = (bf16[512,128]{1,0:T(8,128)(2,1)S(1)}, bf16[512,128]{1,0:T(8,128)(2,1)S(1)}, u32[]{:S(2)}, u32[]{:S(2)}) collective-permute-start(bf16[512,128]{1,0:T(8,128)(2,1)S(1)} %encode.1.refs_0_), channel_id=1, source_target_pairs={{0,16},{8,24},{16,0},{24,8},{1,17},{9,25},{17,1},{25,9},{2,18},{10... | collective-permute-start | bytes 393224 | tf_op jit(solution)/shard_map/ppermute | solution.py:242
  24.1 1.1 %collective-permute-start.3 = (bf16[512,128]{1,0:T(8,128)(2,1)S(1)}, bf16[512,128]{1,0:T(8,128)(2,1)S(1)}, u32[]{:S(2)}, u32[]{:S(2)}) collective-permute-start(bf16[512,128]{1,0:T(8,128)(2,1)S(1)} %encode.1.refs_0_), channel_id=1, source_target_pairs={{0,24},{8,0},{16,8},{24,16},{1,25},{9,1},{17,9},{25,17},{2,26},{10... | collective-permute-start | bytes 393224 | tf_op jit(solution)/shard_map/ppermute | solution.py:242
  25.2 0.9 %collective-permute-start.2 = (bf16[512,128]{1,0:T(8,128)(2,1)S(1)}, bf16[512,128]{1,0:T(8,128)(2,1)S(1)}, u32[]{:S(2)}, u32[]{:S(2)}) collective-permute-start(bf16[512,128]{1,0:T(8,128)(2,1)S(1)} %encode.1.refs_0_), channel_id=1, source_target_pairs={{0,8},{8,16},{16,24},{24,0},{1,9},{9,17},{17,25},{25,1},{2,10},{10... | collective-permute-start | bytes 393224 | tf_op jit(solution)/shard_map/ppermute | solution.py:242
  26.1 0.0 collective-permute-done.6.refs_3_.refs_5_
  26.1 0.0 collective-permute-done.5.refs_2_.refs_4_.refs_7_
  26.1 2.1 %collective-permute-start.8 = (bf16[800,128]{1,0:T(8,128)(2,1)S(1)}, bf16[800,128]{1,0:T(8,128)(2,1)S(1)}, u32[]{:S(2)}, u32[]{:S(2)}) collective-permute-start(bf16[800,128]{1,0:T(8,128)(2,1)S(1)} %collective-permute-done.1.refs_5_.refs_7_.refs_9_), channel_id=1, source_target_pairs={{0,7},{1,0},{2,1},{3,2},{4,3},{5,4},{6,5},{7,6},{32,33},{33,34},{3... | collective-permute-start | bytes 614408 | tf_op jit(solution)/shard_map/ppermute | solution.py:239
  28.2 0.0 collective-permute-start.9
  28.2 1.6 %score_1_6.1 = (f32[32,128]{1,0:T(8,128)S(1)}, bf16[512,128]{1,0:T(8,128)(2,1)S(1)}) custom-call(bf16[512,128]{1,0:T(8,128)(2,1)S(1)} %encode.1.refs_0_, bf16[800,128]{1,0:T(8,128)(2,1)S(1)} %get-tuple-element.26.refs_1_.refs_3_, bf16[800,128]{1,0:T(8,128)(2,1)S(1)} %collective-permute-done.5.refs_2_.refs_4_.refs_7_, ...), custom_call_target="tpu_custom_call" | custom-call | flops 1000 | bytes 1000 | tf_op jit(solution)/shard_map/score_1_6/pallas_call | solution.py:181
  29.9 0.0 collective-permute-done.4.refs_2_
  29.9 0.6 %collective-permute-start.7 = (bf16[800,128]{1,0:T(8,128)(2,1)S(1)}, bf16[800,128]{1,0:T(8,128)(2,1)S(1)}, u32[]{:S(2)}, u32[]{:S(2)}) collective-permute-start(bf16[800,128]{1,0:T(8,128)(2,1)S(1)} %collective-permute-done.refs_4_.refs_6_.refs_11_), channel_id=1, source_target_pairs={{0,1},{1,2},{2,3},{3,4},{4,5},{5,6},{6,7},{7,0},{32,39},{33,32},{3... | collective-permute-start | bytes 614408 | tf_op jit(solution)/shard_map/ppermute | solution.py:239
  30.5 0.0 collective-permute-done.3.refs_1_
  30.5 0.0 collective-permute-start.13
  30.5 0.9 %collective-permute-done.2.refs_0_ = bf16[512,128]{1,0:T(8,128)(2,1)S(1)} collective-permute-done((bf16[512,128]{1,0:T(8,128)(2,1)S(1)}, bf16[512,128]{1,0:T(8,128)(2,1)S(1)}, u32[]{:S(2)}, u32[]{:S(2)}) %collective-permute-start.2) | collective-permute-done | bytes 131104 | tf_op jit(solution)/shard_map/ppermute | solution.py:242
  31.4 0.0 collective-permute-start.14
  31.4 4.1 %score_3_6.1.refs_12_ = f32[32,128]{1,0:T(8,128)S(1)} custom-call(bf16[512,128]{1,0:T(8,128)(2,1)S(1)} %collective-permute-done.2.refs_0_, bf16[512,128]{1,0:T(8,128)(2,1)S(1)} %collective-permute-done.3.refs_1_, bf16[512,128]{1,0:T(8,128)(2,1)S(1)} %collective-permute-done.4.refs_2_, bf16[800,128]{1,0:T(8,128)(2,1)S(1)} %get-tuple-element.26.refs_1_.refs_3_, ...), custom_call_target="tpu_custom_call" | custom-call | flops 1000 | bytes 1000 | tf_op jit(solution)/shard_map/score_3_6/pallas_call | solution.py:181
  35.5 0.5 collective-permute-done.8.refs_5_
  36.0 0.1 collective-permute-start.15
  36.1 0.9 %collective-permute-done.9.refs_6_ = bf16[800,128]{1,0:T(8,128)(2,1)S(1)} collective-permute-done((bf16[800,128]{1,0:T(8,128)(2,1)S(1)}, bf16[800,128]{1,0:T(8,128)(2,1)S(1)}, u32[]{:S(2)}, u32[]{:S(2)}) %collective-permute-start.9) | collective-permute-done | bytes 204832 | tf_op jit(solution)/shard_map/ppermute | solution.py:239
  37.0 0.0 collective-permute-start.16
  37.0 2.0 %collective-permute-done.7.refs_4_ = bf16[800,128]{1,0:T(8,128)(2,1)S(1)} collective-permute-done((bf16[800,128]{1,0:T(8,128)(2,1)S(1)}, bf16[800,128]{1,0:T(8,128)(2,1)S(1)}, u32[]{:S(2)}, u32[]{:S(2)}) %collective-permute-start.7) | collective-permute-done | bytes 204832 | tf_op jit(solution)/shard_map/ppermute | solution.py:239
  38.9 0.0 collective-permute-start.10
  38.9 0.0 collective-permute-done.13.refs_4_
  38.9 0.5 collective-permute-start.11
  39.5 0.0 collective-permute-done.14.refs_6_
  39.5 0.3 collective-permute-start.12
  39.8 0.0 collective-permute-done.15.refs_8_
  39.8 0.0 collective-permute-done.16.refs_10_
  39.8 3.7 %score_4_4.1.refs_10_ = f32[32,128]{1,0:T(8,128)S(1)} custom-call(bf16[512,128]{1,0:T(8,128)(2,1)S(1)} %collective-permute-done.2.refs_0_, bf16[512,128]{1,0:T(8,128)(2,1)S(1)} %collective-permute-done.3.refs_1_, bf16[512,128]{1,0:T(8,128)(2,1)S(1)} %collective-permute-done.4.refs_2_, bf16[512,128]{1,0:T(8,128)(2,1)S(1)} %get-tuple-element.36.refs_3_, ...), custom_call_target="tpu_custom_call" | custom-call | flops 1000 | bytes 1000 | tf_op jit(solution)/shard_map/score_4_4/pallas_call | solution.py:181
  43.4 0.0 collective-permute-done.10.refs_7_
  43.5 0.0 collective-permute-done.11.refs_8_
  43.5 0.0 collective-permute-done.12.refs_9_
  43.5 5.3 %score_4_6.1.refs_0_ = f32[32,128]{1,0:T(8,128)S(1)} custom-call(bf16[512,128]{1,0:T(8,128)(2,1)S(1)} %collective-permute-done.2.refs_0_, bf16[512,128]{1,0:T(8,128)(2,1)S(1)} %collective-permute-done.3.refs_1_, bf16[512,128]{1,0:T(8,128)(2,1)S(1)} %collective-permute-done.4.refs_2_, bf16[512,128]{1,0:T(8,128)(2,1)S(1)} %get-tuple-element.36.refs_3_, ...), custom_call_target="tpu_custom_call" | custom-call | flops 1000 | bytes 1000 | tf_op jit(solution)/shard_map/score_4_6/pallas_call | solution.py:181
  48.8 0.8 %collective-permute-start.19 = (f32[32,128]{1,0:T(8,128)S(1)}, f32[32,128]{1,0:T(8,128)S(1)}, u32[]{:S(2)}, u32[]{:S(2)}) collective-permute-start(f32[32,128]{1,0:T(8,128)S(1)} %score_4_6.1.refs_0_), channel_id=1, source_target_pairs={{0,16},{8,24},{16,0},{24,8},{1,17},{9,25},{17,1},{25,9},{2,18},{10... | collective-permute-start | bytes 49160 | tf_op jit(solution)/shard_map/ppermute | solution.py:242
  49.6 2.5 %collective-permute-start.18 = (f32[32,128]{1,0:T(8,128)S(1)}, f32[32,128]{1,0:T(8,128)S(1)}, u32[]{:S(2)}, u32[]{:S(2)}) collective-permute-start(f32[32,128]{1,0:T(8,128)S(1)} %score_4_6.1.refs_0_), channel_id=1, source_target_pairs={{0,24},{8,0},{16,8},{24,16},{1,25},{9,1},{17,9},{25,17},{2,26},{10... | collective-permute-start | bytes 49160 | tf_op jit(solution)/shard_map/ppermute | solution.py:242
  52.1 0.0 collective-permute-start.17
  52.1 2.0 %collective-permute-done.19.refs_3_ = f32[32,128]{1,0:T(8,128)S(1)} collective-permute-done((f32[32,128]{1,0:T(8,128)S(1)}, f32[32,128]{1,0:T(8,128)S(1)}, u32[]{:S(2)}, u32[]{:S(2)}) %collective-permute-start.19) | collective-permute-done | bytes 16416 | tf_op jit(solution)/shard_map/ppermute | solution.py:242
  54.1 0.0 collective-permute-done.18.refs_2_
  54.1 3.0 %collective-permute-done.17.refs_1_ = f32[32,128]{1,0:T(8,128)S(1)} collective-permute-done((f32[32,128]{1,0:T(8,128)S(1)}, f32[32,128]{1,0:T(8,128)S(1)}, u32[]{:S(2)}, u32[]{:S(2)}) %collective-permute-start.17) | collective-permute-done | bytes 16416 | tf_op jit(solution)/shard_map/ppermute | solution.py:242
  57.1 0.9 %finish.1 = f32[16,4,32]{2,1,0:T(4,128)} custom-call(f32[32,128]{1,0:T(8,128)S(1)} %score_4_6.1.refs_0_, f32[32,128]{1,0:T(8,128)S(1)} %collective-permute-done.17.refs_1_, f32[32,128]{1,0:T(8,128)S(1)} %collective-permute-done.18.refs_2_, f32[32,128]{1,0:T(8,128)S(1)} %collective-permute-done.19.refs_3_), custom_call_target="tpu_custom_call" | custom-call | tf_op jit(solution)/shard_map/finish/pallas_call | solution.py:216
  (4 shorter events, 0.0 us)
Async XLA Ops:
  1.4 1.0 %copy-start.8 = (bf16[12,128,128]{2,1,0:T(8,128)(2,1)S(1)}, bf16[12,128,128]{2,1,0:T(8,128)(2,1)}, u32[]{:S(2)}) copy-start(bf16[12,128,128]{2,1,0:T(8,128)(2,1)} %tiles.1) | copy-start | bytes 1179652
  2.4 10.3 %copy-start = (bf16[768,3072]{1,0:T(8,128)(2,1)S(1)}, bf16[768,3072]{1,0:T(8,128)(2,1)}, u32[]{:S(2)}) copy-start(bf16[768,3072]{1,0:T(8,128)(2,1)} %w_in.1) | copy-start | bytes 14155780
  2.4 10.3 %copy-start.1 = (bf16[3072,768]{1,0:T(8,128)(2,1)S(1)}, bf16[3072,768]{1,0:T(8,128)(2,1)}, u32[]{:S(2)}) copy-start(bf16[3072,768]{1,0:T(8,128)(2,1)} %w_out.1) | copy-start | bytes 14155780
  2.4 10.3 %copy-start.2 = (bf16[16,32,768]{2,1,0:T(8,128)(2,1)S(1)}, bf16[16,32,768]{2,1,0:T(8,128)(2,1)}, u32[]{:S(2)}) copy-start(bf16[16,32,768]{2,1,0:T(8,128)(2,1)} %param.12) | copy-start | bytes 2359300
  2.4 10.3 %copy-start.3 = (bf16[768,128]{1,0:T(8,128)(2,1)S(1)}, bf16[768,128]{1,0:T(8,128)(2,1)}, u32[]{:S(2)}) copy-start(bf16[768,128]{1,0:T(8,128)(2,1)} %proj.1) | copy-start | bytes 589828
  2.4 10.3 %copy-start.4 = (f32[3072]{0:T(1024)S(1)}, f32[3072]{0:T(1024)}, u32[]{:S(2)}) copy-start(f32[3072]{0:T(1024)} %b_in.1) | copy-start | bytes 36868
  2.4 10.3 %copy-start.5 = (f32[768]{0:T(1024)S(1)}, f32[768]{0:T(1024)}, u32[]{:S(2)}) copy-start(f32[768]{0:T(1024)} %b_out.1) | copy-start | bytes 9220
  2.4 10.3 %copy-start.6 = (f32[768]{0:T(1024)S(1)}, f32[768]{0:T(1024)}, u32[]{:S(2)}) copy-start(f32[768]{0:T(1024)} %gain.1) | copy-start | bytes 9220
  2.4 10.3 %copy-start.7 = (f32[768]{0:T(1024)S(1)}, f32[768]{0:T(1024)}, u32[]{:S(2)}) copy-start(f32[768]{0:T(1024)} %shift.1) | copy-start | bytes 9220
  2.6 17.2 %collective-permute-start.1 = (bf16[800,128]{1,0:T(8,128)(2,1)S(1)}, bf16[800,128]{1,0:T(8,128)(2,1)S(1)}, u32[]{:S(2)}, u32[]{:S(2)}) collective-permute-start(bf16[800,128]{1,0:T(8,128)(2,1)S(1)} %get-tuple-element.26.refs_1_.refs_3_), channel_id=1, source_target_pairs={{0,6},{1,7},{2,0},{3,1},{4,2},{5,3},{6,4},{7,5},{32,34},{33,35},{3... | collective-permute-start | bytes 614408 | tf_op jit(solution)/shard_map/ppermute | solution.py:239
  9.0 12.1 %collective-permute-start = (bf16[800,128]{1,0:T(8,128)(2,1)S(1)}, bf16[800,128]{1,0:T(8,128)(2,1)S(1)}, u32[]{:S(2)}, u32[]{:S(2)}) collective-permute-start(bf16[800,128]{1,0:T(8,128)(2,1)S(1)} %get-tuple-element.26.refs_1_.refs_3_), channel_id=1, source_target_pairs={{0,2},{1,3},{2,4},{3,5},{4,6},{5,7},{6,0},{7,1},{32,38},{33,39},{3... | collective-permute-start | bytes 614408 | tf_op jit(solution)/shard_map/ppermute | solution.py:239
  9.0 17.1 %collective-permute-start.6 = (bf16[800,128]{1,0:T(8,128)(2,1)S(1)}, bf16[800,128]{1,0:T(8,128)(2,1)S(1)}, u32[]{:S(2)}, u32[]{:S(2)}) collective-permute-start(bf16[800,128]{1,0:T(8,128)(2,1)S(1)} %get-tuple-element.26.refs_1_.refs_3_), channel_id=1, source_target_pairs={{0,7},{1,0},{2,1},{3,2},{4,3},{5,4},{6,5},{7,6},{32,33},{33,34},{3... | collective-permute-start | bytes 614408 | tf_op jit(solution)/shard_map/ppermute | solution.py:239
  12.7 13.4 %collective-permute-start.5 = (bf16[800,128]{1,0:T(8,128)(2,1)S(1)}, bf16[800,128]{1,0:T(8,128)(2,1)S(1)}, u32[]{:S(2)}, u32[]{:S(2)}) collective-permute-start(bf16[800,128]{1,0:T(8,128)(2,1)S(1)} %get-tuple-element.26.refs_1_.refs_3_), channel_id=1, source_target_pairs={{0,1},{1,2},{2,3},{3,4},{4,5},{5,6},{6,7},{7,0},{32,39},{33,32},{3... | collective-permute-start | bytes 614408 | tf_op jit(solution)/shard_map/ppermute | solution.py:239
  21.1 8.8 %collective-permute-start.4 = (bf16[512,128]{1,0:T(8,128)(2,1)S(1)}, bf16[512,128]{1,0:T(8,128)(2,1)S(1)}, u32[]{:S(2)}, u32[]{:S(2)}) collective-permute-start(bf16[512,128]{1,0:T(8,128)(2,1)S(1)} %encode.1.refs_0_), channel_id=1, source_target_pairs={{0,16},{8,24},{16,0},{24,8},{1,17},{9,25},{17,1},{25,9},{2,18},{10... | collective-permute-start | bytes 393224 | tf_op jit(solution)/shard_map/ppermute | solution.py:242
  24.1 6.4 %collective-permute-start.3 = (bf16[512,128]{1,0:T(8,128)(2,1)S(1)}, bf16[512,128]{1,0:T(8,128)(2,1)S(1)}, u32[]{:S(2)}, u32[]{:S(2)}) collective-permute-start(bf16[512,128]{1,0:T(8,128)(2,1)S(1)} %encode.1.refs_0_), channel_id=1, source_target_pairs={{0,24},{8,0},{16,8},{24,16},{1,25},{9,1},{17,9},{25,17},{2,26},{10... | collective-permute-start | bytes 393224 | tf_op jit(solution)/shard_map/ppermute | solution.py:242
  25.2 6.2 %collective-permute-start.2 = (bf16[512,128]{1,0:T(8,128)(2,1)S(1)}, bf16[512,128]{1,0:T(8,128)(2,1)S(1)}, u32[]{:S(2)}, u32[]{:S(2)}) collective-permute-start(bf16[512,128]{1,0:T(8,128)(2,1)S(1)} %encode.1.refs_0_), channel_id=1, source_target_pairs={{0,8},{8,16},{16,24},{24,0},{1,9},{9,17},{17,25},{25,1},{2,10},{10... | collective-permute-start | bytes 393224 | tf_op jit(solution)/shard_map/ppermute | solution.py:242
  26.1 9.9 %collective-permute-start.8 = (bf16[800,128]{1,0:T(8,128)(2,1)S(1)}, bf16[800,128]{1,0:T(8,128)(2,1)S(1)}, u32[]{:S(2)}, u32[]{:S(2)}) collective-permute-start(bf16[800,128]{1,0:T(8,128)(2,1)S(1)} %collective-permute-done.1.refs_5_.refs_7_.refs_9_), channel_id=1, source_target_pairs={{0,7},{1,0},{2,1},{3,2},{4,3},{5,4},{6,5},{7,6},{32,33},{33,34},{3... | collective-permute-start | bytes 614408 | tf_op jit(solution)/shard_map/ppermute | solution.py:239
  28.2 8.7 %collective-permute-start.9 = (bf16[800,128]{1,0:T(8,128)(2,1)S(1)}, bf16[800,128]{1,0:T(8,128)(2,1)S(1)}, u32[]{:S(2)}, u32[]{:S(2)}) collective-permute-start(bf16[800,128]{1,0:T(8,128)(2,1)S(1)} %collective-permute-done.refs_4_.refs_6_.refs_11_), channel_id=1, source_target_pairs={{0,2},{1,3},{2,4},{3,5},{4,6},{5,7},{6,0},{7,1},{32,38},{33,39},{3... | collective-permute-start | bytes 614408 | tf_op jit(solution)/shard_map/ppermute | solution.py:239
  29.9 9.1 %collective-permute-start.7 = (bf16[800,128]{1,0:T(8,128)(2,1)S(1)}, bf16[800,128]{1,0:T(8,128)(2,1)S(1)}, u32[]{:S(2)}, u32[]{:S(2)}) collective-permute-start(bf16[800,128]{1,0:T(8,128)(2,1)S(1)} %collective-permute-done.refs_4_.refs_6_.refs_11_), channel_id=1, source_target_pairs={{0,1},{1,2},{2,3},{3,4},{4,5},{5,6},{6,7},{7,0},{32,39},{33,32},{3... | collective-permute-start | bytes 614408 | tf_op jit(solution)/shard_map/ppermute | solution.py:239
  30.5 8.5 %collective-permute-start.13 = (bf16[800,128]{1,0:T(8,128)(2,1)S(1)}, bf16[800,128]{1,0:T(8,128)(2,1)S(1)}, u32[]{:S(2)}, u32[]{:S(2)}) collective-permute-start(bf16[800,128]{1,0:T(8,128)(2,1)S(1)} %collective-permute-done.5.refs_2_.refs_4_.refs_7_), channel_id=1, source_target_pairs={{0,32},{32,0},{1,33},{33,1},{2,34},{34,2},{3,35},{35,3},{4,36},{36... | collective-permute-start | bytes 614408 | tf_op jit(solution)/shard_map/ppermute | solution.py:245
  31.4 8.1 %collective-permute-start.14 = (bf16[800,128]{1,0:T(8,128)(2,1)S(1)}, bf16[800,128]{1,0:T(8,128)(2,1)S(1)}, u32[]{:S(2)}, u32[]{:S(2)}) collective-permute-start(bf16[800,128]{1,0:T(8,128)(2,1)S(1)} %collective-permute-done.6.refs_3_.refs_5_), channel_id=1, source_target_pairs={{0,32},{32,0},{1,33},{33,1},{2,34},{34,2},{3,35},{35,3},{4,36},{36... | collective-permute-start | bytes 614408 | tf_op jit(solution)/shard_map/ppermute | solution.py:245
  36.0 3.8 %collective-permute-start.15 = (bf16[800,128]{1,0:T(8,128)(2,1)S(1)}, bf16[800,128]{1,0:T(8,128)(2,1)S(1)}, u32[]{:S(2)}, u32[]{:S(2)}) collective-permute-start(bf16[800,128]{1,0:T(8,128)(2,1)S(1)} %collective-permute-done.refs_4_.refs_6_.refs_11_), channel_id=1, source_target_pairs={{0,32},{32,0},{1,33},{33,1},{2,34},{34,2},{3,35},{35,3},{4,36},{36... | collective-permute-start | bytes 614408 | tf_op jit(solution)/shard_map/ppermute | solution.py:245
  37.0 2.8 %collective-permute-start.16 = (bf16[800,128]{1,0:T(8,128)(2,1)S(1)}, bf16[800,128]{1,0:T(8,128)(2,1)S(1)}, u32[]{:S(2)}, u32[]{:S(2)}) collective-permute-start(bf16[800,128]{1,0:T(8,128)(2,1)S(1)} %collective-permute-done.1.refs_5_.refs_7_.refs_9_), channel_id=1, source_target_pairs={{0,32},{32,0},{1,33},{33,1},{2,34},{34,2},{3,35},{35,3},{4,36},{36... | collective-permute-start | bytes 614408 | tf_op jit(solution)/shard_map/ppermute | solution.py:245
  38.9 4.5 %collective-permute-start.10 = (bf16[800,128]{1,0:T(8,128)(2,1)S(1)}, bf16[800,128]{1,0:T(8,128)(2,1)S(1)}, u32[]{:S(2)}, u32[]{:S(2)}) collective-permute-start(bf16[800,128]{1,0:T(8,128)(2,1)S(1)} %collective-permute-done.7.refs_4_), channel_id=1, source_target_pairs={{0,32},{32,0},{1,33},{33,1},{2,34},{34,2},{3,35},{35,3},{4,36},{36... | collective-permute-start | bytes 614408 | tf_op jit(solution)/shard_map/ppermute | solution.py:245
  38.9 4.5 %collective-permute-start.11 = (bf16[800,128]{1,0:T(8,128)(2,1)S(1)}, bf16[800,128]{1,0:T(8,128)(2,1)S(1)}, u32[]{:S(2)}, u32[]{:S(2)}) collective-permute-start(bf16[800,128]{1,0:T(8,128)(2,1)S(1)} %collective-permute-done.8.refs_5_), channel_id=1, source_target_pairs={{0,32},{32,0},{1,33},{33,1},{2,34},{34,2},{3,35},{35,3},{4,36},{36... | collective-permute-start | bytes 614408 | tf_op jit(solution)/shard_map/ppermute | solution.py:245
  39.5 4.0 %collective-permute-start.12 = (bf16[800,128]{1,0:T(8,128)(2,1)S(1)}, bf16[800,128]{1,0:T(8,128)(2,1)S(1)}, u32[]{:S(2)}, u32[]{:S(2)}) collective-permute-start(bf16[800,128]{1,0:T(8,128)(2,1)S(1)} %collective-permute-done.9.refs_6_), channel_id=1, source_target_pairs={{0,32},{32,0},{1,33},{33,1},{2,34},{34,2},{3,35},{35,3},{4,36},{36... | collective-permute-start | bytes 614408 | tf_op jit(solution)/shard_map/ppermute | solution.py:245
  48.8 5.3 %collective-permute-start.19 = (f32[32,128]{1,0:T(8,128)S(1)}, f32[32,128]{1,0:T(8,128)S(1)}, u32[]{:S(2)}, u32[]{:S(2)}) collective-permute-start(f32[32,128]{1,0:T(8,128)S(1)} %score_4_6.1.refs_0_), channel_id=1, source_target_pairs={{0,16},{8,24},{16,0},{24,8},{1,17},{9,25},{17,1},{25,9},{2,18},{10... | collective-permute-start | bytes 49160 | tf_op jit(solution)/shard_map/ppermute | solution.py:242
  49.6 4.5 %collective-permute-start.18 = (f32[32,128]{1,0:T(8,128)S(1)}, f32[32,128]{1,0:T(8,128)S(1)}, u32[]{:S(2)}, u32[]{:S(2)}) collective-permute-start(f32[32,128]{1,0:T(8,128)S(1)} %score_4_6.1.refs_0_), channel_id=1, source_target_pairs={{0,24},{8,0},{16,8},{24,16},{1,25},{9,1},{17,9},{25,17},{2,26},{10... | collective-permute-start | bytes 49160 | tf_op jit(solution)/shard_map/ppermute | solution.py:242
  52.1 4.9 %collective-permute-start.17 = (f32[32,128]{1,0:T(8,128)S(1)}, f32[32,128]{1,0:T(8,128)S(1)}, u32[]{:S(2)}, u32[]{:S(2)}) collective-permute-start(f32[32,128]{1,0:T(8,128)S(1)} %score_4_6.1.refs_0_), channel_id=1, source_target_pairs={{0,8},{8,16},{16,24},{24,0},{1,9},{9,17},{17,25},{25,1},{2,10},{10... | collective-permute-start | bytes 49160 | tf_op jit(solution)/shard_map/ppermute | solution.py:242

commit v11 on v10

--- a/solution.py
+++ b/solution.py
@@ -53,7 +53,7 @@
         out[...] = turned[...].astype(jnp.bfloat16)
 
 
-def encode(tok, w_in, b_in, w_out, b_out, gain, shift, proj, queries, tokens, chunk=1536):
+def encode(tok, w_in, b_in, w_out, b_out, gain, shift, proj, queries, tokens, chunk=1024):
     rows, width = tok.shape
 
     def whole(a):

time: 58.2 us -> 58.3 us (level)
  transfers between devices with their start and end apart: 20 -> 20, of which waited for: 7 -> 7; matrix products, arithmetic and copies ran while one was open for 0% -> 0% of each run, Pallas kernels for 28% -> 29%
where the time goes in v11:
time: 58.3 us; the launch traced here: 58.1 us
  Pallas kernels  23.3 us (40%)
  starting transfers between devices  22.3 us (38%)
  waiting for transfers between devices  9.97 us (17%)
  local copies, waits for them, and re-layouts  1.69 us (3%)
  other arithmetic  0.71 us (1%)
    pallas_call x4, Pallas kernels, score(): pl.pallas_call(functools.partial(score_kernel, senders=tuple(blocks), ite...  14.7 us
    ppermute x7, starting transfers between devices, along(): return lax.ppermute(a, ('core', 'z'), ways)  12.7 us
    ppermute x6, starting transfers between devices, across(): return lax.ppermute(a, 'x', turn(X, k))  8.4 us
    pallas_call x1, Pallas kernels, encode(): pl.pallas_call(functools.partial(ffn_kernel, queries=queries, tokens=toke...  7.49 us
    ppermute x6, waiting for transfers between devices, across(): return lax.ppermute(a, 'x', turn(X, k))  5.7 us
    ppermute x7, waiting for transfers between devices, along(): return lax.ppermute(a, ('core', 'z'), ways)  4.25 us
    ppermute x7, starting transfers between devices, swap(): return lax.ppermute(a, 'core', turn(CORES, 1))  1.2 us
  transfers between devices with their start and end apart: 20, of which 7 were waited for; matrix products, arithmetic and copies ran while one was open for 0% of the time, Pallas kernels for 29%

profile of v11, /device:TPU:16, one launch (start us, length us, event | category | flops | bytes accessed | tf_op | source)
XLA Modules:
  0.0 58.1 jit_solution(14133470764898740229)
XLA Ops:
  0.0 0.7 %pad.4 = s32[512]{0:T(512)S(1)} pad(s32[12]{0:T(128)} %param.21, s32[]{:T(128)} %constant.1.clone.1), padding=0_500 | pad | bytes 2100 | tf_op jit(solution)/shard_map/jit(_pad)/pad | solution.py:108
  0.7 0.7 %bitcast_select_fusion = s32[4,512]{1,0:T(4,128)S(1)} fusion(s32[512,1,4]{0,2,1:T(4,128)} %param.22, s32[512]{0:T(512)} %bitcast.10), kind=kLoop, calls=%fused_computation.1 | loop fusion | flops 4096 | bytes 18432 | tf_op jit(solution)/shard_map/jit(_where)/select_n | solution.py:107
  1.4 0.0 copy-start.8
  1.4 1.0 %copy-done.8 = bf16[12,128,128]{2,1,0:T(8,128)(2,1)S(1)} copy-done((bf16[12,128,128]{2,1,0:T(8,128)(2,1)S(1)}, bf16[12,128,128]{2,1,0:T(8,128)(2,1)}, u32[]{:S(2)}) %copy-start.8) | copy-done | bytes 393240
  2.4 0.0 copy-start
  2.4 0.0 copy-start.4
  2.4 0.0 copy-start.5
  2.4 0.0 copy-start.6
  2.4 0.0 copy-start.7
  2.4 0.2 parcel.1
  2.6 6.4 %collective-permute-start.1 = (bf16[800,128]{1,0:T(8,128)(2,1)S(1)}, bf16[800,128]{1,0:T(8,128)(2,1)S(1)}, u32[]{:S(2)}, u32[]{:S(2)}) collective-permute-start(bf16[800,128]{1,0:T(8,128)(2,1)S(1)} %get-tuple-element.26.refs_1_.refs_3_), channel_id=1, source_target_pairs={{0,6},{1,7},{2,0},{3,1},{4,2},{5,3},{6,4},{7,5},{32,34},{33,35},{3... | collective-permute-start | bytes 614408 | tf_op jit(solution)/shard_map/ppermute | solution.py:239
  9.0 0.0 collective-permute-start
  9.0 3.7 %collective-permute-start.6 = (bf16[800,128]{1,0:T(8,128)(2,1)S(1)}, bf16[800,128]{1,0:T(8,128)(2,1)S(1)}, u32[]{:S(2)}, u32[]{:S(2)}) collective-permute-start(bf16[800,128]{1,0:T(8,128)(2,1)S(1)} %get-tuple-element.26.refs_1_.refs_3_), channel_id=1, source_target_pairs={{0,7},{1,0},{2,1},{3,2},{4,3},{5,4},{6,5},{7,6},{32,33},{33,34},{3... | collective-permute-start | bytes 614408 | tf_op jit(solution)/shard_map/ppermute | solution.py:239
  12.7 0.0 collective-permute-start.5
  12.7 0.0 copy-done
  12.7 0.0 copy-done.1
  12.7 0.0 copy-done.2
  12.7 0.0 copy-done.3
  12.7 0.0 copy-done.4
  12.7 0.0 copy-done.5
  12.7 0.0 copy-done.6
  12.7 0.0 copy-done.7
  12.8 7.5 %encode.1.refs_0_ = bf16[512,128]{1,0:T(8,128)(2,1)S(1)} custom-call(bf16[512,768]{1,0:T(8,128)(2,1)S(1)} %bitcast.8, bf16[768,3072]{1,0:T(8,128)(2,1)S(1)} %copy-done, f32[3072]{0:T(1024)S(1)} %copy-done.4, bf16[3072,768]{1,0:T(8,128)(2,1)S(1)} %copy-done.1, f32[768]{0:T(1024)S(1)} %copy-done.5, f32[768]{0:T(1024)S(1)} %copy-done.6, f32[768]{0:T(1024)S(1)} %copy-done.7, ...), custom_call_target="tpu_custom_call" | custom-call | flops 1000 | bytes 1000 | tf_op jit(solution)/shard_map/encode/pallas_call | solution.py:62
  20.3 0.0 collective-permute-done.1.refs_5_.refs_7_.refs_9_
  20.3 0.8 %collective-permute-done.refs_4_.refs_6_.refs_11_ = bf16[800,128]{1,0:T(8,128)(2,1)S(1)} collective-permute-done((bf16[800,128]{1,0:T(8,128)(2,1)S(1)}, bf16[800,128]{1,0:T(8,128)(2,1)S(1)}, u32[]{:S(2)}, u32[]{:S(2)}) %collective-permute-start) | collective-permute-done | bytes 204832 | tf_op jit(solution)/shard_map/ppermute | solution.py:239
  21.1 3.0 %collective-permute-start.4 = (bf16[512,128]{1,0:T(8,128)(2,1)S(1)}, bf16[512,128]{1,0:T(8,128)(2,1)S(1)}, u32[]{:S(2)}, u32[]{:S(2)}) collective-permute-start(bf16[512,128]{1,0:T(8,128)(2,1)S(1)} %encode.1.refs_0_), channel_id=1, source_target_pairs={{0,16},{8,24},{16,0},{24,8},{1,17},{9,25},{17,1},{25,9},{2,18},{10... | collective-permute-start | bytes 393224 | tf_op jit(solution)/shard_map/ppermute | solution.py:242
  24.1 1.1 %collective-permute-start.3 = (bf16[512,128]{1,0:T(8,128)(2,1)S(1)}, bf16[512,128]{1,0:T(8,128)(2,1)S(1)}, u32[]{:S(2)}, u32[]{:S(2)}) collective-permute-start(bf16[512,128]{1,0:T(8,128)(2,1)S(1)} %encode.1.refs_0_), channel_id=1, source_target_pairs={{0,24},{8,0},{16,8},{24,16},{1,25},{9,1},{17,9},{25,17},{2,26},{10... | collective-permute-start | bytes 393224 | tf_op jit(solution)/shard_map/ppermute | solution.py:242
  25.2 0.9 %collective-permute-start.2 = (bf16[512,128]{1,0:T(8,128)(2,1)S(1)}, bf16[512,128]{1,0:T(8,128)(2,1)S(1)}, u32[]{:S(2)}, u32[]{:S(2)}) collective-permute-start(bf16[512,128]{1,0:T(8,128)(2,1)S(1)} %encode.1.refs_0_), channel_id=1, source_target_pairs={{0,8},{8,16},{16,24},{24,0},{1,9},{9,17},{17,25},{25,1},{2,10},{10... | collective-permute-start | bytes 393224 | tf_op jit(solution)/shard_map/ppermute | solution.py:242
  26.1 0.0 collective-permute-done.6.refs_3_.refs_5_
  26.1 0.0 collective-permute-done.5.refs_2_.refs_4_.refs_7_
  26.1 2.5 %collective-permute-start.8 = (bf16[800,128]{1,0:T(8,128)(2,1)S(1)}, bf16[800,128]{1,0:T(8,128)(2,1)S(1)}, u32[]{:S(2)}, u32[]{:S(2)}) collective-permute-start(bf16[800,128]{1,0:T(8,128)(2,1)S(1)} %collective-permute-done.1.refs_5_.refs_7_.refs_9_), channel_id=1, source_target_pairs={{0,7},{1,0},{2,1},{3,2},{4,3},{5,4},{6,5},{7,6},{32,33},{33,34},{3... | collective-permute-start | bytes 614408 | tf_op jit(solution)/shard_map/ppermute | solution.py:239
  28.6 0.0 collective-permute-start.9
  28.6 1.6 %score_1_6.1 = (f32[32,128]{1,0:T(8,128)S(1)}, bf16[512,128]{1,0:T(8,128)(2,1)S(1)}) custom-call(bf16[512,128]{1,0:T(8,128)(2,1)S(1)} %encode.1.refs_0_, bf16[800,128]{1,0:T(8,128)(2,1)S(1)} %get-tuple-element.26.refs_1_.refs_3_, bf16[800,128]{1,0:T(8,128)(2,1)S(1)} %collective-permute-done.5.refs_2_.refs_4_.refs_7_, ...), custom_call_target="tpu_custom_call" | custom-call | flops 1000 | bytes 1000 | tf_op jit(solution)/shard_map/score_1_6/pallas_call | solution.py:181
  30.3 0.0 collective-permute-done.4.refs_2_
  30.3 0.1 collective-permute-start.7
  30.4 0.0 collective-permute-done.3.refs_1_
  30.4 0.3 collective-permute-start.13
  30.7 0.8 %collective-permute-done.2.refs_0_ = bf16[512,128]{1,0:T(8,128)(2,1)S(1)} collective-permute-done((bf16[512,128]{1,0:T(8,128)(2,1)S(1)}, bf16[512,128]{1,0:T(8,128)(2,1)S(1)}, u32[]{:S(2)}, u32[]{:S(2)}) %collective-permute-start.2) | collective-permute-done | bytes 131104 | tf_op jit(solution)/shard_map/ppermute | solution.py:242
  31.4 0.0 collective-permute-start.14
  31.4 4.1 %score_3_6.1.refs_12_ = f32[32,128]{1,0:T(8,128)S(1)} custom-call(bf16[512,128]{1,0:T(8,128)(2,1)S(1)} %collective-permute-done.2.refs_0_, bf16[512,128]{1,0:T(8,128)(2,1)S(1)} %collective-permute-done.3.refs_1_, bf16[512,128]{1,0:T(8,128)(2,1)S(1)} %collective-permute-done.4.refs_2_, bf16[800,128]{1,0:T(8,128)(2,1)S(1)} %get-tuple-element.26.refs_1_.refs_3_, ...), custom_call_target="tpu_custom_call" | custom-call | flops 1000 | bytes 1000 | tf_op jit(solution)/shard_map/score_3_6/pallas_call | solution.py:181
  35.5 0.5 collective-permute-done.8.refs_5_
  36.0 0.1 collective-permute-start.15
  36.1 1.4 %collective-permute-done.9.refs_6_ = bf16[800,128]{1,0:T(8,128)(2,1)S(1)} collective-permute-done((bf16[800,128]{1,0:T(8,128)(2,1)S(1)}, bf16[800,128]{1,0:T(8,128)(2,1)S(1)}, u32[]{:S(2)}, u32[]{:S(2)}) %collective-permute-start.9) | collective-permute-done | bytes 204832 | tf_op jit(solution)/shard_map/ppermute | solution.py:239
  37.5 0.0 collective-permute-start.16
  37.5 1.5 %collective-permute-done.7.refs_4_ = bf16[800,128]{1,0:T(8,128)(2,1)S(1)} collective-permute-done((bf16[800,128]{1,0:T(8,128)(2,1)S(1)}, bf16[800,128]{1,0:T(8,128)(2,1)S(1)}, u32[]{:S(2)}, u32[]{:S(2)}) %collective-permute-start.7) | collective-permute-done | bytes 204832 | tf_op jit(solution)/shard_map/ppermute | solution.py:239
  39.0 0.0 collective-permute-start.10
  39.0 0.0 collective-permute-done.13.refs_4_
  39.0 0.5 collective-permute-start.11
  39.6 0.0 collective-permute-done.14.refs_6_
  39.6 0.3 collective-permute-start.12
  39.9 0.0 collective-permute-done.15.refs_8_
  39.9 0.0 collective-permute-done.16.refs_10_
  39.9 3.7 %score_4_4.1.refs_10_ = f32[32,128]{1,0:T(8,128)S(1)} custom-call(bf16[512,128]{1,0:T(8,128)(2,1)S(1)} %collective-permute-done.2.refs_0_, bf16[512,128]{1,0:T(8,128)(2,1)S(1)} %collective-permute-done.3.refs_1_, bf16[512,128]{1,0:T(8,128)(2,1)S(1)} %collective-permute-done.4.refs_2_, bf16[512,128]{1,0:T(8,128)(2,1)S(1)} %get-tuple-element.36.refs_3_, ...), custom_call_target="tpu_custom_call" | custom-call | flops 1000 | bytes 1000 | tf_op jit(solution)/shard_map/score_4_4/pallas_call | solution.py:181
  43.5 0.0 collective-permute-done.10.refs_7_
  43.6 0.0 collective-permute-done.11.refs_8_
  43.6 0.0 collective-permute-done.12.refs_9_
  43.6 5.3 %score_4_6.1.refs_0_ = f32[32,128]{1,0:T(8,128)S(1)} custom-call(bf16[512,128]{1,0:T(8,128)(2,1)S(1)} %collective-permute-done.2.refs_0_, bf16[512,128]{1,0:T(8,128)(2,1)S(1)} %collective-permute-done.3.refs_1_, bf16[512,128]{1,0:T(8,128)(2,1)S(1)} %collective-permute-done.4.refs_2_, bf16[512,128]{1,0:T(8,128)(2,1)S(1)} %get-tuple-element.36.refs_3_, ...), custom_call_target="tpu_custom_call" | custom-call | flops 1000 | bytes 1000 | tf_op jit(solution)/shard_map/score_4_6/pallas_call | solution.py:181
  48.9 0.7 %collective-permute-start.19 = (f32[32,128]{1,0:T(8,128)S(1)}, f32[32,128]{1,0:T(8,128)S(1)}, u32[]{:S(2)}, u32[]{:S(2)}) collective-permute-start(f32[32,128]{1,0:T(8,128)S(1)} %score_4_6.1.refs_0_), channel_id=1, source_target_pairs={{0,16},{8,24},{16,0},{24,8},{1,17},{9,25},{17,1},{25,9},{2,18},{10... | collective-permute-start | bytes 49160 | tf_op jit(solution)/shard_map/ppermute | solution.py:242
  49.6 2.7 %collective-permute-start.18 = (f32[32,128]{1,0:T(8,128)S(1)}, f32[32,128]{1,0:T(8,128)S(1)}, u32[]{:S(2)}, u32[]{:S(2)}) collective-permute-start(f32[32,128]{1,0:T(8,128)S(1)} %score_4_6.1.refs_0_), channel_id=1, source_target_pairs={{0,24},{8,0},{16,8},{24,16},{1,25},{9,1},{17,9},{25,17},{2,26},{10... | collective-permute-start | bytes 49160 | tf_op jit(solution)/shard_map/ppermute | solution.py:242
  52.2 0.0 collective-permute-start.17
  52.2 2.0 %collective-permute-done.19.refs_3_ = f32[32,128]{1,0:T(8,128)S(1)} collective-permute-done((f32[32,128]{1,0:T(8,128)S(1)}, f32[32,128]{1,0:T(8,128)S(1)}, u32[]{:S(2)}, u32[]{:S(2)}) %collective-permute-start.19) | collective-permute-done | bytes 16416 | tf_op jit(solution)/shard_map/ppermute | solution.py:242
  54.2 0.0 collective-permute-done.18.refs_2_
  54.2 3.0 %collective-permute-done.17.refs_1_ = f32[32,128]{1,0:T(8,128)S(1)} collective-permute-done((f32[32,128]{1,0:T(8,128)S(1)}, f32[32,128]{1,0:T(8,128)S(1)}, u32[]{:S(2)}, u32[]{:S(2)}) %collective-permute-start.17) | collective-permute-done | bytes 16416 | tf_op jit(solution)/shard_map/ppermute | solution.py:242
  57.2 0.9 %finish.1 = f32[16,4,32]{2,1,0:T(4,128)} custom-call(f32[32,128]{1,0:T(8,128)S(1)} %score_4_6.1.refs_0_, f32[32,128]{1,0:T(8,128)S(1)} %collective-permute-done.17.refs_1_, f32[32,128]{1,0:T(8,128)S(1)} %collective-permute-done.18.refs_2_, f32[32,128]{1,0:T(8,128)S(1)} %collective-permute-done.19.refs_3_), custom_call_target="tpu_custom_call" | custom-call | tf_op jit(solution)/shard_map/finish/pallas_call | solution.py:216
  (4 shorter events, 0.0 us)
Async XLA Ops:
  1.4 1.0 %copy-start.8 = (bf16[12,128,128]{2,1,0:T(8,128)(2,1)S(1)}, bf16[12,128,128]{2,1,0:T(8,128)(2,1)}, u32[]{:S(2)}) copy-start(bf16[12,128,128]{2,1,0:T(8,128)(2,1)} %tiles.1) | copy-start | bytes 1179652
  2.4 10.3 %copy-start = (bf16[768,3072]{1,0:T(8,128)(2,1)S(1)}, bf16[768,3072]{1,0:T(8,128)(2,1)}, u32[]{:S(2)}) copy-start(bf16[768,3072]{1,0:T(8,128)(2,1)} %w_in.1) | copy-start | bytes 14155780
  2.4 10.3 %copy-start.1 = (bf16[3072,768]{1,0:T(8,128)(2,1)S(1)}, bf16[3072,768]{1,0:T(8,128)(2,1)}, u32[]{:S(2)}) copy-start(bf16[3072,768]{1,0:T(8,128)(2,1)} %w_out.1) | copy-start | bytes 14155780
  2.4 10.3 %copy-start.2 = (bf16[16,32,768]{2,1,0:T(8,128)(2,1)S(1)}, bf16[16,32,768]{2,1,0:T(8,128)(2,1)}, u32[]{:S(2)}) copy-start(bf16[16,32,768]{2,1,0:T(8,128)(2,1)} %param.12) | copy-start | bytes 2359300
  2.4 10.3 %copy-start.3 = (bf16[768,128]{1,0:T(8,128)(2,1)S(1)}, bf16[768,128]{1,0:T(8,128)(2,1)}, u32[]{:S(2)}) copy-start(bf16[768,128]{1,0:T(8,128)(2,1)} %proj.1) | copy-start | bytes 589828
  2.4 10.3 %copy-start.4 = (f32[3072]{0:T(1024)S(1)}, f32[3072]{0:T(1024)}, u32[]{:S(2)}) copy-start(f32[3072]{0:T(1024)} %b_in.1) | copy-start | bytes 36868
  2.4 10.3 %copy-start.5 = (f32[768]{0:T(1024)S(1)}, f32[768]{0:T(1024)}, u32[]{:S(2)}) copy-start(f32[768]{0:T(1024)} %b_out.1) | copy-start | bytes 9220
  2.4 10.3 %copy-start.6 = (f32[768]{0:T(1024)S(1)}, f32[768]{0:T(1024)}, u32[]{:S(2)}) copy-start(f32[768]{0:T(1024)} %gain.1) | copy-start | bytes 9220
  2.4 10.3 %copy-start.7 = (f32[768]{0:T(1024)S(1)}, f32[768]{0:T(1024)}, u32[]{:S(2)}) copy-start(f32[768]{0:T(1024)} %shift.1) | copy-start | bytes 9220
  2.6 17.6 %collective-permute-start.1 = (bf16[800,128]{1,0:T(8,128)(2,1)S(1)}, bf16[800,128]{1,0:T(8,128)(2,1)S(1)}, u32[]{:S(2)}, u32[]{:S(2)}) collective-permute-start(bf16[800,128]{1,0:T(8,128)(2,1)S(1)} %get-tuple-element.26.refs_1_.refs_3_), channel_id=1, source_target_pairs={{0,6},{1,7},{2,0},{3,1},{4,2},{5,3},{6,4},{7,5},{32,34},{33,35},{3... | collective-permute-start | bytes 614408 | tf_op jit(solution)/shard_map/ppermute | solution.py:239
  9.0 12.1 %collective-permute-start = (bf16[800,128]{1,0:T(8,128)(2,1)S(1)}, bf16[800,128]{1,0:T(8,128)(2,1)S(1)}, u32[]{:S(2)}, u32[]{:S(2)}) collective-permute-start(bf16[800,128]{1,0:T(8,128)(2,1)S(1)} %get-tuple-element.26.refs_1_.refs_3_), channel_id=1, source_target_pairs={{0,2},{1,3},{2,4},{3,5},{4,6},{5,7},{6,0},{7,1},{32,38},{33,39},{3... | collective-permute-start | bytes 614408 | tf_op jit(solution)/shard_map/ppermute | solution.py:239
  9.0 17.1 %collective-permute-start.6 = (bf16[800,128]{1,0:T(8,128)(2,1)S(1)}, bf16[800,128]{1,0:T(8,128)(2,1)S(1)}, u32[]{:S(2)}, u32[]{:S(2)}) collective-permute-start(bf16[800,128]{1,0:T(8,128)(2,1)S(1)} %get-tuple-element.26.refs_1_.refs_3_), channel_id=1, source_target_pairs={{0,7},{1,0},{2,1},{3,2},{4,3},{5,4},{6,5},{7,6},{32,33},{33,34},{3... | collective-permute-start | bytes 614408 | tf_op jit(solution)/shard_map/ppermute | solution.py:239
  12.7 13.4 %collective-permute-start.5 = (bf16[800,128]{1,0:T(8,128)(2,1)S(1)}, bf16[800,128]{1,0:T(8,128)(2,1)S(1)}, u32[]{:S(2)}, u32[]{:S(2)}) collective-permute-start(bf16[800,128]{1,0:T(8,128)(2,1)S(1)} %get-tuple-element.26.refs_1_.refs_3_), channel_id=1, source_target_pairs={{0,1},{1,2},{2,3},{3,4},{4,5},{5,6},{6,7},{7,0},{32,39},{33,32},{3... | collective-permute-start | bytes 614408 | tf_op jit(solution)/shard_map/ppermute | solution.py:239
  21.1 9.2 %collective-permute-start.4 = (bf16[512,128]{1,0:T(8,128)(2,1)S(1)}, bf16[512,128]{1,0:T(8,128)(2,1)S(1)}, u32[]{:S(2)}, u32[]{:S(2)}) collective-permute-start(bf16[512,128]{1,0:T(8,128)(2,1)S(1)} %encode.1.refs_0_), channel_id=1, source_target_pairs={{0,16},{8,24},{16,0},{24,8},{1,17},{9,25},{17,1},{25,9},{2,18},{10... | collective-permute-start | bytes 393224 | tf_op jit(solution)/shard_map/ppermute | solution.py:242
  24.1 6.3 %collective-permute-start.3 = (bf16[512,128]{1,0:T(8,128)(2,1)S(1)}, bf16[512,128]{1,0:T(8,128)(2,1)S(1)}, u32[]{:S(2)}, u32[]{:S(2)}) collective-permute-start(bf16[512,128]{1,0:T(8,128)(2,1)S(1)} %encode.1.refs_0_), channel_id=1, source_target_pairs={{0,24},{8,0},{16,8},{24,16},{1,25},{9,1},{17,9},{25,17},{2,26},{10... | collective-permute-start | bytes 393224 | tf_op jit(solution)/shard_map/ppermute | solution.py:242
  25.2 6.2 %collective-permute-start.2 = (bf16[512,128]{1,0:T(8,128)(2,1)S(1)}, bf16[512,128]{1,0:T(8,128)(2,1)S(1)}, u32[]{:S(2)}, u32[]{:S(2)}) collective-permute-start(bf16[512,128]{1,0:T(8,128)(2,1)S(1)} %encode.1.refs_0_), channel_id=1, source_target_pairs={{0,8},{8,16},{16,24},{24,0},{1,9},{9,17},{17,25},{25,1},{2,10},{10... | collective-permute-start | bytes 393224 | tf_op jit(solution)/shard_map/ppermute | solution.py:242
  26.1 9.9 %collective-permute-start.8 = (bf16[800,128]{1,0:T(8,128)(2,1)S(1)}, bf16[800,128]{1,0:T(8,128)(2,1)S(1)}, u32[]{:S(2)}, u32[]{:S(2)}) collective-permute-start(bf16[800,128]{1,0:T(8,128)(2,1)S(1)} %collective-permute-done.1.refs_5_.refs_7_.refs_9_), channel_id=1, source_target_pairs={{0,7},{1,0},{2,1},{3,2},{4,3},{5,4},{6,5},{7,6},{32,33},{33,34},{3... | collective-permute-start | bytes 614408 | tf_op jit(solution)/shard_map/ppermute | solution.py:239
  28.6 8.9 %collective-permute-start.9 = (bf16[800,128]{1,0:T(8,128)(2,1)S(1)}, bf16[800,128]{1,0:T(8,128)(2,1)S(1)}, u32[]{:S(2)}, u32[]{:S(2)}) collective-permute-start(bf16[800,128]{1,0:T(8,128)(2,1)S(1)} %collective-permute-done.refs_4_.refs_6_.refs_11_), channel_id=1, source_target_pairs={{0,2},{1,3},{2,4},{3,5},{4,6},{5,7},{6,0},{7,1},{32,38},{33,39},{3... | collective-permute-start | bytes 614408 | tf_op jit(solution)/shard_map/ppermute | solution.py:239
  30.3 8.8 %collective-permute-start.7 = (bf16[800,128]{1,0:T(8,128)(2,1)S(1)}, bf16[800,128]{1,0:T(8,128)(2,1)S(1)}, u32[]{:S(2)}, u32[]{:S(2)}) collective-permute-start(bf16[800,128]{1,0:T(8,128)(2,1)S(1)} %collective-permute-done.refs_4_.refs_6_.refs_11_), channel_id=1, source_target_pairs={{0,1},{1,2},{2,3},{3,4},{4,5},{5,6},{6,7},{7,0},{32,39},{33,32},{3... | collective-permute-start | bytes 614408 | tf_op jit(solution)/shard_map/ppermute | solution.py:239
  30.4 8.7 %collective-permute-start.13 = (bf16[800,128]{1,0:T(8,128)(2,1)S(1)}, bf16[800,128]{1,0:T(8,128)(2,1)S(1)}, u32[]{:S(2)}, u32[]{:S(2)}) collective-permute-start(bf16[800,128]{1,0:T(8,128)(2,1)S(1)} %collective-permute-done.5.refs_2_.refs_4_.refs_7_), channel_id=1, source_target_pairs={{0,32},{32,0},{1,33},{33,1},{2,34},{34,2},{3,35},{35,3},{4,36},{36... | collective-permute-start | bytes 614408 | tf_op jit(solution)/shard_map/ppermute | solution.py:245
  31.4 8.2 %collective-permute-start.14 = (bf16[800,128]{1,0:T(8,128)(2,1)S(1)}, bf16[800,128]{1,0:T(8,128)(2,1)S(1)}, u32[]{:S(2)}, u32[]{:S(2)}) collective-permute-start(bf16[800,128]{1,0:T(8,128)(2,1)S(1)} %collective-permute-done.6.refs_3_.refs_5_), channel_id=1, source_target_pairs={{0,32},{32,0},{1,33},{33,1},{2,34},{34,2},{3,35},{35,3},{4,36},{36... | collective-permute-start | bytes 614408 | tf_op jit(solution)/shard_map/ppermute | solution.py:245
  36.0 3.9 %collective-permute-start.15 = (bf16[800,128]{1,0:T(8,128)(2,1)S(1)}, bf16[800,128]{1,0:T(8,128)(2,1)S(1)}, u32[]{:S(2)}, u32[]{:S(2)}) collective-permute-start(bf16[800,128]{1,0:T(8,128)(2,1)S(1)} %collective-permute-done.refs_4_.refs_6_.refs_11_), channel_id=1, source_target_pairs={{0,32},{32,0},{1,33},{33,1},{2,34},{34,2},{3,35},{35,3},{4,36},{36... | collective-permute-start | bytes 614408 | tf_op jit(solution)/shard_map/ppermute | solution.py:245
  37.5 2.3 %collective-permute-start.16 = (bf16[800,128]{1,0:T(8,128)(2,1)S(1)}, bf16[800,128]{1,0:T(8,128)(2,1)S(1)}, u32[]{:S(2)}, u32[]{:S(2)}) collective-permute-start(bf16[800,128]{1,0:T(8,128)(2,1)S(1)} %collective-permute-done.1.refs_5_.refs_7_.refs_9_), channel_id=1, source_target_pairs={{0,32},{32,0},{1,33},{33,1},{2,34},{34,2},{3,35},{35,3},{4,36},{36... | collective-permute-start | bytes 614408 | tf_op jit(solution)/shard_map/ppermute | solution.py:245
  39.0 4.5 %collective-permute-start.10 = (bf16[800,128]{1,0:T(8,128)(2,1)S(1)}, bf16[800,128]{1,0:T(8,128)(2,1)S(1)}, u32[]{:S(2)}, u32[]{:S(2)}) collective-permute-start(bf16[800,128]{1,0:T(8,128)(2,1)S(1)} %collective-permute-done.7.refs_4_), channel_id=1, source_target_pairs={{0,32},{32,0},{1,33},{33,1},{2,34},{34,2},{3,35},{35,3},{4,36},{36... | collective-permute-start | bytes 614408 | tf_op jit(solution)/shard_map/ppermute | solution.py:245
  39.0 4.5 %collective-permute-start.11 = (bf16[800,128]{1,0:T(8,128)(2,1)S(1)}, bf16[800,128]{1,0:T(8,128)(2,1)S(1)}, u32[]{:S(2)}, u32[]{:S(2)}) collective-permute-start(bf16[800,128]{1,0:T(8,128)(2,1)S(1)} %collective-permute-done.8.refs_5_), channel_id=1, source_target_pairs={{0,32},{32,0},{1,33},{33,1},{2,34},{34,2},{3,35},{35,3},{4,36},{36... | collective-permute-start | bytes 614408 | tf_op jit(solution)/shard_map/ppermute | solution.py:245
  39.6 4.0 %collective-permute-start.12 = (bf16[800,128]{1,0:T(8,128)(2,1)S(1)}, bf16[800,128]{1,0:T(8,128)(2,1)S(1)}, u32[]{:S(2)}, u32[]{:S(2)}) collective-permute-start(bf16[800,128]{1,0:T(8,128)(2,1)S(1)} %collective-permute-done.9.refs_6_), channel_id=1, source_target_pairs={{0,32},{32,0},{1,33},{33,1},{2,34},{34,2},{3,35},{35,3},{4,36},{36... | collective-permute-start | bytes 614408 | tf_op jit(solution)/shard_map/ppermute | solution.py:245
  48.9 5.3 %collective-permute-start.19 = (f32[32,128]{1,0:T(8,128)S(1)}, f32[32,128]{1,0:T(8,128)S(1)}, u32[]{:S(2)}, u32[]{:S(2)}) collective-permute-start(f32[32,128]{1,0:T(8,128)S(1)} %score_4_6.1.refs_0_), channel_id=1, source_target_pairs={{0,16},{8,24},{16,0},{24,8},{1,17},{9,25},{17,1},{25,9},{2,18},{10... | collective-permute-start | bytes 49160 | tf_op jit(solution)/shard_map/ppermute | solution.py:242
  49.6 4.6 %collective-permute-start.18 = (f32[32,128]{1,0:T(8,128)S(1)}, f32[32,128]{1,0:T(8,128)S(1)}, u32[]{:S(2)}, u32[]{:S(2)}) collective-permute-start(f32[32,128]{1,0:T(8,128)S(1)} %score_4_6.1.refs_0_), channel_id=1, source_target_pairs={{0,24},{8,0},{16,8},{24,16},{1,25},{9,1},{17,9},{25,17},{2,26},{10... | collective-permute-start | bytes 49160 | tf_op jit(solution)/shard_map/ppermute | solution.py:242
  52.2 4.9 %collective-permute-start.17 = (f32[32,128]{1,0:T(8,128)S(1)}, f32[32,128]{1,0:T(8,128)S(1)}, u32[]{:S(2)}, u32[]{:S(2)}) collective-permute-start(f32[32,128]{1,0:T(8,128)S(1)} %score_4_6.1.refs_0_), channel_id=1, source_target_pairs={{0,8},{8,16},{16,24},{24,0},{1,9},{9,17},{17,25},{25,1},{2,10},{10... | collective-permute-start | bytes 49160 | tf_op jit(solution)/shard_map/ppermute | solution.py:242
